TPU v7x, 256 devices: a whole 4x4x8 slice. The times are simulated.
256 devices in a mesh: group: 8 (over z), patch: 32 (over x, y, core).
Axes of the slice: x: 4, y: 4, z: 8, core: 2. Of those that a mesh axis runs over, the one named last changes fastest.
Arguments:
- node_lat: bfloat16 [131072, 512], P(('group', 'patch')), may hold values from -6 to 6
- fine_edge_lat: bfloat16 [262144, 512], P(('group', 'patch')), may hold values from -6 to 6
- fine_send: int32 [262144], P(('group', 'patch')), may hold values from 0 to 767
- fine_recv: int32 [262144], P(('group', 'patch')), may hold values from 0 to 511
- border_rows: int32 [65536], P(('group', 'patch')), may hold values from 0 to 511
- coarse_edge_lat: bfloat16 [32768, 512], P('patch'), may hold values from -6 to 6
- coarse_send: int32 [32768], P('patch'), may hold values from 0 to 2047
- coarse_recv: int32 [32768], P('patch'), may hold values from 0 to 2047
- w_edge_in: bfloat16 [1536, 512], replicated, may hold values from -0.15625 to 0.15625
- w_edge_out: bfloat16 [512, 512], replicated, may hold values from -0.25 to 0.25
- edge_gain: float32 [512], replicated, may hold values from 0.25 to 1.75
- w_node_in: bfloat16 [1024, 512], replicated, may hold values from -0.1875 to 0.1875
- w_node_out: bfloat16 [512, 512], replicated, may hold values from -0.25 to 0.25
- node_gain: float32 [512], replicated, may hold values from 0.25 to 1.75
Outputs:
- node_new: bfloat16 [131072, 512], P(('group', 'patch'))
- fine_edge_new: bfloat16 [262144, 512], P(('group', 'patch'))
- coarse_edge_new: bfloat16 [32768, 512], P('patch')
All inputs are finite; a program needn't handle non-finite values.
Results may differ from a plain program's by a relative error of at most 0.0052.
Values may be sent and summed in bfloat16 or wider, within the bound.
No kernel may reach another device: no remote copies, remote signals or barrier semaphores. Data moves between devices by JAX's collectives and lax.ppermute only.
A program may use at most 64 MiB of HBM per device.

v0:
```python
import jax
import jax.numpy as jnp
from jax import lax
from jax.sharding import PartitionSpec as P


def extended_2(array, sides, width):
    for axis, dim in sides:
        devices, length = (lax.axis_size(axis), array.shape[dim])
        up = [(i, (i + 1) % devices) for i in range(devices)]
        down = [(j, i) for i, j in up]
        last = lax.slice_in_dim(array, length - width, length, axis=dim)
        first = lax.slice_in_dim(array, 0, width, axis=dim)
        before = lax.ppermute(last, axis, up)
        after = lax.ppermute(first, axis, down)
        array = jnp.concatenate([before, array, after], axis=dim)
    return array


def layer_norm(values):
    average = jnp.mean(values, axis=-1, keepdims=True)
    centred = values - average
    variance = jnp.mean(centred * centred, axis=-1, keepdims=True)
    return centred * lax.rsqrt(variance + 1e-05)


def edge_update(edges, senders, receivers, w_edge_in, w_edge_out, edge_gain):
    model_width = edges.shape[1]
    preact = jnp.dot(edges, w_edge_in[:model_width], preferred_element_type=jnp.float32)
    preact = preact + jnp.dot(
        senders, w_edge_in[model_width : 2 * model_width], preferred_element_type=jnp.float32
    )
    preact = preact + jnp.dot(
        receivers, w_edge_in[2 * model_width :], preferred_element_type=jnp.float32
    )
    hidden = jax.nn.silu(preact).astype(jnp.bfloat16)
    projected = jnp.dot(hidden, w_edge_out, preferred_element_type=jnp.float32)
    return (edges.astype(jnp.float32) + layer_norm(projected) * edge_gain).astype(jnp.bfloat16)


def pick_rows(indices, table_rows):
    columns = lax.broadcasted_iota(jnp.int32, (1, table_rows.shape[0]), 1)
    one_hot = (indices[:, None] == columns).astype(jnp.bfloat16)
    return jnp.dot(one_hot, table_rows, preferred_element_type=jnp.float32).astype(jnp.bfloat16)


def fetch_coarse(table_piece, send_ids, recv_ids):
    piece = lax.all_gather(table_piece, ("group", "patch"), axis=0, tiled=True)
    columns = lax.broadcasted_iota(jnp.int32, (1, piece.shape[0]), 1)
    send_hot = (send_ids[:, None] == columns).astype(jnp.bfloat16)
    recv_hot = (recv_ids[:, None] == columns).astype(jnp.bfloat16)
    return (
        jnp.dot(send_hot, piece, preferred_element_type=jnp.float32).astype(jnp.bfloat16),
        jnp.dot(recv_hot, piece, preferred_element_type=jnp.float32).astype(jnp.bfloat16),
    )


def sum_into(recv_ids, renewed, offset, row_count):
    targets = lax.broadcasted_iota(jnp.int32, (row_count, 1), 0) + offset
    hot = (recv_ids[None, :] == targets).astype(jnp.bfloat16)
    return jnp.dot(hot, renewed, preferred_element_type=jnp.float32)


def shards(
    node_lat,
    fine_edge_lat,
    fine_send,
    fine_recv,
    border_rows,
    coarse_edge_lat,
    coarse_send,
    coarse_recv,
    w_edge_in,
    w_edge_out,
    edge_gain,
    w_node_in,
    w_node_out,
    node_gain,
):
    model_width = node_lat.shape[1]
    node_rows = node_lat.shape[0]
    coarse_rows = node_rows // 64
    border = border_rows.shape[0] // 2
    picked = pick_rows(border_rows, node_lat).reshape(2, border, model_width)
    halo_rows = extended_2(picked, (("patch", 0),), 1)
    extended = jnp.concatenate([node_lat, halo_rows[0], halo_rows[3]], axis=0)
    fine_new = edge_update(
        fine_edge_lat,
        pick_rows(fine_send, extended),
        pick_rows(fine_recv, node_lat),
        w_edge_in,
        w_edge_out,
        edge_gain,
    )
    node_columns = lax.broadcasted_iota(jnp.int32, (1, node_rows), 1)
    recv_hot = (fine_recv[:, None] == node_columns).astype(jnp.bfloat16)
    fine_sum = lax.dot_general(
        recv_hot, fine_new, (((0,), (0,)), ((), ())), preferred_element_type=jnp.float32
    )
    group_index = lax.axis_index("group")
    patches = lax.axis_size("patch")
    table_piece = node_lat[:coarse_rows]
    senders, receivers = fetch_coarse(table_piece, coarse_send, coarse_recv)
    coarse_new = edge_update(coarse_edge_lat, senders, receivers, w_edge_in, w_edge_out, edge_gain)
    group_base = group_index * (patches * coarse_rows)
    coarse_sum = lax.psum_scatter(
        sum_into(coarse_recv, coarse_new, group_base, coarse_rows * lax.axis_size("patch")).astype(
            jnp.bfloat16
        ),
        "patch",
        scatter_dimension=0,
        tiled=True,
    ).astype(jnp.float32)
    summed_all = fine_sum.at[:coarse_rows].add(coarse_sum)
    incoming = summed_all.astype(jnp.bfloat16)
    preact = jnp.dot(node_lat, w_node_in[:model_width], preferred_element_type=jnp.float32)
    preact = preact + jnp.dot(incoming, w_node_in[model_width:], preferred_element_type=jnp.float32)
    node_hidden = jax.nn.silu(preact).astype(jnp.bfloat16)
    projected = jnp.dot(node_hidden, w_node_out, preferred_element_type=jnp.float32)
    node_new = (node_lat.astype(jnp.float32) + layer_norm(projected) * node_gain).astype(
        jnp.bfloat16
    )
    return (node_new, fine_new, coarse_new)


def solution(mesh):
    in_specs = (
        P(("group", "patch"), None),
        P(("group", "patch"), None),
        P(("group", "patch")),
        P(("group", "patch")),
        P(("group", "patch")),
        P("patch", None),
        P("patch"),
        P("patch"),
        P(),
        P(),
        P(),
        P(),
        P(),
        P(),
    )
    out_specs = (P(("group", "patch"), None), P(("group", "patch"), None), P("patch", None))
    return jax.shard_map(shards, mesh=mesh, in_specs=in_specs, out_specs=out_specs, check_vma=False)
```

profile of v0, /device:TPU:1, one launch (start us, length us, event | category | flops | bytes accessed | tf_op | source)
XLA Modules:
  0.0 238.7 jit_solution(14447851351422830378)
XLA Ops:
  7.2 0.0 copy-start
  7.2 0.0 all-gather.2.cloned.1.call-start
  7.2 1.3 slice.61
  8.6 0.0 all-gather.2.cloned.1.call-update
  8.6 0.0 reduce-scatter.2.cloned.1.call-start
  8.6 1.4 convolution_convert_fusion.1
  10.1 0.0 copy-start.3
  10.1 2.8 %collective-permute-start = (bf16[1,128,512]{2,1,0:T(8,128)(2,1)S(1)}, bf16[1,128,512]{2,1,0:T(8,128)(2,1)S(1)}, u32[]{:S(2)}, u32[]{:S(2)}) collective-permute-start(bf16[1,128,512]{2,1,0:T(8,128)(2,1)S(1)} %get-tuple-element.18), channel_id=1, source_target_pairs={{0,1},{1,2},{2,3},{3,4},{4,5},{5,6},{6,7},{7,8},{8,9},{9,10},{10,1... | collective-permute-start | bytes 393224 | tf_op jit(solution)/shard_map/ppermute | solution.py:14
  12.9 0.6 collective-permute-start.1
  13.5 3.4 %fusion.51 = f32[1024,512]{1,0:T(8,128)} fusion(bf16[1024,512]{1,0:T(8,128)(2,1)} %param.17, bf16[1536,512]{1,0:T(8,128)(2,1)} %param.24), kind=kOutput, calls=%fused_computation.58 | convolution fusion | flops 536870912 | bytes 3670016 | tf_op jit(solution)/shard_map/dot_general | solution.py:29
  16.9 0.0 copy-done.3
  16.9 0.0 copy-start.7
  16.9 0.0 copy-start.15
  16.9 3.1 %fusion.49 = f32[1024,512]{1,0:T(8,128)} fusion(bf16[1024,512]{1,0:T(8,128)(2,1)S(1)} %copy-done.3, bf16[1536,512]{1,0:T(8,128)(2,1)} %param.24), kind=kOutput, calls=%fused_computation.56 | convolution fusion | flops 536870912 | bytes 3670016 | tf_op jit(solution)/shard_map/dot_general | solution.py:29
  20.0 0.0 copy-done.7
  20.0 0.0 copy-done.15
  20.0 0.0 copy-start.2
  20.0 1.7 fusion.10
  21.8 0.0 copy-done.2
  21.8 0.0 copy-start.12
  21.8 1.3 copy.18
  23.1 1.3 copy.19
  24.4 0.0 collective-permute-done
  24.4 0.0 collective-permute-done.1
  24.4 0.0 copy-done.12
  24.4 4.0 %fusion.14 = f32[1024,512]{1,0:T(8,128)} fusion(s32[1024]{0:T(1024)S(1)} %copy-done.12, bf16[128,512]{1,0:T(8,128)(2,1)} %bitcast.3, bf16[128,512]{1,0:T(8,128)(2,1)S(1)} %bitcast.20, bf16[512,512]{1,0:T(8,128)(2,1)S(1)} %copy-done.7, bf16[1536,512]{1,0:T(8,128)(2,1)} %param.24), kind=kOutput, calls=%fused_computation.27 | convolution fusion | flops 1345847296 | bytes 3411968 | tf_op jit(solution)/shard_map/dot_general | solution.py:30
  28.5 0.0 copy-done
  28.5 4.3 %fusion.63 = (f32[1024]{0:T(1024)S(1)}, f32[1024,512]{0,1:T(8,128)S(1)}) fusion(bf16[512,512]{1,0:T(8,128)(2,1)S(1)} %copy-done, f32[1024,512]{1,0:T(8,128)} %fusion.51, f32[1024,512]{1,0:T(8,128)} %fusion.14, bf16[1024,512]{1,0:T(8,128)(2,1)} %fusion.10, bf16[1536,512]{1,0:T(8,128)(2,1)} %param.24), kind=kOutput, calls=%fused_computation.77 | convolution fusion | flops 1077935104 | bytes 8392704 | tf_op jit(solution)/shard_map/dot_general | solution.py:37
  32.8 0.0 copy-start.13
  32.8 0.3 multiply_reduce_fusion.1
  33.1 0.0 copy-start.14
  33.1 87.4 %all-gather.2.cloned.1.call-done = bf16[2048,512]{1,0:T(8,128)(2,1)} async-done(((bf16[8,512]{1,0:T(8,128)(2,1)}), bf16[2048,512]{1,0:T(8,128)(2,1)}) %all-gather.2.cloned.1.call-update) | async-done | bytes 2097168 | tf_op jit(solution)/shard_map/all_gather | solution.py:48
  120.5 0.0 copy-done.13
  120.5 5.9 %fusion.15 = f32[1024,512]{1,0:T(8,128)} fusion(bf16[2048,512]{1,0:T(8,128)(2,1)} %all-gather.2.cloned.1.call-done, s32[1024]{0:T(1024)S(1)} %copy-done.13, bf16[1536,512]{1,0:T(8,128)(2,1)} %param.24), kind=kOutput, calls=%fused_computation.28 | convolution fusion | flops 2686976000 | bytes 4722688 | tf_op jit(solution)/shard_map/dot_general | solution.py:30
  126.4 0.0 copy-done.14
  126.4 4.9 %fusion.8 = bf16[1024,512]{1,0:T(8,128)(2,1)} fusion(bf16[2048,512]{1,0:T(8,128)(2,1)} %all-gather.2.cloned.1.call-done, s32[1024]{0:T(1024)S(1)} %copy-done.14), kind=kOutput, calls=%fused_computation.18 | convolution fusion | flops 2150105088 | bytes 3149824 | tf_op jit(solution)/shard_map/dot_general | solution.py:54
  131.3 5.6 %fusion.60 = (f32[1024]{0:T(1024)S(1)}, f32[1024,512]{0,1:T(8,128)}) fusion(bf16[512,512]{1,0:T(8,128)(2,1)S(1)} %copy-done, f32[1024,512]{1,0:T(8,128)} %fusion.49, f32[1024,512]{1,0:T(8,128)} %fusion.15, bf16[1024,512]{1,0:T(8,128)(2,1)} %fusion.8, bf16[1536,512]{1,0:T(8,128)(2,1)} %param.24), kind=kOutput, calls=%fused_computation.76 | convolution fusion | flops 1077935104 | bytes 8392704 | tf_op jit(solution)/shard_map/dot_general | solution.py:37
  136.9 0.0 copy-start.10
  137.0 2.0 multiply_reduce_fusion
  139.0 0.2 copy-done.1
  139.2 0.0 copy-done.10
  139.2 3.6 %add_convert_fusion = (bf16[1024,512]{0,1:T(8,128)(2,1)S(1)}, bf16[1024,512]{0,1:T(8,128)(2,1)}) fusion(bf16[1024,512]{0,1:T(8,128)(2,1)} %copy.19, f32[1024,512]{0,1:T(8,128)S(1)} %copy-done.1, f32[1024]{0:T(1024)S(1)} %get-tuple-element.28, f32[1024]{0:T(1024)S(1)} %broadcast_multiply_fusion, f32[512]{0:T(512)S(1)} %copy-done.10, ...), kind=kLoop, calls=%fused_computation.8 | loop fusion | flops 6291456 | bytes 8407040 | tf_op jit(solution)/shard_map/convert_element_type | solution.py:38
  142.8 0.0 copy-start.5
  142.8 0.0 copy-start.9
  142.8 1.0 copy-done.5
  143.8 1.2 convolution_convert_fusion
  145.0 0.0 copy-start.6
  145.0 0.0 reduce-scatter.2.cloned.1.call-update
  145.0 0.0 copy-done.9
  145.0 1.4 fusion.40
  146.4 1.0 copy.17
  147.4 0.0 copy-done.6
  147.4 1.3 copy.22
  148.7 0.0 copy-done.4
  148.7 1.3 copy.21
  150.0 2.1 fusion.16
  152.1 74.1 %reduce-scatter.2.cloned.1.call-done = bf16[8,512]{1,0:T(8,128)(2,1)} async-done(((bf16[256,512]{1,0:T(8,128)(2,1)}), bf16[8,512]{1,0:T(8,128)(2,1)}) %reduce-scatter.2.cloned.1.call-update) | async-done | bytes 8208 | tf_op jit(solution)/shard_map/reduce_scatter | solution.py:106
  226.2 1.3 fusion.54
  227.5 2.9 %fusion.66 = (f32[512]{0:T(512)S(1)}, f32[512,512]{0,1:T(8,128)S(1)}) fusion(bf16[512,512]{1,0:T(8,128)(2,1)} %param.28, f32[512,512]{1,0:T(8,128)} %fusion.40, bf16[1024,512]{1,0:T(8,128)(2,1)} %param.27, f32[512,512]{1,0:T(8,128)} %fusion.54), kind=kOutput, calls=%fused_computation.78 | convolution fusion | flops 538967552 | bytes 4196352 | tf_op jit(solution)/shard_map/dot_general | solution.py:119
  230.5 0.2 multiply_reduce_fusion.2
  230.6 0.0 copy-done.8
  230.6 0.0 copy-done.11
  230.7 0.2 add_convert_fusion.2
  230.9 1.0 copy.20
  (11 shorter events, 0.1 us)
Async XLA Ops:
  7.2 21.3 %copy-start = (bf16[512,512]{1,0:T(8,128)(2,1)S(1)}, bf16[512,512]{1,0:T(8,128)(2,1)}, u32[]{:S(2)}) copy-start(bf16[512,512]{1,0:T(8,128)(2,1)} %param.25) | copy-start | bytes 1572868
  7.2 113.3 %all-gather.2.cloned.1.call-start = ((), (), s32[]{:S(2)}) async-start(), calls=%async_computation.1 | async-start | bytes 2105344 | tf_op jit(solution)/shard_map/all_gather | solution.py:48
  8.6 217.6 %reduce-scatter.2.cloned.1.call-start = ((), (), s32[]{:S(2)}) async-start(), calls=%async_computation.2 | async-start | bytes 270336 | tf_op jit(solution)/shard_map/reduce_scatter | solution.py:106
  10.1 6.8 %copy-start.3 = (bf16[1024,512]{1,0:T(8,128)(2,1)S(1)}, bf16[1024,512]{1,0:T(8,128)(2,1)}, u32[]{:S(2)}) copy-start(bf16[1024,512]{1,0:T(8,128)(2,1)} %param.21) | copy-start | bytes 3145732
  10.1 14.3 %collective-permute-start = (bf16[1,128,512]{2,1,0:T(8,128)(2,1)S(1)}, bf16[1,128,512]{2,1,0:T(8,128)(2,1)S(1)}, u32[]{:S(2)}, u32[]{:S(2)}) collective-permute-start(bf16[1,128,512]{2,1,0:T(8,128)(2,1)S(1)} %get-tuple-element.18), channel_id=1, source_target_pairs={{0,1},{1,2},{2,3},{3,4},{4,5},{5,6},{6,7},{7,8},{8,9},{9,10},{10,1... | collective-permute-start | bytes 393224 | tf_op jit(solution)/shard_map/ppermute | solution.py:14
  12.9 11.6 %collective-permute-start.1 = (bf16[1,128,512]{2,1,0:T(8,128)(2,1)S(1)}, bf16[1,128,512]{2,1,0:T(8,128)(2,1)}, u32[]{:S(2)}, u32[]{:S(2)}) collective-permute-start(bf16[1,128,512]{2,1,0:T(8,128)(2,1)S(1)} %get-tuple-element.19), channel_id=1, source_target_pairs={{1,0},{2,1},{3,2},{4,3},{5,4},{6,5},{7,6},{8,7},{9,8},{10,9},{11,1... | collective-permute-start | bytes 393224 | tf_op jit(solution)/shard_map/ppermute | solution.py:15
  16.9 3.1 %copy-start.7 = (bf16[512,512]{1,0:T(8,128)(2,1)S(1)}, bf16[512,512]{1,0:T(8,128)(2,1)}, u32[]{:S(2)}) copy-start(bf16[512,512]{1,0:T(8,128)(2,1)} %param.16) | copy-start | bytes 1572868
  16.9 3.1 %copy-start.15 = (s32[1024]{0:T(1024)S(1)}, s32[1024]{0:T(1024)}, u32[]{:S(2)}) copy-start(s32[1024]{0:T(1024)} %param.19) | copy-start | bytes 12292
  20.0 1.7 copy-start.2
  21.8 2.7 %copy-start.12 = (s32[1024]{0:T(1024)S(1)}, s32[1024]{0:T(1024)}, u32[]{:S(2)}) copy-start(s32[1024]{0:T(1024)} %param.18) | copy-start | bytes 12292
  32.8 87.7 %copy-start.13 = (s32[1024]{0:T(1024)S(1)}, s32[1024]{0:T(1024)}, u32[]{:S(2)}) copy-start(s32[1024]{0:T(1024)} %param.22) | copy-start | bytes 12292
  33.1 93.3 %copy-start.14 = (s32[1024]{0:T(1024)S(1)}, s32[1024]{0:T(1024)}, u32[]{:S(2)}) copy-start(s32[1024]{0:T(1024)} %param.23) | copy-start | bytes 12292
  136.9 2.2 copy-start.1
  136.9 2.2 copy-start.10
  142.8 1.0 copy-start.5
  142.8 2.2 copy-start.9
  145.0 2.4 %copy-start.6 = (bf16[1024,512]{0,1:T(8,128)(2,1)S(1)}, bf16[1024,512]{0,1:T(8,128)(2,1)}, u32[]{:S(2)}) copy-start(bf16[1024,512]{0,1:T(8,128)(2,1)} %copy-done.5) | copy-start | bytes 3145732
  146.4 2.3 copy-start.4
  227.5 3.1 %copy-start.8 = (bf16[512,512]{0,1:T(8,128)(2,1)S(1)}, bf16[512,512]{0,1:T(8,128)(2,1)}, u32[]{:S(2)}) copy-start(bf16[512,512]{0,1:T(8,128)(2,1)} %copy.17) | copy-start | bytes 1572868
  227.5 3.1 %copy-start.11 = (f32[512]{0:T(512)S(1)}, f32[512]{0:T(512)}, u32[]{:S(2)}) copy-start(f32[512]{0:T(512)} %param.29) | copy-start | bytes 6148
Sparse Core Ops, SparseCore 0:
  12.3 108.1 all-gather.1
  145.1 81.0 reduce-scatter.1
where the time goes:
time: 240 us; the launch traced here: 239 us
  waiting for transfers between devices  162 us (68%)
  matrix products  41.9 us (17%)
  between operations  14.2 us (6%)
  local copies, waits for them, and re-layouts  9.91 us (4%)
  other arithmetic  7.65 us (3%)
  starting transfers between devices  3.49 us (1%)
    all_gather x1, waiting for transfers between devices, fetch_coarse(): piece = lax.all_gather(table_piece, ('group', 'patch'), axis=0, tiled=True)  87.4 us
    reduce_scatter x1, waiting for transfers between devices, shards(): lax.psum_scatter(sum_into(coarse_recv, coarse_new, group_base, coarse_row...  74.1 us
    dot_general x2, matrix products, edge_update(): jnp.dot(senders, w_edge_in[model_width:2 * model_width], preferred_elemen...  9.94 us
    dot_general x2, matrix products, edge_update(): projected = jnp.dot(hidden, w_edge_out, preferred_element_type=jnp.float32)  9.89 us
    unnamed x38, local copies, waits for them, and re-layouts  8.54 us
    dot_general x2, matrix products, edge_update(): jnp.dot(edges, w_edge_in[:model_width], preferred_element_type=jnp.float32)  6.5 us
    dot_general x1, matrix products, fetch_coarse(): jnp.dot(recv_hot, piece, preferred_element_type=jnp.float32)  4.94 us
  transfers between devices with their start and end apart: 4, of which 2 were waited for; matrix products, arithmetic and copies ran while one was open for 12% of the time, Pallas kernels for 0%

commit v1 on v0

v1 whole, which is shorter than its diff:
```python
import jax
import jax.numpy as jnp
from jax import lax
from jax.experimental import pallas as pl
from jax.experimental.pallas import tpu as pltpu
from jax.sharding import PartitionSpec as P

D = 512
GROUPS = 8
SIDE = 4
CORES = 2
PATCHES = SIDE * SIDE * CORES
BORDER = 128
COARSE_ROWS = 8
EDGES = 1024
NODES = 512
EPS = 1e-05
BF = jnp.bfloat16
F32 = jnp.float32
BLOCK = 256
VMEM_LIMIT = 24 * 1024 * 1024


def dot(a, b):
    return jnp.dot(a, b, preferred_element_type=F32)


def silu(values):
    half = 0.5 * values
    return half * jnp.tanh(half) + half


def layer_norm(values):
    average = jnp.mean(values, axis=-1, keepdims=True)
    centred = values - average
    variance = jnp.mean(centred * centred, axis=-1, keepdims=True)
    return centred * lax.rsqrt(variance + EPS)


def column_of(ids_ref, first, rows):
    tiles = []
    for at in range(first // 128, (first + rows) // 128):
        row = jnp.broadcast_to(ids_ref[at : at + 1, :], (128, 128))
        tiles.append(row.T)
    return jnp.concatenate(tiles, axis=0).astype(jnp.int16)


def one_hot(column, width, offset=0):
    lanes = lax.broadcasted_iota(jnp.int16, column.shape, 1)
    one, zero = jnp.ones(column.shape, BF), jnp.zeros(column.shape, BF)
    return jnp.concatenate(
        [
            jnp.where(column == lanes + jnp.int16(offset + 128 * at), one, zero)
            for at in range(width // 128)
        ],
        axis=1,
    )


def one_hot_rows(ids_ref, count, height):
    rows = lax.broadcasted_iota(jnp.int16, (height, 128), 0)
    one, zero = jnp.ones((height, 128), BF), jnp.zeros((height, 128), BF)
    parts = []
    for at in range(count // 128):
        ids = jnp.broadcast_to(ids_ref[at : at + 1, :], (height, 128)).astype(jnp.int16)
        parts.append(jnp.where(ids == rows, one, zero))
    return jnp.concatenate(parts, axis=1)


def finish_edges(pre, edges, w_out, gain):
    hidden = silu(pre).astype(BF)
    projected = dot(hidden, w_out)
    return (edges.astype(F32) + layer_norm(projected) * gain).astype(BF)


def pick_kernel(node_ref, border_ref, low_ref, high_ref):
    hot = one_hot(column_of(border_ref, 0, 2 * BORDER), NODES)
    picked = dot(hot, node_ref[...]).astype(BF)
    low_ref[...] = picked[:BORDER]
    high_ref[...] = picked[BORDER:]


def project_kernel(node_ref, w_ref, out_ref):
    nodes = node_ref[...]
    out_ref[:NODES] = dot(nodes, w_ref[2 * D :]).astype(BF)
    out_ref[NODES:] = dot(nodes, w_ref[D : 2 * D]).astype(BF)


def fine_kernel(
    edge_ref, send_ref, recv_ref, table_ref, low_ref, high_ref, w_in_ref, w_out_ref, gain_ref,
    new_ref, sum_ref, halo_ref,
):
    halo_ref[:BORDER] = dot(low_ref[...], w_in_ref[D : 2 * D]).astype(BF)
    halo_ref[BORDER:] = dot(high_ref[...], w_in_ref[D : 2 * D]).astype(BF)
    gain = gain_ref[...]
    for first in range(0, EDGES, BLOCK):
        rows = slice(first, first + BLOCK)
        edges = edge_ref[rows]
        recv_hot = one_hot(column_of(recv_ref, first, BLOCK), NODES)
        send_hot = one_hot(column_of(send_ref, first, BLOCK), NODES + 2 * BORDER)
        pre = dot(edges, w_in_ref[:D])
        pre = pre + dot(recv_hot, table_ref[:NODES])
        pre = pre + dot(send_hot[:, :NODES], table_ref[NODES:])
        pre = pre + dot(send_hot[:, NODES:], halo_ref[...])
        new_ref[rows] = finish_edges(pre, edges, w_out_ref[...], gain)
    sum_ref[...] = dot(one_hot_rows(recv_ref, EDGES, NODES), new_ref[...])


def gather_kernel(send_ref, recv_ref, table_ref, send_out, recv_out):
    for first in range(0, EDGES, BLOCK):
        rows = slice(first, first + BLOCK)
        for ids_ref, out_ref in ((send_ref, send_out), (recv_ref, recv_out)):
            hot = one_hot(column_of(ids_ref, first, BLOCK), table_ref.shape[0])
            out_ref[rows] = dot(hot, table_ref[...]).astype(BF)


def coarse_kernel(
    edge_ref, send_ref, recv_ref, slot_ref, table_ref, send_part, recv_part, w_in_ref, w_out_ref,
    gain_ref, new_ref, mine_ref, theirs_ref,
):
    gain = gain_ref[...]
    half = table_ref.shape[0]
    for first in range(0, EDGES, BLOCK):
        rows = slice(first, first + BLOCK)
        edges = edge_ref[rows]
        pre = dot(edges, w_in_ref[:D])
        for ids_ref, part_ref, at in ((send_ref, send_part, 1), (recv_ref, recv_part, 2)):
            hot = one_hot(column_of(ids_ref, first, BLOCK), half, half)
            picked = (dot(hot, table_ref[...]) + part_ref[rows].astype(F32)).astype(BF)
            pre = pre + dot(picked, w_in_ref[at * D : (at + 1) * D])
        new_ref[rows] = finish_edges(pre, edges, w_out_ref[...], gain)
    height = 2 * mine_ref.shape[0]
    sums = dot(one_hot_rows(slot_ref, EDGES, height), new_ref[...])
    mine_ref[...] = sums[: height // 2]
    theirs_ref[...] = sums[height // 2 :].astype(BF)


def node_rows(nodes, incoming, w_in_ref, w_out_ref, gain):
    pre = dot(nodes, w_in_ref[:D]) + dot(incoming, w_in_ref[D:])
    projected = dot(silu(pre).astype(BF), w_out_ref[...])
    return (nodes.astype(F32) + layer_norm(projected) * gain).astype(BF)


def node_kernel(node_ref, sum_ref, w_in_ref, w_out_ref, gain_ref, out_ref, first_ref):
    for first in range(0, NODES, BLOCK):
        rows = slice(first, first + BLOCK)
        out_ref[rows] = node_rows(
            node_ref[rows], sum_ref[rows].astype(BF), w_in_ref, w_out_ref, gain_ref[...]
        )
    first_ref[...] = sum_ref[: first_ref.shape[0]]


def tail_kernel(
    node_ref, sum_ref, part0, part1, part2, part3, w_in_ref, w_out_ref, gain_ref, _, out_ref
):
    coarse = part0[...] + (
        part1[...].astype(F32) + part2[...].astype(F32) + part3[...].astype(F32)
    )
    total = sum_ref[...]
    total = jnp.concatenate([total[:COARSE_ROWS] + coarse, total[COARSE_ROWS:]], axis=0)
    out_ref[...] = node_rows(node_ref[...], total.astype(BF), w_in_ref, w_out_ref, gain_ref[...])


def shape(rows, dtype=BF):
    return jax.ShapeDtypeStruct((rows, D), dtype)


def call(kernel, outs, flops, *args, scratch=(), name=None):
    return pl.pallas_call(
        kernel,
        out_shape=outs,
        scratch_shapes=scratch,
        compiler_params=pltpu.CompilerParams(vmem_limit_bytes=VMEM_LIMIT),
        cost_estimate=pl.CostEstimate(flops=flops, bytes_accessed=4 << 20, transcendentals=0),
        name=name,
    )(*args)


def patch_pairs(move):
    pairs = []
    for x in range(SIDE):
        for y in range(SIDE):
            for core in range(CORES):
                to_x, to_y, to_core = move(x, y, core)
                pairs.append(
                    ((x * SIDE + y) * CORES + core, (to_x * SIDE + to_y) * CORES + to_core)
                )
    return pairs


def swap_x(k):
    return patch_pairs(lambda x, y, c: (x ^ k, y, c))


def swap_y(k):
    return patch_pairs(lambda x, y, c: (x, y ^ k, c))


def swap_one(k):
    return patch_pairs(lambda x, y, c: (x ^ k, y, c) if c == 0 else (x, y ^ k, c))


def swap_other(k):
    return patch_pairs(lambda x, y, c: (x, y ^ k, c) if c == 0 else (x ^ k, y, c))


SWAP_CORE = patch_pairs(lambda x, y, c: (x, y, c ^ 1))


def shards(
    node_lat, fine_edge_lat, fine_send, fine_recv, border_rows, coarse_edge_lat, coarse_send,
    coarse_recv, w_edge_in, w_edge_out, edge_gain, w_node_in, w_node_out, node_gain,
):
    group = lax.axis_index("group")
    patch = lax.axis_index("patch")
    my_core, my_y, my_x = patch % CORES, patch // CORES % SIDE, patch // (CORES * SIDE)
    edge_gain = edge_gain[None, :]
    node_gain = node_gain[None, :]
    grid = lambda ids: ids.reshape(-1, 128)

    part = node_lat[:COARSE_ROWS]
    for k in (1, 2, 4):
        other = lax.ppermute(part, "group", [(i, i ^ k) for i in range(GROUPS)])
        part = jnp.concatenate([part, other], axis=0)
    for swap in (swap_one, swap_other):
        part = jnp.concatenate(
            [part] + [lax.ppermute(part, "patch", swap(k)) for k in range(1, SIDE)], axis=0
        )
    other_half = lax.ppermute(part, "patch", SWAP_CORE)

    def place(ids):
        row, at = ids % COARSE_ROWS, ids // COARSE_ROWS
        core, y, x = at % CORES, at // CORES % SIDE ^ my_y, at // (CORES * SIDE) % SIDE ^ my_x
        z = at // PATCHES ^ group
        far = jnp.where(core == 0, y, x)
        near = jnp.where(core == 0, x, y)
        return (((core ^ my_core) * SIDE + far) * SIDE + near) * (GROUPS * COARSE_ROWS) + (
            z * COARSE_ROWS + row
        )

    row, at = coarse_recv % COARSE_ROWS, coarse_recv // COARSE_ROWS
    slot = (
        ((at % CORES ^ my_core) * SIDE + (at // (CORES * SIDE) % SIDE ^ my_x)) * SIDE
        + (at // CORES % SIDE ^ my_y)
    ) * COARSE_ROWS + row
    slot = grid(jnp.where(at // PATCHES == group, slot, -1))
    send_place, recv_place = grid(place(coarse_send)), grid(place(coarse_recv))

    low, high = call(
        pick_kernel, (shape(BORDER), shape(BORDER)), 2 * 256 * 512 * 512, node_lat,
        grid(border_rows), name="pick",
    )
    up = [(i, (i + 1) % PATCHES) for i in range(PATCHES)]
    down = [(j, i) for i, j in up]
    from_low = lax.ppermute(high, "patch", up)
    from_high = lax.ppermute(low, "patch", down)

    table = call(
        project_kernel, shape(2 * NODES), 4 * 512 * 512 * 512, node_lat, w_edge_in, name="project"
    )
    fine_new, fine_sum = call(
        fine_kernel, (shape(EDGES), shape(NODES, F32)), 3 << 30, fine_edge_lat, grid(fine_send),
        grid(fine_recv), table, from_low, from_high, w_edge_in, w_edge_out, edge_gain,
        scratch=[pltpu.VMEM((2 * BORDER, D), BF)], name="fine",
    )
    node_main, first_sum = call(
        node_kernel, (shape(NODES), shape(16, F32)), 768 << 20, node_lat, fine_sum, w_node_in,
        w_node_out, node_gain, name="node",
    )

    send_part, recv_part = call(
        gather_kernel, (shape(EDGES), shape(EDGES)), 2 << 30, send_place, recv_place, part,
        name="gather",
    )
    coarse_new, mine, theirs = call(
        coarse_kernel, (shape(EDGES), shape(128, F32), shape(128)), 4 << 30, coarse_edge_lat,
        send_place, recv_place, slot, other_half, send_part, recv_part, w_edge_in, w_edge_out,
        edge_gain, name="coarse",
    )

    total = mine + lax.ppermute(theirs, "patch", SWAP_CORE).astype(F32)
    width = total.shape[0] // SIDE
    sends = total.astype(BF)
    total = total[:width] + sum(
        lax.ppermute(sends[k * width : (k + 1) * width], "patch", swap_x(k)).astype(F32)
        for k in range(1, SIDE)
    )
    sends = total.astype(BF)
    last = [
        lax.ppermute(sends[k * COARSE_ROWS : (k + 1) * COARSE_ROWS], "patch", swap_y(k))
        for k in range(1, SIDE)
    ]

    whole = lambda rows: pl.BlockSpec((rows, D), lambda i: (0, 0))
    node_new = pl.pallas_call(
        tail_kernel,
        grid=(1,),
        out_shape=shape(NODES),
        in_specs=[whole(16), whole(16)] + [whole(COARSE_ROWS)] * 4
        + [whole(2 * D), whole(D), whole(1), pl.BlockSpec(memory_space=pl.ANY)],
        out_specs=whole(16),
        input_output_aliases={9: 0},
        compiler_params=pltpu.CompilerParams(vmem_limit_bytes=VMEM_LIMIT),
        name="tail",
    )(node_lat, first_sum, total[:COARSE_ROWS], *last, w_node_in, w_node_out, node_gain, node_main)
    return (node_new, fine_new, coarse_new)


def solution(mesh):
    in_specs = (
        P(("group", "patch"), None), P(("group", "patch"), None), P(("group", "patch")),
        P(("group", "patch")), P(("group", "patch")), P("patch", None), P("patch"), P("patch"),
        P(), P(), P(), P(), P(), P(),
    )
    out_specs = (P(("group", "patch"), None), P(("group", "patch"), None), P("patch", None))
    return jax.shard_map(shards, mesh=mesh, in_specs=in_specs, out_specs=out_specs, check_vma=False)
```

time: 240 us -> 76.6 us (0.32)
  the two profiles are of different devices: /device:TPU:1 before, /device:TPU:24 now
where the time goes in v1:
time: 76.6 us; the launch traced here: 76.4 us
  starting transfers between devices  36.5 us (48%)
  waiting for transfers between devices  19.9 us (26%)
  Pallas kernels  18.1 us (24%)
  between operations  0.96 us (1%)
  local copies, waits for them, and re-layouts  0.9 us (1%)
    pallas_call x6, Pallas kernels, call(): pl.pallas_call(kernel, out_shape=outs, scratch_shapes=scratch, compiler_p...  16.9 us
    ppermute x3, starting transfers between devices, shards(): other = lax.ppermute(part, 'group', [(i, i ^ k) for i in range(GROUPS)])  12 us
    ppermute x6, waiting for transfers between devices, shards(): lax.ppermute(part, 'patch', swap(k))  11.9 us
    ppermute x6, starting transfers between devices, shards(): lax.ppermute(part, 'patch', swap(k))  9.48 us
    ppermute x3, starting transfers between devices, shards(): lax.ppermute(sends[k * COARSE_ROWS:(k + 1) * COARSE_ROWS], 'patch', swap_...  7.93 us
    ppermute x3, waiting for transfers between devices, shards(): other = lax.ppermute(part, 'group', [(i, i ^ k) for i in range(GROUPS)])  5.34 us
    ppermute x3, starting transfers between devices, shards(): lax.ppermute(sends[k * width:(k + 1) * width], 'patch', swap_x(k))  4.78 us
    ppermute x3, waiting for transfers between devices, shards(): lax.ppermute(sends[k * COARSE_ROWS:(k + 1) * COARSE_ROWS], 'patch', swap_...  2.57 us
  transfers between devices with their start and end apart: 19, of which 10 were waited for; matrix products, arithmetic and copies ran while one was open for 0% of the time, Pallas kernels for 13%

profile of v1, /device:TPU:24, one launch (start us, length us, event | category | flops | bytes accessed | tf_op | source)
XLA Modules:
  0.0 76.4 jit_solution(1299565672286832123)
XLA Ops:
  0.6 0.0 copy-start.13
  0.6 0.0 copy-start.12
  0.7 0.7 constant_dynamic-update-slice_fusion.6
  1.4 1.9 %collective-permute-start.2 = (bf16[8,512]{1,0:T(8,128)(2,1)S(1)}, bf16[8,512]{1,0:T(8,128)(2,1)S(1)}, u32[]{:S(2)}, u32[]{:S(2)}) collective-permute-start(bf16[8,512]{1,0:T(8,128)(2,1)S(1)} %get-tuple-element.31), channel_id=1, source_target_pairs={{0,32},{32,0},{64,96},{96,64},{128,160},{160,128},{192,224},{224,1... | collective-permute-start | bytes 24584 | tf_op jit(solution)/shard_map/ppermute | solution.py:223
  3.3 1.7 %collective-permute-done.2 = bf16[8,512]{1,0:T(8,128)(2,1)S(1)} collective-permute-done((bf16[8,512]{1,0:T(8,128)(2,1)S(1)}, bf16[8,512]{1,0:T(8,128)(2,1)S(1)}, u32[]{:S(2)}, u32[]{:S(2)}) %collective-permute-start.2) | collective-permute-done | bytes 8224 | tf_op jit(solution)/shard_map/ppermute | solution.py:223
  5.0 3.3 %collective-permute-start.3 = (bf16[16,512]{1,0:T(8,128)(2,1)S(1)}, bf16[16,512]{1,0:T(8,128)(2,1)S(1)}, u32[]{:S(2)}, u32[]{:S(2)}) collective-permute-start(bf16[16,512]{1,0:T(8,128)(2,1)S(1)} %pad_maximum_fusion.2), channel_id=1, source_target_pairs={{0,64},{32,96},{64,0},{96,32},{128,192},{160,224},{192,128},{224,1... | collective-permute-start | bytes 49160 | tf_op jit(solution)/shard_map/ppermute | solution.py:223
  8.3 1.7 %collective-permute-done.3 = bf16[16,512]{1,0:T(8,128)(2,1)S(1)} collective-permute-done((bf16[16,512]{1,0:T(8,128)(2,1)S(1)}, bf16[16,512]{1,0:T(8,128)(2,1)S(1)}, u32[]{:S(2)}, u32[]{:S(2)}) %collective-permute-start.3) | collective-permute-done | bytes 16416 | tf_op jit(solution)/shard_map/ppermute | solution.py:223
  10.0 6.8 %collective-permute-start.4 = (bf16[32,512]{1,0:T(8,128)(2,1)S(1)}, bf16[32,512]{1,0:T(8,128)(2,1)S(1)}, u32[]{:S(2)}, u32[]{:S(2)}) collective-permute-start(bf16[32,512]{1,0:T(8,128)(2,1)S(1)} %pad_maximum_fusion.1), channel_id=1, source_target_pairs={{0,128},{32,160},{64,192},{96,224},{128,0},{160,32},{192,64},{224,... | collective-permute-start | bytes 98312 | tf_op jit(solution)/shard_map/ppermute | solution.py:223
  16.9 1.9 %collective-permute-done.4 = bf16[32,512]{1,0:T(8,128)(2,1)S(1)} collective-permute-done((bf16[32,512]{1,0:T(8,128)(2,1)S(1)}, bf16[32,512]{1,0:T(8,128)(2,1)S(1)}, u32[]{:S(2)}, u32[]{:S(2)}) %collective-permute-start.4) | collective-permute-done | bytes 32800 | tf_op jit(solution)/shard_map/ppermute | solution.py:223
  18.7 1.5 %collective-permute-start.5 = (bf16[64,512]{1,0:T(8,128)(2,1)S(1)}, bf16[64,512]{1,0:T(8,128)(2,1)S(1)}, u32[]{:S(2)}, u32[]{:S(2)}) collective-permute-start(bf16[64,512]{1,0:T(8,128)(2,1)S(1)} %pad_maximum_fusion), channel_id=1, source_target_pairs={{0,8},{1,3},{2,10},{3,1},{4,12},{5,7},{6,14},{7,5},{8,0},{9,11},{1... | collective-permute-start | bytes 196616 | tf_op jit(solution)/shard_map/ppermute | solution.py:227
  20.2 2.7 %collective-permute-start.6 = (bf16[64,512]{1,0:T(8,128)(2,1)S(1)}, bf16[64,512]{1,0:T(8,128)(2,1)S(1)}, u32[]{:S(2)}, u32[]{:S(2)}) collective-permute-start(bf16[64,512]{1,0:T(8,128)(2,1)S(1)} %pad_maximum_fusion), channel_id=1, source_target_pairs={{0,16},{1,5},{2,18},{3,7},{4,20},{5,1},{6,22},{7,3},{8,24},{9,13},... | collective-permute-start | bytes 196616 | tf_op jit(solution)/shard_map/ppermute | solution.py:227
  23.0 0.5 collective-permute-start.7
  23.5 0.0 collective-permute-done.5
  23.5 2.5 %collective-permute-done.6 = bf16[64,512]{1,0:T(8,128)(2,1)S(1)} collective-permute-done((bf16[64,512]{1,0:T(8,128)(2,1)S(1)}, bf16[64,512]{1,0:T(8,128)(2,1)S(1)}, u32[]{:S(2)}, u32[]{:S(2)}) %collective-permute-start.6) | collective-permute-done | bytes 65568 | tf_op jit(solution)/shard_map/ppermute | solution.py:227
  26.0 2.4 %collective-permute-done.7 = bf16[64,512]{1,0:T(8,128)(2,1)S(1)} collective-permute-done((bf16[64,512]{1,0:T(8,128)(2,1)S(1)}, bf16[64,512]{1,0:T(8,128)(2,1)S(1)}, u32[]{:S(2)}, u32[]{:S(2)}) %collective-permute-start.7) | collective-permute-done | bytes 65568 | tf_op jit(solution)/shard_map/ppermute | solution.py:227
  28.5 0.8 %collective-permute-start.8 = (bf16[256,512]{1,0:T(8,128)(2,1)S(1)}, bf16[256,512]{1,0:T(8,128)(2,1)S(1)}, u32[]{:S(2)}, u32[]{:S(2)}) collective-permute-start(bf16[256,512]{1,0:T(8,128)(2,1)S(1)} %get-tuple-element.35), channel_id=1, source_target_pairs={{0,2},{1,9},{2,0},{3,11},{4,6},{5,13},{6,4},{7,15},{8,10},{9,1},{1... | collective-permute-start | bytes 786440 | tf_op jit(solution)/shard_map/ppermute | solution.py:227
  29.3 0.9 %collective-permute-start.9 = (bf16[256,512]{1,0:T(8,128)(2,1)S(1)}, bf16[256,512]{1,0:T(8,128)(2,1)S(1)}, u32[]{:S(2)}, u32[]{:S(2)}) collective-permute-start(bf16[256,512]{1,0:T(8,128)(2,1)S(1)} %get-tuple-element.35), channel_id=1, source_target_pairs={{0,4},{1,17},{2,6},{3,19},{4,0},{5,21},{6,2},{7,23},{8,12},{9,25},... | collective-permute-start | bytes 786440 | tf_op jit(solution)/shard_map/ppermute | solution.py:227
  30.2 3.0 %collective-permute-start.10 = (bf16[256,512]{1,0:T(8,128)(2,1)S(1)}, bf16[256,512]{1,0:T(8,128)(2,1)S(1)}, u32[]{:S(2)}, u32[]{:S(2)}) collective-permute-start(bf16[256,512]{1,0:T(8,128)(2,1)S(1)} %get-tuple-element.35), channel_id=1, source_target_pairs={{0,6},{1,25},{2,4},{3,27},{4,2},{5,29},{6,0},{7,31},{8,14},{9,17},... | collective-permute-start | bytes 786440 | tf_op jit(solution)/shard_map/ppermute | solution.py:227
  33.2 1.7 %collective-permute-done.8 = bf16[256,512]{1,0:T(8,128)(2,1)S(1)} collective-permute-done((bf16[256,512]{1,0:T(8,128)(2,1)S(1)}, bf16[256,512]{1,0:T(8,128)(2,1)S(1)}, u32[]{:S(2)}, u32[]{:S(2)}) %collective-permute-start.8) | collective-permute-done | bytes 262176 | tf_op jit(solution)/shard_map/ppermute | solution.py:227
  34.9 2.5 %collective-permute-done.9 = bf16[256,512]{1,0:T(8,128)(2,1)S(1)} collective-permute-done((bf16[256,512]{1,0:T(8,128)(2,1)S(1)}, bf16[256,512]{1,0:T(8,128)(2,1)S(1)}, u32[]{:S(2)}, u32[]{:S(2)}) %collective-permute-start.9) | collective-permute-done | bytes 262176 | tf_op jit(solution)/shard_map/ppermute | solution.py:227
  37.5 2.7 %collective-permute-done.10 = bf16[256,512]{1,0:T(8,128)(2,1)S(1)} collective-permute-done((bf16[256,512]{1,0:T(8,128)(2,1)S(1)}, bf16[256,512]{1,0:T(8,128)(2,1)S(1)}, u32[]{:S(2)}, u32[]{:S(2)}) %collective-permute-start.10) | collective-permute-done | bytes 262176 | tf_op jit(solution)/shard_map/ppermute | solution.py:227
  40.2 0.1 collective-permute-start.11
  40.4 0.0 copy-done.13
  40.4 0.0 copy-done.12
  40.4 0.0 copy-start.3
  40.4 0.0 copy-start.6
  40.5 0.0 copy-start.8
  40.5 0.0 copy-start.11
  40.5 2.4 %gather.1 = (bf16[1024,512]{1,0:T(8,128)(2,1)S(1)}, bf16[1024,512]{1,0:T(8,128)(2,1)S(1)}) custom-call(s32[8,128]{1,0:T(8,128)S(1)} %get-tuple-element.52.send_ref, s32[8,128]{1,0:T(8,128)S(1)} %get-tuple-element.51.recv_ref, bf16[1024,512]{1,0:T(8,128)(2,1)S(1)} %constant_dynamic-update-slice_fusion.7.table_ref), custom_call_target="tpu_custom_call" | custom-call | flops 2147483648 | bytes 4194304 | tf_op jit(solution)/shard_map/gather/pallas_call | solution.py:169
  42.9 0.1 collective-permute-done.11.table_ref
  43.0 0.0 copy-start
  43.0 0.0 copy-start.5
  43.0 6.8 %coarse.1 = (bf16[1024,512]{1,0:T(8,128)(2,1)}, f32[128,512]{1,0:T(8,128)S(1)}, bf16[128,512]{1,0:T(8,128)(2,1)S(1)}) custom-call(bf16[1024,512]{1,0:T(8,128)(2,1)S(1)} %copy-done.6, s32[8,128]{1,0:T(8,128)S(1)} %get-tuple-element.52.send_ref, s32[8,128]{1,0:T(8,128)S(1)} %get-tuple-element.51.recv_ref, s32[8,128]{1,0:T(8,128)S(1)} %get-tuple-element.50.slot_ref, ...), custom_call_target="tpu_custom_call" | custom-call | flops 4294967296 | bytes 4194304 | tf_op jit(solution)/shard_map/coarse/pallas_call | solution.py:169
  49.8 0.3 collective-permute-start.12
  50.2 0.0 copy-done.5
  50.2 0.3 pick.1
  50.5 0.2 collective-permute-start
  50.8 1.6 %collective-permute-start.1 = (bf16[128,512]{1,0:T(8,128)(2,1)S(1)}, bf16[128,512]{1,0:T(8,128)(2,1)S(1)}, u32[]{:S(2)}, u32[]{:S(2)}) collective-permute-start(bf16[128,512]{1,0:T(8,128)(2,1)S(1)} %get-tuple-element.15), channel_id=1, source_target_pairs={{1,0},{2,1},{3,2},{4,3},{5,4},{6,5},{7,6},{8,7},{9,8},{10,9},{11,1... | collective-permute-start | bytes 393224 | tf_op jit(solution)/shard_map/ppermute | solution.py:256
  52.4 0.7 project.1.table_ref
  53.1 0.0 collective-permute-done.12
  53.1 0.1 collective-permute-start.13
  53.2 2.5 %collective-permute-start.14 = (bf16[32,512]{1,0:T(8,128)(2,1)S(1)}, bf16[32,512]{1,0:T(8,128)(2,1)S(1)}, u32[]{:S(2)}, u32[]{:S(2)}) collective-permute-start(bf16[32,512]{1,0:T(8,128)(2,1)S(1)} %get-tuple-element.34), channel_id=1, source_target_pairs={{0,16},{1,17},{2,18},{3,19},{4,20},{5,21},{6,22},{7,23},{8,24},{9,... | collective-permute-start | bytes 98312 | tf_op jit(solution)/shard_map/ppermute | solution.py:285
  55.8 2.1 %collective-permute-start.15 = (bf16[32,512]{1,0:T(8,128)(2,1)S(1)}, bf16[32,512]{1,0:T(8,128)(2,1)S(1)}, u32[]{:S(2)}, u32[]{:S(2)}) collective-permute-start(bf16[32,512]{1,0:T(8,128)(2,1)S(1)} %get-tuple-element.33), channel_id=1, source_target_pairs={{0,24},{1,25},{2,26},{3,27},{4,28},{5,29},{6,30},{7,31},{8,16},{9,... | collective-permute-start | bytes 98312 | tf_op jit(solution)/shard_map/ppermute | solution.py:285
  57.9 0.0 collective-permute-done.low_ref
  57.9 0.0 collective-permute-done.1.high_ref
  57.9 0.0 copy-done.7
  57.9 0.0 copy-done.9
  57.9 0.0 copy-done.10
  58.0 0.0 copy-start.1
  58.0 0.0 copy-start.2
  58.0 0.0 copy-start.4
  58.0 4.4 %fine.1 = (bf16[1024,512]{1,0:T(8,128)(2,1)}, f32[512,512]{1,0:T(8,128)S(1)}) custom-call(bf16[1024,512]{1,0:T(8,128)(2,1)S(1)} %copy-done.7, s32[8,128]{1,0:T(8,128)S(1)} %bitcast.14, s32[8,128]{1,0:T(8,128)S(1)} %bitcast.15, bf16[1024,512]{1,0:T(8,128)(2,1)S(1)} %project.1.table_ref, bf16[128,512]{1,0:T(8,128)(2,1)S(1)} %collective-permute-done.low_ref, ...), custom_call_target="tpu_custom_call" | custom-call | flops 3221225472 | bytes 4194304 | tf_op jit(solution)/shard_map/fine/pallas_call | solution.py:169
  62.4 0.0 collective-permute-done.13
  62.4 0.0 collective-permute-done.14
  62.4 0.0 collective-permute-done.15
  62.5 0.3 collective-permute-start.16
  62.8 7.6 %collective-permute-start.17 = (bf16[8,512]{1,0:T(8,128)(2,1)S(1)}, bf16[8,512]{1,0:T(8,128)(2,1)S(1)}, u32[]{:S(2)}, u32[]{:S(2)}) collective-permute-start(bf16[8,512]{1,0:T(8,128)(2,1)S(1)} %get-tuple-element.42), channel_id=1, source_target_pairs={{0,4},{1,5},{2,6},{3,7},{4,0},{5,1},{6,2},{7,3},{8,12},{9,13},{10,... | collective-permute-start | bytes 24584 | tf_op jit(solution)/shard_map/ppermute | solution.py:290
  70.4 0.0 collective-permute-start.18
  70.4 0.0 copy-done.1
  70.4 2.3 %node.1 = (bf16[512,512]{1,0:T(8,128)(2,1)}, f32[16,512]{1,0:T(8,128)S(1)}) custom-call(bf16[512,512]{1,0:T(8,128)(2,1)S(1)} %copy-done, f32[512,512]{1,0:T(8,128)S(1)} %get-tuple-element.16.sum_ref, bf16[1024,512]{1,0:T(8,128)(2,1)S(1)} %copy-done.1, bf16[512,512]{1,0:T(8,128)(2,1)S(1)} %copy-done.2, f32[1,512]{1,0:T(1,128)S(1)} %bitcast.11), custom_call_target="tpu_custom_call" | custom-call | flops 805306368 | bytes 4194304 | tf_op jit(solution)/shard_map/node/pallas_call | solution.py:169
  72.7 0.0 collective-permute-done.16.part1
  72.7 0.0 collective-permute-done.17.part2
  72.7 2.6 %collective-permute-done.18.part3 = bf16[8,512]{1,0:T(8,128)(2,1)S(1)} collective-permute-done((bf16[8,512]{1,0:T(8,128)(2,1)S(1)}, bf16[8,512]{1,0:T(8,128)(2,1)S(1)}, u32[]{:S(2)}, u32[]{:S(2)}) %collective-permute-start.18) | collective-permute-done | bytes 8224 | tf_op jit(solution)/shard_map/ppermute | solution.py:290
  75.3 1.2 %tail.1 = bf16[512,512]{1,0:T(8,128)(2,1)} custom-call(bf16[512,512]{1,0:T(8,128)(2,1)S(1)} %copy-done, f32[16,512]{1,0:T(8,128)S(1)} %get-tuple-element.17.sum_ref, f32[8,512]{1,0:T(8,128)S(1)} %slice.40.part0, bf16[8,512]{1,0:T(8,128)(2,1)S(1)} %collective-permute-done.16.part1, ...), custom_call_target="tpu_custom_call", output_to_operand_aliasing={{}: (9, {})} | custom-call | tf_op jit(solution)/shard_map/tail/pallas_call | solution.py:295
  (28 shorter events, 0.2 us)
Async XLA Ops:
  0.6 39.7 %copy-start.13 = (s32[1024]{0:T(1024)S(1)}, s32[1024]{0:T(1024)}, u32[]{:S(2)}) copy-start(s32[1024]{0:T(1024)} %param.20) | copy-start | bytes 12292
  0.6 39.7 %copy-start.12 = (s32[1024]{0:T(1024)S(1)}, s32[1024]{0:T(1024)}, u32[]{:S(2)}) copy-start(s32[1024]{0:T(1024)} %param.21) | copy-start | bytes 12292
  1.4 3.7 %collective-permute-start.2 = (bf16[8,512]{1,0:T(8,128)(2,1)S(1)}, bf16[8,512]{1,0:T(8,128)(2,1)S(1)}, u32[]{:S(2)}, u32[]{:S(2)}) collective-permute-start(bf16[8,512]{1,0:T(8,128)(2,1)S(1)} %get-tuple-element.31), channel_id=1, source_target_pairs={{0,32},{32,0},{64,96},{96,64},{128,160},{160,128},{192,224},{224,1... | collective-permute-start | bytes 24584 | tf_op jit(solution)/shard_map/ppermute | solution.py:223
  5.0 5.0 %collective-permute-start.3 = (bf16[16,512]{1,0:T(8,128)(2,1)S(1)}, bf16[16,512]{1,0:T(8,128)(2,1)S(1)}, u32[]{:S(2)}, u32[]{:S(2)}) collective-permute-start(bf16[16,512]{1,0:T(8,128)(2,1)S(1)} %pad_maximum_fusion.2), channel_id=1, source_target_pairs={{0,64},{32,96},{64,0},{96,32},{128,192},{160,224},{192,128},{224,1... | collective-permute-start | bytes 49160 | tf_op jit(solution)/shard_map/ppermute | solution.py:223
  10.0 8.7 %collective-permute-start.4 = (bf16[32,512]{1,0:T(8,128)(2,1)S(1)}, bf16[32,512]{1,0:T(8,128)(2,1)S(1)}, u32[]{:S(2)}, u32[]{:S(2)}) collective-permute-start(bf16[32,512]{1,0:T(8,128)(2,1)S(1)} %pad_maximum_fusion.1), channel_id=1, source_target_pairs={{0,128},{32,160},{64,192},{96,224},{128,0},{160,32},{192,64},{224,... | collective-permute-start | bytes 98312 | tf_op jit(solution)/shard_map/ppermute | solution.py:223
  18.7 4.7 %collective-permute-start.5 = (bf16[64,512]{1,0:T(8,128)(2,1)S(1)}, bf16[64,512]{1,0:T(8,128)(2,1)S(1)}, u32[]{:S(2)}, u32[]{:S(2)}) collective-permute-start(bf16[64,512]{1,0:T(8,128)(2,1)S(1)} %pad_maximum_fusion), channel_id=1, source_target_pairs={{0,8},{1,3},{2,10},{3,1},{4,12},{5,7},{6,14},{7,5},{8,0},{9,11},{1... | collective-permute-start | bytes 196616 | tf_op jit(solution)/shard_map/ppermute | solution.py:227
  20.2 5.8 %collective-permute-start.6 = (bf16[64,512]{1,0:T(8,128)(2,1)S(1)}, bf16[64,512]{1,0:T(8,128)(2,1)S(1)}, u32[]{:S(2)}, u32[]{:S(2)}) collective-permute-start(bf16[64,512]{1,0:T(8,128)(2,1)S(1)} %pad_maximum_fusion), channel_id=1, source_target_pairs={{0,16},{1,5},{2,18},{3,7},{4,20},{5,1},{6,22},{7,3},{8,24},{9,13},... | collective-permute-start | bytes 196616 | tf_op jit(solution)/shard_map/ppermute | solution.py:227
  23.0 5.5 %collective-permute-start.7 = (bf16[64,512]{1,0:T(8,128)(2,1)S(1)}, bf16[64,512]{1,0:T(8,128)(2,1)S(1)}, u32[]{:S(2)}, u32[]{:S(2)}) collective-permute-start(bf16[64,512]{1,0:T(8,128)(2,1)S(1)} %pad_maximum_fusion), channel_id=1, source_target_pairs={{0,24},{1,7},{2,26},{3,5},{4,28},{5,3},{6,30},{7,1},{8,16},{9,15},... | collective-permute-start | bytes 196616 | tf_op jit(solution)/shard_map/ppermute | solution.py:227
  28.5 6.5 %collective-permute-start.8 = (bf16[256,512]{1,0:T(8,128)(2,1)S(1)}, bf16[256,512]{1,0:T(8,128)(2,1)S(1)}, u32[]{:S(2)}, u32[]{:S(2)}) collective-permute-start(bf16[256,512]{1,0:T(8,128)(2,1)S(1)} %get-tuple-element.35), channel_id=1, source_target_pairs={{0,2},{1,9},{2,0},{3,11},{4,6},{5,13},{6,4},{7,15},{8,10},{9,1},{1... | collective-permute-start | bytes 786440 | tf_op jit(solution)/shard_map/ppermute | solution.py:227
  29.3 8.2 %collective-permute-start.9 = (bf16[256,512]{1,0:T(8,128)(2,1)S(1)}, bf16[256,512]{1,0:T(8,128)(2,1)S(1)}, u32[]{:S(2)}, u32[]{:S(2)}) collective-permute-start(bf16[256,512]{1,0:T(8,128)(2,1)S(1)} %get-tuple-element.35), channel_id=1, source_target_pairs={{0,4},{1,17},{2,6},{3,19},{4,0},{5,21},{6,2},{7,23},{8,12},{9,25},... | collective-permute-start | bytes 786440 | tf_op jit(solution)/shard_map/ppermute | solution.py:227
  30.2 10.0 %collective-permute-start.10 = (bf16[256,512]{1,0:T(8,128)(2,1)S(1)}, bf16[256,512]{1,0:T(8,128)(2,1)S(1)}, u32[]{:S(2)}, u32[]{:S(2)}) collective-permute-start(bf16[256,512]{1,0:T(8,128)(2,1)S(1)} %get-tuple-element.35), channel_id=1, source_target_pairs={{0,6},{1,25},{2,4},{3,27},{4,2},{5,29},{6,0},{7,31},{8,14},{9,17},... | collective-permute-start | bytes 786440 | tf_op jit(solution)/shard_map/ppermute | solution.py:227
  40.2 2.7 %collective-permute-start.11 = (bf16[1024,512]{1,0:T(8,128)(2,1)S(1)}, bf16[1024,512]{1,0:T(8,128)(2,1)S(1)}, u32[]{:S(2)}, u32[]{:S(2)}) collective-permute-start(bf16[1024,512]{1,0:T(8,128)(2,1)S(1)} %constant_dynamic-update-slice_fusion.7.table_ref), channel_id=1, source_target_pairs={{0,1},{1,0},{2,3},{3,2},{4,5},{5,4},{6,7},{7,6},{8,9},{9,8},{10,11... | collective-permute-start | bytes 3145736 | tf_op jit(solution)/shard_map/ppermute | solution.py:229
  40.4 2.5 %copy-start.3 = (bf16[1536,512]{1,0:T(8,128)(2,1)S(1)}, bf16[1536,512]{1,0:T(8,128)(2,1)}, u32[]{:S(2)}) copy-start(bf16[1536,512]{1,0:T(8,128)(2,1)} %w_in_ref.6) | copy-start | bytes 4718596
  40.4 2.5 %copy-start.6 = (bf16[1024,512]{1,0:T(8,128)(2,1)S(1)}, bf16[1024,512]{1,0:T(8,128)(2,1)}, u32[]{:S(2)}) copy-start(bf16[1024,512]{1,0:T(8,128)(2,1)} %edge_ref.3) | copy-start | bytes 3145732
  40.5 2.5 %copy-start.8 = (bf16[512,512]{1,0:T(8,128)(2,1)S(1)}, bf16[512,512]{1,0:T(8,128)(2,1)}, u32[]{:S(2)}) copy-start(bf16[512,512]{1,0:T(8,128)(2,1)} %w_out_ref.6) | copy-start | bytes 1572868
  40.5 2.5 %copy-start.11 = (f32[512]{0:T(512)S(1)}, f32[512]{0:T(512)}, u32[]{:S(2)}) copy-start(f32[512]{0:T(512)} %param.24) | copy-start | bytes 6148
  43.0 7.2 %copy-start = (bf16[512,512]{1,0:T(8,128)(2,1)S(1)}, bf16[512,512]{1,0:T(8,128)(2,1)}, u32[]{:S(2)}) copy-start(bf16[512,512]{1,0:T(8,128)(2,1)} %node_ref.7) | copy-start | bytes 1572868
  43.0 7.2 %copy-start.5 = (s32[256]{0:T(256)S(1)}, s32[256]{0:T(256)}, u32[]{:S(2)}) copy-start(s32[256]{0:T(256)} %param.18) | copy-start | bytes 3076
  49.8 3.2 %collective-permute-start.12 = (bf16[128,512]{1,0:T(8,128)(2,1)S(1)}, bf16[128,512]{1,0:T(8,128)(2,1)S(1)}, u32[]{:S(2)}, u32[]{:S(2)}) collective-permute-start(bf16[128,512]{1,0:T(8,128)(2,1)S(1)} %get-tuple-element.21), channel_id=1, source_target_pairs={{0,1},{1,0},{2,3},{3,2},{4,5},{5,4},{6,7},{7,6},{8,9},{9,8},{10,11... | collective-permute-start | bytes 393224 | tf_op jit(solution)/shard_map/ppermute | solution.py:281
  50.5 7.4 %collective-permute-start = (bf16[128,512]{1,0:T(8,128)(2,1)S(1)}, bf16[128,512]{1,0:T(8,128)(2,1)S(1)}, u32[]{:S(2)}, u32[]{:S(2)}) collective-permute-start(bf16[128,512]{1,0:T(8,128)(2,1)S(1)} %get-tuple-element.14), channel_id=1, source_target_pairs={{0,1},{1,2},{2,3},{3,4},{4,5},{5,6},{6,7},{7,8},{8,9},{9,10},{10,1... | collective-permute-start | bytes 393224 | tf_op jit(solution)/shard_map/ppermute | solution.py:255
  50.8 7.2 %copy-start.7 = (bf16[1024,512]{1,0:T(8,128)(2,1)S(1)}, bf16[1024,512]{1,0:T(8,128)(2,1)}, u32[]{:S(2)}) copy-start(bf16[1024,512]{1,0:T(8,128)(2,1)} %edge_ref.2) | copy-start | bytes 3145732
  50.8 7.2 %copy-start.9 = (s32[1024]{0:T(1024)S(1)}, s32[1024]{0:T(1024)}, u32[]{:S(2)}) copy-start(s32[1024]{0:T(1024)} %param.16) | copy-start | bytes 12292
  50.8 7.2 %copy-start.10 = (s32[1024]{0:T(1024)S(1)}, s32[1024]{0:T(1024)}, u32[]{:S(2)}) copy-start(s32[1024]{0:T(1024)} %param.17) | copy-start | bytes 12292
  50.8 7.2 %collective-permute-start.1 = (bf16[128,512]{1,0:T(8,128)(2,1)S(1)}, bf16[128,512]{1,0:T(8,128)(2,1)S(1)}, u32[]{:S(2)}, u32[]{:S(2)}) collective-permute-start(bf16[128,512]{1,0:T(8,128)(2,1)S(1)} %get-tuple-element.15), channel_id=1, source_target_pairs={{1,0},{2,1},{3,2},{4,3},{5,4},{6,5},{7,6},{8,7},{9,8},{10,9},{11,1... | collective-permute-start | bytes 393224 | tf_op jit(solution)/shard_map/ppermute | solution.py:256
  53.1 9.3 %collective-permute-start.13 = (bf16[32,512]{1,0:T(8,128)(2,1)S(1)}, bf16[32,512]{1,0:T(8,128)(2,1)S(1)}, u32[]{:S(2)}, u32[]{:S(2)}) collective-permute-start(bf16[32,512]{1,0:T(8,128)(2,1)S(1)} %get-tuple-element.32), channel_id=1, source_target_pairs={{0,8},{1,9},{2,10},{3,11},{4,12},{5,13},{6,14},{7,15},{8,0},{9,1},... | collective-permute-start | bytes 98312 | tf_op jit(solution)/shard_map/ppermute | solution.py:285
  53.2 9.2 %collective-permute-start.14 = (bf16[32,512]{1,0:T(8,128)(2,1)S(1)}, bf16[32,512]{1,0:T(8,128)(2,1)S(1)}, u32[]{:S(2)}, u32[]{:S(2)}) collective-permute-start(bf16[32,512]{1,0:T(8,128)(2,1)S(1)} %get-tuple-element.34), channel_id=1, source_target_pairs={{0,16},{1,17},{2,18},{3,19},{4,20},{5,21},{6,22},{7,23},{8,24},{9,... | collective-permute-start | bytes 98312 | tf_op jit(solution)/shard_map/ppermute | solution.py:285
  55.8 6.6 %collective-permute-start.15 = (bf16[32,512]{1,0:T(8,128)(2,1)S(1)}, bf16[32,512]{1,0:T(8,128)(2,1)S(1)}, u32[]{:S(2)}, u32[]{:S(2)}) collective-permute-start(bf16[32,512]{1,0:T(8,128)(2,1)S(1)} %get-tuple-element.33), channel_id=1, source_target_pairs={{0,24},{1,25},{2,26},{3,27},{4,28},{5,29},{6,30},{7,31},{8,16},{9,... | collective-permute-start | bytes 98312 | tf_op jit(solution)/shard_map/ppermute | solution.py:285
  58.0 12.4 %copy-start.1 = (bf16[1024,512]{1,0:T(8,128)(2,1)S(1)}, bf16[1024,512]{1,0:T(8,128)(2,1)}, u32[]{:S(2)}) copy-start(bf16[1024,512]{1,0:T(8,128)(2,1)} %w_in_ref.7) | copy-start | bytes 3145732
  58.0 12.4 %copy-start.2 = (bf16[512,512]{1,0:T(8,128)(2,1)S(1)}, bf16[512,512]{1,0:T(8,128)(2,1)}, u32[]{:S(2)}) copy-start(bf16[512,512]{1,0:T(8,128)(2,1)} %w_out_ref.7) | copy-start | bytes 1572868
  58.0 12.4 %copy-start.4 = (f32[512]{0:T(512)S(1)}, f32[512]{0:T(512)}, u32[]{:S(2)}) copy-start(f32[512]{0:T(512)} %param.27) | copy-start | bytes 6148
  62.5 10.2 %collective-permute-start.16 = (bf16[8,512]{1,0:T(8,128)(2,1)S(1)}, bf16[8,512]{1,0:T(8,128)(2,1)S(1)}, u32[]{:S(2)}, u32[]{:S(2)}) collective-permute-start(bf16[8,512]{1,0:T(8,128)(2,1)S(1)} %get-tuple-element.43), channel_id=1, source_target_pairs={{0,2},{1,3},{2,0},{3,1},{4,6},{5,7},{6,4},{7,5},{8,10},{9,11},{10,... | collective-permute-start | bytes 24584 | tf_op jit(solution)/shard_map/ppermute | solution.py:290
  62.8 9.9 %collective-permute-start.17 = (bf16[8,512]{1,0:T(8,128)(2,1)S(1)}, bf16[8,512]{1,0:T(8,128)(2,1)S(1)}, u32[]{:S(2)}, u32[]{:S(2)}) collective-permute-start(bf16[8,512]{1,0:T(8,128)(2,1)S(1)} %get-tuple-element.42), channel_id=1, source_target_pairs={{0,4},{1,5},{2,6},{3,7},{4,0},{5,1},{6,2},{7,3},{8,12},{9,13},{10,... | collective-permute-start | bytes 24584 | tf_op jit(solution)/shard_map/ppermute | solution.py:290
  70.4 4.9 %collective-permute-start.18 = (bf16[8,512]{1,0:T(8,128)(2,1)S(1)}, bf16[8,512]{1,0:T(8,128)(2,1)S(1)}, u32[]{:S(2)}, u32[]{:S(2)}) collective-permute-start(bf16[8,512]{1,0:T(8,128)(2,1)S(1)} %get-tuple-element.41), channel_id=1, source_target_pairs={{0,6},{1,7},{2,4},{3,5},{4,2},{5,3},{6,0},{7,1},{8,14},{9,15},{10,... | collective-permute-start | bytes 24584 | tf_op jit(solution)/shard_map/ppermute | solution.py:290

commit v2 on v1

v2 whole, which is shorter than its diff:
```python
import functools

import jax
import jax.numpy as jnp
from jax import lax
from jax.experimental import pallas as pl
from jax.experimental.pallas import tpu as pltpu
from jax.sharding import PartitionSpec as P

D = 512
GROUPS = 8
SIDE = 4
CORES = 2
PATCHES = SIDE * SIDE * CORES
BORDER = 128
COARSE_ROWS = 8
EDGES = 1024
HALF = 512
NODES = 512
TAIL = 16
EPS = 1e-05
BF = jnp.bfloat16
F32 = jnp.float32
BLOCK = 256
VMEM_LIMIT = 24 * 1024 * 1024


def dot(a, b):
    return jnp.dot(a, b, preferred_element_type=F32)


def silu(values):
    half = 0.5 * values
    return half * jnp.tanh(half) + half


def layer_norm(values):
    average = jnp.mean(values, axis=-1, keepdims=True)
    centred = values - average
    variance = jnp.mean(centred * centred, axis=-1, keepdims=True)
    return centred * lax.rsqrt(variance + EPS)


def column_of(ids_ref, first, rows):
    tiles = []
    for at in range(first // 128, (first + rows) // 128):
        row = jnp.broadcast_to(ids_ref[at : at + 1, :], (128, 128))
        tiles.append(row.T)
    return jnp.concatenate(tiles, axis=0).astype(jnp.int16)


def one_hot(column, width, offset=0):
    lanes = lax.broadcasted_iota(jnp.int16, column.shape, 1)
    one, zero = jnp.ones(column.shape, BF), jnp.zeros(column.shape, BF)
    return jnp.concatenate(
        [
            jnp.where(column == lanes + jnp.int16(offset + 128 * at), one, zero)
            for at in range(width // 128)
        ],
        axis=1,
    )


def one_hot_rows(ids_ref, first, count, height):
    rows = lax.broadcasted_iota(jnp.int16, (height, 128), 0)
    one, zero = jnp.ones((height, 128), BF), jnp.zeros((height, 128), BF)
    parts = []
    for at in range(first // 128, (first + count) // 128):
        ids = jnp.broadcast_to(ids_ref[at : at + 1, :], (height, 128)).astype(jnp.int16)
        parts.append(jnp.where(ids == rows, one, zero))
    return jnp.concatenate(parts, axis=1)


def finish_edges(pre, edges, w_out, gain):
    hidden = silu(pre).astype(BF)
    projected = dot(hidden, w_out)
    return (edges.astype(F32) + layer_norm(projected) * gain).astype(BF)


def pick_kernel(node_ref, border_ref, low_ref, high_ref):
    hot = one_hot(column_of(border_ref, 0, 2 * BORDER), NODES)
    picked = dot(hot, node_ref[...]).astype(BF)
    low_ref[...] = picked[:BORDER]
    high_ref[...] = picked[BORDER:]


def project_kernel(node_ref, w_ref, out_ref):
    nodes = node_ref[...]
    out_ref[:NODES] = dot(nodes, w_ref[2 * D :]).astype(BF)
    out_ref[NODES:] = dot(nodes, w_ref[D : 2 * D]).astype(BF)


def fine_kernel(
    first_row, edge_ref, send_ref, recv_ref, table_ref, low_ref, high_ref, w_in_ref, w_out_ref,
    gain_ref, *rest,
):
    if first_row:
        before_ref, _, new_ref, sum_ref, halo_ref, rows_ref, sems = rest
    else:
        new_ref, sum_ref, halo_ref, rows_ref, sems = rest
    halo_ref[:BORDER] = dot(low_ref[...], w_in_ref[D : 2 * D]).astype(BF)
    halo_ref[BORDER:] = dot(high_ref[...], w_in_ref[D : 2 * D]).astype(BF)
    gain = gain_ref[...]
    copies = []
    for at in range(HALF // BLOCK):
        first = first_row + at * BLOCK
        edges = edge_ref[first : first + BLOCK]
        recv_hot = one_hot(column_of(recv_ref, first, BLOCK), NODES)
        send_hot = one_hot(column_of(send_ref, first, BLOCK), NODES + 2 * BORDER)
        pre = dot(edges, w_in_ref[:D])
        pre = pre + dot(recv_hot, table_ref[:NODES])
        pre = pre + dot(send_hot[:, :NODES], table_ref[NODES:])
        pre = pre + dot(send_hot[:, NODES:], halo_ref[...])
        rows_ref[at * BLOCK : (at + 1) * BLOCK] = finish_edges(pre, edges, w_out_ref[...], gain)
        copies.append(
            pltpu.make_async_copy(
                rows_ref.at[pl.ds(at * BLOCK, BLOCK)], new_ref.at[pl.ds(first, BLOCK)], sems.at[at]
            )
        )
        copies[-1].start()
    hot = one_hot_rows(recv_ref, first_row, HALF, NODES)
    sums = dot(hot, rows_ref[...])
    sum_ref[...] = sums + before_ref[...] if first_row else sums
    for copy in copies:
        copy.wait()


def gather_kernel(send_ref, recv_ref, table_ref, send_out, recv_out):
    for first in range(0, EDGES, BLOCK):
        rows = slice(first, first + BLOCK)
        for ids_ref, out_ref in ((send_ref, send_out), (recv_ref, recv_out)):
            hot = one_hot(column_of(ids_ref, first, BLOCK), table_ref.shape[0])
            out_ref[rows] = dot(hot, table_ref[...]).astype(BF)


def coarse_kernel(
    edge_ref, send_ref, recv_ref, slot_ref, table_ref, send_part, recv_part, w_in_ref, w_out_ref,
    gain_ref, new_ref, mine_ref, theirs_ref,
):
    gain = gain_ref[...]
    half = table_ref.shape[0]
    for first in range(0, EDGES, BLOCK):
        rows = slice(first, first + BLOCK)
        edges = edge_ref[rows]
        pre = dot(edges, w_in_ref[:D])
        for ids_ref, part_ref, at in ((send_ref, send_part, 1), (recv_ref, recv_part, 2)):
            hot = one_hot(column_of(ids_ref, first, BLOCK), half, half)
            picked = (dot(hot, table_ref[...]) + part_ref[rows].astype(F32)).astype(BF)
            pre = pre + dot(picked, w_in_ref[at * D : (at + 1) * D])
        new_ref[rows] = finish_edges(pre, edges, w_out_ref[...], gain)
    height = 2 * mine_ref.shape[0]
    sums = dot(one_hot_rows(slot_ref, 0, EDGES, height), new_ref[...])
    mine_ref[...] = sums[: height // 2]
    theirs_ref[...] = sums[height // 2 :].astype(BF)


def node_rows(nodes, incoming, w_in_ref, w_out_ref, gain):
    pre = dot(nodes, w_in_ref[:D]) + dot(incoming, w_in_ref[D:])
    projected = dot(silu(pre).astype(BF), w_out_ref[...])
    return (nodes.astype(F32) + layer_norm(projected) * gain).astype(BF)


def node_kernel(node_ref, sum_ref, w_in_ref, w_out_ref, gain_ref, out_ref, first_ref):
    for first in range(0, NODES, BLOCK):
        rows = slice(first, first + BLOCK)
        out_ref[rows] = node_rows(
            node_ref[rows], sum_ref[rows].astype(BF), w_in_ref, w_out_ref, gain_ref[...]
        )
    first_ref[...] = sum_ref[:TAIL]


def tail_kernel(
    node_ref, sum_ref, mine_ref, theirs_ref, w_in_ref, w_out_ref, gain_ref, _, out_ref, rows_ref,
    sem,
):
    coarse = mine_ref[:COARSE_ROWS] + theirs_ref[...].astype(F32)
    total = sum_ref[...]
    total = jnp.concatenate([total[:COARSE_ROWS] + coarse, total[COARSE_ROWS:]], axis=0)
    rows_ref[...] = node_rows(
        node_ref[:TAIL], total.astype(BF), w_in_ref, w_out_ref, gain_ref[...]
    )
    copy = pltpu.make_async_copy(rows_ref, out_ref.at[pl.ds(0, TAIL)], sem)
    copy.start()
    copy.wait()


def shape(rows, dtype=BF):
    return jax.ShapeDtypeStruct((rows, D), dtype)


VMEM_SPEC = pl.BlockSpec(memory_space=pltpu.VMEM)
ANY_SPEC = pl.BlockSpec(memory_space=pl.ANY)


def call(kernel, outs, flops, *args, name, scratch=(), out_any=(), in_any=(), aliases=None):
    return pl.pallas_call(
        kernel,
        out_shape=outs,
        in_specs=[ANY_SPEC if at in in_any else VMEM_SPEC for at in range(len(args))],
        out_specs=tuple(
            ANY_SPEC if at in out_any else VMEM_SPEC for at in range(len(outs))
        ),
        scratch_shapes=scratch,
        input_output_aliases=aliases or {},
        compiler_params=pltpu.CompilerParams(vmem_limit_bytes=VMEM_LIMIT),
        cost_estimate=pl.CostEstimate(flops=flops, bytes_accessed=4 << 20, transcendentals=0),
        name=name,
    )(*args)


def patch_pairs(move):
    pairs = []
    for x in range(SIDE):
        for y in range(SIDE):
            for core in range(CORES):
                to_x, to_y, to_core = move(x, y, core)
                pairs.append(
                    ((x * SIDE + y) * CORES + core, (to_x * SIDE + to_y) * CORES + to_core)
                )
    return pairs


def even(i, length):
    return i ^ 1


def odd(i, length):
    return ((i + 1) ^ 1) - 1 if i < length - 1 and i > 0 else length - 1 - i


def along_x(pair):
    return patch_pairs(lambda x, y, c: (pair(x, SIDE), y, c))


def along_y(pair):
    return patch_pairs(lambda x, y, c: (x, pair(y, SIDE), c))


def crossed(pair, turn):
    return patch_pairs(
        lambda x, y, c: (pair(x, SIDE), y, c) if c == turn else (x, pair(y, SIDE), c)
    )


SWAP_CORE = patch_pairs(lambda x, y, c: (x, y, c ^ 1))
Z_EVEN = [(i, even(i, GROUPS)) for i in range(GROUPS)]
Z_ODD = [(i, odd(i, GROUPS)) for i in range(GROUPS)]
tie = lambda *arrays: lax.optimization_barrier(arrays)


def ring_offset(other, mine, length, sign):
    step = jnp.where(mine % 2 == 0, sign, -sign)
    return (other - mine) * step & (length - 1)


def place_4(offset):
    return offset ^ (offset >> 1)


def place_8(offset):
    low, mid, high = offset & 1, offset >> 1 & 1, offset >> 2
    return (low ^ high) | high << 1 | (mid ^ high) << 2


def shards(
    node_lat, fine_edge_lat, fine_send, fine_recv, border_rows, coarse_edge_lat, coarse_send,
    coarse_recv, w_edge_in, w_edge_out, edge_gain, w_node_in, w_node_out, node_gain,
):
    group = lax.axis_index("group")
    patch = lax.axis_index("patch")
    my_core, my_y, my_x = patch & 1, patch >> 1 & 3, patch >> 3
    edge_gain = edge_gain[None, :]
    node_gain = node_gain[None, :]
    grid = lambda ids: ids.reshape(-1, 128)
    swap = lambda rows, pairs: lax.ppermute(rows, "patch", pairs)
    join = lambda *rows: jnp.concatenate(rows, axis=0)

    own = node_lat[:COARSE_ROWS]
    picked_from = tie(own, node_lat)[1]
    pair = lax.ppermute(own, "group", Z_EVEN)
    low, high = call(
        pick_kernel, (shape(BORDER), shape(BORDER)), 2 * 256 * 512 * 512, picked_from,
        grid(border_rows), name="pick",
    )
    pair, low, high = tie(pair, low, high)
    near = join(own, pair)
    near, project_from = tie(near, node_lat)
    next_two = lax.ppermute(near, "group", Z_ODD)
    (table,) = call(
        project_kernel, (shape(2 * NODES),), 4 * 512 * 512 * 512, project_from, w_edge_in,
        name="project",
    )
    next_two, table = tie(next_two, table)
    up = [(i, (i + 1) % PATCHES) for i in range(PATCHES)]
    down = [(j, i) for i, j in up]
    next_two, high = tie(next_two, high)
    far_two = lax.ppermute(next_two, "group", Z_EVEN)
    from_low = lax.ppermute(high, "patch", up)
    far_two, low = tie(far_two, low)
    last_two = lax.ppermute(far_two, "group", Z_ODD)
    from_high = lax.ppermute(low, "patch", down)
    block = join(near, next_two, far_two, last_two)

    block = join(block, swap(block, crossed(even, 0)))
    block, from_low, from_high = tie(block, from_low, from_high)
    other = swap(block, crossed(odd, 0))
    fine_args = (
        fine_edge_lat, grid(fine_send), grid(fine_recv), table, from_low, from_high, w_edge_in,
        w_edge_out, edge_gain,
    )
    fine_scratch = [
        pltpu.VMEM((2 * BORDER, D), BF), pltpu.VMEM((HALF, D), BF),
        pltpu.SemaphoreType.DMA((HALF // BLOCK,)),
    ]
    fine_outs = (shape(EDGES), shape(NODES, F32))
    fine_new, fine_sum = call(
        functools.partial(fine_kernel, 0), fine_outs, 2 << 30, *fine_args, name="fine_first",
        scratch=fine_scratch, out_any=(0,),
    )
    other, fine_sum = tie(other, fine_sum)
    block = join(block, other)

    middle = block.shape[0] // 2
    one, two = block[:middle], block[middle:]
    one, two, fine_sum = tie(one, two, fine_sum)
    one_next, two_next = swap(one, crossed(even, 1)), swap(two, crossed(odd, 1))
    fine_new, fine_sum = call(
        functools.partial(fine_kernel, HALF), fine_outs, 2 << 30, *fine_args, fine_sum, fine_new,
        name="fine_second", scratch=fine_scratch, out_any=(0,), in_any=(len(fine_args) + 1,),
        aliases={len(fine_args) + 1: 0},
    )
    one_next, two_next, fine_sum = tie(one_next, two_next, fine_sum)
    one, two = join(one, one_next), join(two, two_next)
    one, two, fine_sum = tie(one, two, fine_sum)
    one_next, two_next = swap(one, crossed(odd, 1)), swap(two, crossed(even, 1))
    node_main, first_sum = call(
        node_kernel, (shape(NODES), shape(TAIL, F32)), 768 << 20, node_lat, fine_sum, w_node_in,
        w_node_out, node_gain, name="node",
    )
    one_next, two_next, first_sum = tie(one_next, two_next, first_sum)
    part = join(one, one_next, two, two_next)
    other_half = swap(part, SWAP_CORE)

    def place(ids):
        row, at = ids & 7, ids >> 3
        core, y, x, z = at & 1, at >> 1 & 3, at >> 3 & 3, at >> 5
        z = place_8(ring_offset(z, group, GROUPS, 1))
        first, mine_first = jnp.where(core == 0, x, y), jnp.where(core == 0, my_x, my_y)
        second, mine_second = jnp.where(core == 0, y, x), jnp.where(core == 0, my_y, my_x)
        first = place_4(ring_offset(first, mine_first, SIDE, 1))
        second = place_4(ring_offset(second, mine_second, SIDE, 1 - (first >> 1) * 2))
        return (
            (core ^ my_core) << 10 | (first >> 1) << 9 | second << 7 | (first & 1) << 6 | z << 3
            | row
        )

    row, at = coarse_recv & 7, coarse_recv >> 3
    slot = (
        (at & 1 ^ my_core) << 7
        | place_4(ring_offset(at >> 3 & 3, my_x, SIDE, 1)) << 5
        | place_4(ring_offset(at >> 1 & 3, my_y, SIDE, 1)) << 3
        | row
    )
    slot = grid(jnp.where(at >> 5 == group, slot, -1))
    send_place, recv_place = grid(place(coarse_send)), grid(place(coarse_recv))

    send_part, recv_part = call(
        gather_kernel, (shape(EDGES), shape(EDGES)), 2 << 30, send_place, recv_place, part,
        name="gather",
    )
    coarse_new, total, theirs = call(
        coarse_kernel, (shape(EDGES), shape(128, F32), shape(128)), 4 << 30, coarse_edge_lat,
        send_place, recv_place, slot, other_half, send_part, recv_part, w_edge_in, w_edge_out,
        edge_gain, name="coarse",
    )

    total = total + swap(theirs, SWAP_CORE).astype(F32)
    for pairs in (along_x(odd), along_x(even), along_y(odd)):
        width = total.shape[0] // 2
        total = total[:width] + swap(total[width:].astype(BF), pairs).astype(F32)
    theirs = swap(total[COARSE_ROWS:].astype(BF), along_y(even))
    (node_new,) = call(
        tail_kernel, (shape(NODES),), 24 << 20, node_lat, first_sum, total, theirs, w_node_in,
        w_node_out, node_gain, node_main, name="tail",
        scratch=[pltpu.VMEM((TAIL, D), BF), pltpu.SemaphoreType.DMA], out_any=(0,), in_any=(7,),
        aliases={7: 0},
    )
    return (node_new, fine_new, coarse_new)


def solution(mesh):
    in_specs = (
        P(("group", "patch"), None), P(("group", "patch"), None), P(("group", "patch")),
        P(("group", "patch")), P(("group", "patch")), P("patch", None), P("patch"), P("patch"),
        P(), P(), P(), P(), P(), P(),
    )
    out_specs = (P(("group", "patch"), None), P(("group", "patch"), None), P("patch", None))
    return jax.shard_map(shards, mesh=mesh, in_specs=in_specs, out_specs=out_specs, check_vma=False)
```

time: 76.6 us -> 81.2 us (1.060)
  the two profiles are of different devices: /device:TPU:24 before, /device:TPU:6 now
where the time goes in v2:
time: 81.2 us; the launch traced here: 81 us
  waiting for transfers between devices  35.1 us (43%)
  Pallas kernels  20.5 us (25%)
  starting transfers between devices  20.1 us (25%)
  local copies, waits for them, and re-layouts  4.02 us (5%)
  between operations  1.15 us (1%)
    ppermute x12, waiting for transfers between devices, shards(): swap = lambda rows, pairs: lax.ppermute(rows, 'patch', pairs)  29.2 us
    pallas_call x8, Pallas kernels, call(): pl.pallas_call(kernel, out_shape=outs, in_specs=[ANY_SPEC if at in in_any...  20.5 us
    ppermute x12, starting transfers between devices, shards(): swap = lambda rows, pairs: lax.ppermute(rows, 'patch', pairs)  9.81 us
    ppermute x1, starting transfers between devices, shards(): next_two = lax.ppermute(near, 'group', Z_ODD)  5.51 us
    ppermute x1, waiting for transfers between devices, shards(): far_two = lax.ppermute(next_two, 'group', Z_EVEN)  3.62 us
    unnamed x43, local copies, waits for them, and re-layouts  3.26 us
    ppermute x1, starting transfers between devices, shards(): last_two = lax.ppermute(far_two, 'group', Z_ODD)  2.69 us
    ppermute x1, waiting for transfers between devices, shards(): last_two = lax.ppermute(far_two, 'group', Z_ODD)  2.25 us
  transfers between devices with their start and end apart: 18, of which 13 were waited for; matrix products, arithmetic and copies ran while one was open for 0% of the time, Pallas kernels for 14%

profile of v2, /device:TPU:6, one launch (start us, length us, event | category | flops | bytes accessed | tf_op | source)
XLA Modules:
  0.0 81.0 jit_solution(3421912898910419069)
XLA Ops:
  0.6 0.7 slice.28
  1.3 1.9 %collective-permute-start = (bf16[8,512]{1,0:T(8,128)(2,1)S(1)}, bf16[8,512]{1,0:T(8,128)(2,1)S(1)}, u32[]{:S(2)}, u32[]{:S(2)}) collective-permute-start(bf16[8,512]{1,0:T(8,128)(2,1)S(1)} %slice.28), channel_id=1, source_target_pairs={{0,32},{32,0},{64,96},{96,64},{128,160},{160,128},{192,224},{224,1... | collective-permute-start | bytes 24584 | tf_op jit(solution)/shard_map/ppermute | solution.py:280
  3.2 1.0 %copy-done = bf16[512,512]{1,0:T(8,128)(2,1)S(1)} copy-done((bf16[512,512]{1,0:T(8,128)(2,1)S(1)}, bf16[512,512]{1,0:T(8,128)(2,1)}, u32[]{:S(2)}) %copy-start) | copy-done | bytes 524312
  4.3 0.7 copy-done.8
  5.0 0.3 pick.1
  5.3 0.0 collective-permute-done
  5.3 5.5 %collective-permute-start.1 = (bf16[16,512]{1,0:T(8,128)(2,1)S(1)}, bf16[16,512]{1,0:T(8,128)(2,1)S(1)}, u32[]{:S(2)}, u32[]{:S(2)}) collective-permute-start(bf16[16,512]{1,0:T(8,128)(2,1)S(1)} %pad_maximum_fusion.3), channel_id=1, source_target_pairs={{0,224},{32,64},{64,32},{96,128},{128,96},{160,192},{192,160},{224... | collective-permute-start | bytes 49160 | tf_op jit(solution)/shard_map/ppermute | solution.py:288
  10.8 1.4 %copy-done.4 = bf16[1536,512]{1,0:T(8,128)(2,1)S(1)} copy-done((bf16[1536,512]{1,0:T(8,128)(2,1)S(1)}, bf16[1536,512]{1,0:T(8,128)(2,1)}, u32[]{:S(2)}) %copy-start.4) | copy-done | bytes 1572888
  12.3 0.0 copy-start.14
  12.3 0.0 copy-start.15
  12.3 0.7 project.1.table_ref
  13.0 0.0 collective-permute-done.1
  13.0 0.1 collective-permute-start.2
  13.1 0.1 collective-permute-start.5
  13.2 3.6 %collective-permute-done.2 = bf16[16,512]{1,0:T(8,128)(2,1)S(1)} collective-permute-done((bf16[16,512]{1,0:T(8,128)(2,1)S(1)}, bf16[16,512]{1,0:T(8,128)(2,1)S(1)}, u32[]{:S(2)}, u32[]{:S(2)}) %collective-permute-start.2) | collective-permute-done | bytes 16416 | tf_op jit(solution)/shard_map/ppermute | solution.py:297
  16.8 2.7 %collective-permute-start.3 = (bf16[16,512]{1,0:T(8,128)(2,1)S(1)}, bf16[16,512]{1,0:T(8,128)(2,1)S(1)}, u32[]{:S(2)}, u32[]{:S(2)}) collective-permute-start(bf16[16,512]{1,0:T(8,128)(2,1)S(1)} %collective-permute-done.2), channel_id=1, source_target_pairs={{0,224},{32,64},{64,32},{96,128},{128,96},{160,192},{192,160},{224... | collective-permute-start | bytes 49160 | tf_op jit(solution)/shard_map/ppermute | solution.py:300
  19.5 0.0 collective-permute-start.6
  19.5 2.3 %collective-permute-done.3 = bf16[16,512]{1,0:T(8,128)(2,1)S(1)} collective-permute-done((bf16[16,512]{1,0:T(8,128)(2,1)S(1)}, bf16[16,512]{1,0:T(8,128)(2,1)S(1)}, u32[]{:S(2)}, u32[]{:S(2)}) %collective-permute-start.3) | collective-permute-done | bytes 16416 | tf_op jit(solution)/shard_map/ppermute | solution.py:300
  21.8 0.8 %collective-permute-start.4 = (bf16[64,512]{1,0:T(8,128)(2,1)S(1)}, bf16[64,512]{1,0:T(8,128)(2,1)S(1)}, u32[]{:S(2)}, u32[]{:S(2)}) collective-permute-start(bf16[64,512]{1,0:T(8,128)(2,1)S(1)} %pad_maximum_fusion.2), channel_id=1, source_target_pairs={{0,8},{1,3},{2,10},{3,1},{4,12},{5,7},{6,14},{7,5},{8,0},{9,11},{1... | collective-permute-start | bytes 196616 | tf_op jit(solution)/shard_map/ppermute | solution.py:275
  22.6 3.4 %collective-permute-done.4 = bf16[64,512]{1,0:T(8,128)(2,1)S(1)} collective-permute-done((bf16[64,512]{1,0:T(8,128)(2,1)S(1)}, bf16[64,512]{1,0:T(8,128)(2,1)S(1)}, u32[]{:S(2)}, u32[]{:S(2)}) %collective-permute-start.4) | collective-permute-done | bytes 65568 | tf_op jit(solution)/shard_map/ppermute | solution.py:275
  26.1 0.0 collective-permute-done.5.low_ref
  26.1 0.0 collective-permute-done.6.high_ref
  26.1 0.6 collective-permute-start.7
  26.6 0.0 copy-done.5
  26.7 0.0 copy-done.9
  26.7 0.0 copy-done.11
  26.7 0.0 copy-done.13
  26.7 0.0 copy-done.14
  26.7 0.0 copy-done.15
  26.7 2.8 %fine_first.1 = (bf16[1024,512]{1,0:T(8,128)(2,1)}, f32[512,512]{1,0:T(8,128)S(1)}) custom-call(bf16[1024,512]{1,0:T(8,128)(2,1)S(1)} %copy-done.9, s32[8,128]{1,0:T(8,128)S(1)} %bitcast.14, s32[8,128]{1,0:T(8,128)S(1)} %bitcast.16, bf16[1024,512]{1,0:T(8,128)(2,1)S(1)} %project.1.table_ref, bf16[128,512]{1,0:T(8,128)(2,1)S(1)} %collective-permute-done.5.low_ref, ...), custom_call_target="tpu_custom_call" | custom-call | flops 2147483648 | bytes 4194304 | tf_op jit(solution)/shard_map/fine_first/pallas_call | solution.py:196
  29.5 2.9 %collective-permute-done.7 = bf16[128,512]{1,0:T(8,128)(2,1)S(1)} collective-permute-done((bf16[128,512]{1,0:T(8,128)(2,1)S(1)}, bf16[128,512]{1,0:T(8,128)(2,1)S(1)}, u32[]{:S(2)}, u32[]{:S(2)}) %collective-permute-start.7) | collective-permute-done | bytes 131104 | tf_op jit(solution)/shard_map/ppermute | solution.py:275
  32.3 1.6 %collective-permute-start.8 = (bf16[128,512]{1,0:T(8,128)(2,1)S(1)}, bf16[128,512]{1,0:T(8,128)(2,1)S(1)}, u32[]{:S(2)}, u32[]{:S(2)}) collective-permute-start(bf16[128,512]{1,0:T(8,128)(2,1)S(1)} %constant_dynamic-update-slice_fusion), channel_id=1, source_target_pairs={{0,2},{1,9},{2,0},{3,11},{4,6},{5,13},{6,4},{7,15},{8,10},{9,1},{1... | collective-permute-start | bytes 393224 | tf_op jit(solution)/shard_map/ppermute | solution.py:275
  33.9 2.2 %collective-permute-start.9 = (bf16[128,512]{1,0:T(8,128)(2,1)S(1)}, bf16[128,512]{1,0:T(8,128)(2,1)S(1)}, u32[]{:S(2)}, u32[]{:S(2)}) collective-permute-start(bf16[128,512]{1,0:T(8,128)(2,1)S(1)} %collective-permute-done.7), channel_id=1, source_target_pairs={{0,6},{1,25},{2,4},{3,27},{4,2},{5,29},{6,0},{7,31},{8,14},{9,17},... | collective-permute-start | bytes 393224 | tf_op jit(solution)/shard_map/ppermute | solution.py:275
  36.1 2.8 %fine_second.1 = (bf16[1024,512]{1,0:T(8,128)(2,1)}, f32[512,512]{1,0:T(8,128)S(1)}) custom-call(bf16[1024,512]{1,0:T(8,128)(2,1)S(1)} %copy-done.9, s32[8,128]{1,0:T(8,128)S(1)} %bitcast.15, s32[8,128]{1,0:T(8,128)S(1)} %bitcast.17, bf16[1024,512]{1,0:T(8,128)(2,1)S(1)} %project.1.table_ref, ...), custom_call_target="tpu_custom_call", output_to_operand_aliasing={{0}: (10, {})} | custom-call | flops 2147483648 | bytes 4194304 | tf_op jit(solution)/shard_map/fine_second/pallas_call | solution.py:196
  38.9 0.0 collective-permute-done.8
  38.9 1.2 %collective-permute-done.9 = bf16[128,512]{1,0:T(8,128)(2,1)S(1)} collective-permute-done((bf16[128,512]{1,0:T(8,128)(2,1)S(1)}, bf16[128,512]{1,0:T(8,128)(2,1)S(1)}, u32[]{:S(2)}, u32[]{:S(2)}) %collective-permute-start.9) | collective-permute-done | bytes 131104 | tf_op jit(solution)/shard_map/ppermute | solution.py:275
  40.1 2.3 %collective-permute-start.10 = (bf16[256,512]{1,0:T(8,128)(2,1)S(1)}, bf16[256,512]{1,0:T(8,128)(2,1)S(1)}, u32[]{:S(2)}, u32[]{:S(2)}) collective-permute-start(bf16[256,512]{1,0:T(8,128)(2,1)S(1)} %get-tuple-element.73), channel_id=1, source_target_pairs={{0,6},{1,25},{2,4},{3,27},{4,2},{5,29},{6,0},{7,31},{8,14},{9,17},... | collective-permute-start | bytes 786440 | tf_op jit(solution)/shard_map/ppermute | solution.py:275
  42.4 0.0 collective-permute-start.11
  42.4 0.0 copy-done.1
  42.4 0.0 copy-done.2
  42.4 0.0 copy-done.3
  42.4 2.3 %node.1 = (bf16[512,512]{1,0:T(8,128)(2,1)}, f32[16,512]{1,0:T(8,128)S(1)}) custom-call(bf16[512,512]{1,0:T(8,128)(2,1)S(1)} %copy-done.1, f32[512,512]{1,0:T(8,128)S(1)} %get-tuple-element.75.sum_ref, bf16[1024,512]{1,0:T(8,128)(2,1)S(1)} %copy-done.2, bf16[512,512]{1,0:T(8,128)(2,1)S(1)} %copy-done.3, f32[1,512]{1,0:T(1,128)S(1)} %bitcast.11), custom_call_target="tpu_custom_call" | custom-call | flops 805306368 | bytes 4194304 | tf_op jit(solution)/shard_map/node/pallas_call | solution.py:196
  44.7 3.1 %collective-permute-done.10 = bf16[256,512]{1,0:T(8,128)(2,1)S(1)} collective-permute-done((bf16[256,512]{1,0:T(8,128)(2,1)S(1)}, bf16[256,512]{1,0:T(8,128)(2,1)S(1)}, u32[]{:S(2)}, u32[]{:S(2)}) %collective-permute-start.10) | collective-permute-done | bytes 262176 | tf_op jit(solution)/shard_map/ppermute | solution.py:275
  47.8 1.0 %collective-permute-done.11 = bf16[256,512]{1,0:T(8,128)(2,1)S(1)} collective-permute-done((bf16[256,512]{1,0:T(8,128)(2,1)S(1)}, bf16[256,512]{1,0:T(8,128)(2,1)S(1)}, u32[]{:S(2)}, u32[]{:S(2)}) %collective-permute-start.11) | collective-permute-done | bytes 262176 | tf_op jit(solution)/shard_map/ppermute | solution.py:275
  48.9 0.1 collective-permute-start.12
  49.1 0.0 copy-start.6
  49.1 0.0 copy-start.10
  49.1 0.0 copy-start.12
  49.1 2.4 %gather.1 = (bf16[1024,512]{1,0:T(8,128)(2,1)S(1)}, bf16[1024,512]{1,0:T(8,128)(2,1)S(1)}) custom-call(s32[8,128]{1,0:T(8,128)S(1)} %get-tuple-element.91.send_ref, s32[8,128]{1,0:T(8,128)S(1)} %get-tuple-element.88.recv_ref, bf16[1024,512]{1,0:T(8,128)(2,1)S(1)} %constant_dynamic-update-slice_fusion.5.table_ref), custom_call_target="tpu_custom_call" | custom-call | flops 2147483648 | bytes 4194304 | tf_op jit(solution)/shard_map/gather/pallas_call | solution.py:196
  51.5 0.3 collective-permute-done.12.table_ref
  51.7 0.0 copy-done.6
  51.7 0.0 copy-done.12
  51.8 8.0 %coarse.1 = (bf16[1024,512]{1,0:T(8,128)(2,1)}, f32[128,512]{1,0:T(8,128)S(1)}, bf16[128,512]{1,0:T(8,128)(2,1)S(1)}) custom-call(bf16[1024,512]{1,0:T(8,128)(2,1)S(1)} %copy-done.10, s32[8,128]{1,0:T(8,128)S(1)} %get-tuple-element.91.send_ref, s32[8,128]{1,0:T(8,128)S(1)} %get-tuple-element.88.recv_ref, s32[8,128]{1,0:T(8,128)S(1)} %get-tuple-element.87.slot_ref, ...), custom_call_target="tpu_custom_call" | custom-call | flops 4294967296 | bytes 4194304 | tf_op jit(solution)/shard_map/coarse/pallas_call | solution.py:196
  59.8 0.2 collective-permute-start.13
  60.0 1.1 %collective-permute-done.13 = bf16[128,512]{1,0:T(8,128)(2,1)S(1)} collective-permute-done((bf16[128,512]{1,0:T(8,128)(2,1)S(1)}, bf16[128,512]{1,0:T(8,128)(2,1)S(1)}, u32[]{:S(2)}, u32[]{:S(2)}) %collective-permute-start.13) | collective-permute-done | bytes 131104 | tf_op jit(solution)/shard_map/ppermute | solution.py:275
  61.2 0.6 collective-permute-start.14
  61.8 5.0 %collective-permute-done.14 = bf16[64,512]{1,0:T(8,128)(2,1)S(1)} collective-permute-done((bf16[64,512]{1,0:T(8,128)(2,1)S(1)}, bf16[64,512]{1,0:T(8,128)(2,1)S(1)}, u32[]{:S(2)}, u32[]{:S(2)}) %collective-permute-start.14) | collective-permute-done | bytes 65568 | tf_op jit(solution)/shard_map/ppermute | solution.py:275
  66.8 0.1 collective-permute-start.15
  66.9 3.9 %collective-permute-done.15 = bf16[32,512]{1,0:T(8,128)(2,1)S(1)} collective-permute-done((bf16[32,512]{1,0:T(8,128)(2,1)S(1)}, bf16[32,512]{1,0:T(8,128)(2,1)S(1)}, u32[]{:S(2)}, u32[]{:S(2)}) %collective-permute-start.15) | collective-permute-done | bytes 32800 | tf_op jit(solution)/shard_map/ppermute | solution.py:275
  70.8 1.3 %collective-permute-start.16 = (bf16[16,512]{1,0:T(8,128)(2,1)S(1)}, bf16[16,512]{1,0:T(8,128)(2,1)S(1)}, u32[]{:S(2)}, u32[]{:S(2)}) collective-permute-start(bf16[16,512]{1,0:T(8,128)(2,1)S(1)} %slice.52), channel_id=1, source_target_pairs={{0,6},{1,7},{2,4},{3,5},{4,2},{5,3},{6,0},{7,1},{8,14},{9,15},{10,... | collective-permute-start | bytes 49160 | tf_op jit(solution)/shard_map/ppermute | solution.py:275
  72.1 3.7 %collective-permute-done.16 = bf16[16,512]{1,0:T(8,128)(2,1)S(1)} collective-permute-done((bf16[16,512]{1,0:T(8,128)(2,1)S(1)}, bf16[16,512]{1,0:T(8,128)(2,1)S(1)}, u32[]{:S(2)}, u32[]{:S(2)}) %collective-permute-start.16) | collective-permute-done | bytes 16416 | tf_op jit(solution)/shard_map/ppermute | solution.py:275
  75.9 0.1 collective-permute-start.17
  76.0 3.6 %collective-permute-done.17.theirs_ref = bf16[8,512]{1,0:T(8,128)(2,1)S(1)} collective-permute-done((bf16[8,512]{1,0:T(8,128)(2,1)S(1)}, bf16[8,512]{1,0:T(8,128)(2,1)S(1)}, u32[]{:S(2)}, u32[]{:S(2)}) %collective-permute-start.17) | collective-permute-done | bytes 8224 | tf_op jit(solution)/shard_map/ppermute | solution.py:275
  79.6 1.2 %tail.1 = bf16[512,512]{1,0:T(8,128)(2,1)} custom-call(bf16[512,512]{1,0:T(8,128)(2,1)S(1)} %copy-done.1, f32[16,512]{1,0:T(8,128)S(1)} %get-tuple-element.77.sum_ref, f32[16,512]{1,0:T(8,128)S(1)} %slice_add_fusion.2.mine_ref, bf16[8,512]{1,0:T(8,128)(2,1)S(1)} %collective-permute-done.17.theirs_ref, ...), custom_call_target="tpu_custom_call", output_to_operand_aliasing={{}: (7, {})} | custom-call | flops 25165824 | bytes 4194304 | tf_op jit(solution)/shard_map/tail/pallas_call | solution.py:196
  (38 shorter events, 0.3 us)
Async XLA Ops:
  1.3 4.0 %collective-permute-start = (bf16[8,512]{1,0:T(8,128)(2,1)S(1)}, bf16[8,512]{1,0:T(8,128)(2,1)S(1)}, u32[]{:S(2)}, u32[]{:S(2)}) collective-permute-start(bf16[8,512]{1,0:T(8,128)(2,1)S(1)} %slice.28), channel_id=1, source_target_pairs={{0,32},{32,0},{64,96},{96,64},{128,160},{160,128},{192,224},{224,1... | collective-permute-start | bytes 24584 | tf_op jit(solution)/shard_map/ppermute | solution.py:280
  3.2 1.0 %copy-start = (bf16[512,512]{1,0:T(8,128)(2,1)S(1)}, bf16[512,512]{1,0:T(8,128)(2,1)}, u32[]{:S(2)}) copy-start(bf16[512,512]{1,0:T(8,128)(2,1)} %node_ref.5) | copy-start | bytes 1572868
  4.3 0.7 copy-start.8
  5.3 7.7 %collective-permute-start.1 = (bf16[16,512]{1,0:T(8,128)(2,1)S(1)}, bf16[16,512]{1,0:T(8,128)(2,1)S(1)}, u32[]{:S(2)}, u32[]{:S(2)}) collective-permute-start(bf16[16,512]{1,0:T(8,128)(2,1)S(1)} %pad_maximum_fusion.3), channel_id=1, source_target_pairs={{0,224},{32,64},{64,32},{96,128},{128,96},{160,192},{192,160},{224... | collective-permute-start | bytes 49160 | tf_op jit(solution)/shard_map/ppermute | solution.py:288
  10.8 1.4 %copy-start.4 = (bf16[1536,512]{1,0:T(8,128)(2,1)S(1)}, bf16[1536,512]{1,0:T(8,128)(2,1)}, u32[]{:S(2)}) copy-start(bf16[1536,512]{1,0:T(8,128)(2,1)} %w_in_ref.8) | copy-start | bytes 4718596
  12.3 14.4 %copy-start.5 = (bf16[1536,512]{1,0:T(8,128)(2,1)S(1)}, bf16[1536,512]{1,0:T(8,128)(2,1)}, u32[]{:S(2)}) copy-start(bf16[1536,512]{1,0:T(8,128)(2,1)} %w_in_ref.8) | copy-start | bytes 4718596
  12.3 14.4 %copy-start.9 = (bf16[1024,512]{1,0:T(8,128)(2,1)S(1)}, bf16[1024,512]{1,0:T(8,128)(2,1)}, u32[]{:S(2)}) copy-start(bf16[1024,512]{1,0:T(8,128)(2,1)} %edge_ref.4) | copy-start | bytes 3145732
  12.3 14.4 %copy-start.11 = (bf16[512,512]{1,0:T(8,128)(2,1)S(1)}, bf16[512,512]{1,0:T(8,128)(2,1)}, u32[]{:S(2)}) copy-start(bf16[512,512]{1,0:T(8,128)(2,1)} %w_out_ref.8) | copy-start | bytes 1572868
  12.3 14.4 %copy-start.13 = (s32[1024]{0:T(1024)S(1)}, s32[1024]{0:T(1024)}, u32[]{:S(2)}) copy-start(s32[1024]{0:T(1024)} %param.16) | copy-start | bytes 12292
  12.3 14.4 %copy-start.14 = (s32[1024]{0:T(1024)S(1)}, s32[1024]{0:T(1024)}, u32[]{:S(2)}) copy-start(s32[1024]{0:T(1024)} %param.17) | copy-start | bytes 12292
  12.3 14.4 %copy-start.15 = (f32[512]{0:T(512)S(1)}, f32[512]{0:T(512)}, u32[]{:S(2)}) copy-start(f32[512]{0:T(512)} %param.24) | copy-start | bytes 6148
  13.0 3.8 %collective-permute-start.2 = (bf16[16,512]{1,0:T(8,128)(2,1)S(1)}, bf16[16,512]{1,0:T(8,128)(2,1)S(1)}, u32[]{:S(2)}, u32[]{:S(2)}) collective-permute-start(bf16[16,512]{1,0:T(8,128)(2,1)S(1)} %collective-permute-done.1), channel_id=1, source_target_pairs={{0,32},{32,0},{64,96},{96,64},{128,160},{160,128},{192,224},{224,1... | collective-permute-start | bytes 49160 | tf_op jit(solution)/shard_map/ppermute | solution.py:297
  13.1 12.9 %collective-permute-start.5 = (bf16[128,512]{1,0:T(8,128)(2,1)S(1)}, bf16[128,512]{1,0:T(8,128)(2,1)S(1)}, u32[]{:S(2)}, u32[]{:S(2)}) collective-permute-start(bf16[128,512]{1,0:T(8,128)(2,1)S(1)} %get-tuple-element.56), channel_id=1, source_target_pairs={{0,1},{1,2},{2,3},{3,4},{4,5},{5,6},{6,7},{7,8},{8,9},{9,10},{10,1... | collective-permute-start | bytes 393224 | tf_op jit(solution)/shard_map/ppermute | solution.py:298
  16.8 4.9 %collective-permute-start.3 = (bf16[16,512]{1,0:T(8,128)(2,1)S(1)}, bf16[16,512]{1,0:T(8,128)(2,1)S(1)}, u32[]{:S(2)}, u32[]{:S(2)}) collective-permute-start(bf16[16,512]{1,0:T(8,128)(2,1)S(1)} %collective-permute-done.2), channel_id=1, source_target_pairs={{0,224},{32,64},{64,32},{96,128},{128,96},{160,192},{192,160},{224... | collective-permute-start | bytes 49160 | tf_op jit(solution)/shard_map/ppermute | solution.py:300
  19.5 6.5 %collective-permute-start.6 = (bf16[128,512]{1,0:T(8,128)(2,1)S(1)}, bf16[128,512]{1,0:T(8,128)(2,1)S(1)}, u32[]{:S(2)}, u32[]{:S(2)}) collective-permute-start(bf16[128,512]{1,0:T(8,128)(2,1)S(1)} %get-tuple-element.57), channel_id=1, source_target_pairs={{1,0},{2,1},{3,2},{4,3},{5,4},{6,5},{7,6},{8,7},{9,8},{10,9},{11,1... | collective-permute-start | bytes 393224 | tf_op jit(solution)/shard_map/ppermute | solution.py:301
  21.8 4.3 %collective-permute-start.4 = (bf16[64,512]{1,0:T(8,128)(2,1)S(1)}, bf16[64,512]{1,0:T(8,128)(2,1)S(1)}, u32[]{:S(2)}, u32[]{:S(2)}) collective-permute-start(bf16[64,512]{1,0:T(8,128)(2,1)S(1)} %pad_maximum_fusion.2), channel_id=1, source_target_pairs={{0,8},{1,3},{2,10},{3,1},{4,12},{5,7},{6,14},{7,5},{8,0},{9,11},{1... | collective-permute-start | bytes 196616 | tf_op jit(solution)/shard_map/ppermute | solution.py:275
  26.1 6.3 %collective-permute-start.7 = (bf16[128,512]{1,0:T(8,128)(2,1)S(1)}, bf16[128,512]{1,0:T(8,128)(2,1)S(1)}, u32[]{:S(2)}, u32[]{:S(2)}) collective-permute-start(bf16[128,512]{1,0:T(8,128)(2,1)S(1)} %constant_dynamic-update-slice_fusion), channel_id=1, source_target_pairs={{0,24},{1,7},{2,26},{3,5},{4,28},{5,3},{6,30},{7,1},{8,16},{9,15},... | collective-permute-start | bytes 393224 | tf_op jit(solution)/shard_map/ppermute | solution.py:275
  32.3 6.6 %collective-permute-start.8 = (bf16[128,512]{1,0:T(8,128)(2,1)S(1)}, bf16[128,512]{1,0:T(8,128)(2,1)S(1)}, u32[]{:S(2)}, u32[]{:S(2)}) collective-permute-start(bf16[128,512]{1,0:T(8,128)(2,1)S(1)} %constant_dynamic-update-slice_fusion), channel_id=1, source_target_pairs={{0,2},{1,9},{2,0},{3,11},{4,6},{5,13},{6,4},{7,15},{8,10},{9,1},{1... | collective-permute-start | bytes 393224 | tf_op jit(solution)/shard_map/ppermute | solution.py:275
  33.9 6.2 %collective-permute-start.9 = (bf16[128,512]{1,0:T(8,128)(2,1)S(1)}, bf16[128,512]{1,0:T(8,128)(2,1)S(1)}, u32[]{:S(2)}, u32[]{:S(2)}) collective-permute-start(bf16[128,512]{1,0:T(8,128)(2,1)S(1)} %collective-permute-done.7), channel_id=1, source_target_pairs={{0,6},{1,25},{2,4},{3,27},{4,2},{5,29},{6,0},{7,31},{8,14},{9,17},... | collective-permute-start | bytes 393224 | tf_op jit(solution)/shard_map/ppermute | solution.py:275
  36.1 6.3 %copy-start.1 = (bf16[512,512]{1,0:T(8,128)(2,1)S(1)}, bf16[512,512]{1,0:T(8,128)(2,1)}, u32[]{:S(2)}) copy-start(bf16[512,512]{1,0:T(8,128)(2,1)} %node_ref.5) | copy-start | bytes 1572868
  36.1 6.3 %copy-start.2 = (bf16[1024,512]{1,0:T(8,128)(2,1)S(1)}, bf16[1024,512]{1,0:T(8,128)(2,1)}, u32[]{:S(2)}) copy-start(bf16[1024,512]{1,0:T(8,128)(2,1)} %w_in_ref.9) | copy-start | bytes 3145732
  36.1 6.3 %copy-start.3 = (bf16[512,512]{1,0:T(8,128)(2,1)S(1)}, bf16[512,512]{1,0:T(8,128)(2,1)}, u32[]{:S(2)}) copy-start(bf16[512,512]{1,0:T(8,128)(2,1)} %w_out_ref.9) | copy-start | bytes 1572868
  36.1 6.3 %copy-start.7 = (f32[512]{0:T(512)S(1)}, f32[512]{0:T(512)}, u32[]{:S(2)}) copy-start(f32[512]{0:T(512)} %param.27) | copy-start | bytes 6148
  40.1 7.7 %collective-permute-start.10 = (bf16[256,512]{1,0:T(8,128)(2,1)S(1)}, bf16[256,512]{1,0:T(8,128)(2,1)S(1)}, u32[]{:S(2)}, u32[]{:S(2)}) collective-permute-start(bf16[256,512]{1,0:T(8,128)(2,1)S(1)} %get-tuple-element.73), channel_id=1, source_target_pairs={{0,6},{1,25},{2,4},{3,27},{4,2},{5,29},{6,0},{7,31},{8,14},{9,17},... | collective-permute-start | bytes 786440 | tf_op jit(solution)/shard_map/ppermute | solution.py:275
  42.4 6.4 %collective-permute-start.11 = (bf16[256,512]{1,0:T(8,128)(2,1)S(1)}, bf16[256,512]{1,0:T(8,128)(2,1)S(1)}, u32[]{:S(2)}, u32[]{:S(2)}) collective-permute-start(bf16[256,512]{1,0:T(8,128)(2,1)S(1)} %get-tuple-element.74), channel_id=1, source_target_pairs={{0,2},{1,9},{2,0},{3,11},{4,6},{5,13},{6,4},{7,15},{8,10},{9,1},{1... | collective-permute-start | bytes 786440 | tf_op jit(solution)/shard_map/ppermute | solution.py:275
  44.7 4.3 %copy-start.16 = (s32[1024]{0:T(1024)S(1)}, s32[1024]{0:T(1024)}, u32[]{:S(2)}) copy-start(s32[1024]{0:T(1024)} %param.21) | copy-start | bytes 12292
  44.7 4.3 %copy-start.17 = (s32[1024]{0:T(1024)S(1)}, s32[1024]{0:T(1024)}, u32[]{:S(2)}) copy-start(s32[1024]{0:T(1024)} %param.20) | copy-start | bytes 12292
  48.9 2.9 %collective-permute-start.12 = (bf16[1024,512]{1,0:T(8,128)(2,1)S(1)}, bf16[1024,512]{1,0:T(8,128)(2,1)}, u32[]{:S(2)}, u32[]{:S(2)}) collective-permute-start(bf16[1024,512]{1,0:T(8,128)(2,1)S(1)} %constant_dynamic-update-slice_fusion.5.table_ref), channel_id=1, source_target_pairs={{0,1},{1,0},{2,3},{3,2},{4,5},{5,4},{6,7},{7,6},{8,9},{9,8},{10,11... | collective-permute-start | bytes 3145736 | tf_op jit(solution)/shard_map/ppermute | solution.py:275
  49.1 2.7 %copy-start.6 = (bf16[1536,512]{1,0:T(8,128)(2,1)S(1)}, bf16[1536,512]{1,0:T(8,128)(2,1)}, u32[]{:S(2)}) copy-start(bf16[1536,512]{1,0:T(8,128)(2,1)} %w_in_ref.8) | copy-start | bytes 4718596
  49.1 2.7 %copy-start.10 = (bf16[1024,512]{1,0:T(8,128)(2,1)S(1)}, bf16[1024,512]{1,0:T(8,128)(2,1)}, u32[]{:S(2)}) copy-start(bf16[1024,512]{1,0:T(8,128)(2,1)} %edge_ref.5) | copy-start | bytes 3145732
  49.1 2.7 %copy-start.12 = (bf16[512,512]{1,0:T(8,128)(2,1)S(1)}, bf16[512,512]{1,0:T(8,128)(2,1)}, u32[]{:S(2)}) copy-start(bf16[512,512]{1,0:T(8,128)(2,1)} %w_out_ref.8) | copy-start | bytes 1572868
  59.8 1.3 %collective-permute-start.13 = (bf16[128,512]{1,0:T(8,128)(2,1)S(1)}, bf16[128,512]{1,0:T(8,128)(2,1)S(1)}, u32[]{:S(2)}, u32[]{:S(2)}) collective-permute-start(bf16[128,512]{1,0:T(8,128)(2,1)S(1)} %get-tuple-element.83), channel_id=1, source_target_pairs={{0,1},{1,0},{2,3},{3,2},{4,5},{5,4},{6,7},{7,6},{8,9},{9,8},{10,11... | collective-permute-start | bytes 393224 | tf_op jit(solution)/shard_map/ppermute | solution.py:275
  61.2 5.6 %collective-permute-start.14 = (bf16[64,512]{1,0:T(8,128)(2,1)S(1)}, bf16[64,512]{1,0:T(8,128)(2,1)S(1)}, u32[]{:S(2)}, u32[]{:S(2)}) collective-permute-start(bf16[64,512]{1,0:T(8,128)(2,1)S(1)} %slice.50), channel_id=1, source_target_pairs={{0,24},{1,25},{2,26},{3,27},{4,28},{5,29},{6,30},{7,31},{8,16},{9,... | collective-permute-start | bytes 196616 | tf_op jit(solution)/shard_map/ppermute | solution.py:275
  66.8 4.0 %collective-permute-start.15 = (bf16[32,512]{1,0:T(8,128)(2,1)S(1)}, bf16[32,512]{1,0:T(8,128)(2,1)S(1)}, u32[]{:S(2)}, u32[]{:S(2)}) collective-permute-start(bf16[32,512]{1,0:T(8,128)(2,1)S(1)} %slice.51), channel_id=1, source_target_pairs={{0,8},{1,9},{2,10},{3,11},{4,12},{5,13},{6,14},{7,15},{8,0},{9,1},... | collective-permute-start | bytes 98312 | tf_op jit(solution)/shard_map/ppermute | solution.py:275
  70.8 5.0 %collective-permute-start.16 = (bf16[16,512]{1,0:T(8,128)(2,1)S(1)}, bf16[16,512]{1,0:T(8,128)(2,1)S(1)}, u32[]{:S(2)}, u32[]{:S(2)}) collective-permute-start(bf16[16,512]{1,0:T(8,128)(2,1)S(1)} %slice.52), channel_id=1, source_target_pairs={{0,6},{1,7},{2,4},{3,5},{4,2},{5,3},{6,0},{7,1},{8,14},{9,15},{10,... | collective-permute-start | bytes 49160 | tf_op jit(solution)/shard_map/ppermute | solution.py:275
  75.9 3.7 %collective-permute-start.17 = (bf16[8,512]{1,0:T(8,128)(2,1)S(1)}, bf16[8,512]{1,0:T(8,128)(2,1)S(1)}, u32[]{:S(2)}, u32[]{:S(2)}) collective-permute-start(bf16[8,512]{1,0:T(8,128)(2,1)S(1)} %slice.53), channel_id=1, source_target_pairs={{0,2},{1,3},{2,0},{3,1},{4,6},{5,7},{6,4},{7,5},{8,10},{9,11},{10,... | collective-permute-start | bytes 24584 | tf_op jit(solution)/shard_map/ppermute | solution.py:275

commit v3 on v1

v3 whole, which is shorter than its diff:
```python
import functools

import jax
import jax.numpy as jnp
from jax import lax
from jax.experimental import pallas as pl
from jax.experimental.pallas import tpu as pltpu
from jax.sharding import PartitionSpec as P

D = 512
GROUPS = 8
SIDE = 4
CORES = 2
PATCHES = SIDE * SIDE * CORES
BORDER = 128
COARSE_ROWS = 8
EDGES = 1024
NODES = 512
TAIL = 16
EPS = 1e-05
BF = jnp.bfloat16
F32 = jnp.float32
BLOCK = 256
VMEM_LIMIT = 24 * 1024 * 1024


def dot(a, b):
    return jnp.dot(a, b, preferred_element_type=F32)


def silu(values):
    half = 0.5 * values
    return half * jnp.tanh(half) + half


def layer_norm(values):
    average = jnp.mean(values, axis=-1, keepdims=True)
    centred = values - average
    variance = jnp.mean(centred * centred, axis=-1, keepdims=True)
    return centred * lax.rsqrt(variance + EPS)


def column_of(ids_ref, first, rows):
    tiles = []
    for at in range(first // 128, (first + rows) // 128):
        row = jnp.broadcast_to(ids_ref[at : at + 1, :], (128, 128))
        tiles.append(row.T)
    return jnp.concatenate(tiles, axis=0).astype(jnp.int16)


def one_hot(column, width, offset=0):
    lanes = lax.broadcasted_iota(jnp.int16, column.shape, 1)
    one, zero = jnp.ones(column.shape, BF), jnp.zeros(column.shape, BF)
    return jnp.concatenate(
        [
            jnp.where(column == lanes + jnp.int16(offset + 128 * at), one, zero)
            for at in range(width // 128)
        ],
        axis=1,
    )


def one_hot_rows(ids_ref, count, height):
    rows = lax.broadcasted_iota(jnp.int16, (height, 128), 0)
    one, zero = jnp.ones((height, 128), BF), jnp.zeros((height, 128), BF)
    parts = []
    for at in range(count // 128):
        ids = jnp.broadcast_to(ids_ref[at : at + 1, :], (height, 128)).astype(jnp.int16)
        parts.append(jnp.where(ids == rows, one, zero))
    return jnp.concatenate(parts, axis=1)


def send_rows(rows_ref, out_ref, sems, at):
    rows = pl.ds(at * BLOCK, BLOCK)
    copy = pltpu.make_async_copy(rows_ref.at[rows], out_ref.at[rows], sems.at[at])
    copy.start()
    return copy


def load_kernel(*refs):
    count = len(refs) // 2
    sems = refs[-1]
    copies = [
        pltpu.make_async_copy(refs[at], refs[count + at], sems.at[at]) for at in range(count)
    ]
    for copy in copies:
        copy.start()
    for copy in copies:
        copy.wait()


def finish_edges(pre, edges, w_out, gain):
    hidden = silu(pre).astype(BF)
    projected = dot(hidden, w_out)
    return (edges.astype(F32) + layer_norm(projected) * gain).astype(BF)


def pick_kernel(node_ref, border_ref, low_ref, high_ref):
    hot = one_hot(column_of(border_ref, 0, 2 * BORDER), NODES)
    picked = dot(hot, node_ref[...]).astype(BF)
    low_ref[...] = picked[:BORDER]
    high_ref[...] = picked[BORDER:]


def project_kernel(node_ref, w_ref, out_ref):
    nodes = node_ref[...]
    out_ref[:NODES] = dot(nodes, w_ref[2 * D :]).astype(BF)
    out_ref[NODES:] = dot(nodes, w_ref[D : 2 * D]).astype(BF)


def fine_kernel(
    edge_ref, send_ref, recv_ref, table_ref, low_ref, high_ref, w_in_ref, w_out_ref, gain_ref,
    new_ref, sum_ref, halo_ref, rows_ref, sems,
):
    halo_ref[:BORDER] = dot(low_ref[...], w_in_ref[D : 2 * D]).astype(BF)
    halo_ref[BORDER:] = dot(high_ref[...], w_in_ref[D : 2 * D]).astype(BF)
    gain = gain_ref[...]
    copies = []
    for at in range(EDGES // BLOCK):
        first = at * BLOCK
        edges = edge_ref[first : first + BLOCK]
        recv_hot = one_hot(column_of(recv_ref, first, BLOCK), NODES)
        send_hot = one_hot(column_of(send_ref, first, BLOCK), NODES + 2 * BORDER)
        pre = dot(edges, w_in_ref[:D])
        pre = pre + dot(recv_hot, table_ref[:NODES])
        pre = pre + dot(send_hot[:, :NODES], table_ref[NODES:])
        pre = pre + dot(send_hot[:, NODES:], halo_ref[...])
        rows_ref[first : first + BLOCK] = finish_edges(pre, edges, w_out_ref[...], gain)
        copies.append(send_rows(rows_ref, new_ref, sems, at))
    sum_ref[...] = dot(one_hot_rows(recv_ref, EDGES, NODES), rows_ref[...])
    for copy in copies:
        copy.wait()


def gather_kernel(send_ref, recv_ref, table_ref, send_out, recv_out):
    for first in range(0, EDGES, BLOCK):
        rows = slice(first, first + BLOCK)
        for ids_ref, out_ref in ((send_ref, send_out), (recv_ref, recv_out)):
            hot = one_hot(column_of(ids_ref, first, BLOCK), table_ref.shape[0])
            out_ref[rows] = dot(hot, table_ref[...]).astype(BF)


def coarse_kernel(
    edge_ref, send_ref, recv_ref, slot_ref, table_ref, send_part, recv_part, w_in_ref, w_out_ref,
    gain_ref, new_ref, sum_ref, rows_ref, sems,
):
    gain = gain_ref[...]
    half = table_ref.shape[0]
    copies = []
    for at in range(EDGES // BLOCK):
        first = at * BLOCK
        rows = slice(first, first + BLOCK)
        edges = edge_ref[rows]
        pre = dot(edges, w_in_ref[:D])
        for ids_ref, part_ref, part in ((send_ref, send_part, 1), (recv_ref, recv_part, 2)):
            hot = one_hot(column_of(ids_ref, first, BLOCK), half, half)
            picked = (dot(hot, table_ref[...]) + part_ref[rows].astype(F32)).astype(BF)
            pre = pre + dot(picked, w_in_ref[part * D : (part + 1) * D])
        rows_ref[rows] = finish_edges(pre, edges, w_out_ref[...], gain)
        copies.append(send_rows(rows_ref, new_ref, sems, at))
    sum_ref[...] = dot(one_hot_rows(slot_ref, EDGES, sum_ref.shape[0]), rows_ref[...]).astype(BF)
    for copy in copies:
        copy.wait()


def node_rows(nodes, incoming, w_in_ref, w_out_ref, gain):
    pre = dot(nodes, w_in_ref[:D]) + dot(incoming, w_in_ref[D:])
    projected = dot(silu(pre).astype(BF), w_out_ref[...])
    return (nodes.astype(F32) + layer_norm(projected) * gain).astype(BF)


def node_kernel(node_ref, sum_ref, w_in_ref, w_out_ref, gain_ref, out_ref, first_ref):
    for first in range(0, NODES, BLOCK):
        rows = slice(first, first + BLOCK)
        out_ref[rows] = node_rows(
            node_ref[rows], sum_ref[rows].astype(BF), w_in_ref, w_out_ref, gain_ref[...]
        )
    first_ref[...] = sum_ref[:TAIL]


def tail_kernel(
    node_ref, sum_ref, parts_ref, w_in_ref, w_out_ref, gain_ref, _, out_ref, rows_ref, sem
):
    parts = parts_ref[...].astype(F32).reshape(PATCHES, COARSE_ROWS, D)
    total = sum_ref[...]
    total = jnp.concatenate(
        [total[:COARSE_ROWS] + jnp.sum(parts, axis=0), total[COARSE_ROWS:]], axis=0
    )
    rows_ref[...] = node_rows(
        node_ref[:TAIL], total.astype(BF), w_in_ref, w_out_ref, gain_ref[...]
    )
    copy = pltpu.make_async_copy(rows_ref, out_ref.at[pl.ds(0, TAIL)], sem)
    copy.start()
    copy.wait()


def shape(rows, dtype=BF):
    return jax.ShapeDtypeStruct((rows, D), dtype)


VMEM_SPEC = pl.BlockSpec(memory_space=pltpu.VMEM)
ANY_SPEC = pl.BlockSpec(memory_space=pl.ANY)
HBM_SPEC = pl.BlockSpec(memory_space=pltpu.HBM)


def call(
    kernel, outs, flops, *args, name, scratch=(), out_any=(), in_any=(), aliases=None, spec=ANY_SPEC
):
    return pl.pallas_call(
        kernel,
        out_shape=outs,
        in_specs=[spec if at in in_any else VMEM_SPEC for at in range(len(args))],
        out_specs=tuple(
            ANY_SPEC if at in out_any else VMEM_SPEC for at in range(len(outs))
        ),
        scratch_shapes=scratch,
        input_output_aliases=aliases or {},
        compiler_params=pltpu.CompilerParams(vmem_limit_bytes=VMEM_LIMIT),
        cost_estimate=pl.CostEstimate(flops=flops, bytes_accessed=4 << 20, transcendentals=0),
        name=name,
    )(*args)


def patch_pairs(move):
    pairs = []
    for x in range(SIDE):
        for y in range(SIDE):
            for core in range(CORES):
                to_x, to_y, to_core = move(x, y, core)
                pairs.append(
                    ((x * SIDE + y) * CORES + core, (to_x * SIDE + to_y) * CORES + to_core)
                )
    return pairs


def even(i, length):
    return i ^ 1


def odd(i, length):
    return ((i + 1) ^ 1) - 1 if i < length - 1 and i > 0 else length - 1 - i


def crossed(k, turn):
    return patch_pairs(lambda x, y, c: (x ^ k, y, c) if c == turn else (x, y ^ k, c))


SWAP_CORE = patch_pairs(lambda x, y, c: (x, y, c ^ 1))
Z_EVEN = [(i, even(i, GROUPS)) for i in range(GROUPS)]
Z_ODD = [(i, odd(i, GROUPS)) for i in range(GROUPS)]
tie = lambda *arrays: lax.optimization_barrier(arrays)


def ring_offset(other, mine, length):
    step = jnp.where(mine & 1 == 0, 1, -1)
    return (other - mine) * step & (length - 1)


def place_8(offset):
    low, mid, high = offset & 1, offset >> 1 & 1, offset >> 2
    return (low ^ high) | high << 1 | (mid ^ high) << 2


def shards(
    node_lat, fine_edge_lat, fine_send, fine_recv, border_rows, coarse_edge_lat, coarse_send,
    coarse_recv, w_edge_in, w_edge_out, edge_gain, w_node_in, w_node_out, node_gain,
):
    group = lax.axis_index("group")
    patch = lax.axis_index("patch")
    my_core, my_y, my_x = patch & 1, patch >> 1 & 3, patch >> 3
    edge_gain = edge_gain[None, :]
    node_gain = node_gain[None, :]
    grid = lambda ids: ids.reshape(-1, 128)
    swap = lambda rows, pairs: lax.ppermute(rows, "patch", pairs)
    join = lambda *rows: jnp.concatenate(rows, axis=0)

    def place(ids):
        row, at = ids & 7, ids >> 3
        core, y, x, z = at & 1, (at >> 1 & 3) ^ my_y, (at >> 3 & 3) ^ my_x, at >> 5
        first, second = jnp.where(core == 0, x, y), jnp.where(core == 0, y, x)
        return (
            (core ^ my_core) << 10 | second << 8 | first << 6
            | place_8(ring_offset(z, group, GROUPS)) << 3 | row
        )

    send_place, recv_place = grid(place(coarse_send)), grid(place(coarse_recv))
    slot = grid(jnp.where(coarse_recv >> 8 == group, coarse_recv & 255, -1))

    def load(name, *arrays):
        return call(
            load_kernel, [jax.ShapeDtypeStruct(a.shape, a.dtype) for a in arrays], 0,
            *[pltpu.with_memory_space_constraint(a, pltpu.HBM) for a in arrays],
            name=name, scratch=[pltpu.SemaphoreType.DMA((len(arrays),))],
            in_any=range(len(arrays)), spec=HBM_SPEC,
        )

    own = node_lat[:COARSE_ROWS]
    own, *loads = tie(own, node_lat, w_edge_in, w_edge_out, border_rows)
    pair = lax.ppermute(own, "group", Z_EVEN)
    nodes, w_in, w_out = load("load_first", *loads[:3])
    pair, nodes, w_in, w_out = tie(pair, nodes, w_in, w_out)
    near = join(own, pair)
    near, nodes, *loads = tie(
        near, nodes, fine_edge_lat, coarse_edge_lat, w_node_in, w_node_out
    )
    next_two = lax.ppermute(near, "group", Z_ODD)
    low, high = call(
        pick_kernel, (shape(BORDER), shape(BORDER)), 2 * 256 * 512 * 512, nodes,
        grid(border_rows), name="pick",
    )
    fine_edges, coarse_edges, w_node, w_node_last = load("load_second", *loads)
    next_two, low, high, fine_edges, coarse_edges, w_node, w_node_last = tie(
        next_two, low, high, fine_edges, coarse_edges, w_node, w_node_last
    )
    up = [(i, (i + 1) % PATCHES) for i in range(PATCHES)]
    down = [(j, i) for i, j in up]
    far_two = lax.ppermute(next_two, "group", Z_EVEN)
    from_low = lax.ppermute(high, "patch", up)
    far_two, low = tie(far_two, low)
    last_two = lax.ppermute(far_two, "group", Z_ODD)
    from_high = lax.ppermute(low, "patch", down)
    block = join(near, next_two, far_two, last_two)

    block, nodes, w_in = tie(block, nodes, w_in)
    others = [swap(block, crossed(k, 0)) for k in (1, 2, 3)]
    (table,) = call(
        project_kernel, (shape(2 * NODES),), 4 * 512 * 512 * 512, nodes, w_in, name="project"
    )
    *others, table, from_low, from_high = tie(*others, table, from_low, from_high)
    block = join(block, *others)

    block, table = tie(block, table)
    others = [swap(block, crossed(k, 1)) for k in (1, 2, 3)]
    fine_new, fine_sum = call(
        fine_kernel, (shape(EDGES), shape(NODES, F32)), 4 << 30, fine_edges, grid(fine_send),
        grid(fine_recv), table, from_low, from_high, w_in, w_out, edge_gain, name="fine",
        scratch=[
            pltpu.VMEM((2 * BORDER, D), BF), pltpu.VMEM((EDGES, D), BF),
            pltpu.SemaphoreType.DMA((EDGES // BLOCK,)),
        ], out_any=(0,),
    )
    node_main, first_sum = call(
        node_kernel, (shape(NODES), shape(TAIL, F32)), 768 << 20, nodes, fine_sum, w_node,
        w_node_last, node_gain, name="node",
    )
    *others, first_sum = tie(*others, first_sum)
    part = join(block, *others)
    other_half = swap(part, SWAP_CORE)

    send_part, recv_part = call(
        gather_kernel, (shape(EDGES), shape(EDGES)), 2 << 30, send_place, recv_place, part,
        name="gather",
    )
    coarse_new, sums = call(
        coarse_kernel, (shape(EDGES), shape(PATCHES * COARSE_ROWS)), 4 << 30, coarse_edges,
        send_place, recv_place, slot, other_half, send_part, recv_part, w_in, w_out, edge_gain,
        name="coarse",
        scratch=[pltpu.VMEM((EDGES, D), BF), pltpu.SemaphoreType.DMA((EDGES // BLOCK,))],
        out_any=(0,),
    )

    parts = lax.all_to_all(sums.reshape(PATCHES, COARSE_ROWS, D), "patch", 0, 0)
    (node_new,) = call(
        tail_kernel, (shape(NODES),), 24 << 20, nodes, first_sum, parts.reshape(-1, D), w_node,
        w_node_last, node_gain, node_main, name="tail",
        scratch=[pltpu.VMEM((TAIL, D), BF), pltpu.SemaphoreType.DMA], out_any=(0,), in_any=(6,),
        aliases={6: 0},
    )
    return (node_new, fine_new, coarse_new)


def solution(mesh):
    in_specs = (
        P(("group", "patch"), None), P(("group", "patch"), None), P(("group", "patch")),
        P(("group", "patch")), P(("group", "patch")), P("patch", None), P("patch"), P("patch"),
        P(), P(), P(), P(), P(), P(),
    )
    out_specs = (P(("group", "patch"), None), P(("group", "patch"), None), P("patch", None))
    return jax.shard_map(shards, mesh=mesh, in_specs=in_specs, out_specs=out_specs, check_vma=False)
```

time: 76.6 us -> 71.1 us (0.928)
  the two profiles are of different devices: /device:TPU:24 before, /device:TPU:1 now
where the time goes in v3:
time: 71.1 us; the launch traced here: 70.8 us
  starting transfers between devices  26.5 us (37%)
  Pallas kernels  22.7 us (32%)
  blocking collectives  13.7 us (19%)
  waiting for transfers between devices  5.81 us (8%)
  between operations  1.11 us (2%)
  local copies, waits for them, and re-layouts  0.84 us (1%)
    pallas_call x9, Pallas kernels, call(): pl.pallas_call(kernel, out_shape=outs, in_specs=[spec if at in in_any els...  22.7 us
    all_to_all x1, blocking collectives, shards(): parts = lax.all_to_all(sums.reshape(PATCHES, COARSE_ROWS, D), 'patch', 0, 0)  13.7 us
    ppermute x7, starting transfers between devices, shards(): swap = lambda rows, pairs: lax.ppermute(rows, 'patch', pairs)  12.4 us
    ppermute x1, starting transfers between devices, shards(): from_low = lax.ppermute(high, 'patch', up)  5.5 us
    ppermute x1, starting transfers between devices, shards(): next_two = lax.ppermute(near, 'group', Z_ODD)  4.75 us
    ppermute x7, waiting for transfers between devices, shards(): swap = lambda rows, pairs: lax.ppermute(rows, 'patch', pairs)  3.22 us
    ppermute x1, waiting for transfers between devices, shards(): far_two = lax.ppermute(next_two, 'group', Z_EVEN)  2.58 us
    ppermute x1, starting transfers between devices, shards(): pair = lax.ppermute(own, 'group', Z_EVEN)  2.47 us
  transfers between devices with their start and end apart: 13, of which 4 were waited for; matrix products, arithmetic and copies ran while one was open for 0% of the time, Pallas kernels for 19%

profile of v3, /device:TPU:1, one launch (start us, length us, event | category | flops | bytes accessed | tf_op | source)
XLA Modules:
  0.0 70.8 jit_solution(7376686691886293042)
XLA Ops:
  0.6 0.7 slice.3
  1.3 2.5 %collective-permute-start = (bf16[8,512]{1,0:T(8,128)(2,1)S(1)}, bf16[8,512]{1,0:T(8,128)(2,1)S(1)}, u32[]{:S(2)}, u32[]{:S(2)}) collective-permute-start(bf16[8,512]{1,0:T(8,128)(2,1)S(1)} %slice.3), channel_id=1, source_target_pairs={{0,32},{32,0},{64,96},{96,64},{128,160},{160,128},{192,224},{224,1... | collective-permute-start | bytes 24584 | tf_op jit(solution)/shard_map/ppermute | solution.py:299
  3.8 1.7 %load_first.1 = (bf16[512,512]{1,0:T(8,128)(2,1)S(1)}, bf16[1536,512]{1,0:T(8,128)(2,1)S(1)}, bf16[512,512]{1,0:T(8,128)(2,1)S(1)}) custom-call(bf16[512,512]{1,0:T(8,128)(2,1)} %refs_0_, bf16[1536,512]{1,0:T(8,128)(2,1)} %refs_1_, bf16[512,512]{1,0:T(8,128)(2,1)} %refs_2_), custom_call_target="tpu_custom_call" | custom-call | bytes 4194304 | tf_op jit(solution)/shard_map/load_first/pallas_call | solution.py:209
  5.5 0.0 copy-start
  5.5 0.0 copy-start.6
  5.5 0.0 collective-permute-done
  5.6 0.0 copy-start.3
  5.6 4.8 %collective-permute-start.1 = (bf16[16,512]{1,0:T(8,128)(2,1)S(1)}, bf16[16,512]{1,0:T(8,128)(2,1)S(1)}, u32[]{:S(2)}, u32[]{:S(2)}) collective-permute-start(bf16[16,512]{1,0:T(8,128)(2,1)S(1)} %pad_maximum_fusion.2), channel_id=1, source_target_pairs={{0,224},{32,64},{64,32},{96,128},{128,96},{160,192},{192,160},{224... | collective-permute-start | bytes 49160 | tf_op jit(solution)/shard_map/ppermute | solution.py:306
  10.3 2.0 %load_second.1 = (bf16[1024,512]{1,0:T(8,128)(2,1)S(1)}, bf16[1024,512]{1,0:T(8,128)(2,1)S(1)}, bf16[1024,512]{1,0:T(8,128)(2,1)S(1)}, bf16[512,512]{1,0:T(8,128)(2,1)S(1)}) custom-call(bf16[1024,512]{1,0:T(8,128)(2,1)} %refs_0_.1, bf16[1024,512]{1,0:T(8,128)(2,1)} %refs_1_.1, bf16[1024,512]{1,0:T(8,128)(2,1)} %refs_2_.1, bf16[512,512]{1,0:T(8,128)(2,1)} %refs_3_), custom_call_target="tpu_custom_call" | custom-call | bytes 4194304 | tf_op jit(solution)/shard_map/load_second/pallas_call | solution.py:209
  12.4 0.0 copy-start.4
  12.4 0.0 copy-done.3
  12.4 0.3 pick.1
  12.7 0.0 collective-permute-done.1
  12.7 0.1 collective-permute-start.2
  12.8 2.6 %collective-permute-done.2 = bf16[16,512]{1,0:T(8,128)(2,1)S(1)} collective-permute-done((bf16[16,512]{1,0:T(8,128)(2,1)S(1)}, bf16[16,512]{1,0:T(8,128)(2,1)S(1)}, u32[]{:S(2)}, u32[]{:S(2)}) %collective-permute-start.2) | collective-permute-done | bytes 16416 | tf_op jit(solution)/shard_map/ppermute | solution.py:317
  15.4 1.3 %collective-permute-start.3 = (bf16[16,512]{1,0:T(8,128)(2,1)S(1)}, bf16[16,512]{1,0:T(8,128)(2,1)S(1)}, u32[]{:S(2)}, u32[]{:S(2)}) collective-permute-start(bf16[16,512]{1,0:T(8,128)(2,1)S(1)} %collective-permute-done.2), channel_id=1, source_target_pairs={{0,224},{32,64},{64,32},{96,128},{128,96},{160,192},{192,160},{224... | collective-permute-start | bytes 49160 | tf_op jit(solution)/shard_map/ppermute | solution.py:320
  16.7 5.5 %collective-permute-start.7 = (bf16[128,512]{1,0:T(8,128)(2,1)S(1)}, bf16[128,512]{1,0:T(8,128)(2,1)S(1)}, u32[]{:S(2)}, u32[]{:S(2)}) collective-permute-start(bf16[128,512]{1,0:T(8,128)(2,1)S(1)} %get-tuple-element.86), channel_id=1, source_target_pairs={{0,1},{1,2},{2,3},{3,4},{4,5},{5,6},{6,7},{7,8},{8,9},{9,10},{10,1... | collective-permute-start | bytes 393224 | tf_op jit(solution)/shard_map/ppermute | solution.py:318
  22.2 0.0 collective-permute-start.8
  22.2 0.0 collective-permute-done.3
  22.2 0.0 copy-start.8
  22.2 0.0 copy-start.9
  22.3 0.0 copy-start.10
  22.3 2.4 %collective-permute-start.6 = (bf16[64,512]{1,0:T(8,128)(2,1)S(1)}, bf16[64,512]{1,0:T(8,128)(2,1)S(1)}, u32[]{:S(2)}, u32[]{:S(2)}) collective-permute-start(bf16[64,512]{1,0:T(8,128)(2,1)S(1)} %pad_maximum_fusion.1), channel_id=1, source_target_pairs={{0,24},{1,7},{2,26},{3,5},{4,28},{5,3},{6,30},{7,1},{8,16},{9,15},... | collective-permute-start | bytes 196616 | tf_op jit(solution)/shard_map/ppermute | solution.py:274
  24.7 0.8 %collective-permute-start.5 = (bf16[64,512]{1,0:T(8,128)(2,1)S(1)}, bf16[64,512]{1,0:T(8,128)(2,1)S(1)}, u32[]{:S(2)}, u32[]{:S(2)}) collective-permute-start(bf16[64,512]{1,0:T(8,128)(2,1)S(1)} %pad_maximum_fusion.1), channel_id=1, source_target_pairs={{0,16},{1,5},{2,18},{3,7},{4,20},{5,1},{6,22},{7,3},{8,24},{9,13},... | collective-permute-start | bytes 196616 | tf_op jit(solution)/shard_map/ppermute | solution.py:274
  25.4 0.2 collective-permute-start.4
  25.6 0.7 %project.1.table_ref = bf16[1024,512]{1,0:T(8,128)(2,1)S(1)} custom-call(bf16[512,512]{1,0:T(8,128)(2,1)S(1)} %get-tuple-element.83.node_ref, bf16[1536,512]{1,0:T(8,128)(2,1)S(1)} %get-tuple-element.85.w_ref.w_in_ref), custom_call_target="tpu_custom_call" | custom-call | flops 536870912 | bytes 4194304 | tf_op jit(solution)/shard_map/project/pallas_call | solution.py:209
  26.3 0.0 copy-done.4
  26.3 0.7 collective-permute-done.6
  27.0 2.3 %collective-permute-done.5 = bf16[64,512]{1,0:T(8,128)(2,1)S(1)} collective-permute-done((bf16[64,512]{1,0:T(8,128)(2,1)S(1)}, bf16[64,512]{1,0:T(8,128)(2,1)S(1)}, u32[]{:S(2)}, u32[]{:S(2)}) %collective-permute-start.5) | collective-permute-done | bytes 65568 | tf_op jit(solution)/shard_map/ppermute | solution.py:274
  29.3 0.0 collective-permute-done.4
  29.3 0.0 collective-permute-done.7.low_ref
  29.3 0.0 collective-permute-done.8.high_ref
  29.3 1.8 %collective-permute-start.11 = (bf16[256,512]{1,0:T(8,128)(2,1)S(1)}, bf16[256,512]{1,0:T(8,128)(2,1)S(1)}, u32[]{:S(2)}, u32[]{:S(2)}) collective-permute-start(bf16[256,512]{1,0:T(8,128)(2,1)S(1)} %pad_maximum_fusion), channel_id=1, source_target_pairs={{0,6},{1,25},{2,4},{3,27},{4,2},{5,29},{6,0},{7,31},{8,14},{9,17},... | collective-permute-start | bytes 786440 | tf_op jit(solution)/shard_map/ppermute | solution.py:274
  31.2 1.3 %collective-permute-start.10 = (bf16[256,512]{1,0:T(8,128)(2,1)S(1)}, bf16[256,512]{1,0:T(8,128)(2,1)S(1)}, u32[]{:S(2)}, u32[]{:S(2)}) collective-permute-start(bf16[256,512]{1,0:T(8,128)(2,1)S(1)} %pad_maximum_fusion), channel_id=1, source_target_pairs={{0,4},{1,17},{2,6},{3,19},{4,0},{5,21},{6,2},{7,23},{8,12},{9,25},... | collective-permute-start | bytes 786440 | tf_op jit(solution)/shard_map/ppermute | solution.py:274
  32.4 0.3 collective-permute-start.9
  32.7 0.0 copy-done
  32.7 0.0 copy-done.6
  32.7 0.0 copy-done.8
  32.7 0.0 copy-done.9
  32.7 0.0 copy-done.10
  32.7 0.0 copy-start.2
  32.7 4.3 %fine.1 = (bf16[1024,512]{1,0:T(8,128)(2,1)}, f32[512,512]{1,0:T(8,128)S(1)}) custom-call(bf16[1024,512]{1,0:T(8,128)(2,1)S(1)} %get-tuple-element.93.edge_ref, s32[8,128]{1,0:T(8,128)S(1)} %bitcast.18, s32[8,128]{1,0:T(8,128)S(1)} %bitcast.19, bf16[1024,512]{1,0:T(8,128)(2,1)S(1)} %project.1.table_ref, bf16[128,512]{1,0:T(8,128)(2,1)S(1)} %collective-permute-done.7.low_ref, ...), custom_call_target="tpu_custom_call" | custom-call | flops 4294967296 | bytes 4194304 | tf_op jit(solution)/shard_map/fine/pallas_call | solution.py:209
  37.0 0.0 copy-done.2
  37.0 2.3 %node.1 = (bf16[512,512]{1,0:T(8,128)(2,1)}, f32[16,512]{1,0:T(8,128)S(1)}) custom-call(bf16[512,512]{1,0:T(8,128)(2,1)S(1)} %get-tuple-element.83.node_ref, f32[512,512]{1,0:T(8,128)S(1)} %get-tuple-element.98.sum_ref, bf16[1024,512]{1,0:T(8,128)(2,1)S(1)} %get-tuple-element.99.w_in_ref, bf16[512,512]{1,0:T(8,128)(2,1)S(1)} %get-tuple-element.100.w_out_ref, ...), custom_call_target="tpu_custom_call" | custom-call | flops 805306368 | bytes 4194304 | tf_op jit(solution)/shard_map/node/pallas_call | solution.py:209
  39.3 0.0 copy-start.11
  39.3 0.0 copy-start.12
  39.3 0.0 collective-permute-done.11
  39.3 0.0 collective-permute-done.10
  39.3 0.3 collective-permute-done.9
  39.7 5.7 %collective-permute-start.12 = (bf16[1024,512]{1,0:T(8,128)(2,1)S(1)}, bf16[1024,512]{1,0:T(8,128)(2,1)}, u32[]{:S(2)}, u32[]{:S(2)}) collective-permute-start(bf16[1024,512]{1,0:T(8,128)(2,1)S(1)} %constant_dynamic-update-slice_fusion.table_ref), channel_id=1, source_target_pairs={{0,1},{1,0},{2,3},{3,2},{4,5},{5,4},{6,7},{7,6},{8,9},{9,8},{10,11... | collective-permute-start | bytes 3145736 | tf_op jit(solution)/shard_map/ppermute | solution.py:274
  45.3 0.0 copy-done.11
  45.3 0.0 copy-done.12
  45.4 0.0 copy-start.1
  45.4 0.0 copy-start.5
  45.4 0.0 copy-start.7
  45.4 2.4 %gather.1 = (bf16[1024,512]{1,0:T(8,128)(2,1)S(1)}, bf16[1024,512]{1,0:T(8,128)(2,1)S(1)}) custom-call(s32[8,128]{1,0:T(8,128)S(1)} %or_bitcast_fusion.1.send_ref, s32[8,128]{1,0:T(8,128)S(1)} %get-tuple-element.114.recv_ref, bf16[1024,512]{1,0:T(8,128)(2,1)S(1)} %constant_dynamic-update-slice_fusion.table_ref), custom_call_target="tpu_custom_call" | custom-call | flops 2147483648 | bytes 4194304 | tf_op jit(solution)/shard_map/gather/pallas_call | solution.py:209
  47.8 0.0 collective-permute-done.12.table_ref
  47.8 0.0 copy-done.1
  47.8 0.0 copy-done.5
  47.8 0.0 copy-done.7
  47.8 7.8 %coarse.1 = (bf16[1024,512]{1,0:T(8,128)(2,1)}, bf16[256,512]{1,0:T(8,128)(2,1)S(1)}) custom-call(bf16[1024,512]{1,0:T(8,128)(2,1)S(1)} %copy-done.5, s32[8,128]{1,0:T(8,128)S(1)} %or_bitcast_fusion.1.send_ref, s32[8,128]{1,0:T(8,128)S(1)} %get-tuple-element.114.recv_ref, s32[8,128]{1,0:T(8,128)S(1)} %get-tuple-element.113.slot_ref, ...), custom_call_target="tpu_custom_call" | custom-call | flops 4294967296 | bytes 4194304 | tf_op jit(solution)/shard_map/coarse/pallas_call | solution.py:209
  55.7 13.7 %all_to_all.5 = bf16[32,8,512]{2,1,0:T(8,128)(2,1)S(1)} all-to-all(bf16[32,8,512]{2,1,0:T(8,128)(2,1)S(1)} %bitcast.14), channel_id=1, replica_groups=mesh['group'=8,'patch'=32] {'patch'}, dimensions={0} | all-to-all | bytes 524288 | tf_op jit(solution)/shard_map/all_to_all | solution.py:362
  69.4 1.2 %tail.1 = bf16[512,512]{1,0:T(8,128)(2,1)} custom-call(bf16[512,512]{1,0:T(8,128)(2,1)S(1)} %get-tuple-element.83.node_ref, f32[16,512]{1,0:T(8,128)S(1)} %get-tuple-element.102.sum_ref, bf16[256,512]{1,0:T(8,128)(2,1)S(1)} %bitcast.13, bf16[1024,512]{1,0:T(8,128)(2,1)S(1)} %get-tuple-element.99.w_in_ref, ...), custom_call_target="tpu_custom_call", output_to_operand_aliasing={{}: (6, {})} | custom-call | flops 25165824 | bytes 4194304 | tf_op jit(solution)/shard_map/tail/pallas_call | solution.py:209
  (9 shorter events, 0.1 us)
Async XLA Ops:
  1.3 4.2 %collective-permute-start = (bf16[8,512]{1,0:T(8,128)(2,1)S(1)}, bf16[8,512]{1,0:T(8,128)(2,1)S(1)}, u32[]{:S(2)}, u32[]{:S(2)}) collective-permute-start(bf16[8,512]{1,0:T(8,128)(2,1)S(1)} %slice.3), channel_id=1, source_target_pairs={{0,32},{32,0},{64,96},{96,64},{128,160},{160,128},{192,224},{224,1... | collective-permute-start | bytes 24584 | tf_op jit(solution)/shard_map/ppermute | solution.py:299
  5.5 27.2 %copy-start = (bf16[1536,512]{1,0:T(8,128)(2,1)}, bf16[1536,512]{1,0:T(8,128)(2,1)S(1)}, u32[]{:S(2)}) copy-start(bf16[1536,512]{1,0:T(8,128)(2,1)S(1)} %get-tuple-element.85.w_ref.w_in_ref) | copy-start | bytes 4718596
  5.5 27.1 %copy-start.6 = (bf16[512,512]{1,0:T(8,128)(2,1)}, bf16[512,512]{1,0:T(8,128)(2,1)S(1)}, u32[]{:S(2)}) copy-start(bf16[512,512]{1,0:T(8,128)(2,1)S(1)} %get-tuple-element.97.w_out_ref) | copy-start | bytes 1572868
  5.6 6.8 %copy-start.3 = (s32[256]{0:T(256)S(1)}, s32[256]{0:T(256)}, u32[]{:S(2)}) copy-start(s32[256]{0:T(256)} %param.18) | copy-start | bytes 3076
  5.6 7.2 %collective-permute-start.1 = (bf16[16,512]{1,0:T(8,128)(2,1)S(1)}, bf16[16,512]{1,0:T(8,128)(2,1)S(1)}, u32[]{:S(2)}, u32[]{:S(2)}) collective-permute-start(bf16[16,512]{1,0:T(8,128)(2,1)S(1)} %pad_maximum_fusion.2), channel_id=1, source_target_pairs={{0,224},{32,64},{64,32},{96,128},{128,96},{160,192},{192,160},{224... | collective-permute-start | bytes 49160 | tf_op jit(solution)/shard_map/ppermute | solution.py:306
  12.4 14.0 %copy-start.4 = (bf16[1024,512]{1,0:T(8,128)(2,1)}, bf16[1024,512]{1,0:T(8,128)(2,1)S(1)}, u32[]{:S(2)}) copy-start(bf16[1024,512]{1,0:T(8,128)(2,1)S(1)} %get-tuple-element.103.edge_ref) | copy-start | bytes 3145732
  12.7 2.7 %collective-permute-start.2 = (bf16[16,512]{1,0:T(8,128)(2,1)S(1)}, bf16[16,512]{1,0:T(8,128)(2,1)S(1)}, u32[]{:S(2)}, u32[]{:S(2)}) collective-permute-start(bf16[16,512]{1,0:T(8,128)(2,1)S(1)} %collective-permute-done.1), channel_id=1, source_target_pairs={{0,32},{32,0},{64,96},{96,64},{128,160},{160,128},{192,224},{224,1... | collective-permute-start | bytes 49160 | tf_op jit(solution)/shard_map/ppermute | solution.py:317
  15.4 6.8 %collective-permute-start.3 = (bf16[16,512]{1,0:T(8,128)(2,1)S(1)}, bf16[16,512]{1,0:T(8,128)(2,1)S(1)}, u32[]{:S(2)}, u32[]{:S(2)}) collective-permute-start(bf16[16,512]{1,0:T(8,128)(2,1)S(1)} %collective-permute-done.2), channel_id=1, source_target_pairs={{0,224},{32,64},{64,32},{96,128},{128,96},{160,192},{192,160},{224... | collective-permute-start | bytes 49160 | tf_op jit(solution)/shard_map/ppermute | solution.py:320
  16.7 12.6 %collective-permute-start.7 = (bf16[128,512]{1,0:T(8,128)(2,1)S(1)}, bf16[128,512]{1,0:T(8,128)(2,1)S(1)}, u32[]{:S(2)}, u32[]{:S(2)}) collective-permute-start(bf16[128,512]{1,0:T(8,128)(2,1)S(1)} %get-tuple-element.86), channel_id=1, source_target_pairs={{0,1},{1,2},{2,3},{3,4},{4,5},{5,6},{6,7},{7,8},{8,9},{9,10},{10,1... | collective-permute-start | bytes 393224 | tf_op jit(solution)/shard_map/ppermute | solution.py:318
  22.2 7.1 %collective-permute-start.8 = (bf16[128,512]{1,0:T(8,128)(2,1)S(1)}, bf16[128,512]{1,0:T(8,128)(2,1)S(1)}, u32[]{:S(2)}, u32[]{:S(2)}) collective-permute-start(bf16[128,512]{1,0:T(8,128)(2,1)S(1)} %get-tuple-element.87), channel_id=1, source_target_pairs={{1,0},{2,1},{3,2},{4,3},{5,4},{6,5},{7,6},{8,7},{9,8},{10,9},{11,1... | collective-permute-start | bytes 393224 | tf_op jit(solution)/shard_map/ppermute | solution.py:321
  22.2 10.4 %copy-start.8 = (s32[1024]{0:T(1024)S(1)}, s32[1024]{0:T(1024)}, u32[]{:S(2)}) copy-start(s32[1024]{0:T(1024)} %param.16) | copy-start | bytes 12292
  22.2 10.4 %copy-start.9 = (s32[1024]{0:T(1024)S(1)}, s32[1024]{0:T(1024)}, u32[]{:S(2)}) copy-start(s32[1024]{0:T(1024)} %param.17) | copy-start | bytes 12292
  22.3 10.4 %copy-start.10 = (f32[512]{0:T(512)S(1)}, f32[512]{0:T(512)}, u32[]{:S(2)}) copy-start(f32[512]{0:T(512)} %param.24) | copy-start | bytes 6148
  22.3 4.7 %collective-permute-start.6 = (bf16[64,512]{1,0:T(8,128)(2,1)S(1)}, bf16[64,512]{1,0:T(8,128)(2,1)S(1)}, u32[]{:S(2)}, u32[]{:S(2)}) collective-permute-start(bf16[64,512]{1,0:T(8,128)(2,1)S(1)} %pad_maximum_fusion.1), channel_id=1, source_target_pairs={{0,24},{1,7},{2,26},{3,5},{4,28},{5,3},{6,30},{7,1},{8,16},{9,15},... | collective-permute-start | bytes 196616 | tf_op jit(solution)/shard_map/ppermute | solution.py:274
  24.7 4.6 %collective-permute-start.5 = (bf16[64,512]{1,0:T(8,128)(2,1)S(1)}, bf16[64,512]{1,0:T(8,128)(2,1)S(1)}, u32[]{:S(2)}, u32[]{:S(2)}) collective-permute-start(bf16[64,512]{1,0:T(8,128)(2,1)S(1)} %pad_maximum_fusion.1), channel_id=1, source_target_pairs={{0,16},{1,5},{2,18},{3,7},{4,20},{5,1},{6,22},{7,3},{8,24},{9,13},... | collective-permute-start | bytes 196616 | tf_op jit(solution)/shard_map/ppermute | solution.py:274
  25.4 3.8 %collective-permute-start.4 = (bf16[64,512]{1,0:T(8,128)(2,1)S(1)}, bf16[64,512]{1,0:T(8,128)(2,1)S(1)}, u32[]{:S(2)}, u32[]{:S(2)}) collective-permute-start(bf16[64,512]{1,0:T(8,128)(2,1)S(1)} %pad_maximum_fusion.1), channel_id=1, source_target_pairs={{0,8},{1,3},{2,10},{3,1},{4,12},{5,7},{6,14},{7,5},{8,0},{9,11},{1... | collective-permute-start | bytes 196616 | tf_op jit(solution)/shard_map/ppermute | solution.py:274
  29.3 10.0 %collective-permute-start.11 = (bf16[256,512]{1,0:T(8,128)(2,1)S(1)}, bf16[256,512]{1,0:T(8,128)(2,1)S(1)}, u32[]{:S(2)}, u32[]{:S(2)}) collective-permute-start(bf16[256,512]{1,0:T(8,128)(2,1)S(1)} %pad_maximum_fusion), channel_id=1, source_target_pairs={{0,6},{1,25},{2,4},{3,27},{4,2},{5,29},{6,0},{7,31},{8,14},{9,17},... | collective-permute-start | bytes 786440 | tf_op jit(solution)/shard_map/ppermute | solution.py:274
  31.2 8.2 %collective-permute-start.10 = (bf16[256,512]{1,0:T(8,128)(2,1)S(1)}, bf16[256,512]{1,0:T(8,128)(2,1)S(1)}, u32[]{:S(2)}, u32[]{:S(2)}) collective-permute-start(bf16[256,512]{1,0:T(8,128)(2,1)S(1)} %pad_maximum_fusion), channel_id=1, source_target_pairs={{0,4},{1,17},{2,6},{3,19},{4,0},{5,21},{6,2},{7,23},{8,12},{9,25},... | collective-permute-start | bytes 786440 | tf_op jit(solution)/shard_map/ppermute | solution.py:274
  32.4 7.2 %collective-permute-start.9 = (bf16[256,512]{1,0:T(8,128)(2,1)S(1)}, bf16[256,512]{1,0:T(8,128)(2,1)S(1)}, u32[]{:S(2)}, u32[]{:S(2)}) collective-permute-start(bf16[256,512]{1,0:T(8,128)(2,1)S(1)} %pad_maximum_fusion), channel_id=1, source_target_pairs={{0,2},{1,9},{2,0},{3,11},{4,6},{5,13},{6,4},{7,15},{8,10},{9,1},{1... | collective-permute-start | bytes 786440 | tf_op jit(solution)/shard_map/ppermute | solution.py:274
  32.7 4.3 %copy-start.2 = (f32[512]{0:T(512)S(1)}, f32[512]{0:T(512)}, u32[]{:S(2)}) copy-start(f32[512]{0:T(512)} %param.27) | copy-start | bytes 6148
  39.3 6.1 %copy-start.11 = (s32[1024]{0:T(1024)S(1)}, s32[1024]{0:T(1024)}, u32[]{:S(2)}) copy-start(s32[1024]{0:T(1024)} %param.20) | copy-start | bytes 12292
  39.3 6.1 %copy-start.12 = (s32[1024]{0:T(1024)S(1)}, s32[1024]{0:T(1024)}, u32[]{:S(2)}) copy-start(s32[1024]{0:T(1024)} %param.21) | copy-start | bytes 12292
  39.7 8.1 %collective-permute-start.12 = (bf16[1024,512]{1,0:T(8,128)(2,1)S(1)}, bf16[1024,512]{1,0:T(8,128)(2,1)}, u32[]{:S(2)}, u32[]{:S(2)}) collective-permute-start(bf16[1024,512]{1,0:T(8,128)(2,1)S(1)} %constant_dynamic-update-slice_fusion.table_ref), channel_id=1, source_target_pairs={{0,1},{1,0},{2,3},{3,2},{4,5},{5,4},{6,7},{7,6},{8,9},{9,8},{10,11... | collective-permute-start | bytes 3145736 | tf_op jit(solution)/shard_map/ppermute | solution.py:274
  45.4 2.4 %copy-start.1 = (bf16[1536,512]{1,0:T(8,128)(2,1)S(1)}, bf16[1536,512]{1,0:T(8,128)(2,1)}, u32[]{:S(2)}) copy-start(bf16[1536,512]{1,0:T(8,128)(2,1)} %copy-done) | copy-start | bytes 4718596
  45.4 2.4 %copy-start.5 = (bf16[1024,512]{1,0:T(8,128)(2,1)S(1)}, bf16[1024,512]{1,0:T(8,128)(2,1)}, u32[]{:S(2)}) copy-start(bf16[1024,512]{1,0:T(8,128)(2,1)} %copy-done.4) | copy-start | bytes 3145732
  45.4 2.4 %copy-start.7 = (bf16[512,512]{1,0:T(8,128)(2,1)S(1)}, bf16[512,512]{1,0:T(8,128)(2,1)}, u32[]{:S(2)}) copy-start(bf16[512,512]{1,0:T(8,128)(2,1)} %copy-done.6) | copy-start | bytes 1572868

commit v4 on v3

v4 whole, which is shorter than its diff:
```python
import functools

import jax
import jax.numpy as jnp
from jax import lax
from jax.experimental import pallas as pl
from jax.experimental.pallas import tpu as pltpu
from jax.sharding import PartitionSpec as P

D = 512
GROUPS = 8
SIDE = 4
CORES = 2
PATCHES = SIDE * SIDE * CORES
BORDER = 128
COARSE_ROWS = 8
EDGES = 1024
NODES = 512
TAIL = 16
EPS = 1e-05
BF = jnp.bfloat16
F32 = jnp.float32
BLOCK = 512
VMEM_LIMIT = 24 * 1024 * 1024


def dot(a, b):
    return jnp.dot(a, b, preferred_element_type=F32)


def silu(values):
    half = 0.5 * values
    return half * jnp.tanh(half) + half


def layer_norm(values):
    average = jnp.mean(values, axis=-1, keepdims=True)
    centred = values - average
    variance = jnp.mean(centred * centred, axis=-1, keepdims=True)
    return centred * lax.rsqrt(variance + EPS)


def column_of(ids_ref, first, rows):
    tiles = []
    for at in range(first // 128, (first + rows) // 128):
        row = jnp.broadcast_to(ids_ref[at : at + 1, :], (128, 128))
        tiles.append(row.T)
    return jnp.concatenate(tiles, axis=0).astype(jnp.int16)


def one_hot(column, width, offset=0):
    lanes = lax.broadcasted_iota(jnp.int16, column.shape, 1)
    one, zero = jnp.ones(column.shape, BF), jnp.zeros(column.shape, BF)
    return jnp.concatenate(
        [
            jnp.where(column == lanes + jnp.int16(offset + 128 * at), one, zero)
            for at in range(width // 128)
        ],
        axis=1,
    )


def one_hot_rows(ids_ref, count, height):
    rows = lax.broadcasted_iota(jnp.int16, (height, 128), 0)
    one, zero = jnp.ones((height, 128), BF), jnp.zeros((height, 128), BF)
    parts = []
    for at in range(count // 128):
        ids = jnp.broadcast_to(ids_ref[at : at + 1, :], (height, 128)).astype(jnp.int16)
        parts.append(jnp.where(ids == rows, one, zero))
    return jnp.concatenate(parts, axis=1)


def send_rows(rows_ref, out_ref, sems, at):
    rows = pl.ds(at * BLOCK, BLOCK)
    copy = pltpu.make_async_copy(rows_ref.at[rows], out_ref.at[rows], sems.at[at])
    copy.start()
    return copy


def load_kernel(*refs):
    count = len(refs) // 2
    sems = refs[-1]
    copies = [
        pltpu.make_async_copy(refs[at], refs[count + at], sems.at[at]) for at in range(count)
    ]
    for copy in copies:
        copy.start()
    for copy in copies:
        copy.wait()


def finish_edges(pre, edges, w_out, gain):
    hidden = silu(pre).astype(BF)
    projected = dot(hidden, w_out)
    return (edges.astype(F32) + layer_norm(projected) * gain).astype(BF)


def pick_kernel(
    border_ref, node_in, w_in, w_out, inner_ref, outer_ref, node_ref, w_in_ref, w_out_ref, sems
):
    copies = [
        pltpu.make_async_copy(source, target, sems.at[at])
        for at, (source, target) in enumerate(
            ((node_in, node_ref), (w_in, w_in_ref), (w_out, w_out_ref))
        )
    ]
    for copy in copies:
        copy.start()
    hot = one_hot(column_of(border_ref, 0, 2 * BORDER), NODES)
    copies[0].wait()
    picked = dot(hot, node_ref[...]).astype(BF)
    inner_ref[...] = picked[:BORDER]
    outer_ref[...] = picked[BORDER:]
    for copy in copies[1:]:
        copy.wait()


def project_kernel(node_ref, w_ref, out_ref):
    nodes = node_ref[...]
    out_ref[:NODES] = dot(nodes, w_ref[2 * D :]).astype(BF)
    out_ref[NODES:] = dot(nodes, w_ref[D : 2 * D]).astype(BF)


def fine_kernel(
    edge_ref, send_ref, recv_ref, table_ref, inner_ref, outer_ref, w_in_ref, w_out_ref, gain_ref,
    new_ref, sum_ref, halo_ref, rows_ref, sem,
):
    halo_ref[:BORDER] = dot(inner_ref[...], w_in_ref[D : 2 * D]).astype(BF)
    halo_ref[BORDER:] = dot(outer_ref[...], w_in_ref[D : 2 * D]).astype(BF)
    edges = edge_ref[...]
    recv_hot = one_hot(column_of(recv_ref, 0, EDGES), NODES)
    send_hot = one_hot(column_of(send_ref, 0, EDGES), NODES + 2 * BORDER)
    pre = dot(edges, w_in_ref[:D])
    pre = pre + dot(jnp.concatenate([recv_hot, send_hot[:, :NODES]], axis=1), table_ref[...])
    pre = pre + dot(send_hot[:, NODES:], halo_ref[...])
    rows_ref[...] = finish_edges(pre, edges, w_out_ref[...], gain_ref[...])
    copy = pltpu.make_async_copy(rows_ref, new_ref, sem)
    copy.start()
    sum_ref[...] = dot(one_hot_rows(recv_ref, EDGES, NODES), rows_ref[...])
    copy.wait()


def gather_kernel(send_ref, recv_ref, table_ref, send_out, recv_out):
    for first in range(0, EDGES, BLOCK):
        rows = slice(first, first + BLOCK)
        for ids_ref, out_ref in ((send_ref, send_out), (recv_ref, recv_out)):
            hot = one_hot(column_of(ids_ref, first, BLOCK), table_ref.shape[0])
            out_ref[rows] = dot(hot, table_ref[...]).astype(BF)


def coarse_kernel(
    edge_ref, send_ref, recv_ref, slot_ref, table_ref, send_part, recv_part, w_in_ref, w_out_ref,
    gain_ref, new_ref, mine_ref, theirs_ref, rows_ref, sems,
):
    gain = gain_ref[...]
    half = table_ref.shape[0]
    copies = []
    for at in range(EDGES // BLOCK):
        rows = slice(at * BLOCK, (at + 1) * BLOCK)
        edges = edge_ref[rows]
        joined = [edges]
        for ids_ref, part_ref in ((send_ref, send_part), (recv_ref, recv_part)):
            hot = one_hot(column_of(ids_ref, at * BLOCK, BLOCK), half, half)
            joined.append((dot(hot, table_ref[...]) + part_ref[rows].astype(F32)).astype(BF))
        pre = dot(jnp.concatenate(joined, axis=1), w_in_ref[...])
        rows_ref[rows] = finish_edges(pre, edges, w_out_ref[...], gain)
        copies.append(send_rows(rows_ref, new_ref, sems, at))
    sums = dot(one_hot_rows(slot_ref, EDGES, 2 * mine_ref.shape[0]), rows_ref[...])
    mine_ref[...] = sums[: mine_ref.shape[0]]
    theirs_ref[...] = sums[mine_ref.shape[0] :].astype(BF)
    for copy in copies:
        copy.wait()


def finish_nodes(pre, nodes, w_out_ref, gain):
    projected = dot(silu(pre).astype(BF), w_out_ref[...])
    return (nodes.astype(F32) + layer_norm(projected) * gain).astype(BF)


def node_kernel(node_ref, sum_ref, w_in_ref, w_out_ref, gain_ref, out_ref, first_ref, pre_ref):
    nodes = node_ref[...]
    pre = dot(nodes, w_in_ref[:D])
    pre_ref[...] = pre[:TAIL]
    first_ref[...] = sum_ref[:TAIL]
    pre = pre + dot(sum_ref[...].astype(BF), w_in_ref[D:])
    out_ref[...] = finish_nodes(pre, nodes, w_out_ref, gain_ref[...])


def tail_kernel(
    node_ref, sum_ref, pre_ref, parts_ref, w_in_ref, w_out_ref, gain_ref, _, out_ref, rows_ref, sem
):
    parts = parts_ref[...].astype(F32).reshape(-1, COARSE_ROWS, D)
    total = sum_ref[...]
    total = jnp.concatenate(
        [total[:COARSE_ROWS] + jnp.sum(parts, axis=0), total[COARSE_ROWS:]], axis=0
    )
    pre = pre_ref[...] + dot(total.astype(BF), w_in_ref[D:])
    rows_ref[...] = finish_nodes(pre, node_ref[:TAIL], w_out_ref, gain_ref[...])
    copy = pltpu.make_async_copy(rows_ref, out_ref.at[pl.ds(0, TAIL)], sem)
    copy.start()
    copy.wait()


def shape(rows, dtype=BF):
    return jax.ShapeDtypeStruct((rows, D), dtype)


VMEM_SPEC = pl.BlockSpec(memory_space=pltpu.VMEM)
ANY_SPEC = pl.BlockSpec(memory_space=pl.ANY)
HBM_SPEC = pl.BlockSpec(memory_space=pltpu.HBM)


def call(
    kernel, outs, flops, *args, name, scratch=(), out_any=(), in_any=(), aliases=None, spec=ANY_SPEC
):
    return pl.pallas_call(
        kernel,
        out_shape=outs,
        in_specs=[spec if at in in_any else VMEM_SPEC for at in range(len(args))],
        out_specs=tuple(
            ANY_SPEC if at in out_any else VMEM_SPEC for at in range(len(outs))
        ),
        scratch_shapes=scratch,
        input_output_aliases=aliases or {},
        compiler_params=pltpu.CompilerParams(vmem_limit_bytes=VMEM_LIMIT),
        cost_estimate=pl.CostEstimate(flops=flops, bytes_accessed=4 << 20, transcendentals=0),
        name=name,
    )(*args)


def patch_pairs(move):
    pairs = []
    for x in range(SIDE):
        for y in range(SIDE):
            for core in range(CORES):
                to_x, to_y, to_core = move(x, y, core)
                pairs.append(
                    ((x * SIDE + y) * CORES + core, (to_x * SIDE + to_y) * CORES + to_core)
                )
    return pairs


def crossed(k, turn):
    return patch_pairs(lambda x, y, c: (x ^ k, y, c) if c == turn else (x, y ^ k, c))


SWAP_CORE = patch_pairs(lambda x, y, c: (x, y, c ^ 1))


def along_z(move):
    pairs = []
    for group in range(GROUPS):
        pair, member = move(group >> 1, group & 1)
        target = ((pair % (GROUPS // 2)) << 1 | member) * PATCHES
        pairs += [(group * PATCHES + i, target + (i ^ 1)) for i in range(PATCHES)]
    return pairs


Z_PAIR = along_z(lambda pair, member: (pair, member ^ 1))
Z_FAR = along_z(lambda pair, member: (pair + 2, member ^ 1))
Z_MID = along_z(lambda pair, member: (pair - 1 + 2 * member, member))
Z_NEAR = along_z(lambda pair, member: (pair - 1 + 2 * member, member ^ 1))
OUTER = [(i, (i + 1 if i & 1 else i - 1) % PATCHES) for i in range(PATCHES)]
SAME_CORE = [[2 * i + core for i in range(PATCHES // 2)] for core in range(CORES)]
tie = lambda *arrays: lax.optimization_barrier(arrays)


def place_z(group, mine):
    away = ((group >> 1) - (mine >> 1)) * jnp.where(mine & 1 == 0, 1, -1) & 3
    high = away >> 1
    place = ((away ^ high) & 1) << 2 | high << 1 | ((group ^ mine) & 1 ^ high)
    return place, (place & 1) ^ jnp.where(place >= 2, 1, 0)


def shards(
    node_lat, fine_edge_lat, fine_send, fine_recv, border_rows, coarse_edge_lat, coarse_send,
    coarse_recv, w_edge_in, w_edge_out, edge_gain, w_node_in, w_node_out, node_gain,
):
    group = lax.axis_index("group")
    patch = lax.axis_index("patch")
    my_core, my_y, my_x = patch & 1, patch >> 1 & 3, patch >> 3
    edge_gain = edge_gain[None, :]
    node_gain = node_gain[None, :]
    grid = lambda ids: ids.reshape(-1, 128)
    swap = lambda rows, pairs: lax.ppermute(rows, "patch", pairs)
    join = lambda *rows: jnp.concatenate(rows, axis=0)

    turn = lambda away: away ^ (away >> 1)

    def place(ids):
        row, at = ids & 7, ids >> 3
        core, y, x = at & 1, turn(at >> 1 & 3 ^ my_y), turn(at >> 3 & 3 ^ my_x)
        z, exchanged = place_z(at >> 5, group)
        half = core ^ my_core ^ exchanged
        x_first = half == my_core
        first, second = jnp.where(x_first, x, y), jnp.where(x_first, y, x)
        return half << 10 | second << 8 | first << 6 | z << 3 | row

    send_place, recv_place = grid(place(coarse_send)), grid(place(coarse_recv))
    slot = (coarse_recv >> 3 & 1 ^ my_core) << 7 | (coarse_recv >> 4 & 15) << 3 | coarse_recv & 7
    slot = grid(jnp.where(coarse_recv >> 8 == group, slot, -1))
    lower, upper = border_rows[:BORDER], border_rows[BORDER:]
    borders = jnp.stack(
        [jnp.where(my_core == 0, upper, lower), jnp.where(my_core == 0, lower, upper)]
    )
    fine_place = grid(
        jnp.where((fine_send >= NODES) & (my_core == 0), fine_send ^ BORDER, fine_send)
    )
    in_hbm = lambda *arrays: [pltpu.with_memory_space_constraint(a, pltpu.HBM) for a in arrays]
    like = lambda *arrays: [jax.ShapeDtypeStruct(a.shape, a.dtype) for a in arrays]

    own = node_lat[:COARSE_ROWS]
    own, *loads = tie(own, node_lat, w_edge_in, w_edge_out)
    pair = lax.ppermute(own, ("group", "patch"), Z_PAIR)
    inner, outer, nodes, w_in, w_out = call(
        pick_kernel, [shape(BORDER), shape(BORDER), *like(*loads)], 2 * 256 * 512 * 512, borders,
        *in_hbm(*loads), name="pick", scratch=[pltpu.SemaphoreType.DMA((3,))], in_any=(1, 2, 3),
        spec=HBM_SPEC,
    )
    pair, inner, outer, nodes, w_in, w_out = tie(pair, inner, outer, nodes, w_in, w_out)
    near = join(own, pair)
    near, inner, outer = tie(near, inner, outer)
    others = [lax.ppermute(near, ("group", "patch"), to) for to in (Z_NEAR, Z_MID, Z_FAR)]
    inner, outer = swap(inner, SWAP_CORE), swap(outer, OUTER)
    block = join(near, *others)

    block, nodes, w_in, *loads = tie(
        block, nodes, w_in, fine_edge_lat, coarse_edge_lat, w_node_in, w_node_out
    )
    others = [swap(block, crossed(k, 0)) for k in (1, 3, 2)]
    (table,) = call(
        project_kernel, (shape(2 * NODES),), 4 * 512 * 512 * 512, nodes, w_in, name="project"
    )
    fine_edges, coarse_edges, w_node, w_node_last = call(
        load_kernel, like(*loads), 0, *in_hbm(*loads), name="load",
        scratch=[pltpu.SemaphoreType.DMA((len(loads),))], in_any=range(len(loads)), spec=HBM_SPEC,
    )
    *others, table, inner, outer, fine_edges, coarse_edges, w_node, w_node_last = tie(
        *others, table, inner, outer, fine_edges, coarse_edges, w_node, w_node_last
    )
    block = join(block, *others)

    block, table = tie(block, table)
    others = [swap(block, crossed(k, 1)) for k in (1, 3, 2)]
    fine_new, fine_sum = call(
        fine_kernel, (shape(EDGES), shape(NODES, F32)), 4 << 30, fine_edges, fine_place,
        grid(fine_recv), table, inner, outer, w_in, w_out, edge_gain, name="fine",
        scratch=[
            pltpu.VMEM((2 * BORDER, D), BF), pltpu.VMEM((EDGES, D), BF), pltpu.SemaphoreType.DMA
        ], out_any=(0,),
    )
    node_main, first_sum, first_pre = call(
        node_kernel, (shape(NODES), shape(TAIL, F32), shape(TAIL, F32)), 768 << 20, nodes,
        fine_sum, w_node, w_node_last, node_gain, name="node",
    )
    *others, first_sum = tie(*others, first_sum)
    part = join(block, *others)
    other_half = swap(part, SWAP_CORE)

    send_part, recv_part = call(
        gather_kernel, (shape(EDGES), shape(EDGES)), 2 << 30, send_place, recv_place, part,
        name="gather",
    )
    coarse_new, mine, theirs = call(
        coarse_kernel, (shape(EDGES), shape(128, F32), shape(128)), 4 << 30, coarse_edges,
        send_place, recv_place, slot, other_half, send_part, recv_part, w_in, w_out, edge_gain,
        name="coarse",
        scratch=[pltpu.VMEM((EDGES, D), BF), pltpu.SemaphoreType.DMA((EDGES // BLOCK,))],
        out_any=(0,),
    )

    sums = (mine + swap(theirs, SWAP_CORE).astype(F32)).astype(BF)
    parts = lax.all_to_all(
        sums.reshape(-1, COARSE_ROWS, D), "patch", 0, 0, axis_index_groups=SAME_CORE
    )
    (node_new,) = call(
        tail_kernel, (shape(NODES),), 24 << 20, nodes, first_sum, first_pre, parts.reshape(-1, D),
        w_node, w_node_last, node_gain, node_main, name="tail",
        scratch=[pltpu.VMEM((TAIL, D), BF), pltpu.SemaphoreType.DMA], out_any=(0,), in_any=(7,),
        aliases={7: 0},
    )
    return (node_new, fine_new, coarse_new)


def solution(mesh):
    in_specs = (
        P(("group", "patch"), None), P(("group", "patch"), None), P(("group", "patch")),
        P(("group", "patch")), P(("group", "patch")), P("patch", None), P("patch"), P("patch"),
        P(), P(), P(), P(), P(), P(),
    )
    out_specs = (P(("group", "patch"), None), P(("group", "patch"), None), P("patch", None))
    return jax.shard_map(shards, mesh=mesh, in_specs=in_specs, out_specs=out_specs, check_vma=False)
```

time: 71.1 us -> 63.8 us (0.90)
  waiting for transfers between devices: 5.81 us -> 1.89 us
  blocking collectives: 13.7 us -> 11.6 us
  starting transfers between devices: 26.5 us -> 25.3 us
  Pallas kernels: 22.7 us -> 21.7 us
  other arithmetic: 0.07 us -> 0.88 us
    ppermute x6 -> x4, waiting for transfers between devices: 2.59 us -> 0.28 us  [the longest x3 0.28 us: shards(): lax.ppermute(near, ('group', 'patch'), to)]
    ppermute x6 -> x4, starting transfers between devices: 14.1 us -> 11.9 us  [the longest x3 8.84 us: shards(): lax.ppermute(near, ('group', 'patch'), to)]
    all_to_all x1, blocking collectives: 13.7 us -> 11.6 us  [shards(): lax.all_to_all(sums.reshape(-1, COARSE_ROWS, D), 'patch', 0, 0, axis_inde...]
    ppermute x7 -> x10, waiting for transfers between devices: 3.22 us -> 1.61 us  [shards(): swap = lambda rows, pairs: lax.ppermute(rows, 'patch', pairs)]
    ppermute x7 -> x10, starting transfers between devices: 12.4 us -> 13.4 us  [shards(): swap = lambda rows, pairs: lax.ppermute(rows, 'patch', pairs)]
    pallas_call x9 -> x8, Pallas kernels: 22.7 us -> 21.7 us  [call(): pl.pallas_call(kernel, out_shape=outs, in_specs=[spec if at in in_any els...]
    another operation x0 -> x2, other arithmetic: none -> 0.77 us  [shards(): jnp.stack([jnp.where(my_core == 0, upper, lower), jnp.where(my_core == 0,...]
  transfers between devices with their start and end apart: 13 -> 14, of which waited for: 4 -> 3; matrix products, arithmetic and copies ran while one was open for 0% -> 1% of each run, Pallas kernels for 19% -> 21%
where the time goes in v4:
time: 63.8 us; the launch traced here: 63.5 us
  starting transfers between devices  25.3 us (40%)
  Pallas kernels  21.7 us (34%)
  blocking collectives  11.6 us (18%)
  waiting for transfers between devices  1.89 us (3%)
  between operations  1.08 us (2%)
  local copies, waits for them, and re-layouts  1.06 us (2%)
  other arithmetic  0.88 us (1%)
    pallas_call x8, Pallas kernels, call(): pl.pallas_call(kernel, out_shape=outs, in_specs=[spec if at in in_any els...  21.7 us
    ppermute x10, starting transfers between devices, shards(): swap = lambda rows, pairs: lax.ppermute(rows, 'patch', pairs)  13.4 us
    all_to_all x1, blocking collectives, shards(): lax.all_to_all(sums.reshape(-1, COARSE_ROWS, D), 'patch', 0, 0, axis_inde...  11.6 us
    ppermute x3, starting transfers between devices, shards(): lax.ppermute(near, ('group', 'patch'), to)  8.84 us
    ppermute x1, starting transfers between devices, shards(): pair = lax.ppermute(own, ('group', 'patch'), Z_PAIR)  3.03 us
    ppermute x10, waiting for transfers between devices, shards(): swap = lambda rows, pairs: lax.ppermute(rows, 'patch', pairs)  1.61 us
  transfers between devices with their start and end apart: 14, of which 3 were waited for; matrix products, arithmetic and copies ran while one was open for 1% of the time, Pallas kernels for 21%

profile of v4, /device:TPU:1, one launch (start us, length us, event | category | flops | bytes accessed | tf_op | source)
XLA Modules:
  0.0 63.5 jit_solution(18435901278671207869)
XLA Ops:
  0.6 0.0 copy-start.9
  0.6 0.7 %slice.9 = bf16[8,512]{1,0:T(8,128)(2,1)S(1)} slice(bf16[512,512]{1,0:T(8,128)(2,1)} %node_in), slice={[0:8], [0:512]} | slice | bytes 16384 | tf_op jit(solution)/shard_map/slice | solution.py:312
  1.3 3.0 %collective-permute-start = (bf16[8,512]{1,0:T(8,128)(2,1)S(1)}, bf16[8,512]{1,0:T(8,128)(2,1)S(1)}, u32[]{:S(2)}, u32[]{:S(2)}) collective-permute-start(bf16[8,512]{1,0:T(8,128)(2,1)S(1)} %slice.9), channel_id=1, source_target_pairs={{0,33},{1,32},{2,35},{3,34},{4,37},{5,36},{6,39},{7,38},{8,41},{9,... | collective-permute-start | bytes 24584 | tf_op jit(solution)/shard_map/ppermute | solution.py:314
  4.4 0.8 %fusion.12 = (s32[1,128]{1,0:T(1,128)S(1)}, s32[1,128]{1,0:T(1,128)S(1)}) fusion(pred[]{:T(512)S(6)} %eq.10, s32[256]{0:T(256)} %param.18), kind=kLoop, calls=%fused_computation.42 | loop fusion | flops 256 | bytes 2049 | tf_op jit(solution)/shard_map/stack | solution.py:303
  5.1 1.7 %pick.1 = (bf16[128,512]{1,0:T(8,128)(2,1)S(1)}, bf16[128,512]{1,0:T(8,128)(2,1)S(1)}, bf16[512,512]{1,0:T(8,128)(2,1)S(1)}, bf16[1536,512]{1,0:T(8,128)(2,1)S(1)}, bf16[512,512]{1,0:T(8,128)(2,1)S(1)}) custom-call(s32[2,128]{1,0:T(2,128)S(1)} %pad_add_fusion.border_ref, bf16[512,512]{1,0:T(8,128)(2,1)} %node_in, bf16[1536,512]{1,0:T(8,128)(2,1)} %w_in, ...), custom_call_target="tpu_custom_call" | custom-call | flops 134217728 | bytes 4194304 | tf_op jit(solution)/shard_map/pick/pallas_call | solution.py:216
  6.9 0.0 copy-start
  6.9 0.0 copy-start.5
  6.9 0.0 collective-permute-done
  6.9 5.4 %collective-permute-start.3 = (bf16[16,512]{1,0:T(8,128)(2,1)S(1)}, bf16[16,512]{1,0:T(8,128)(2,1)S(1)}, u32[]{:S(2)}, u32[]{:S(2)}) collective-permute-start(bf16[16,512]{1,0:T(8,128)(2,1)S(1)} %pad_maximum_fusion.2), channel_id=1, source_target_pairs={{0,161},{1,160},{2,163},{3,162},{4,165},{5,164},{6,167},{7,166},{8... | collective-permute-start | bytes 49160 | tf_op jit(solution)/shard_map/ppermute | solution.py:323
  12.4 0.3 collective-permute-start.2
  12.6 3.1 %collective-permute-start.1 = (bf16[16,512]{1,0:T(8,128)(2,1)S(1)}, bf16[16,512]{1,0:T(8,128)(2,1)S(1)}, u32[]{:S(2)}, u32[]{:S(2)}) collective-permute-start(bf16[16,512]{1,0:T(8,128)(2,1)S(1)} %pad_maximum_fusion.2), channel_id=1, source_target_pairs={{0,225},{1,224},{2,227},{3,226},{4,229},{5,228},{6,231},{7,230},{8... | collective-permute-start | bytes 49160 | tf_op jit(solution)/shard_map/ppermute | solution.py:323
  15.8 0.6 collective-permute-start.7
  16.4 1.2 %collective-permute-start.8 = (bf16[128,512]{1,0:T(8,128)(2,1)S(1)}, bf16[128,512]{1,0:T(8,128)(2,1)S(1)}, u32[]{:S(2)}, u32[]{:S(2)}) collective-permute-start(bf16[128,512]{1,0:T(8,128)(2,1)S(1)} %get-tuple-element.77), channel_id=1, source_target_pairs={{0,31},{1,2},{2,1},{3,4},{4,3},{5,6},{6,5},{7,8},{8,7},{9,10},{10,... | collective-permute-start | bytes 393224 | tf_op jit(solution)/shard_map/ppermute | solution.py:285
  17.5 0.0 collective-permute-done.3
  17.5 0.0 collective-permute-done.2
  17.5 0.3 collective-permute-done.1
  17.8 2.9 %collective-permute-start.6 = (bf16[64,512]{1,0:T(8,128)(2,1)S(1)}, bf16[64,512]{1,0:T(8,128)(2,1)S(1)}, u32[]{:S(2)}, u32[]{:S(2)}) collective-permute-start(bf16[64,512]{1,0:T(8,128)(2,1)S(1)} %pad_maximum_fusion.1), channel_id=1, source_target_pairs={{0,16},{1,5},{2,18},{3,7},{4,20},{5,1},{6,22},{7,3},{8,24},{9,13},... | collective-permute-start | bytes 196616 | tf_op jit(solution)/shard_map/ppermute | solution.py:285
  20.7 0.8 %collective-permute-start.5 = (bf16[64,512]{1,0:T(8,128)(2,1)S(1)}, bf16[64,512]{1,0:T(8,128)(2,1)S(1)}, u32[]{:S(2)}, u32[]{:S(2)}) collective-permute-start(bf16[64,512]{1,0:T(8,128)(2,1)S(1)} %pad_maximum_fusion.1), channel_id=1, source_target_pairs={{0,24},{1,7},{2,26},{3,5},{4,28},{5,3},{6,30},{7,1},{8,16},{9,15},... | collective-permute-start | bytes 196616 | tf_op jit(solution)/shard_map/ppermute | solution.py:285
  21.5 0.0 collective-permute-start.4
  21.5 0.0 copy-done.9
  21.5 2.0 %load.1 = (bf16[1024,512]{1,0:T(8,128)(2,1)S(1)}, bf16[1024,512]{1,0:T(8,128)(2,1)S(1)}, bf16[1024,512]{1,0:T(8,128)(2,1)S(1)}, bf16[512,512]{1,0:T(8,128)(2,1)S(1)}) custom-call(bf16[1024,512]{1,0:T(8,128)(2,1)} %refs_0_, bf16[1024,512]{1,0:T(8,128)(2,1)} %refs_1_, bf16[1024,512]{1,0:T(8,128)(2,1)} %refs_2_, bf16[512,512]{1,0:T(8,128)(2,1)} %refs_3_), custom_call_target="tpu_custom_call" | custom-call | bytes 4194304 | tf_op jit(solution)/shard_map/load/pallas_call | solution.py:216
  23.6 0.0 copy-start.3
  23.6 0.0 copy-start.7
  23.6 0.0 copy-start.8
  23.6 0.7 %project.1.table_ref = bf16[1024,512]{1,0:T(8,128)(2,1)S(1)} custom-call(bf16[512,512]{1,0:T(8,128)(2,1)S(1)} %get-tuple-element.73.node_ref, bf16[1536,512]{1,0:T(8,128)(2,1)S(1)} %get-tuple-element.75.w_ref.w_in_ref), custom_call_target="tpu_custom_call" | custom-call | flops 536870912 | bytes 4194304 | tf_op jit(solution)/shard_map/project/pallas_call | solution.py:216
  24.3 0.2 copy-done.3
  24.5 0.0 collective-permute-done.6
  24.5 0.5 collective-permute-done.5
  25.1 0.0 collective-permute-done.4
  25.1 0.0 collective-permute-done.7.inner_ref
  25.1 0.0 collective-permute-done.8.outer_ref
  25.1 2.8 %collective-permute-start.11 = (bf16[256,512]{1,0:T(8,128)(2,1)S(1)}, bf16[256,512]{1,0:T(8,128)(2,1)S(1)}, u32[]{:S(2)}, u32[]{:S(2)}) collective-permute-start(bf16[256,512]{1,0:T(8,128)(2,1)S(1)} %pad_maximum_fusion), channel_id=1, source_target_pairs={{0,4},{1,17},{2,6},{3,19},{4,0},{5,21},{6,2},{7,23},{8,12},{9,25},... | collective-permute-start | bytes 786440 | tf_op jit(solution)/shard_map/ppermute | solution.py:285
  27.9 1.0 %collective-permute-start.10 = (bf16[256,512]{1,0:T(8,128)(2,1)S(1)}, bf16[256,512]{1,0:T(8,128)(2,1)S(1)}, u32[]{:S(2)}, u32[]{:S(2)}) collective-permute-start(bf16[256,512]{1,0:T(8,128)(2,1)S(1)} %pad_maximum_fusion), channel_id=1, source_target_pairs={{0,6},{1,25},{2,4},{3,27},{4,2},{5,29},{6,0},{7,31},{8,14},{9,17},... | collective-permute-start | bytes 786440 | tf_op jit(solution)/shard_map/ppermute | solution.py:285
  28.9 0.0 collective-permute-start.9
  28.9 0.0 copy-done
  28.9 0.0 copy-done.5
  28.9 0.0 copy-done.7
  29.0 0.0 copy-done.8
  29.0 0.0 copy-start.2
  29.0 4.5 %fine.1 = (bf16[1024,512]{1,0:T(8,128)(2,1)}, f32[512,512]{1,0:T(8,128)S(1)}) custom-call(bf16[1024,512]{1,0:T(8,128)(2,1)S(1)} %get-tuple-element.91.edge_ref, s32[8,128]{1,0:T(8,128)S(1)} %fusion.9.send_ref, s32[8,128]{1,0:T(8,128)S(1)} %bitcast.21, bf16[1024,512]{1,0:T(8,128)(2,1)S(1)} %project.1.table_ref, ...), custom_call_target="tpu_custom_call" | custom-call | flops 4294967296 | bytes 4194304 | tf_op jit(solution)/shard_map/fine/pallas_call | solution.py:216
  33.5 0.0 copy-done.2
  33.5 2.1 %node.1 = (bf16[512,512]{1,0:T(8,128)(2,1)}, f32[16,512]{1,0:T(8,128)S(1)}, f32[16,512]{1,0:T(8,128)S(1)}) custom-call(bf16[512,512]{1,0:T(8,128)(2,1)S(1)} %get-tuple-element.73.node_ref, f32[512,512]{1,0:T(8,128)S(1)} %get-tuple-element.96.sum_ref, bf16[1024,512]{1,0:T(8,128)(2,1)S(1)} %get-tuple-element.97.w_in_ref, ...), custom_call_target="tpu_custom_call" | custom-call | flops 805306368 | bytes 4194304 | tf_op jit(solution)/shard_map/node/pallas_call | solution.py:216
  35.6 0.0 copy-start.10
  35.6 0.0 copy-start.11
  35.6 0.0 collective-permute-done.11
  35.6 0.0 collective-permute-done.10
  35.6 0.0 collective-permute-done.9
  35.7 3.7 %collective-permute-start.12 = (bf16[1024,512]{1,0:T(8,128)(2,1)S(1)}, bf16[1024,512]{1,0:T(8,128)(2,1)}, u32[]{:S(2)}, u32[]{:S(2)}) collective-permute-start(bf16[1024,512]{1,0:T(8,128)(2,1)S(1)} %constant_dynamic-update-slice_fusion.table_ref), channel_id=1, source_target_pairs={{0,1},{1,0},{2,3},{3,2},{4,5},{5,4},{6,7},{7,6},{8,9},{9,8},{10,11... | collective-permute-start | bytes 3145736 | tf_op jit(solution)/shard_map/ppermute | solution.py:285
  39.5 0.0 copy-done.10
  39.5 0.0 copy-done.11
  39.5 0.0 copy-start.1
  39.6 0.0 copy-start.4
  39.6 0.0 copy-start.6
  39.6 2.4 %gather.1 = (bf16[1024,512]{1,0:T(8,128)(2,1)S(1)}, bf16[1024,512]{1,0:T(8,128)(2,1)S(1)}) custom-call(s32[8,128]{1,0:T(8,128)S(1)} %or_bitcast_fusion.1.send_ref, s32[8,128]{1,0:T(8,128)S(1)} %get-tuple-element.114.recv_ref, bf16[1024,512]{1,0:T(8,128)(2,1)S(1)} %constant_dynamic-update-slice_fusion.table_ref), custom_call_target="tpu_custom_call" | custom-call | flops 2147483648 | bytes 4194304 | tf_op jit(solution)/shard_map/gather/pallas_call | solution.py:216
  42.0 0.0 collective-permute-done.12.table_ref
  42.0 0.0 copy-done.1
  42.0 0.0 copy-done.4
  42.0 0.0 copy-done.6
  42.0 7.1 %coarse.1 = (bf16[1024,512]{1,0:T(8,128)(2,1)}, f32[128,512]{1,0:T(8,128)S(1)}, bf16[128,512]{1,0:T(8,128)(2,1)S(1)}) custom-call(bf16[1024,512]{1,0:T(8,128)(2,1)S(1)} %copy-done.4, s32[8,128]{1,0:T(8,128)S(1)} %or_bitcast_fusion.1.send_ref, s32[8,128]{1,0:T(8,128)S(1)} %get-tuple-element.114.recv_ref, s32[8,128]{1,0:T(8,128)S(1)} %get-tuple-element.113.slot_ref, ...), custom_call_target="tpu_custom_call" | custom-call | flops 4294967296 | bytes 4194304 | tf_op jit(solution)/shard_map/coarse/pallas_call | solution.py:216
  49.1 0.4 collective-permute-start.13
  49.5 1.1 %collective-permute-done.13 = bf16[128,512]{1,0:T(8,128)(2,1)S(1)} collective-permute-done((bf16[128,512]{1,0:T(8,128)(2,1)S(1)}, bf16[128,512]{1,0:T(8,128)(2,1)S(1)}, u32[]{:S(2)}, u32[]{:S(2)}) %collective-permute-start.13) | collective-permute-done | bytes 131104 | tf_op jit(solution)/shard_map/ppermute | solution.py:285
  50.6 11.6 %all_to_all.5 = bf16[16,8,512]{2,1,0:T(8,128)(2,1)S(1)} all-to-all(bf16[16,8,512]{2,1,0:T(8,128)(2,1)S(1)} %fusion), channel_id=1, replica_groups={{0,2,4,6,8,10,12,14,16,18,20,22,24,26,28,30},{1,3,5,7,9,11,13,15,17,19,..., dimensions={0} | all-to-all | bytes 262144 | tf_op jit(solution)/shard_map/all_to_all | solution.py:373
  62.2 1.1 %tail.1 = bf16[512,512]{1,0:T(8,128)(2,1)} custom-call(bf16[512,512]{1,0:T(8,128)(2,1)S(1)} %get-tuple-element.73.node_ref, f32[16,512]{1,0:T(8,128)S(1)} %get-tuple-element.100.sum_ref, f32[16,512]{1,0:T(8,128)S(1)} %get-tuple-element.101.pre_ref, bf16[128,512]{1,0:T(8,128)(2,1)S(1)} %bitcast.18, ...), custom_call_target="tpu_custom_call", output_to_operand_aliasing={{}: (7, {})} | custom-call | flops 25165824 | bytes 4194304 | tf_op jit(solution)/shard_map/tail/pallas_call | solution.py:216
  (12 shorter events, 0.2 us)
Async XLA Ops:
  0.6 20.9 %copy-start.9 = (s32[1024]{0:T(1024)S(1)}, s32[1024]{0:T(1024)}, u32[]{:S(2)}) copy-start(s32[1024]{0:T(1024)} %param.16) | copy-start | bytes 12292
  1.3 5.5 %collective-permute-start = (bf16[8,512]{1,0:T(8,128)(2,1)S(1)}, bf16[8,512]{1,0:T(8,128)(2,1)S(1)}, u32[]{:S(2)}, u32[]{:S(2)}) collective-permute-start(bf16[8,512]{1,0:T(8,128)(2,1)S(1)} %slice.9), channel_id=1, source_target_pairs={{0,33},{1,32},{2,35},{3,34},{4,37},{5,36},{6,39},{7,38},{8,41},{9,... | collective-permute-start | bytes 24584 | tf_op jit(solution)/shard_map/ppermute | solution.py:314
  6.9 22.1 %copy-start = (bf16[1536,512]{1,0:T(8,128)(2,1)}, bf16[1536,512]{1,0:T(8,128)(2,1)S(1)}, u32[]{:S(2)}) copy-start(bf16[1536,512]{1,0:T(8,128)(2,1)S(1)} %get-tuple-element.75.w_ref.w_in_ref) | copy-start | bytes 4718596
  6.9 22.1 %copy-start.5 = (bf16[512,512]{1,0:T(8,128)(2,1)}, bf16[512,512]{1,0:T(8,128)(2,1)S(1)}, u32[]{:S(2)}) copy-start(bf16[512,512]{1,0:T(8,128)(2,1)S(1)} %get-tuple-element.95.w_out_ref) | copy-start | bytes 1572868
  6.9 10.6 %collective-permute-start.3 = (bf16[16,512]{1,0:T(8,128)(2,1)S(1)}, bf16[16,512]{1,0:T(8,128)(2,1)S(1)}, u32[]{:S(2)}, u32[]{:S(2)}) collective-permute-start(bf16[16,512]{1,0:T(8,128)(2,1)S(1)} %pad_maximum_fusion.2), channel_id=1, source_target_pairs={{0,161},{1,160},{2,163},{3,162},{4,165},{5,164},{6,167},{7,166},{8... | collective-permute-start | bytes 49160 | tf_op jit(solution)/shard_map/ppermute | solution.py:323
  12.4 5.2 %collective-permute-start.2 = (bf16[16,512]{1,0:T(8,128)(2,1)S(1)}, bf16[16,512]{1,0:T(8,128)(2,1)S(1)}, u32[]{:S(2)}, u32[]{:S(2)}) collective-permute-start(bf16[16,512]{1,0:T(8,128)(2,1)S(1)} %pad_maximum_fusion.2), channel_id=1, source_target_pairs={{0,193},{1,192},{2,195},{3,194},{4,197},{5,196},{6,199},{7,198},{8... | collective-permute-start | bytes 49160 | tf_op jit(solution)/shard_map/ppermute | solution.py:323
  12.6 5.2 %collective-permute-start.1 = (bf16[16,512]{1,0:T(8,128)(2,1)S(1)}, bf16[16,512]{1,0:T(8,128)(2,1)S(1)}, u32[]{:S(2)}, u32[]{:S(2)}) collective-permute-start(bf16[16,512]{1,0:T(8,128)(2,1)S(1)} %pad_maximum_fusion.2), channel_id=1, source_target_pairs={{0,225},{1,224},{2,227},{3,226},{4,229},{5,228},{6,231},{7,230},{8... | collective-permute-start | bytes 49160 | tf_op jit(solution)/shard_map/ppermute | solution.py:323
  15.8 9.3 %collective-permute-start.7 = (bf16[128,512]{1,0:T(8,128)(2,1)S(1)}, bf16[128,512]{1,0:T(8,128)(2,1)S(1)}, u32[]{:S(2)}, u32[]{:S(2)}) collective-permute-start(bf16[128,512]{1,0:T(8,128)(2,1)S(1)} %get-tuple-element.76), channel_id=1, source_target_pairs={{0,1},{1,0},{2,3},{3,2},{4,5},{5,4},{6,7},{7,6},{8,9},{9,8},{10,11... | collective-permute-start | bytes 393224 | tf_op jit(solution)/shard_map/ppermute | solution.py:285
  16.4 8.7 %collective-permute-start.8 = (bf16[128,512]{1,0:T(8,128)(2,1)S(1)}, bf16[128,512]{1,0:T(8,128)(2,1)S(1)}, u32[]{:S(2)}, u32[]{:S(2)}) collective-permute-start(bf16[128,512]{1,0:T(8,128)(2,1)S(1)} %get-tuple-element.77), channel_id=1, source_target_pairs={{0,31},{1,2},{2,1},{3,4},{4,3},{5,6},{6,5},{7,8},{8,7},{9,10},{10,... | collective-permute-start | bytes 393224 | tf_op jit(solution)/shard_map/ppermute | solution.py:285
  17.8 6.7 %collective-permute-start.6 = (bf16[64,512]{1,0:T(8,128)(2,1)S(1)}, bf16[64,512]{1,0:T(8,128)(2,1)S(1)}, u32[]{:S(2)}, u32[]{:S(2)}) collective-permute-start(bf16[64,512]{1,0:T(8,128)(2,1)S(1)} %pad_maximum_fusion.1), channel_id=1, source_target_pairs={{0,16},{1,5},{2,18},{3,7},{4,20},{5,1},{6,22},{7,3},{8,24},{9,13},... | collective-permute-start | bytes 196616 | tf_op jit(solution)/shard_map/ppermute | solution.py:285
  20.7 4.3 %collective-permute-start.5 = (bf16[64,512]{1,0:T(8,128)(2,1)S(1)}, bf16[64,512]{1,0:T(8,128)(2,1)S(1)}, u32[]{:S(2)}, u32[]{:S(2)}) collective-permute-start(bf16[64,512]{1,0:T(8,128)(2,1)S(1)} %pad_maximum_fusion.1), channel_id=1, source_target_pairs={{0,24},{1,7},{2,26},{3,5},{4,28},{5,3},{6,30},{7,1},{8,16},{9,15},... | collective-permute-start | bytes 196616 | tf_op jit(solution)/shard_map/ppermute | solution.py:285
  21.5 3.6 %collective-permute-start.4 = (bf16[64,512]{1,0:T(8,128)(2,1)S(1)}, bf16[64,512]{1,0:T(8,128)(2,1)S(1)}, u32[]{:S(2)}, u32[]{:S(2)}) collective-permute-start(bf16[64,512]{1,0:T(8,128)(2,1)S(1)} %pad_maximum_fusion.1), channel_id=1, source_target_pairs={{0,8},{1,3},{2,10},{3,1},{4,12},{5,7},{6,14},{7,5},{8,0},{9,11},{1... | collective-permute-start | bytes 196616 | tf_op jit(solution)/shard_map/ppermute | solution.py:285
  23.6 1.0 %copy-start.3 = (bf16[1024,512]{1,0:T(8,128)(2,1)}, bf16[1024,512]{1,0:T(8,128)(2,1)S(1)}, u32[]{:S(2)}) copy-start(bf16[1024,512]{1,0:T(8,128)(2,1)S(1)} %get-tuple-element.102.edge_ref) | copy-start | bytes 3145732
  23.6 5.4 %copy-start.7 = (s32[1024]{0:T(1024)S(1)}, s32[1024]{0:T(1024)}, u32[]{:S(2)}) copy-start(s32[1024]{0:T(1024)} %param.17) | copy-start | bytes 12292
  23.6 5.4 %copy-start.8 = (f32[512]{0:T(512)S(1)}, f32[512]{0:T(512)}, u32[]{:S(2)}) copy-start(f32[512]{0:T(512)} %param.24) | copy-start | bytes 6148
  25.1 10.5 %collective-permute-start.11 = (bf16[256,512]{1,0:T(8,128)(2,1)S(1)}, bf16[256,512]{1,0:T(8,128)(2,1)S(1)}, u32[]{:S(2)}, u32[]{:S(2)}) collective-permute-start(bf16[256,512]{1,0:T(8,128)(2,1)S(1)} %pad_maximum_fusion), channel_id=1, source_target_pairs={{0,4},{1,17},{2,6},{3,19},{4,0},{5,21},{6,2},{7,23},{8,12},{9,25},... | collective-permute-start | bytes 786440 | tf_op jit(solution)/shard_map/ppermute | solution.py:285
  27.9 7.7 %collective-permute-start.10 = (bf16[256,512]{1,0:T(8,128)(2,1)S(1)}, bf16[256,512]{1,0:T(8,128)(2,1)S(1)}, u32[]{:S(2)}, u32[]{:S(2)}) collective-permute-start(bf16[256,512]{1,0:T(8,128)(2,1)S(1)} %pad_maximum_fusion), channel_id=1, source_target_pairs={{0,6},{1,25},{2,4},{3,27},{4,2},{5,29},{6,0},{7,31},{8,14},{9,17},... | collective-permute-start | bytes 786440 | tf_op jit(solution)/shard_map/ppermute | solution.py:285
  28.9 6.7 %collective-permute-start.9 = (bf16[256,512]{1,0:T(8,128)(2,1)S(1)}, bf16[256,512]{1,0:T(8,128)(2,1)S(1)}, u32[]{:S(2)}, u32[]{:S(2)}) collective-permute-start(bf16[256,512]{1,0:T(8,128)(2,1)S(1)} %pad_maximum_fusion), channel_id=1, source_target_pairs={{0,2},{1,9},{2,0},{3,11},{4,6},{5,13},{6,4},{7,15},{8,10},{9,1},{1... | collective-permute-start | bytes 786440 | tf_op jit(solution)/shard_map/ppermute | solution.py:285
  29.0 4.5 %copy-start.2 = (f32[512]{0:T(512)S(1)}, f32[512]{0:T(512)}, u32[]{:S(2)}) copy-start(f32[512]{0:T(512)} %param.27) | copy-start | bytes 6148
  35.6 3.9 %copy-start.10 = (s32[1024]{0:T(1024)S(1)}, s32[1024]{0:T(1024)}, u32[]{:S(2)}) copy-start(s32[1024]{0:T(1024)} %param.20) | copy-start | bytes 12292
  35.6 3.9 %copy-start.11 = (s32[1024]{0:T(1024)S(1)}, s32[1024]{0:T(1024)}, u32[]{:S(2)}) copy-start(s32[1024]{0:T(1024)} %param.21) | copy-start | bytes 12292
  35.7 6.2 %collective-permute-start.12 = (bf16[1024,512]{1,0:T(8,128)(2,1)S(1)}, bf16[1024,512]{1,0:T(8,128)(2,1)}, u32[]{:S(2)}, u32[]{:S(2)}) collective-permute-start(bf16[1024,512]{1,0:T(8,128)(2,1)S(1)} %constant_dynamic-update-slice_fusion.table_ref), channel_id=1, source_target_pairs={{0,1},{1,0},{2,3},{3,2},{4,5},{5,4},{6,7},{7,6},{8,9},{9,8},{10,11... | collective-permute-start | bytes 3145736 | tf_op jit(solution)/shard_map/ppermute | solution.py:285
  39.5 2.4 %copy-start.1 = (bf16[1536,512]{1,0:T(8,128)(2,1)S(1)}, bf16[1536,512]{1,0:T(8,128)(2,1)}, u32[]{:S(2)}) copy-start(bf16[1536,512]{1,0:T(8,128)(2,1)} %copy-done) | copy-start | bytes 4718596
  39.6 2.4 %copy-start.4 = (bf16[1024,512]{1,0:T(8,128)(2,1)S(1)}, bf16[1024,512]{1,0:T(8,128)(2,1)}, u32[]{:S(2)}) copy-start(bf16[1024,512]{1,0:T(8,128)(2,1)} %copy-done.3) | copy-start | bytes 3145732
  39.6 2.4 %copy-start.6 = (bf16[512,512]{1,0:T(8,128)(2,1)S(1)}, bf16[512,512]{1,0:T(8,128)(2,1)}, u32[]{:S(2)}) copy-start(bf16[512,512]{1,0:T(8,128)(2,1)} %copy-done.5) | copy-start | bytes 1572868
  49.1 1.4 %collective-permute-start.13 = (bf16[128,512]{1,0:T(8,128)(2,1)S(1)}, bf16[128,512]{1,0:T(8,128)(2,1)S(1)}, u32[]{:S(2)}, u32[]{:S(2)}) collective-permute-start(bf16[128,512]{1,0:T(8,128)(2,1)S(1)} %get-tuple-element.109), channel_id=1, source_target_pairs={{0,1},{1,0},{2,3},{3,2},{4,5},{5,4},{6,7},{7,6},{8,9},{9,8},{10,11... | collective-permute-start | bytes 393224 | tf_op jit(solution)/shard_map/ppermute | solution.py:285

commit v5 on v4

--- a/solution.py
+++ b/solution.py
@@ -15,13 +15,14 @@
 BORDER = 128
 COARSE_ROWS = 8
 EDGES = 1024
+HALF = 512
 NODES = 512
 TAIL = 16
 EPS = 1e-05
 BF = jnp.bfloat16
 F32 = jnp.float32
 BLOCK = 512
-VMEM_LIMIT = 24 * 1024 * 1024
+VMEM_LIMIT = 10 * 1024 * 1024
 
 
 def dot(a, b):
@@ -60,11 +61,11 @@
     )
 
 
-def one_hot_rows(ids_ref, count, height):
+def one_hot_rows(ids_ref, first, count, height):
     rows = lax.broadcasted_iota(jnp.int16, (height, 128), 0)
     one, zero = jnp.ones((height, 128), BF), jnp.zeros((height, 128), BF)
     parts = []
-    for at in range(count // 128):
+    for at in range(first // 128, (first + count) // 128):
         ids = jnp.broadcast_to(ids_ref[at : at + 1, :], (height, 128)).astype(jnp.int16)
         parts.append(jnp.where(ids == rows, one, zero))
     return jnp.concatenate(parts, axis=1)
@@ -77,18 +78,6 @@
     return copy
 
 
-def load_kernel(*refs):
-    count = len(refs) // 2
-    sems = refs[-1]
-    copies = [
-        pltpu.make_async_copy(refs[at], refs[count + at], sems.at[at]) for at in range(count)
-    ]
-    for copy in copies:
-        copy.start()
-    for copy in copies:
-        copy.wait()
-
-
 def finish_edges(pre, edges, w_out, gain):
     hidden = silu(pre).astype(BF)
     projected = dot(hidden, w_out)
@@ -96,22 +85,29 @@
 
 
 def pick_kernel(
-    border_ref, node_in, w_in, w_out, inner_ref, outer_ref, node_ref, w_in_ref, w_out_ref, sems
+    border_in, node_in, w_in, w_out, inner_ref, outer_ref, node_ref, w_in_ref, w_out_ref,
+    border_ref, sems,
 ):
     copies = [
         pltpu.make_async_copy(source, target, sems.at[at])
         for at, (source, target) in enumerate(
-            ((node_in, node_ref), (w_in, w_in_ref), (w_out, w_out_ref))
+            (
+                (border_in, border_ref), (node_in, node_ref), (w_in, w_in_ref),
+                (w_out, w_out_ref),
+            )
         )
     ]
     for copy in copies:
         copy.start()
+    copies[0].wait()
     hot = one_hot(column_of(border_ref, 0, 2 * BORDER), NODES)
-    copies[0].wait()
+    copies[1].wait()
     picked = dot(hot, node_ref[...]).astype(BF)
-    inner_ref[...] = picked[:BORDER]
-    outer_ref[...] = picked[BORDER:]
-    for copy in copies[1:]:
+    lower, upper = picked[:BORDER], picked[BORDER:]
+    on_first = lax.axis_index("patch") % CORES == 0
+    inner_ref[...] = jnp.where(on_first, upper, lower)
+    outer_ref[...] = jnp.where(on_first, lower, upper)
+    for copy in copies[2:]:
         copy.wait()
 
 
@@ -122,21 +118,28 @@
 
 
 def fine_kernel(
-    edge_ref, send_ref, recv_ref, table_ref, inner_ref, outer_ref, w_in_ref, w_out_ref, gain_ref,
-    new_ref, sum_ref, halo_ref, rows_ref, sem,
-):
-    halo_ref[:BORDER] = dot(inner_ref[...], w_in_ref[D : 2 * D]).astype(BF)
-    halo_ref[BORDER:] = dot(outer_ref[...], w_in_ref[D : 2 * D]).astype(BF)
-    edges = edge_ref[...]
-    recv_hot = one_hot(column_of(recv_ref, 0, EDGES), NODES)
-    send_hot = one_hot(column_of(send_ref, 0, EDGES), NODES + 2 * BORDER)
+    first, edge_ref, send_ref, recv_ref, table_ref, inner_ref, outer_ref, w_in_ref, w_out_ref,
+    gain_ref, *rest,
+):
+    if first:
+        halo_in, before_ref, _, new_ref, sum_ref, rows_ref, sem = rest
+        halo = halo_in[...]
+    else:
+        new_ref, sum_ref, halo_out, rows_ref, sem = rest
+        halo_out[:BORDER] = dot(inner_ref[...], w_in_ref[D : 2 * D]).astype(BF)
+        halo_out[BORDER:] = dot(outer_ref[...], w_in_ref[D : 2 * D]).astype(BF)
+        halo = halo_out[...]
+    edges = edge_ref[first : first + HALF]
+    recv_hot = one_hot(column_of(recv_ref, first, HALF), NODES)
+    send_hot = one_hot(column_of(send_ref, first, HALF), NODES + 2 * BORDER)
     pre = dot(edges, w_in_ref[:D])
     pre = pre + dot(jnp.concatenate([recv_hot, send_hot[:, :NODES]], axis=1), table_ref[...])
-    pre = pre + dot(send_hot[:, NODES:], halo_ref[...])
+    pre = pre + dot(send_hot[:, NODES:], halo)
     rows_ref[...] = finish_edges(pre, edges, w_out_ref[...], gain_ref[...])
-    copy = pltpu.make_async_copy(rows_ref, new_ref, sem)
+    copy = pltpu.make_async_copy(rows_ref, new_ref.at[pl.ds(first, HALF)], sem)
     copy.start()
-    sum_ref[...] = dot(one_hot_rows(recv_ref, EDGES, NODES), rows_ref[...])
+    sums = dot(one_hot_rows(recv_ref, first, HALF, NODES), rows_ref[...])
+    sum_ref[...] = before_ref[...] + sums if first else sums
     copy.wait()
 
 
@@ -150,7 +153,7 @@
 
 def coarse_kernel(
     edge_ref, send_ref, recv_ref, slot_ref, table_ref, send_part, recv_part, w_in_ref, w_out_ref,
-    gain_ref, new_ref, mine_ref, theirs_ref, rows_ref, sems,
+    gain_ref, new_ref, sum_ref, rows_ref, sems,
 ):
     gain = gain_ref[...]
     half = table_ref.shape[0]
@@ -165,9 +168,8 @@
         pre = dot(jnp.concatenate(joined, axis=1), w_in_ref[...])
         rows_ref[rows] = finish_edges(pre, edges, w_out_ref[...], gain)
         copies.append(send_rows(rows_ref, new_ref, sems, at))
-    sums = dot(one_hot_rows(slot_ref, EDGES, 2 * mine_ref.shape[0]), rows_ref[...])
-    mine_ref[...] = sums[: mine_ref.shape[0]]
-    theirs_ref[...] = sums[mine_ref.shape[0] :].astype(BF)
+    hot = one_hot_rows(slot_ref, 0, EDGES, sum_ref.shape[0])
+    sum_ref[...] = dot(hot, rows_ref[...]).astype(BF)
     for copy in copies:
         copy.wait()
 
@@ -261,7 +263,6 @@
 Z_MID = along_z(lambda pair, member: (pair - 1 + 2 * member, member))
 Z_NEAR = along_z(lambda pair, member: (pair - 1 + 2 * member, member ^ 1))
 OUTER = [(i, (i + 1 if i & 1 else i - 1) % PATCHES) for i in range(PATCHES)]
-SAME_CORE = [[2 * i + core for i in range(PATCHES // 2)] for core in range(CORES)]
 tie = lambda *arrays: lax.optimization_barrier(arrays)
 
 
@@ -297,12 +298,7 @@
         return half << 10 | second << 8 | first << 6 | z << 3 | row
 
     send_place, recv_place = grid(place(coarse_send)), grid(place(coarse_recv))
-    slot = (coarse_recv >> 3 & 1 ^ my_core) << 7 | (coarse_recv >> 4 & 15) << 3 | coarse_recv & 7
-    slot = grid(jnp.where(coarse_recv >> 8 == group, slot, -1))
-    lower, upper = border_rows[:BORDER], border_rows[BORDER:]
-    borders = jnp.stack(
-        [jnp.where(my_core == 0, upper, lower), jnp.where(my_core == 0, lower, upper)]
-    )
+    slot = grid(jnp.where(coarse_recv >> 8 == group, coarse_recv & 255, -1))
     fine_place = grid(
         jnp.where((fine_send >= NODES) & (my_core == 0), fine_send ^ BORDER, fine_send)
     )
@@ -310,48 +306,49 @@
     like = lambda *arrays: [jax.ShapeDtypeStruct(a.shape, a.dtype) for a in arrays]
 
     own = node_lat[:COARSE_ROWS]
-    own, *loads = tie(own, node_lat, w_edge_in, w_edge_out)
+    own, *loads = tie(own, border_rows, node_lat, w_edge_in, w_edge_out)
+    loads[0] = grid(loads[0])
     pair = lax.ppermute(own, ("group", "patch"), Z_PAIR)
     inner, outer, nodes, w_in, w_out = call(
-        pick_kernel, [shape(BORDER), shape(BORDER), *like(*loads)], 2 * 256 * 512 * 512, borders,
-        *in_hbm(*loads), name="pick", scratch=[pltpu.SemaphoreType.DMA((3,))], in_any=(1, 2, 3),
-        spec=HBM_SPEC,
+        pick_kernel, [shape(BORDER), shape(BORDER), *like(*loads[1:])], 2 * 256 * 512 * 512,
+        *in_hbm(*loads), name="pick",
+        scratch=[pltpu.VMEM((2, BORDER), jnp.int32), pltpu.SemaphoreType.DMA((4,))],
+        in_any=range(4), spec=HBM_SPEC,
     )
     pair, inner, outer, nodes, w_in, w_out = tie(pair, inner, outer, nodes, w_in, w_out)
     near = join(own, pair)
-    near, inner, outer = tie(near, inner, outer)
+    near, inner, outer, nodes = tie(near, inner, outer, nodes)
     others = [lax.ppermute(near, ("group", "patch"), to) for to in (Z_NEAR, Z_MID, Z_FAR)]
     inner, outer = swap(inner, SWAP_CORE), swap(outer, OUTER)
-    block = join(near, *others)
-
-    block, nodes, w_in, *loads = tie(
-        block, nodes, w_in, fine_edge_lat, coarse_edge_lat, w_node_in, w_node_out
-    )
-    others = [swap(block, crossed(k, 0)) for k in (1, 3, 2)]
     (table,) = call(
         project_kernel, (shape(2 * NODES),), 4 * 512 * 512 * 512, nodes, w_in, name="project"
     )
-    fine_edges, coarse_edges, w_node, w_node_last = call(
-        load_kernel, like(*loads), 0, *in_hbm(*loads), name="load",
-        scratch=[pltpu.SemaphoreType.DMA((len(loads),))], in_any=range(len(loads)), spec=HBM_SPEC,
-    )
-    *others, table, inner, outer, fine_edges, coarse_edges, w_node, w_node_last = tie(
-        *others, table, inner, outer, fine_edges, coarse_edges, w_node, w_node_last
-    )
+    *others, table = tie(*others, table)
+    block = join(near, *others)
+
+    block, table = tie(block, table)
+    others = [swap(block, crossed(k, 0)) for k in (1, 3, 2)]
+    fine_args = (
+        fine_edge_lat, fine_place, grid(fine_recv), table, inner, outer, w_in, w_out, edge_gain
+    )
+    fine_scratch = [pltpu.VMEM((HALF, D), BF), pltpu.SemaphoreType.DMA]
+    fine_new, fine_sum, halo = call(
+        functools.partial(fine_kernel, 0), (shape(EDGES), shape(NODES, F32), shape(2 * BORDER)),
+        2 << 30, *fine_args, name="fine_first", scratch=fine_scratch, out_any=(0,),
+    )
+    *others, fine_sum = tie(*others, fine_sum)
     block = join(block, *others)
 
-    block, table = tie(block, table)
+    block, fine_sum = tie(block, fine_sum)
     others = [swap(block, crossed(k, 1)) for k in (1, 3, 2)]
     fine_new, fine_sum = call(
-        fine_kernel, (shape(EDGES), shape(NODES, F32)), 4 << 30, fine_edges, fine_place,
-        grid(fine_recv), table, inner, outer, w_in, w_out, edge_gain, name="fine",
-        scratch=[
-            pltpu.VMEM((2 * BORDER, D), BF), pltpu.VMEM((EDGES, D), BF), pltpu.SemaphoreType.DMA
-        ], out_any=(0,),
+        functools.partial(fine_kernel, HALF), (shape(EDGES), shape(NODES, F32)), 2 << 30,
+        *fine_args, halo, fine_sum, fine_new, name="fine_second", scratch=fine_scratch,
+        out_any=(0,), in_any=(len(fine_args) + 2,), aliases={len(fine_args) + 2: 0},
     )
     node_main, first_sum, first_pre = call(
         node_kernel, (shape(NODES), shape(TAIL, F32), shape(TAIL, F32)), 768 << 20, nodes,
-        fine_sum, w_node, w_node_last, node_gain, name="node",
+        fine_sum, w_node_in, w_node_out, node_gain, name="node",
     )
     *others, first_sum = tie(*others, first_sum)
     part = join(block, *others)
@@ -361,21 +358,18 @@
         gather_kernel, (shape(EDGES), shape(EDGES)), 2 << 30, send_place, recv_place, part,
         name="gather",
     )
-    coarse_new, mine, theirs = call(
-        coarse_kernel, (shape(EDGES), shape(128, F32), shape(128)), 4 << 30, coarse_edges,
+    coarse_new, sums = call(
+        coarse_kernel, (shape(EDGES), shape(PATCHES * COARSE_ROWS)), 4 << 30, coarse_edge_lat,
         send_place, recv_place, slot, other_half, send_part, recv_part, w_in, w_out, edge_gain,
         name="coarse",
         scratch=[pltpu.VMEM((EDGES, D), BF), pltpu.SemaphoreType.DMA((EDGES // BLOCK,))],
         out_any=(0,),
     )
 
-    sums = (mine + swap(theirs, SWAP_CORE).astype(F32)).astype(BF)
-    parts = lax.all_to_all(
-        sums.reshape(-1, COARSE_ROWS, D), "patch", 0, 0, axis_index_groups=SAME_CORE
-    )
+    parts = lax.all_to_all(sums.reshape(PATCHES, COARSE_ROWS, D), "patch", 0, 0)
     (node_new,) = call(
         tail_kernel, (shape(NODES),), 24 << 20, nodes, first_sum, first_pre, parts.reshape(-1, D),
-        w_node, w_node_last, node_gain, node_main, name="tail",
+        w_node_in, w_node_out, node_gain, node_main, name="tail",
         scratch=[pltpu.VMEM((TAIL, D), BF), pltpu.SemaphoreType.DMA], out_any=(0,), in_any=(7,),
         aliases={7: 0},
     )

time: 63.8 us -> 64.2 us (level)
  blocking collectives: 11.6 us -> 12.8 us
  Pallas kernels: 21.7 us -> 20.6 us
    all_to_all x1, blocking collectives: 11.6 us -> 12.8 us  [shards(): parts = lax.all_to_all(sums.reshape(PATCHES, COARSE_ROWS, D), 'patch', 0, 0)]
    pallas_call x8, Pallas kernels: 21.7 us -> 20.6 us  [call(): pl.pallas_call(kernel, out_shape=outs, in_specs=[spec if at in in_any els...]
    another operation x2 -> x0, other arithmetic: 0.77 us -> none  [shards(): jnp.stack([jnp.where(my_core == 0, upper, lower), jnp.where(my_core == 0,...]
    reshape x3, other arithmetic: 0.06 us -> 0.75 us  [shards(): grid = lambda ids: ids.reshape(-1, 128)]
    ppermute x10 -> x9, waiting for transfers between devices: 1.61 us -> 2.09 us  [shards(): swap = lambda rows, pairs: lax.ppermute(rows, 'patch', pairs)]
    ppermute x10 -> x9, starting transfers between devices: 13.4 us -> 13.6 us  [shards(): swap = lambda rows, pairs: lax.ppermute(rows, 'patch', pairs)]
  transfers between devices with their start and end apart: 14 -> 13, of which waited for: 3 -> 3; matrix products, arithmetic and copies ran while one was open for 1% -> 1% of each run, Pallas kernels for 21% -> 19%
where the time goes in v5:
time: 64.2 us; the launch traced here: 63.9 us
  starting transfers between devices  25.6 us (40%)
  Pallas kernels  20.6 us (32%)
  blocking collectives  12.8 us (20%)
  waiting for transfers between devices  2.11 us (3%)
  between operations  1.12 us (2%)
  local copies, waits for them, and re-layouts  0.85 us (1%)
  other arithmetic  0.77 us (1%)
    pallas_call x8, Pallas kernels, call(): pl.pallas_call(kernel, out_shape=outs, in_specs=[spec if at in in_any els...  20.6 us
    ppermute x9, starting transfers between devices, shards(): swap = lambda rows, pairs: lax.ppermute(rows, 'patch', pairs)  13.6 us
    all_to_all x1, blocking collectives, shards(): parts = lax.all_to_all(sums.reshape(PATCHES, COARSE_ROWS, D), 'patch', 0, 0)  12.8 us
    ppermute x3, starting transfers between devices, shards(): lax.ppermute(near, ('group', 'patch'), to)  8.98 us
    ppermute x1, starting transfers between devices, shards(): pair = lax.ppermute(own, ('group', 'patch'), Z_PAIR)  3.03 us
    ppermute x9, waiting for transfers between devices, shards(): swap = lambda rows, pairs: lax.ppermute(rows, 'patch', pairs)  2.09 us
  transfers between devices with their start and end apart: 13, of which 3 were waited for; matrix products, arithmetic and copies ran while one was open for 1% of the time, Pallas kernels for 19%

profile of v5, /device:TPU:1, one launch (start us, length us, event | category | flops | bytes accessed | tf_op | source)
XLA Modules:
  0.0 63.9 jit_solution(8312406066806462395)
XLA Ops:
  0.6 0.7 %slice.3 = bf16[8,512]{1,0:T(8,128)(2,1)S(1)} slice(bf16[512,512]{1,0:T(8,128)(2,1)} %node_in), slice={[0:8], [0:512]} | slice | bytes 16384 | tf_op jit(solution)/shard_map/slice | solution.py:308
  1.3 3.0 %collective-permute-start = (bf16[8,512]{1,0:T(8,128)(2,1)S(1)}, bf16[8,512]{1,0:T(8,128)(2,1)S(1)}, u32[]{:S(2)}, u32[]{:S(2)}) collective-permute-start(bf16[8,512]{1,0:T(8,128)(2,1)S(1)} %slice.3), channel_id=1, source_target_pairs={{0,33},{1,32},{2,35},{3,34},{4,37},{5,36},{6,39},{7,38},{8,41},{9,... | collective-permute-start | bytes 24584 | tf_op jit(solution)/shard_map/ppermute | solution.py:311
  4.4 0.7 %fusion.8.send_ref = s32[8,128]{1,0:T(8,128)S(1)} fusion(s32[1024]{0:T(1024)} %param.16, pred[]{:T(512)S(6)} %eq.19), kind=kLoop, calls=%fused_computation.26 | loop fusion | flops 4096 | bytes 8193 | tf_op jit(solution)/shard_map/reshape | solution.py:285
  5.0 1.7 %pick.1 = (bf16[128,512]{1,0:T(8,128)(2,1)S(1)}, bf16[128,512]{1,0:T(8,128)(2,1)S(1)}, bf16[512,512]{1,0:T(8,128)(2,1)S(1)}, bf16[1536,512]{1,0:T(8,128)(2,1)S(1)}, bf16[512,512]{1,0:T(8,128)(2,1)S(1)}) custom-call(s32[2,128]{1,0:T(2,128)} %bitcast.23, bf16[512,512]{1,0:T(8,128)(2,1)} %node_in, bf16[1536,512]{1,0:T(8,128)(2,1)} %w_in, bf16[512,512]{1,0:T(8,128)(2,1)} %w_out), custom_call_target="tpu_custom_call" | custom-call | flops 134217728 | bytes 4194304 | tf_op jit(solution)/shard_map/pick/pallas_call | solution.py:218
  6.8 0.0 copy-start.2
  6.8 0.0 copy-start.7
  6.8 0.0 collective-permute-done
  6.8 0.0 copy-start.5
  6.8 0.0 copy-start.9
  6.8 0.0 copy-start.10
  6.9 5.6 %collective-permute-start.3 = (bf16[16,512]{1,0:T(8,128)(2,1)S(1)}, bf16[16,512]{1,0:T(8,128)(2,1)S(1)}, u32[]{:S(2)}, u32[]{:S(2)}) collective-permute-start(bf16[16,512]{1,0:T(8,128)(2,1)S(1)} %pad_maximum_fusion.2), channel_id=1, source_target_pairs={{0,161},{1,160},{2,163},{3,162},{4,165},{5,164},{6,167},{7,166},{8... | collective-permute-start | bytes 49160 | tf_op jit(solution)/shard_map/ppermute | solution.py:321
  12.4 0.3 collective-permute-start.2
  12.7 3.1 %collective-permute-start.1 = (bf16[16,512]{1,0:T(8,128)(2,1)S(1)}, bf16[16,512]{1,0:T(8,128)(2,1)S(1)}, u32[]{:S(2)}, u32[]{:S(2)}) collective-permute-start(bf16[16,512]{1,0:T(8,128)(2,1)S(1)} %pad_maximum_fusion.2), channel_id=1, source_target_pairs={{0,225},{1,224},{2,227},{3,226},{4,229},{5,228},{6,231},{7,230},{8... | collective-permute-start | bytes 49160 | tf_op jit(solution)/shard_map/ppermute | solution.py:321
  15.8 0.5 collective-permute-start.7
  16.3 1.2 %collective-permute-start.8 = (bf16[128,512]{1,0:T(8,128)(2,1)S(1)}, bf16[128,512]{1,0:T(8,128)(2,1)S(1)}, u32[]{:S(2)}, u32[]{:S(2)}) collective-permute-start(bf16[128,512]{1,0:T(8,128)(2,1)S(1)} %get-tuple-element.75), channel_id=1, source_target_pairs={{0,31},{1,2},{2,1},{3,4},{4,3},{5,6},{6,5},{7,8},{8,7},{9,10},{10,... | collective-permute-start | bytes 393224 | tf_op jit(solution)/shard_map/ppermute | solution.py:286
  17.5 0.7 %project.1.table_ref = bf16[1024,512]{1,0:T(8,128)(2,1)S(1)} custom-call(bf16[512,512]{1,0:T(8,128)(2,1)S(1)} %get-tuple-element.65.node_ref, bf16[1536,512]{1,0:T(8,128)(2,1)S(1)} %get-tuple-element.67.w_ref.w_in_ref), custom_call_target="tpu_custom_call" | custom-call | flops 536870912 | bytes 4194304 | tf_op jit(solution)/shard_map/project/pallas_call | solution.py:218
  18.2 0.0 collective-permute-done.3
  18.3 0.0 collective-permute-done.2
  18.3 0.0 collective-permute-done.1
  18.3 2.7 %collective-permute-start.6 = (bf16[64,512]{1,0:T(8,128)(2,1)S(1)}, bf16[64,512]{1,0:T(8,128)(2,1)S(1)}, u32[]{:S(2)}, u32[]{:S(2)}) collective-permute-start(bf16[64,512]{1,0:T(8,128)(2,1)S(1)} %pad_maximum_fusion.1), channel_id=1, source_target_pairs={{0,16},{1,5},{2,18},{3,7},{4,20},{5,1},{6,22},{7,3},{8,24},{9,13},... | collective-permute-start | bytes 196616 | tf_op jit(solution)/shard_map/ppermute | solution.py:286
  21.0 1.1 %collective-permute-start.5 = (bf16[64,512]{1,0:T(8,128)(2,1)S(1)}, bf16[64,512]{1,0:T(8,128)(2,1)S(1)}, u32[]{:S(2)}, u32[]{:S(2)}) collective-permute-start(bf16[64,512]{1,0:T(8,128)(2,1)S(1)} %pad_maximum_fusion.1), channel_id=1, source_target_pairs={{0,24},{1,7},{2,26},{3,5},{4,28},{5,3},{6,30},{7,1},{8,16},{9,15},... | collective-permute-start | bytes 196616 | tf_op jit(solution)/shard_map/ppermute | solution.py:286
  22.1 0.0 collective-permute-start.4
  22.1 0.0 collective-permute-done.7.inner_ref
  22.1 0.0 collective-permute-done.8.outer_ref
  22.1 0.0 copy-done.5
  22.1 0.0 copy-done.9
  22.1 0.0 copy-done.10
  22.1 2.8 %fine_first.1 = (bf16[1024,512]{1,0:T(8,128)(2,1)}, f32[512,512]{1,0:T(8,128)S(1)}, bf16[256,512]{1,0:T(8,128)(2,1)S(1)}) custom-call(bf16[1024,512]{1,0:T(8,128)(2,1)S(1)} %copy-done.5, s32[8,128]{1,0:T(8,128)S(1)} %fusion.8.send_ref, s32[8,128]{1,0:T(8,128)S(1)} %bitcast.18, bf16[1024,512]{1,0:T(8,128)(2,1)S(1)} %project.1.table_ref, ...), custom_call_target="tpu_custom_call" | custom-call | flops 2147483648 | bytes 4194304 | tf_op jit(solution)/shard_map/fine_first/pallas_call | solution.py:218
  24.9 0.0 collective-permute-done.6
  24.9 0.4 collective-permute-done.5
  25.3 0.0 collective-permute-done.4
  25.4 3.0 %collective-permute-start.11 = (bf16[256,512]{1,0:T(8,128)(2,1)S(1)}, bf16[256,512]{1,0:T(8,128)(2,1)S(1)}, u32[]{:S(2)}, u32[]{:S(2)}) collective-permute-start(bf16[256,512]{1,0:T(8,128)(2,1)S(1)} %pad_maximum_fusion), channel_id=1, source_target_pairs={{0,4},{1,17},{2,6},{3,19},{4,0},{5,21},{6,2},{7,23},{8,12},{9,25},... | collective-permute-start | bytes 786440 | tf_op jit(solution)/shard_map/ppermute | solution.py:286
  28.3 0.9 %collective-permute-start.10 = (bf16[256,512]{1,0:T(8,128)(2,1)S(1)}, bf16[256,512]{1,0:T(8,128)(2,1)S(1)}, u32[]{:S(2)}, u32[]{:S(2)}) collective-permute-start(bf16[256,512]{1,0:T(8,128)(2,1)S(1)} %pad_maximum_fusion), channel_id=1, source_target_pairs={{0,6},{1,25},{2,4},{3,27},{4,2},{5,29},{6,0},{7,31},{8,14},{9,17},... | collective-permute-start | bytes 786440 | tf_op jit(solution)/shard_map/ppermute | solution.py:286
  29.2 0.0 collective-permute-start.9
  29.2 0.0 copy-done.2
  29.2 0.0 copy-done.7
  29.2 0.0 copy-start
  29.2 0.0 copy-start.1
  29.2 0.0 copy-start.4
  29.2 2.6 %fine_second.1 = (bf16[1024,512]{1,0:T(8,128)(2,1)}, f32[512,512]{1,0:T(8,128)S(1)}) custom-call(bf16[1024,512]{1,0:T(8,128)(2,1)S(1)} %copy-done.5, s32[8,128]{1,0:T(8,128)S(1)} %fusion.8.send_ref, s32[8,128]{1,0:T(8,128)S(1)} %bitcast.19, bf16[1024,512]{1,0:T(8,128)(2,1)S(1)} %project.1.table_ref, ...), custom_call_target="tpu_custom_call", output_to_operand_aliasing={{0}: (11, {})} | custom-call | flops 2147483648 | bytes 4194304 | tf_op jit(solution)/shard_map/fine_second/pallas_call | solution.py:218
  31.9 0.0 copy-done
  31.9 0.0 copy-done.1
  31.9 0.0 copy-done.4
  31.9 2.1 %node.1 = (bf16[512,512]{1,0:T(8,128)(2,1)}, f32[16,512]{1,0:T(8,128)S(1)}, f32[16,512]{1,0:T(8,128)S(1)}) custom-call(bf16[512,512]{1,0:T(8,128)(2,1)S(1)} %get-tuple-element.65.node_ref, f32[512,512]{1,0:T(8,128)S(1)} %get-tuple-element.86.sum_ref, bf16[1024,512]{1,0:T(8,128)(2,1)S(1)} %copy-done, bf16[512,512]{1,0:T(8,128)(2,1)S(1)} %copy-done.1, ...), custom_call_target="tpu_custom_call" | custom-call | flops 805306368 | bytes 4194304 | tf_op jit(solution)/shard_map/node/pallas_call | solution.py:218
  34.0 0.0 copy-start.11
  34.0 0.0 copy-start.12
  34.0 0.0 collective-permute-done.11
  34.1 1.4 %collective-permute-done.10 = bf16[256,512]{1,0:T(8,128)(2,1)S(1)} collective-permute-done((bf16[256,512]{1,0:T(8,128)(2,1)S(1)}, bf16[256,512]{1,0:T(8,128)(2,1)S(1)}, u32[]{:S(2)}, u32[]{:S(2)}) %collective-permute-start.10) | collective-permute-done | bytes 262176 | tf_op jit(solution)/shard_map/ppermute | solution.py:286
  35.4 0.2 collective-permute-done.9
  35.8 4.3 %collective-permute-start.12 = (bf16[1024,512]{1,0:T(8,128)(2,1)S(1)}, bf16[1024,512]{1,0:T(8,128)(2,1)}, u32[]{:S(2)}, u32[]{:S(2)}) collective-permute-start(bf16[1024,512]{1,0:T(8,128)(2,1)S(1)} %constant_dynamic-update-slice_fusion.table_ref), channel_id=1, source_target_pairs={{0,1},{1,0},{2,3},{3,2},{4,5},{5,4},{6,7},{7,6},{8,9},{9,8},{10,11... | collective-permute-start | bytes 3145736 | tf_op jit(solution)/shard_map/ppermute | solution.py:286
  40.1 0.0 copy-done.11
  40.1 0.0 copy-done.12
  40.2 0.0 copy-start.3
  40.2 0.0 copy-start.6
  40.2 0.0 copy-start.8
  40.2 2.4 %gather.1 = (bf16[1024,512]{1,0:T(8,128)(2,1)S(1)}, bf16[1024,512]{1,0:T(8,128)(2,1)S(1)}) custom-call(s32[8,128]{1,0:T(8,128)S(1)} %or_bitcast_fusion.1.send_ref, s32[8,128]{1,0:T(8,128)S(1)} %get-tuple-element.100.recv_ref, bf16[1024,512]{1,0:T(8,128)(2,1)S(1)} %constant_dynamic-update-slice_fusion.table_ref), custom_call_target="tpu_custom_call" | custom-call | flops 2147483648 | bytes 4194304 | tf_op jit(solution)/shard_map/gather/pallas_call | solution.py:218
  42.6 0.0 collective-permute-done.12.table_ref
  42.6 0.0 copy-done.3
  42.6 0.0 copy-done.6
  42.6 0.0 copy-done.8
  42.6 7.2 %coarse.1 = (bf16[1024,512]{1,0:T(8,128)(2,1)}, bf16[256,512]{1,0:T(8,128)(2,1)S(1)}) custom-call(bf16[1024,512]{1,0:T(8,128)(2,1)S(1)} %copy-done.6, s32[8,128]{1,0:T(8,128)S(1)} %or_bitcast_fusion.1.send_ref, s32[8,128]{1,0:T(8,128)S(1)} %get-tuple-element.100.recv_ref, s32[8,128]{1,0:T(8,128)S(1)} %get-tuple-element.99.slot_ref, ...), custom_call_target="tpu_custom_call" | custom-call | flops 4294967296 | bytes 4194304 | tf_op jit(solution)/shard_map/coarse/pallas_call | solution.py:218
  49.8 12.8 %all_to_all.5 = bf16[32,8,512]{2,1,0:T(8,128)(2,1)S(1)} all-to-all(bf16[32,8,512]{2,1,0:T(8,128)(2,1)S(1)} %bitcast.15), channel_id=1, replica_groups=mesh['group'=8,'patch'=32] {'patch'}, dimensions={0} | all-to-all | bytes 524288 | tf_op jit(solution)/shard_map/all_to_all | solution.py:369
  62.6 1.2 %tail.1 = bf16[512,512]{1,0:T(8,128)(2,1)} custom-call(bf16[512,512]{1,0:T(8,128)(2,1)S(1)} %get-tuple-element.65.node_ref, f32[16,512]{1,0:T(8,128)S(1)} %get-tuple-element.88.sum_ref, f32[16,512]{1,0:T(8,128)S(1)} %get-tuple-element.89.pre_ref, bf16[256,512]{1,0:T(8,128)(2,1)S(1)} %bitcast.14, ...), custom_call_target="tpu_custom_call", output_to_operand_aliasing={{}: (7, {})} | custom-call | flops 25165824 | bytes 4194304 | tf_op jit(solution)/shard_map/tail/pallas_call | solution.py:218
  (9 shorter events, 0.2 us)
Async XLA Ops:
  1.3 5.5 %collective-permute-start = (bf16[8,512]{1,0:T(8,128)(2,1)S(1)}, bf16[8,512]{1,0:T(8,128)(2,1)S(1)}, u32[]{:S(2)}, u32[]{:S(2)}) collective-permute-start(bf16[8,512]{1,0:T(8,128)(2,1)S(1)} %slice.3), channel_id=1, source_target_pairs={{0,33},{1,32},{2,35},{3,34},{4,37},{5,36},{6,39},{7,38},{8,41},{9,... | collective-permute-start | bytes 24584 | tf_op jit(solution)/shard_map/ppermute | solution.py:311
  6.8 22.4 %copy-start.2 = (bf16[1536,512]{1,0:T(8,128)(2,1)}, bf16[1536,512]{1,0:T(8,128)(2,1)S(1)}, u32[]{:S(2)}) copy-start(bf16[1536,512]{1,0:T(8,128)(2,1)S(1)} %get-tuple-element.67.w_ref.w_in_ref) | copy-start | bytes 4718596
  6.8 22.4 %copy-start.7 = (bf16[512,512]{1,0:T(8,128)(2,1)}, bf16[512,512]{1,0:T(8,128)(2,1)S(1)}, u32[]{:S(2)}) copy-start(bf16[512,512]{1,0:T(8,128)(2,1)S(1)} %get-tuple-element.76.w_out_ref) | copy-start | bytes 1572868
  6.8 15.3 %copy-start.5 = (bf16[1024,512]{1,0:T(8,128)(2,1)S(1)}, bf16[1024,512]{1,0:T(8,128)(2,1)}, u32[]{:S(2)}) copy-start(bf16[1024,512]{1,0:T(8,128)(2,1)} %edge_ref.4) | copy-start | bytes 3145732
  6.8 15.3 %copy-start.9 = (s32[1024]{0:T(1024)S(1)}, s32[1024]{0:T(1024)}, u32[]{:S(2)}) copy-start(s32[1024]{0:T(1024)} %param.17) | copy-start | bytes 12292
  6.8 15.3 %copy-start.10 = (f32[512]{0:T(512)S(1)}, f32[512]{0:T(512)}, u32[]{:S(2)}) copy-start(f32[512]{0:T(512)} %param.24) | copy-start | bytes 6148
  6.9 11.4 %collective-permute-start.3 = (bf16[16,512]{1,0:T(8,128)(2,1)S(1)}, bf16[16,512]{1,0:T(8,128)(2,1)S(1)}, u32[]{:S(2)}, u32[]{:S(2)}) collective-permute-start(bf16[16,512]{1,0:T(8,128)(2,1)S(1)} %pad_maximum_fusion.2), channel_id=1, source_target_pairs={{0,161},{1,160},{2,163},{3,162},{4,165},{5,164},{6,167},{7,166},{8... | collective-permute-start | bytes 49160 | tf_op jit(solution)/shard_map/ppermute | solution.py:321
  12.4 5.8 %collective-permute-start.2 = (bf16[16,512]{1,0:T(8,128)(2,1)S(1)}, bf16[16,512]{1,0:T(8,128)(2,1)S(1)}, u32[]{:S(2)}, u32[]{:S(2)}) collective-permute-start(bf16[16,512]{1,0:T(8,128)(2,1)S(1)} %pad_maximum_fusion.2), channel_id=1, source_target_pairs={{0,193},{1,192},{2,195},{3,194},{4,197},{5,196},{6,199},{7,198},{8... | collective-permute-start | bytes 49160 | tf_op jit(solution)/shard_map/ppermute | solution.py:321
  12.7 5.6 %collective-permute-start.1 = (bf16[16,512]{1,0:T(8,128)(2,1)S(1)}, bf16[16,512]{1,0:T(8,128)(2,1)S(1)}, u32[]{:S(2)}, u32[]{:S(2)}) collective-permute-start(bf16[16,512]{1,0:T(8,128)(2,1)S(1)} %pad_maximum_fusion.2), channel_id=1, source_target_pairs={{0,225},{1,224},{2,227},{3,226},{4,229},{5,228},{6,231},{7,230},{8... | collective-permute-start | bytes 49160 | tf_op jit(solution)/shard_map/ppermute | solution.py:321
  15.8 6.2 %collective-permute-start.7 = (bf16[128,512]{1,0:T(8,128)(2,1)S(1)}, bf16[128,512]{1,0:T(8,128)(2,1)S(1)}, u32[]{:S(2)}, u32[]{:S(2)}) collective-permute-start(bf16[128,512]{1,0:T(8,128)(2,1)S(1)} %get-tuple-element.74), channel_id=1, source_target_pairs={{0,1},{1,0},{2,3},{3,2},{4,5},{5,4},{6,7},{7,6},{8,9},{9,8},{10,11... | collective-permute-start | bytes 393224 | tf_op jit(solution)/shard_map/ppermute | solution.py:286
  16.3 5.8 %collective-permute-start.8 = (bf16[128,512]{1,0:T(8,128)(2,1)S(1)}, bf16[128,512]{1,0:T(8,128)(2,1)S(1)}, u32[]{:S(2)}, u32[]{:S(2)}) collective-permute-start(bf16[128,512]{1,0:T(8,128)(2,1)S(1)} %get-tuple-element.75), channel_id=1, source_target_pairs={{0,31},{1,2},{2,1},{3,4},{4,3},{5,6},{6,5},{7,8},{8,7},{9,10},{10,... | collective-permute-start | bytes 393224 | tf_op jit(solution)/shard_map/ppermute | solution.py:286
  18.3 6.6 %collective-permute-start.6 = (bf16[64,512]{1,0:T(8,128)(2,1)S(1)}, bf16[64,512]{1,0:T(8,128)(2,1)S(1)}, u32[]{:S(2)}, u32[]{:S(2)}) collective-permute-start(bf16[64,512]{1,0:T(8,128)(2,1)S(1)} %pad_maximum_fusion.1), channel_id=1, source_target_pairs={{0,16},{1,5},{2,18},{3,7},{4,20},{5,1},{6,22},{7,3},{8,24},{9,13},... | collective-permute-start | bytes 196616 | tf_op jit(solution)/shard_map/ppermute | solution.py:286
  21.0 4.3 %collective-permute-start.5 = (bf16[64,512]{1,0:T(8,128)(2,1)S(1)}, bf16[64,512]{1,0:T(8,128)(2,1)S(1)}, u32[]{:S(2)}, u32[]{:S(2)}) collective-permute-start(bf16[64,512]{1,0:T(8,128)(2,1)S(1)} %pad_maximum_fusion.1), channel_id=1, source_target_pairs={{0,24},{1,7},{2,26},{3,5},{4,28},{5,3},{6,30},{7,1},{8,16},{9,15},... | collective-permute-start | bytes 196616 | tf_op jit(solution)/shard_map/ppermute | solution.py:286
  22.1 3.3 %collective-permute-start.4 = (bf16[64,512]{1,0:T(8,128)(2,1)S(1)}, bf16[64,512]{1,0:T(8,128)(2,1)S(1)}, u32[]{:S(2)}, u32[]{:S(2)}) collective-permute-start(bf16[64,512]{1,0:T(8,128)(2,1)S(1)} %pad_maximum_fusion.1), channel_id=1, source_target_pairs={{0,8},{1,3},{2,10},{3,1},{4,12},{5,7},{6,14},{7,5},{8,0},{9,11},{1... | collective-permute-start | bytes 196616 | tf_op jit(solution)/shard_map/ppermute | solution.py:286
  25.4 8.7 %collective-permute-start.11 = (bf16[256,512]{1,0:T(8,128)(2,1)S(1)}, bf16[256,512]{1,0:T(8,128)(2,1)S(1)}, u32[]{:S(2)}, u32[]{:S(2)}) collective-permute-start(bf16[256,512]{1,0:T(8,128)(2,1)S(1)} %pad_maximum_fusion), channel_id=1, source_target_pairs={{0,4},{1,17},{2,6},{3,19},{4,0},{5,21},{6,2},{7,23},{8,12},{9,25},... | collective-permute-start | bytes 786440 | tf_op jit(solution)/shard_map/ppermute | solution.py:286
  28.3 7.1 %collective-permute-start.10 = (bf16[256,512]{1,0:T(8,128)(2,1)S(1)}, bf16[256,512]{1,0:T(8,128)(2,1)S(1)}, u32[]{:S(2)}, u32[]{:S(2)}) collective-permute-start(bf16[256,512]{1,0:T(8,128)(2,1)S(1)} %pad_maximum_fusion), channel_id=1, source_target_pairs={{0,6},{1,25},{2,4},{3,27},{4,2},{5,29},{6,0},{7,31},{8,14},{9,17},... | collective-permute-start | bytes 786440 | tf_op jit(solution)/shard_map/ppermute | solution.py:286
  29.2 6.5 %collective-permute-start.9 = (bf16[256,512]{1,0:T(8,128)(2,1)S(1)}, bf16[256,512]{1,0:T(8,128)(2,1)S(1)}, u32[]{:S(2)}, u32[]{:S(2)}) collective-permute-start(bf16[256,512]{1,0:T(8,128)(2,1)S(1)} %pad_maximum_fusion), channel_id=1, source_target_pairs={{0,2},{1,9},{2,0},{3,11},{4,6},{5,13},{6,4},{7,15},{8,10},{9,1},{1... | collective-permute-start | bytes 786440 | tf_op jit(solution)/shard_map/ppermute | solution.py:286
  29.2 2.7 %copy-start = (bf16[1024,512]{1,0:T(8,128)(2,1)S(1)}, bf16[1024,512]{1,0:T(8,128)(2,1)}, u32[]{:S(2)}) copy-start(bf16[1024,512]{1,0:T(8,128)(2,1)} %w_in_ref.3) | copy-start | bytes 3145732
  29.2 2.7 %copy-start.1 = (bf16[512,512]{1,0:T(8,128)(2,1)S(1)}, bf16[512,512]{1,0:T(8,128)(2,1)}, u32[]{:S(2)}) copy-start(bf16[512,512]{1,0:T(8,128)(2,1)} %w_out_ref.3) | copy-start | bytes 1572868
  29.2 2.7 %copy-start.4 = (f32[512]{0:T(512)S(1)}, f32[512]{0:T(512)}, u32[]{:S(2)}) copy-start(f32[512]{0:T(512)} %param.27) | copy-start | bytes 6148
  34.0 6.1 %copy-start.11 = (s32[1024]{0:T(1024)S(1)}, s32[1024]{0:T(1024)}, u32[]{:S(2)}) copy-start(s32[1024]{0:T(1024)} %param.20) | copy-start | bytes 12292
  34.0 6.1 %copy-start.12 = (s32[1024]{0:T(1024)S(1)}, s32[1024]{0:T(1024)}, u32[]{:S(2)}) copy-start(s32[1024]{0:T(1024)} %param.21) | copy-start | bytes 12292
  35.8 6.8 %collective-permute-start.12 = (bf16[1024,512]{1,0:T(8,128)(2,1)S(1)}, bf16[1024,512]{1,0:T(8,128)(2,1)}, u32[]{:S(2)}, u32[]{:S(2)}) collective-permute-start(bf16[1024,512]{1,0:T(8,128)(2,1)S(1)} %constant_dynamic-update-slice_fusion.table_ref), channel_id=1, source_target_pairs={{0,1},{1,0},{2,3},{3,2},{4,5},{5,4},{6,7},{7,6},{8,9},{9,8},{10,11... | collective-permute-start | bytes 3145736 | tf_op jit(solution)/shard_map/ppermute | solution.py:286
  40.2 2.4 %copy-start.3 = (bf16[1536,512]{1,0:T(8,128)(2,1)S(1)}, bf16[1536,512]{1,0:T(8,128)(2,1)}, u32[]{:S(2)}) copy-start(bf16[1536,512]{1,0:T(8,128)(2,1)} %copy-done.2) | copy-start | bytes 4718596
  40.2 2.4 %copy-start.6 = (bf16[1024,512]{1,0:T(8,128)(2,1)S(1)}, bf16[1024,512]{1,0:T(8,128)(2,1)}, u32[]{:S(2)}) copy-start(bf16[1024,512]{1,0:T(8,128)(2,1)} %edge_ref.5) | copy-start | bytes 3145732
  40.2 2.4 %copy-start.8 = (bf16[512,512]{1,0:T(8,128)(2,1)S(1)}, bf16[512,512]{1,0:T(8,128)(2,1)}, u32[]{:S(2)}) copy-start(bf16[512,512]{1,0:T(8,128)(2,1)} %copy-done.7) | copy-start | bytes 1572868

commit v6 on v5

--- a/solution.py
+++ b/solution.py
@@ -21,7 +21,6 @@
 EPS = 1e-05
 BF = jnp.bfloat16
 F32 = jnp.float32
-BLOCK = 512
 VMEM_LIMIT = 10 * 1024 * 1024
 
 
@@ -71,13 +70,6 @@
     return jnp.concatenate(parts, axis=1)
 
 
-def send_rows(rows_ref, out_ref, sems, at):
-    rows = pl.ds(at * BLOCK, BLOCK)
-    copy = pltpu.make_async_copy(rows_ref.at[rows], out_ref.at[rows], sems.at[at])
-    copy.start()
-    return copy
-
-
 def finish_edges(pre, edges, w_out, gain):
     hidden = silu(pre).astype(BF)
     projected = dot(hidden, w_out)
@@ -85,15 +77,13 @@
 
 
 def pick_kernel(
-    border_in, node_in, w_in, w_out, inner_ref, outer_ref, node_ref, w_in_ref, w_out_ref,
-    border_ref, sems,
+    border_in, node_in, w_in, inner_ref, outer_ref, node_ref, w_in_ref, border_ref, sems
 ):
     copies = [
         pltpu.make_async_copy(source, target, sems.at[at])
         for at, (source, target) in enumerate(
             (
-                (border_in, border_ref), (node_in, node_ref), (w_in, w_in_ref),
-                (w_out, w_out_ref),
+                (border_in, border_ref), (node_in, node_ref), (w_in, w_in_ref)
             )
         )
     ]
@@ -130,8 +120,11 @@
         halo_out[BORDER:] = dot(outer_ref[...], w_in_ref[D : 2 * D]).astype(BF)
         halo = halo_out[...]
     edges = edge_ref[first : first + HALF]
+    senders = send_ref[...]
+    on_first = lax.axis_index("patch") % CORES == 0
+    senders = jnp.where((senders >= NODES) & on_first, senders ^ BORDER, senders)
     recv_hot = one_hot(column_of(recv_ref, first, HALF), NODES)
-    send_hot = one_hot(column_of(send_ref, first, HALF), NODES + 2 * BORDER)
+    send_hot = one_hot(column_of(senders, first, HALF), NODES + 2 * BORDER)
     pre = dot(edges, w_in_ref[:D])
     pre = pre + dot(jnp.concatenate([recv_hot, send_hot[:, :NODES]], axis=1), table_ref[...])
     pre = pre + dot(send_hot[:, NODES:], halo)
@@ -143,35 +136,56 @@
     copy.wait()
 
 
-def gather_kernel(send_ref, recv_ref, table_ref, send_out, recv_out):
-    for first in range(0, EDGES, BLOCK):
-        rows = slice(first, first + BLOCK)
-        for ids_ref, out_ref in ((send_ref, send_out), (recv_ref, recv_out)):
-            hot = one_hot(column_of(ids_ref, first, BLOCK), table_ref.shape[0])
-            out_ref[rows] = dot(hot, table_ref[...]).astype(BF)
+def place_z(group, mine):
+    away = ((group >> 1) - (mine >> 1)) * jnp.where(mine & 1 == 0, 1, -1) & 3
+    high = away >> 1
+    place = ((away ^ high) & 1) << 2 | high << 1 | ((group ^ mine) & 1 ^ high)
+    return place, (place & 1) ^ jnp.where(place >= 2, 1, 0)
+
+
+def place(ids):
+    group, patch = lax.axis_index("group"), lax.axis_index("patch")
+    my_core, my_y, my_x = patch & 1, patch >> 1 & 3, patch >> 3
+    row, at = ids & 7, ids >> 3
+    turn = lambda away: away ^ (away >> 1)
+    core, y, x = at & 1, turn(at >> 1 & 3 ^ my_y), turn(at >> 3 & 3 ^ my_x)
+    z, exchanged = place_z(at >> 5, group)
+    half = core ^ my_core ^ exchanged
+    x_first = half == my_core
+    first, second = jnp.where(x_first, x, y), jnp.where(x_first, y, x)
+    return half << 10 | second << 8 | first << 6 | z << 3 | row
+
+
+def gather_kernel(
+    send_ref, recv_ref, table_ref, send_place, recv_place, send_out, recv_out
+):
+    for ids_ref, place_ref, out_ref in (
+        (send_ref, send_place, send_out), (recv_ref, recv_place, recv_out)
+    ):
+        place_ref[...] = place(ids_ref[...])
+        hot = one_hot(column_of(place_ref, 0, EDGES), table_ref.shape[0])
+        out_ref[...] = dot(hot, table_ref[...]).astype(BF)
 
 
 def coarse_kernel(
-    edge_ref, send_ref, recv_ref, slot_ref, table_ref, send_part, recv_part, w_in_ref, w_out_ref,
-    gain_ref, new_ref, sum_ref, rows_ref, sems,
-):
-    gain = gain_ref[...]
+    edge_ref, send_ref, recv_ref, node_ref, table_ref, send_part, recv_part, w_in_ref, w_out_ref,
+    gain_ref, new_ref, sum_ref, rows_ref, slot_ref, sem,
+):
     half = table_ref.shape[0]
-    copies = []
-    for at in range(EDGES // BLOCK):
-        rows = slice(at * BLOCK, (at + 1) * BLOCK)
-        edges = edge_ref[rows]
-        joined = [edges]
-        for ids_ref, part_ref in ((send_ref, send_part), (recv_ref, recv_part)):
-            hot = one_hot(column_of(ids_ref, at * BLOCK, BLOCK), half, half)
-            joined.append((dot(hot, table_ref[...]) + part_ref[rows].astype(F32)).astype(BF))
-        pre = dot(jnp.concatenate(joined, axis=1), w_in_ref[...])
-        rows_ref[rows] = finish_edges(pre, edges, w_out_ref[...], gain)
-        copies.append(send_rows(rows_ref, new_ref, sems, at))
+    edges = edge_ref[...]
+    joined = [edges]
+    for ids_ref, part_ref in ((send_ref, send_part), (recv_ref, recv_part)):
+        hot = one_hot(column_of(ids_ref, 0, EDGES), half, half)
+        joined.append((dot(hot, table_ref[...]) + part_ref[...].astype(F32)).astype(BF))
+    pre = dot(jnp.concatenate(joined, axis=1), w_in_ref[...])
+    rows_ref[...] = finish_edges(pre, edges, w_out_ref[...], gain_ref[...])
+    copy = pltpu.make_async_copy(rows_ref, new_ref, sem)
+    copy.start()
+    nodes = node_ref[...]
+    slot_ref[...] = jnp.where(nodes >> 8 == lax.axis_index("group"), nodes & 255, -1)
     hot = one_hot_rows(slot_ref, 0, EDGES, sum_ref.shape[0])
     sum_ref[...] = dot(hot, rows_ref[...]).astype(BF)
-    for copy in copies:
-        copy.wait()
+    copy.wait()
 
 
 def finish_nodes(pre, nodes, w_out_ref, gain):
@@ -266,56 +280,30 @@
 tie = lambda *arrays: lax.optimization_barrier(arrays)
 
 
-def place_z(group, mine):
-    away = ((group >> 1) - (mine >> 1)) * jnp.where(mine & 1 == 0, 1, -1) & 3
-    high = away >> 1
-    place = ((away ^ high) & 1) << 2 | high << 1 | ((group ^ mine) & 1 ^ high)
-    return place, (place & 1) ^ jnp.where(place >= 2, 1, 0)
-
-
 def shards(
     node_lat, fine_edge_lat, fine_send, fine_recv, border_rows, coarse_edge_lat, coarse_send,
     coarse_recv, w_edge_in, w_edge_out, edge_gain, w_node_in, w_node_out, node_gain,
 ):
-    group = lax.axis_index("group")
-    patch = lax.axis_index("patch")
-    my_core, my_y, my_x = patch & 1, patch >> 1 & 3, patch >> 3
     edge_gain = edge_gain[None, :]
     node_gain = node_gain[None, :]
     grid = lambda ids: ids.reshape(-1, 128)
     swap = lambda rows, pairs: lax.ppermute(rows, "patch", pairs)
     join = lambda *rows: jnp.concatenate(rows, axis=0)
 
-    turn = lambda away: away ^ (away >> 1)
-
-    def place(ids):
-        row, at = ids & 7, ids >> 3
-        core, y, x = at & 1, turn(at >> 1 & 3 ^ my_y), turn(at >> 3 & 3 ^ my_x)
-        z, exchanged = place_z(at >> 5, group)
-        half = core ^ my_core ^ exchanged
-        x_first = half == my_core
-        first, second = jnp.where(x_first, x, y), jnp.where(x_first, y, x)
-        return half << 10 | second << 8 | first << 6 | z << 3 | row
-
-    send_place, recv_place = grid(place(coarse_send)), grid(place(coarse_recv))
-    slot = grid(jnp.where(coarse_recv >> 8 == group, coarse_recv & 255, -1))
-    fine_place = grid(
-        jnp.where((fine_send >= NODES) & (my_core == 0), fine_send ^ BORDER, fine_send)
-    )
     in_hbm = lambda *arrays: [pltpu.with_memory_space_constraint(a, pltpu.HBM) for a in arrays]
     like = lambda *arrays: [jax.ShapeDtypeStruct(a.shape, a.dtype) for a in arrays]
 
     own = node_lat[:COARSE_ROWS]
-    own, *loads = tie(own, border_rows, node_lat, w_edge_in, w_edge_out)
+    own, *loads = tie(own, border_rows, node_lat, w_edge_in)
     loads[0] = grid(loads[0])
     pair = lax.ppermute(own, ("group", "patch"), Z_PAIR)
-    inner, outer, nodes, w_in, w_out = call(
+    inner, outer, nodes, w_in = call(
         pick_kernel, [shape(BORDER), shape(BORDER), *like(*loads[1:])], 2 * 256 * 512 * 512,
         *in_hbm(*loads), name="pick",
-        scratch=[pltpu.VMEM((2, BORDER), jnp.int32), pltpu.SemaphoreType.DMA((4,))],
-        in_any=range(4), spec=HBM_SPEC,
-    )
-    pair, inner, outer, nodes, w_in, w_out = tie(pair, inner, outer, nodes, w_in, w_out)
+        scratch=[pltpu.VMEM((2, BORDER), jnp.int32), pltpu.SemaphoreType.DMA((3,))],
+        in_any=range(3), spec=HBM_SPEC,
+    )
+    pair, inner, outer, nodes, w_in = tie(pair, inner, outer, nodes, w_in)
     near = join(own, pair)
     near, inner, outer, nodes = tie(near, inner, outer, nodes)
     others = [lax.ppermute(near, ("group", "patch"), to) for to in (Z_NEAR, Z_MID, Z_FAR)]
@@ -329,7 +317,7 @@
     block, table = tie(block, table)
     others = [swap(block, crossed(k, 0)) for k in (1, 3, 2)]
     fine_args = (
-        fine_edge_lat, fine_place, grid(fine_recv), table, inner, outer, w_in, w_out, edge_gain
+        fine_edge_lat, grid(fine_send), grid(fine_recv), table, inner, outer, w_in, w_edge_out, edge_gain
     )
     fine_scratch = [pltpu.VMEM((HALF, D), BF), pltpu.SemaphoreType.DMA]
     fine_new, fine_sum, halo = call(
@@ -354,15 +342,19 @@
     part = join(block, *others)
     other_half = swap(part, SWAP_CORE)
 
-    send_part, recv_part = call(
-        gather_kernel, (shape(EDGES), shape(EDGES)), 2 << 30, send_place, recv_place, part,
-        name="gather",
+    ids = jax.ShapeDtypeStruct((EDGES // 128, 128), jnp.int32)
+    send_place, recv_place, send_part, recv_part = call(
+        gather_kernel, (ids, ids, shape(EDGES), shape(EDGES)), 2 << 30, grid(coarse_send),
+        grid(coarse_recv), part, name="gather",
     )
     coarse_new, sums = call(
         coarse_kernel, (shape(EDGES), shape(PATCHES * COARSE_ROWS)), 4 << 30, coarse_edge_lat,
-        send_place, recv_place, slot, other_half, send_part, recv_part, w_in, w_out, edge_gain,
-        name="coarse",
-        scratch=[pltpu.VMEM((EDGES, D), BF), pltpu.SemaphoreType.DMA((EDGES // BLOCK,))],
+        send_place, recv_place, grid(coarse_recv), other_half, send_part, recv_part, w_in,
+        w_edge_out, edge_gain, name="coarse",
+        scratch=[
+            pltpu.VMEM((EDGES, D), BF), pltpu.VMEM((EDGES // 128, 128), jnp.int32),
+            pltpu.SemaphoreType.DMA,
+        ],
         out_any=(0,),
     )
 

time: 64.2 us -> 62.8 us (0.978)
  Pallas kernels: 20.6 us -> 19.7 us
  other arithmetic: 0.77 us -> 0.03 us
    pallas_call x8, Pallas kernels: 20.6 us -> 19.7 us  [call(): pl.pallas_call(kernel, out_shape=outs, in_specs=[spec if at in in_any els...]
    ppermute x3, starting transfers between devices: 8.98 us -> 9.83 us  [shards(): lax.ppermute(near, ('group', 'patch'), to)]
    reshape x3 -> x0, other arithmetic: 0.75 us -> none  [shards(): grid = lambda ids: ids.reshape(-1, 128)]
  transfers between devices with their start and end apart: 13 -> 13, of which waited for: 3 -> 3; matrix products, arithmetic and copies ran while one was open for 1% -> 0% of each run, Pallas kernels for 19% -> 20%
where the time goes in v6:
time: 62.8 us; the launch traced here: 62.6 us
  starting transfers between devices  26.2 us (42%)
  Pallas kernels  19.7 us (31%)
  blocking collectives  12.8 us (20%)
  waiting for transfers between devices  2.03 us (3%)
  between operations  1.07 us (2%)
  local copies, waits for them, and re-layouts  0.83 us (1%)
    pallas_call x8, Pallas kernels, call(): pl.pallas_call(kernel, out_shape=outs, in_specs=[spec if at in in_any els...  19.7 us
    ppermute x9, starting transfers between devices, shards(): swap = lambda rows, pairs: lax.ppermute(rows, 'patch', pairs)  13.3 us
    all_to_all x1, blocking collectives, shards(): parts = lax.all_to_all(sums.reshape(PATCHES, COARSE_ROWS, D), 'patch', 0, 0)  12.8 us
    ppermute x3, starting transfers between devices, shards(): lax.ppermute(near, ('group', 'patch'), to)  9.83 us
    ppermute x1, starting transfers between devices, shards(): pair = lax.ppermute(own, ('group', 'patch'), Z_PAIR)  3.03 us
    ppermute x9, waiting for transfers between devices, shards(): swap = lambda rows, pairs: lax.ppermute(rows, 'patch', pairs)  2.02 us
  transfers between devices with their start and end apart: 13, of which 3 were waited for; matrix products, arithmetic and copies ran while one was open for 0% of the time, Pallas kernels for 20%

profile of v6, /device:TPU:1, one launch (start us, length us, event | category | flops | bytes accessed | tf_op | source)
XLA Modules:
  0.0 62.6 jit_solution(7344324743417037611)
XLA Ops:
  0.6 0.7 %slice.3 = bf16[8,512]{1,0:T(8,128)(2,1)S(1)} slice(bf16[512,512]{1,0:T(8,128)(2,1)} %node_in), slice={[0:8], [0:512]} | slice | bytes 16384 | tf_op jit(solution)/shard_map/slice | solution.py:296
  1.3 3.0 %collective-permute-start = (bf16[8,512]{1,0:T(8,128)(2,1)S(1)}, bf16[8,512]{1,0:T(8,128)(2,1)S(1)}, u32[]{:S(2)}, u32[]{:S(2)}) collective-permute-start(bf16[8,512]{1,0:T(8,128)(2,1)S(1)} %slice.3), channel_id=1, source_target_pairs={{0,33},{1,32},{2,35},{3,34},{4,37},{5,36},{6,39},{7,38},{8,41},{9,... | collective-permute-start | bytes 24584 | tf_op jit(solution)/shard_map/ppermute | solution.py:299
  4.4 1.6 %pick.1 = (bf16[128,512]{1,0:T(8,128)(2,1)S(1)}, bf16[128,512]{1,0:T(8,128)(2,1)S(1)}, bf16[512,512]{1,0:T(8,128)(2,1)S(1)}, bf16[1536,512]{1,0:T(8,128)(2,1)S(1)}) custom-call(s32[2,128]{1,0:T(2,128)} %bitcast.23, bf16[512,512]{1,0:T(8,128)(2,1)} %node_in, bf16[1536,512]{1,0:T(8,128)(2,1)} %w_in), custom_call_target="tpu_custom_call" | custom-call | flops 134217728 | bytes 4194304 | tf_op jit(solution)/shard_map/pick/pallas_call | solution.py:232
  6.0 0.0 collective-permute-done
  6.0 0.0 copy-start.3
  6.0 0.0 copy-start.5
  6.0 0.0 copy-start.6
  6.0 0.0 copy-start.7
  6.1 0.0 copy-start.10
  6.1 6.4 %collective-permute-start.3 = (bf16[16,512]{1,0:T(8,128)(2,1)S(1)}, bf16[16,512]{1,0:T(8,128)(2,1)S(1)}, u32[]{:S(2)}, u32[]{:S(2)}) collective-permute-start(bf16[16,512]{1,0:T(8,128)(2,1)S(1)} %pad_maximum_fusion.2), channel_id=1, source_target_pairs={{0,161},{1,160},{2,163},{3,162},{4,165},{5,164},{6,167},{7,166},{8... | collective-permute-start | bytes 49160 | tf_op jit(solution)/shard_map/ppermute | solution.py:309
  12.5 0.3 collective-permute-start.2
  12.7 3.2 %collective-permute-start.1 = (bf16[16,512]{1,0:T(8,128)(2,1)S(1)}, bf16[16,512]{1,0:T(8,128)(2,1)S(1)}, u32[]{:S(2)}, u32[]{:S(2)}) collective-permute-start(bf16[16,512]{1,0:T(8,128)(2,1)S(1)} %pad_maximum_fusion.2), channel_id=1, source_target_pairs={{0,225},{1,224},{2,227},{3,226},{4,229},{5,228},{6,231},{7,230},{8... | collective-permute-start | bytes 49160 | tf_op jit(solution)/shard_map/ppermute | solution.py:309
  15.9 0.1 collective-permute-start.7
  16.0 1.6 %collective-permute-start.8 = (bf16[128,512]{1,0:T(8,128)(2,1)S(1)}, bf16[128,512]{1,0:T(8,128)(2,1)S(1)}, u32[]{:S(2)}, u32[]{:S(2)}) collective-permute-start(bf16[128,512]{1,0:T(8,128)(2,1)S(1)} %get-tuple-element.72), channel_id=1, source_target_pairs={{0,31},{1,2},{2,1},{3,4},{4,3},{5,6},{6,5},{7,8},{8,7},{9,10},{10,... | collective-permute-start | bytes 393224 | tf_op jit(solution)/shard_map/ppermute | solution.py:290
  17.6 0.7 %project.1.table_ref = bf16[1024,512]{1,0:T(8,128)(2,1)S(1)} custom-call(bf16[512,512]{1,0:T(8,128)(2,1)S(1)} %get-tuple-element.62.node_ref, bf16[1536,512]{1,0:T(8,128)(2,1)S(1)} %get-tuple-element.64.w_ref.w_in_ref), custom_call_target="tpu_custom_call" | custom-call | flops 536870912 | bytes 4194304 | tf_op jit(solution)/shard_map/project/pallas_call | solution.py:232
  18.3 0.0 collective-permute-done.3
  18.3 0.0 collective-permute-done.2
  18.3 0.0 collective-permute-done.1
  18.3 2.7 %collective-permute-start.6 = (bf16[64,512]{1,0:T(8,128)(2,1)S(1)}, bf16[64,512]{1,0:T(8,128)(2,1)S(1)}, u32[]{:S(2)}, u32[]{:S(2)}) collective-permute-start(bf16[64,512]{1,0:T(8,128)(2,1)S(1)} %pad_maximum_fusion.1), channel_id=1, source_target_pairs={{0,16},{1,5},{2,18},{3,7},{4,20},{5,1},{6,22},{7,3},{8,24},{9,13},... | collective-permute-start | bytes 196616 | tf_op jit(solution)/shard_map/ppermute | solution.py:290
  21.1 1.1 %collective-permute-start.5 = (bf16[64,512]{1,0:T(8,128)(2,1)S(1)}, bf16[64,512]{1,0:T(8,128)(2,1)S(1)}, u32[]{:S(2)}, u32[]{:S(2)}) collective-permute-start(bf16[64,512]{1,0:T(8,128)(2,1)S(1)} %pad_maximum_fusion.1), channel_id=1, source_target_pairs={{0,24},{1,7},{2,26},{3,5},{4,28},{5,3},{6,30},{7,1},{8,16},{9,15},... | collective-permute-start | bytes 196616 | tf_op jit(solution)/shard_map/ppermute | solution.py:290
  22.1 0.0 collective-permute-start.4
  22.1 0.0 collective-permute-done.7.inner_ref
  22.1 0.0 collective-permute-done.8.outer_ref
  22.1 0.0 copy-done.3
  22.1 0.0 copy-done.5
  22.2 0.0 copy-done.6
  22.2 0.0 copy-done.7
  22.2 0.0 copy-done.10
  22.2 2.7 %fine_first.1 = (bf16[1024,512]{1,0:T(8,128)(2,1)}, f32[512,512]{1,0:T(8,128)S(1)}, bf16[256,512]{1,0:T(8,128)(2,1)S(1)}) custom-call(bf16[1024,512]{1,0:T(8,128)(2,1)S(1)} %copy-done.3, s32[8,128]{1,0:T(8,128)S(1)} %bitcast.13, s32[8,128]{1,0:T(8,128)S(1)} %bitcast.15, bf16[1024,512]{1,0:T(8,128)(2,1)S(1)} %project.1.table_ref, ...), custom_call_target="tpu_custom_call" | custom-call | flops 2147483648 | bytes 4194304 | tf_op jit(solution)/shard_map/fine_first/pallas_call | solution.py:232
  24.9 0.0 collective-permute-done.6
  25.0 0.4 collective-permute-done.5
  25.4 0.0 collective-permute-done.4
  25.4 2.8 %collective-permute-start.11 = (bf16[256,512]{1,0:T(8,128)(2,1)S(1)}, bf16[256,512]{1,0:T(8,128)(2,1)S(1)}, u32[]{:S(2)}, u32[]{:S(2)}) collective-permute-start(bf16[256,512]{1,0:T(8,128)(2,1)S(1)} %pad_maximum_fusion), channel_id=1, source_target_pairs={{0,4},{1,17},{2,6},{3,19},{4,0},{5,21},{6,2},{7,23},{8,12},{9,25},... | collective-permute-start | bytes 786440 | tf_op jit(solution)/shard_map/ppermute | solution.py:290
  28.2 1.0 %collective-permute-start.10 = (bf16[256,512]{1,0:T(8,128)(2,1)S(1)}, bf16[256,512]{1,0:T(8,128)(2,1)S(1)}, u32[]{:S(2)}, u32[]{:S(2)}) collective-permute-start(bf16[256,512]{1,0:T(8,128)(2,1)S(1)} %pad_maximum_fusion), channel_id=1, source_target_pairs={{0,6},{1,25},{2,4},{3,27},{4,2},{5,29},{6,0},{7,31},{8,14},{9,17},... | collective-permute-start | bytes 786440 | tf_op jit(solution)/shard_map/ppermute | solution.py:290
  29.2 0.0 collective-permute-start.9
  29.3 0.0 copy-start
  29.3 0.0 copy-start.1
  29.3 0.0 copy-start.2
  29.3 2.6 %fine_second.1 = (bf16[1024,512]{1,0:T(8,128)(2,1)}, f32[512,512]{1,0:T(8,128)S(1)}) custom-call(bf16[1024,512]{1,0:T(8,128)(2,1)S(1)} %copy-done.3, s32[8,128]{1,0:T(8,128)S(1)} %bitcast.14, s32[8,128]{1,0:T(8,128)S(1)} %bitcast.16, bf16[1024,512]{1,0:T(8,128)(2,1)S(1)} %project.1.table_ref, ...), custom_call_target="tpu_custom_call", output_to_operand_aliasing={{0}: (11, {})} | custom-call | flops 2147483648 | bytes 4194304 | tf_op jit(solution)/shard_map/fine_second/pallas_call | solution.py:232
  31.9 0.0 copy-done
  31.9 0.0 copy-done.1
  31.9 0.0 copy-done.2
  31.9 2.1 %node.1 = (bf16[512,512]{1,0:T(8,128)(2,1)}, f32[16,512]{1,0:T(8,128)S(1)}, f32[16,512]{1,0:T(8,128)S(1)}) custom-call(bf16[512,512]{1,0:T(8,128)(2,1)S(1)} %get-tuple-element.62.node_ref, f32[512,512]{1,0:T(8,128)S(1)} %get-tuple-element.82.sum_ref, bf16[1024,512]{1,0:T(8,128)(2,1)S(1)} %copy-done, bf16[512,512]{1,0:T(8,128)(2,1)S(1)} %copy-done.1, ...), custom_call_target="tpu_custom_call" | custom-call | flops 805306368 | bytes 4194304 | tf_op jit(solution)/shard_map/node/pallas_call | solution.py:232
  34.0 0.0 copy-start.8
  34.1 0.0 copy-start.9
  34.1 0.0 collective-permute-done.11
  34.1 1.2 %collective-permute-done.10 = bf16[256,512]{1,0:T(8,128)(2,1)S(1)} collective-permute-done((bf16[256,512]{1,0:T(8,128)(2,1)S(1)}, bf16[256,512]{1,0:T(8,128)(2,1)S(1)}, u32[]{:S(2)}, u32[]{:S(2)}) %collective-permute-start.10) | collective-permute-done | bytes 262176 | tf_op jit(solution)/shard_map/ppermute | solution.py:290
  35.3 0.3 collective-permute-done.9
  35.7 4.0 %collective-permute-start.12 = (bf16[1024,512]{1,0:T(8,128)(2,1)S(1)}, bf16[1024,512]{1,0:T(8,128)(2,1)S(1)}, u32[]{:S(2)}, u32[]{:S(2)}) collective-permute-start(bf16[1024,512]{1,0:T(8,128)(2,1)S(1)} %constant_dynamic-update-slice_fusion.table_ref), channel_id=1, source_target_pairs={{0,1},{1,0},{2,3},{3,2},{4,5},{5,4},{6,7},{7,6},{8,9},{9,8},{10,11... | collective-permute-start | bytes 3145736 | tf_op jit(solution)/shard_map/ppermute | solution.py:290
  39.8 0.0 copy-done.8
  39.8 0.0 copy-done.9
  39.8 0.0 copy-start.4
  39.8 2.4 %gather.1 = (s32[8,128]{1,0:T(8,128)S(1)}, s32[8,128]{1,0:T(8,128)S(1)}, bf16[1024,512]{1,0:T(8,128)(2,1)S(1)}, bf16[1024,512]{1,0:T(8,128)(2,1)S(1)}) custom-call(s32[8,128]{1,0:T(8,128)S(1)} %bitcast.17, s32[8,128]{1,0:T(8,128)S(1)} %bitcast.18, bf16[1024,512]{1,0:T(8,128)(2,1)S(1)} %constant_dynamic-update-slice_fusion.table_ref), custom_call_target="tpu_custom_call" | custom-call | flops 2147483648 | bytes 4194304 | tf_op jit(solution)/shard_map/gather/pallas_call | solution.py:232
  42.2 0.0 collective-permute-done.12.table_ref
  42.2 0.0 copy-done.4
  42.2 6.3 %coarse.1 = (bf16[1024,512]{1,0:T(8,128)(2,1)}, bf16[256,512]{1,0:T(8,128)(2,1)S(1)}) custom-call(bf16[1024,512]{1,0:T(8,128)(2,1)S(1)} %copy-done.4, s32[8,128]{1,0:T(8,128)S(1)} %get-tuple-element.89.send_ref, s32[8,128]{1,0:T(8,128)S(1)} %get-tuple-element.90.recv_ref, s32[8,128]{1,0:T(8,128)S(1)} %bitcast.19, ...), custom_call_target="tpu_custom_call" | custom-call | flops 4294967296 | bytes 4194304 | tf_op jit(solution)/shard_map/coarse/pallas_call | solution.py:232
  48.5 12.8 %all_to_all.5 = bf16[32,8,512]{2,1,0:T(8,128)(2,1)S(1)} all-to-all(bf16[32,8,512]{2,1,0:T(8,128)(2,1)S(1)} %bitcast.10), channel_id=1, replica_groups=mesh['group'=8,'patch'=32] {'patch'}, dimensions={0} | all-to-all | bytes 524288 | tf_op jit(solution)/shard_map/all_to_all | solution.py:361
  61.2 1.2 %tail.1 = bf16[512,512]{1,0:T(8,128)(2,1)} custom-call(bf16[512,512]{1,0:T(8,128)(2,1)S(1)} %get-tuple-element.62.node_ref, f32[16,512]{1,0:T(8,128)S(1)} %get-tuple-element.84.sum_ref, f32[16,512]{1,0:T(8,128)S(1)} %get-tuple-element.85.pre_ref, bf16[256,512]{1,0:T(8,128)(2,1)S(1)} %bitcast.9, ...), custom_call_target="tpu_custom_call", output_to_operand_aliasing={{}: (7, {})} | custom-call | flops 25165824 | bytes 4194304 | tf_op jit(solution)/shard_map/tail/pallas_call | solution.py:232
  (7 shorter events, 0.1 us)
Async XLA Ops:
  1.3 4.7 %collective-permute-start = (bf16[8,512]{1,0:T(8,128)(2,1)S(1)}, bf16[8,512]{1,0:T(8,128)(2,1)S(1)}, u32[]{:S(2)}, u32[]{:S(2)}) collective-permute-start(bf16[8,512]{1,0:T(8,128)(2,1)S(1)} %slice.3), channel_id=1, source_target_pairs={{0,33},{1,32},{2,35},{3,34},{4,37},{5,36},{6,39},{7,38},{8,41},{9,... | collective-permute-start | bytes 24584 | tf_op jit(solution)/shard_map/ppermute | solution.py:299
  6.0 16.1 %copy-start.3 = (bf16[1024,512]{1,0:T(8,128)(2,1)S(1)}, bf16[1024,512]{1,0:T(8,128)(2,1)}, u32[]{:S(2)}) copy-start(bf16[1024,512]{1,0:T(8,128)(2,1)} %edge_ref.4) | copy-start | bytes 3145732
  6.0 16.1 %copy-start.5 = (bf16[512,512]{1,0:T(8,128)(2,1)S(1)}, bf16[512,512]{1,0:T(8,128)(2,1)}, u32[]{:S(2)}) copy-start(bf16[512,512]{1,0:T(8,128)(2,1)} %w_out_ref.8) | copy-start | bytes 1572868
  6.0 16.1 %copy-start.6 = (s32[1024]{0:T(1024)S(1)}, s32[1024]{0:T(1024)}, u32[]{:S(2)}) copy-start(s32[1024]{0:T(1024)} %param.16) | copy-start | bytes 12292
  6.0 16.1 %copy-start.7 = (s32[1024]{0:T(1024)S(1)}, s32[1024]{0:T(1024)}, u32[]{:S(2)}) copy-start(s32[1024]{0:T(1024)} %param.17) | copy-start | bytes 12292
  6.1 16.1 %copy-start.10 = (f32[512]{0:T(512)S(1)}, f32[512]{0:T(512)}, u32[]{:S(2)}) copy-start(f32[512]{0:T(512)} %param.24) | copy-start | bytes 6148
  6.1 12.2 %collective-permute-start.3 = (bf16[16,512]{1,0:T(8,128)(2,1)S(1)}, bf16[16,512]{1,0:T(8,128)(2,1)S(1)}, u32[]{:S(2)}, u32[]{:S(2)}) collective-permute-start(bf16[16,512]{1,0:T(8,128)(2,1)S(1)} %pad_maximum_fusion.2), channel_id=1, source_target_pairs={{0,161},{1,160},{2,163},{3,162},{4,165},{5,164},{6,167},{7,166},{8... | collective-permute-start | bytes 49160 | tf_op jit(solution)/shard_map/ppermute | solution.py:309
  12.5 5.9 %collective-permute-start.2 = (bf16[16,512]{1,0:T(8,128)(2,1)S(1)}, bf16[16,512]{1,0:T(8,128)(2,1)S(1)}, u32[]{:S(2)}, u32[]{:S(2)}) collective-permute-start(bf16[16,512]{1,0:T(8,128)(2,1)S(1)} %pad_maximum_fusion.2), channel_id=1, source_target_pairs={{0,193},{1,192},{2,195},{3,194},{4,197},{5,196},{6,199},{7,198},{8... | collective-permute-start | bytes 49160 | tf_op jit(solution)/shard_map/ppermute | solution.py:309
  12.7 5.6 %collective-permute-start.1 = (bf16[16,512]{1,0:T(8,128)(2,1)S(1)}, bf16[16,512]{1,0:T(8,128)(2,1)S(1)}, u32[]{:S(2)}, u32[]{:S(2)}) collective-permute-start(bf16[16,512]{1,0:T(8,128)(2,1)S(1)} %pad_maximum_fusion.2), channel_id=1, source_target_pairs={{0,225},{1,224},{2,227},{3,226},{4,229},{5,228},{6,231},{7,230},{8... | collective-permute-start | bytes 49160 | tf_op jit(solution)/shard_map/ppermute | solution.py:309
  15.9 6.2 %collective-permute-start.7 = (bf16[128,512]{1,0:T(8,128)(2,1)S(1)}, bf16[128,512]{1,0:T(8,128)(2,1)S(1)}, u32[]{:S(2)}, u32[]{:S(2)}) collective-permute-start(bf16[128,512]{1,0:T(8,128)(2,1)S(1)} %get-tuple-element.71), channel_id=1, source_target_pairs={{0,1},{1,0},{2,3},{3,2},{4,5},{5,4},{6,7},{7,6},{8,9},{9,8},{10,11... | collective-permute-start | bytes 393224 | tf_op jit(solution)/shard_map/ppermute | solution.py:290
  16.0 6.2 %collective-permute-start.8 = (bf16[128,512]{1,0:T(8,128)(2,1)S(1)}, bf16[128,512]{1,0:T(8,128)(2,1)S(1)}, u32[]{:S(2)}, u32[]{:S(2)}) collective-permute-start(bf16[128,512]{1,0:T(8,128)(2,1)S(1)} %get-tuple-element.72), channel_id=1, source_target_pairs={{0,31},{1,2},{2,1},{3,4},{4,3},{5,6},{6,5},{7,8},{8,7},{9,10},{10,... | collective-permute-start | bytes 393224 | tf_op jit(solution)/shard_map/ppermute | solution.py:290
  18.3 6.6 %collective-permute-start.6 = (bf16[64,512]{1,0:T(8,128)(2,1)S(1)}, bf16[64,512]{1,0:T(8,128)(2,1)S(1)}, u32[]{:S(2)}, u32[]{:S(2)}) collective-permute-start(bf16[64,512]{1,0:T(8,128)(2,1)S(1)} %pad_maximum_fusion.1), channel_id=1, source_target_pairs={{0,16},{1,5},{2,18},{3,7},{4,20},{5,1},{6,22},{7,3},{8,24},{9,13},... | collective-permute-start | bytes 196616 | tf_op jit(solution)/shard_map/ppermute | solution.py:290
  21.1 4.3 %collective-permute-start.5 = (bf16[64,512]{1,0:T(8,128)(2,1)S(1)}, bf16[64,512]{1,0:T(8,128)(2,1)S(1)}, u32[]{:S(2)}, u32[]{:S(2)}) collective-permute-start(bf16[64,512]{1,0:T(8,128)(2,1)S(1)} %pad_maximum_fusion.1), channel_id=1, source_target_pairs={{0,24},{1,7},{2,26},{3,5},{4,28},{5,3},{6,30},{7,1},{8,16},{9,15},... | collective-permute-start | bytes 196616 | tf_op jit(solution)/shard_map/ppermute | solution.py:290
  22.1 3.3 %collective-permute-start.4 = (bf16[64,512]{1,0:T(8,128)(2,1)S(1)}, bf16[64,512]{1,0:T(8,128)(2,1)S(1)}, u32[]{:S(2)}, u32[]{:S(2)}) collective-permute-start(bf16[64,512]{1,0:T(8,128)(2,1)S(1)} %pad_maximum_fusion.1), channel_id=1, source_target_pairs={{0,8},{1,3},{2,10},{3,1},{4,12},{5,7},{6,14},{7,5},{8,0},{9,11},{1... | collective-permute-start | bytes 196616 | tf_op jit(solution)/shard_map/ppermute | solution.py:290
  25.4 8.7 %collective-permute-start.11 = (bf16[256,512]{1,0:T(8,128)(2,1)S(1)}, bf16[256,512]{1,0:T(8,128)(2,1)S(1)}, u32[]{:S(2)}, u32[]{:S(2)}) collective-permute-start(bf16[256,512]{1,0:T(8,128)(2,1)S(1)} %pad_maximum_fusion), channel_id=1, source_target_pairs={{0,4},{1,17},{2,6},{3,19},{4,0},{5,21},{6,2},{7,23},{8,12},{9,25},... | collective-permute-start | bytes 786440 | tf_op jit(solution)/shard_map/ppermute | solution.py:290
  28.2 7.1 %collective-permute-start.10 = (bf16[256,512]{1,0:T(8,128)(2,1)S(1)}, bf16[256,512]{1,0:T(8,128)(2,1)S(1)}, u32[]{:S(2)}, u32[]{:S(2)}) collective-permute-start(bf16[256,512]{1,0:T(8,128)(2,1)S(1)} %pad_maximum_fusion), channel_id=1, source_target_pairs={{0,6},{1,25},{2,4},{3,27},{4,2},{5,29},{6,0},{7,31},{8,14},{9,17},... | collective-permute-start | bytes 786440 | tf_op jit(solution)/shard_map/ppermute | solution.py:290
  29.2 6.4 %collective-permute-start.9 = (bf16[256,512]{1,0:T(8,128)(2,1)S(1)}, bf16[256,512]{1,0:T(8,128)(2,1)S(1)}, u32[]{:S(2)}, u32[]{:S(2)}) collective-permute-start(bf16[256,512]{1,0:T(8,128)(2,1)S(1)} %pad_maximum_fusion), channel_id=1, source_target_pairs={{0,2},{1,9},{2,0},{3,11},{4,6},{5,13},{6,4},{7,15},{8,10},{9,1},{1... | collective-permute-start | bytes 786440 | tf_op jit(solution)/shard_map/ppermute | solution.py:290
  29.3 2.7 %copy-start = (bf16[1024,512]{1,0:T(8,128)(2,1)S(1)}, bf16[1024,512]{1,0:T(8,128)(2,1)}, u32[]{:S(2)}) copy-start(bf16[1024,512]{1,0:T(8,128)(2,1)} %w_in_ref.3) | copy-start | bytes 3145732
  29.3 2.7 %copy-start.1 = (bf16[512,512]{1,0:T(8,128)(2,1)S(1)}, bf16[512,512]{1,0:T(8,128)(2,1)}, u32[]{:S(2)}) copy-start(bf16[512,512]{1,0:T(8,128)(2,1)} %w_out_ref.9) | copy-start | bytes 1572868
  29.3 2.7 %copy-start.2 = (f32[512]{0:T(512)S(1)}, f32[512]{0:T(512)}, u32[]{:S(2)}) copy-start(f32[512]{0:T(512)} %param.27) | copy-start | bytes 6148
  34.0 5.7 %copy-start.8 = (s32[1024]{0:T(1024)S(1)}, s32[1024]{0:T(1024)}, u32[]{:S(2)}) copy-start(s32[1024]{0:T(1024)} %param.20) | copy-start | bytes 12292
  34.1 5.7 %copy-start.9 = (s32[1024]{0:T(1024)S(1)}, s32[1024]{0:T(1024)}, u32[]{:S(2)}) copy-start(s32[1024]{0:T(1024)} %param.21) | copy-start | bytes 12292
  35.7 6.5 %collective-permute-start.12 = (bf16[1024,512]{1,0:T(8,128)(2,1)S(1)}, bf16[1024,512]{1,0:T(8,128)(2,1)S(1)}, u32[]{:S(2)}, u32[]{:S(2)}) collective-permute-start(bf16[1024,512]{1,0:T(8,128)(2,1)S(1)} %constant_dynamic-update-slice_fusion.table_ref), channel_id=1, source_target_pairs={{0,1},{1,0},{2,3},{3,2},{4,5},{5,4},{6,7},{7,6},{8,9},{9,8},{10,11... | collective-permute-start | bytes 3145736 | tf_op jit(solution)/shard_map/ppermute | solution.py:290
  39.8 2.4 %copy-start.4 = (bf16[1024,512]{1,0:T(8,128)(2,1)S(1)}, bf16[1024,512]{1,0:T(8,128)(2,1)}, u32[]{:S(2)}) copy-start(bf16[1024,512]{1,0:T(8,128)(2,1)} %edge_ref.5) | copy-start | bytes 3145732

commit v7 on v6

--- a/solution.py
+++ b/solution.py
@@ -16,6 +16,7 @@
 COARSE_ROWS = 8
 EDGES = 1024
 HALF = 512
+EARLY = 256
 NODES = 512
 TAIL = 16
 EPS = 1e-05
@@ -68,6 +69,12 @@
         ids = jnp.broadcast_to(ids_ref[at : at + 1, :], (height, 128)).astype(jnp.int16)
         parts.append(jnp.where(ids == rows, one, zero))
     return jnp.concatenate(parts, axis=1)
+
+
+def put_rows(rows_ref, out_ref, first, sem):
+    copy = pltpu.make_async_copy(rows_ref, out_ref.at[pl.ds(first, rows_ref.shape[0])], sem)
+    copy.start()
+    return copy
 
 
 def finish_edges(pre, edges, w_out, gain):
@@ -112,10 +119,11 @@
     gain_ref, *rest,
 ):
     if first:
-        halo_in, before_ref, _, new_ref, sum_ref, rows_ref, sem = rest
+        halo_in, before_ref, earlier_ref, rows_ref, sum_ref, new_ref, sem = rest
+        copy = put_rows(earlier_ref, new_ref, 0, sem)
         halo = halo_in[...]
     else:
-        new_ref, sum_ref, halo_out, rows_ref, sem = rest
+        rows_ref, sum_ref, halo_out = rest
         halo_out[:BORDER] = dot(inner_ref[...], w_in_ref[D : 2 * D]).astype(BF)
         halo_out[BORDER:] = dot(outer_ref[...], w_in_ref[D : 2 * D]).astype(BF)
         halo = halo_out[...]
@@ -129,11 +137,10 @@
     pre = pre + dot(jnp.concatenate([recv_hot, send_hot[:, :NODES]], axis=1), table_ref[...])
     pre = pre + dot(send_hot[:, NODES:], halo)
     rows_ref[...] = finish_edges(pre, edges, w_out_ref[...], gain_ref[...])
-    copy = pltpu.make_async_copy(rows_ref, new_ref.at[pl.ds(first, HALF)], sem)
-    copy.start()
     sums = dot(one_hot_rows(recv_ref, first, HALF, NODES), rows_ref[...])
     sum_ref[...] = before_ref[...] + sums if first else sums
-    copy.wait()
+    if first:
+        copy.wait()
 
 
 def place_z(group, mine):
@@ -156,36 +163,48 @@
     return half << 10 | second << 8 | first << 6 | z << 3 | row
 
 
-def gather_kernel(
-    send_ref, recv_ref, table_ref, send_place, recv_place, send_out, recv_out
-):
+def early_kernel(
+    edge_ref, send_ref, recv_ref, mine_ref, theirs_ref, w_in_ref, send_place, recv_place,
+    send_out, recv_out, pre_ref, table_ref,
+):
+    table_ref[:EARLY] = mine_ref[...]
+    table_ref[EARLY:] = theirs_ref[...]
+    pre_ref[...] = dot(edge_ref[...], w_in_ref[:D])
     for ids_ref, place_ref, out_ref in (
         (send_ref, send_place, send_out), (recv_ref, recv_place, recv_out)
     ):
         place_ref[...] = place(ids_ref[...])
-        hot = one_hot(column_of(place_ref, 0, EDGES), table_ref.shape[0])
-        out_ref[...] = dot(hot, table_ref[...]).astype(BF)
+        column = column_of(place_ref, 0, EDGES)
+        hot = [one_hot(column, EARLY, first) for first in (0, SIDE * EARLY)]
+        out_ref[...] = dot(jnp.concatenate(hot, axis=1), table_ref[...]).astype(BF)
+
+
+def gather_kernel(
+    send_ref, recv_ref, send_part, recv_part, table_ref, rows_ref, send_out, recv_out, new_ref, sem
+):
+    copy = put_rows(rows_ref, new_ref, 0, sem)
+    for ids_ref, part_ref, out_ref in (
+        (send_ref, send_part, send_out), (recv_ref, recv_part, recv_out)
+    ):
+        hot = one_hot(column_of(ids_ref, 0, EDGES), table_ref.shape[0], EARLY)
+        out_ref[...] = (dot(hot, table_ref[...]) + part_ref[...].astype(F32)).astype(BF)
+    copy.wait()
 
 
 def coarse_kernel(
-    edge_ref, send_ref, recv_ref, node_ref, table_ref, send_part, recv_part, w_in_ref, w_out_ref,
-    gain_ref, new_ref, sum_ref, rows_ref, slot_ref, sem,
-):
-    half = table_ref.shape[0]
-    edges = edge_ref[...]
-    joined = [edges]
+    edge_ref, pre_ref, send_ref, recv_ref, node_ref, table_ref, send_part, recv_part, w_in_ref,
+    w_out_ref, gain_ref, rows_ref, sum_ref, slot_ref,
+):
+    joined = []
     for ids_ref, part_ref in ((send_ref, send_part), (recv_ref, recv_part)):
-        hot = one_hot(column_of(ids_ref, 0, EDGES), half, half)
+        hot = one_hot(column_of(ids_ref, 0, EDGES), table_ref.shape[0], (SIDE + 1) * EARLY)
         joined.append((dot(hot, table_ref[...]) + part_ref[...].astype(F32)).astype(BF))
-    pre = dot(jnp.concatenate(joined, axis=1), w_in_ref[...])
-    rows_ref[...] = finish_edges(pre, edges, w_out_ref[...], gain_ref[...])
-    copy = pltpu.make_async_copy(rows_ref, new_ref, sem)
-    copy.start()
+    pre = pre_ref[...] + dot(jnp.concatenate(joined, axis=1), w_in_ref[D:])
+    rows_ref[...] = finish_edges(pre, edge_ref[...], w_out_ref[...], gain_ref[...])
     nodes = node_ref[...]
     slot_ref[...] = jnp.where(nodes >> 8 == lax.axis_index("group"), nodes & 255, -1)
     hot = one_hot_rows(slot_ref, 0, EDGES, sum_ref.shape[0])
     sum_ref[...] = dot(hot, rows_ref[...]).astype(BF)
-    copy.wait()
 
 
 def finish_nodes(pre, nodes, w_out_ref, gain):
@@ -193,18 +212,25 @@
     return (nodes.astype(F32) + layer_norm(projected) * gain).astype(BF)
 
 
-def node_kernel(node_ref, sum_ref, w_in_ref, w_out_ref, gain_ref, out_ref, first_ref, pre_ref):
+def node_kernel(
+    node_ref, sum_ref, w_in_ref, w_out_ref, gain_ref, edge_rows, _, out_ref, first_ref, pre_ref,
+    new_ref, sem,
+):
+    copy = put_rows(edge_rows, new_ref, HALF, sem)
     nodes = node_ref[...]
     pre = dot(nodes, w_in_ref[:D])
     pre_ref[...] = pre[:TAIL]
     first_ref[...] = sum_ref[:TAIL]
     pre = pre + dot(sum_ref[...].astype(BF), w_in_ref[D:])
     out_ref[...] = finish_nodes(pre, nodes, w_out_ref, gain_ref[...])
+    copy.wait()
 
 
 def tail_kernel(
-    node_ref, sum_ref, pre_ref, parts_ref, w_in_ref, w_out_ref, gain_ref, _, out_ref, rows_ref, sem
-):
+    node_ref, sum_ref, pre_ref, parts_ref, w_in_ref, w_out_ref, gain_ref, edge_rows, _, out_ref,
+    new_ref, rows_ref, sems,
+):
+    edge_copy = put_rows(edge_rows, new_ref, 0, sems.at[0])
     parts = parts_ref[...].astype(F32).reshape(-1, COARSE_ROWS, D)
     total = sum_ref[...]
     total = jnp.concatenate(
@@ -212,9 +238,8 @@
     )
     pre = pre_ref[...] + dot(total.astype(BF), w_in_ref[D:])
     rows_ref[...] = finish_nodes(pre, node_ref[:TAIL], w_out_ref, gain_ref[...])
-    copy = pltpu.make_async_copy(rows_ref, out_ref.at[pl.ds(0, TAIL)], sem)
-    copy.start()
-    copy.wait()
+    put_rows(rows_ref, out_ref, 0, sems.at[1]).wait()
+    edge_copy.wait()
 
 
 def shape(rows, dtype=BF):
@@ -312,58 +337,61 @@
         project_kernel, (shape(2 * NODES),), 4 * 512 * 512 * 512, nodes, w_in, name="project"
     )
     *others, table = tie(*others, table)
-    block = join(near, *others)
+    block = join(near, others[0], others[1], others[2])
 
     block, table = tie(block, table)
     others = [swap(block, crossed(k, 0)) for k in (1, 3, 2)]
     fine_args = (
         fine_edge_lat, grid(fine_send), grid(fine_recv), table, inner, outer, w_in, w_edge_out, edge_gain
     )
-    fine_scratch = [pltpu.VMEM((HALF, D), BF), pltpu.SemaphoreType.DMA]
-    fine_new, fine_sum, halo = call(
-        functools.partial(fine_kernel, 0), (shape(EDGES), shape(NODES, F32), shape(2 * BORDER)),
-        2 << 30, *fine_args, name="fine_first", scratch=fine_scratch, out_any=(0,),
+    rows, fine_sum, halo = call(
+        functools.partial(fine_kernel, 0), (shape(HALF), shape(NODES, F32), shape(2 * BORDER)),
+        2 << 30, *fine_args, name="fine_first",
     )
     *others, fine_sum = tie(*others, fine_sum)
-    block = join(block, *others)
+    block = join(block, others[0], others[1], others[2])
 
     block, fine_sum = tie(block, fine_sum)
     others = [swap(block, crossed(k, 1)) for k in (1, 3, 2)]
-    fine_new, fine_sum = call(
-        functools.partial(fine_kernel, HALF), (shape(EDGES), shape(NODES, F32)), 2 << 30,
-        *fine_args, halo, fine_sum, fine_new, name="fine_second", scratch=fine_scratch,
-        out_any=(0,), in_any=(len(fine_args) + 2,), aliases={len(fine_args) + 2: 0},
-    )
-    node_main, first_sum, first_pre = call(
-        node_kernel, (shape(NODES), shape(TAIL, F32), shape(TAIL, F32)), 768 << 20, nodes,
-        fine_sum, w_node_in, w_node_out, node_gain, name="node",
-    )
-    *others, first_sum = tie(*others, first_sum)
-    part = join(block, *others)
-    other_half = swap(part, SWAP_CORE)
-
+    other_block = swap(block, SWAP_CORE)
+    rows, fine_sum, fine_new = call(
+        functools.partial(fine_kernel, HALF), (shape(HALF), shape(NODES, F32), shape(EDGES)),
+        2 << 30, *fine_args, halo, fine_sum, rows, name="fine_second",
+        scratch=[pltpu.SemaphoreType.DMA], out_any=(2,),
+    )
+    node_rows, first_sum, first_pre, fine_new = call(
+        node_kernel, (shape(NODES), shape(TAIL, F32), shape(TAIL, F32), shape(EDGES)), 768 << 20,
+        nodes, fine_sum, w_node_in, w_node_out, node_gain, rows, fine_new, name="node",
+        scratch=[pltpu.SemaphoreType.DMA], out_any=(3,), in_any=(6,), aliases={6: 3},
+    )
+    other_block, first_sum = tie(other_block, first_sum)
     ids = jax.ShapeDtypeStruct((EDGES // 128, 128), jnp.int32)
-    send_place, recv_place, send_part, recv_part = call(
-        gather_kernel, (ids, ids, shape(EDGES), shape(EDGES)), 2 << 30, grid(coarse_send),
-        grid(coarse_recv), part, name="gather",
-    )
-    coarse_new, sums = call(
+    send_place, recv_place, send_part, recv_part, pre = call(
+        early_kernel, (ids, ids, shape(EDGES), shape(EDGES), shape(EDGES, F32)), 2 << 30,
+        coarse_edge_lat, grid(coarse_send), grid(coarse_recv), block, other_block, w_in,
+        name="early", scratch=[pltpu.VMEM((2 * EARLY, D), BF)],
+    )
+    *others, pre = tie(*others, pre)
+    part = join(others[0], others[1], others[2])
+    other_part = swap(part, SWAP_CORE)
+    send_part, recv_part, node_new = call(
+        gather_kernel, (shape(EDGES), shape(EDGES), shape(NODES)), 2 << 30, send_place,
+        recv_place, send_part, recv_part, part, node_rows, name="gather",
+        scratch=[pltpu.SemaphoreType.DMA], out_any=(2,),
+    )
+    coarse_rows, sums = call(
         coarse_kernel, (shape(EDGES), shape(PATCHES * COARSE_ROWS)), 4 << 30, coarse_edge_lat,
-        send_place, recv_place, grid(coarse_recv), other_half, send_part, recv_part, w_in,
+        pre, send_place, recv_place, grid(coarse_recv), other_part, send_part, recv_part, w_in,
         w_edge_out, edge_gain, name="coarse",
-        scratch=[
-            pltpu.VMEM((EDGES, D), BF), pltpu.VMEM((EDGES // 128, 128), jnp.int32),
-            pltpu.SemaphoreType.DMA,
-        ],
-        out_any=(0,),
+        scratch=[pltpu.VMEM((EDGES // 128, 128), jnp.int32)],
     )
 
     parts = lax.all_to_all(sums.reshape(PATCHES, COARSE_ROWS, D), "patch", 0, 0)
-    (node_new,) = call(
-        tail_kernel, (shape(NODES),), 24 << 20, nodes, first_sum, first_pre, parts.reshape(-1, D),
-        w_node_in, w_node_out, node_gain, node_main, name="tail",
-        scratch=[pltpu.VMEM((TAIL, D), BF), pltpu.SemaphoreType.DMA], out_any=(0,), in_any=(7,),
-        aliases={7: 0},
+    node_new, coarse_new = call(
+        tail_kernel, (shape(NODES), shape(EDGES)), 24 << 20, nodes, first_sum, first_pre,
+        parts.reshape(-1, D), w_node_in, w_node_out, node_gain, coarse_rows, node_new,
+        name="tail", scratch=[pltpu.VMEM((TAIL, D), BF), pltpu.SemaphoreType.DMA((2,))],
+        out_any=(0, 1), in_any=(8,), aliases={8: 0},
     )
     return (node_new, fine_new, coarse_new)
 

time: 62.8 us -> 60.2 us (0.959)
  Pallas kernels: 19.7 us -> 17.7 us
  waiting for transfers between devices: 2.03 us -> 1.04 us
    pallas_call x8 -> x9, Pallas kernels: 19.7 us -> 17.7 us  [call(): pl.pallas_call(kernel, out_shape=outs, in_specs=[spec if at in in_any els...]
    ppermute x9 -> x10, waiting for transfers between devices: 2.02 us -> 1.02 us  [shards(): swap = lambda rows, pairs: lax.ppermute(rows, 'patch', pairs)]
    ppermute x9 -> x10, starting transfers between devices: 13.3 us -> 13.7 us  [shards(): swap = lambda rows, pairs: lax.ppermute(rows, 'patch', pairs)]
  transfers between devices with their start and end apart: 13 -> 14, of which waited for: 3 -> 1; matrix products, arithmetic and copies ran while one was open for 0% -> 0% of each run, Pallas kernels for 20% -> 20%
where the time goes in v7:
time: 60.2 us; the launch traced here: 60 us
  starting transfers between devices  26.5 us (44%)
  Pallas kernels  17.7 us (29%)
  blocking collectives  12.7 us (21%)
  between operations  1.11 us (2%)
  waiting for transfers between devices  1.04 us (2%)
  local copies, waits for them, and re-layouts  0.84 us (1%)
    pallas_call x9, Pallas kernels, call(): pl.pallas_call(kernel, out_shape=outs, in_specs=[spec if at in in_any els...  17.7 us
    ppermute x10, starting transfers between devices, shards(): swap = lambda rows, pairs: lax.ppermute(rows, 'patch', pairs)  13.7 us
    all_to_all x1, blocking collectives, shards(): parts = lax.all_to_all(sums.reshape(PATCHES, COARSE_ROWS, D), 'patch', 0, 0)  12.7 us
    ppermute x3, starting transfers between devices, shards(): lax.ppermute(near, ('group', 'patch'), to)  9.83 us
    ppermute x1, starting transfers between devices, shards(): pair = lax.ppermute(own, ('group', 'patch'), Z_PAIR)  3.03 us
  transfers between devices with their start and end apart: 14, of which 1 were waited for; matrix products, arithmetic and copies ran while one was open for 0% of the time, Pallas kernels for 20%

profile of v7, /device:TPU:1, one launch (start us, length us, event | category | flops | bytes accessed | tf_op | source)
XLA Modules:
  0.0 60.0 jit_solution(4206197810992804)
XLA Ops:
  0.6 0.7 %slice.3 = bf16[8,512]{1,0:T(8,128)(2,1)S(1)} slice(bf16[512,512]{1,0:T(8,128)(2,1)} %node_in), slice={[0:8], [0:512]} | slice | bytes 16384 | tf_op jit(solution)/shard_map/slice | solution.py:321
  1.3 3.0 %collective-permute-start = (bf16[8,512]{1,0:T(8,128)(2,1)S(1)}, bf16[8,512]{1,0:T(8,128)(2,1)S(1)}, u32[]{:S(2)}, u32[]{:S(2)}) collective-permute-start(bf16[8,512]{1,0:T(8,128)(2,1)S(1)} %slice.3), channel_id=1, source_target_pairs={{0,33},{1,32},{2,35},{3,34},{4,37},{5,36},{6,39},{7,38},{8,41},{9,... | collective-permute-start | bytes 24584 | tf_op jit(solution)/shard_map/ppermute | solution.py:324
  4.4 1.6 %pick.1 = (bf16[128,512]{1,0:T(8,128)(2,1)S(1)}, bf16[128,512]{1,0:T(8,128)(2,1)S(1)}, bf16[512,512]{1,0:T(8,128)(2,1)S(1)}, bf16[1536,512]{1,0:T(8,128)(2,1)S(1)}) custom-call(s32[2,128]{1,0:T(2,128)} %bitcast.23, bf16[512,512]{1,0:T(8,128)(2,1)} %node_in, bf16[1536,512]{1,0:T(8,128)(2,1)} %w_in), custom_call_target="tpu_custom_call" | custom-call | flops 134217728 | bytes 4194304 | tf_op jit(solution)/shard_map/pick/pallas_call | solution.py:257
  6.0 0.0 collective-permute-done
  6.0 0.0 copy-start.3
  6.0 0.0 copy-start.5
  6.0 0.0 copy-start.6
  6.0 0.0 copy-start.7
  6.1 0.0 copy-start.10
  6.1 6.4 %collective-permute-start.3 = (bf16[16,512]{1,0:T(8,128)(2,1)S(1)}, bf16[16,512]{1,0:T(8,128)(2,1)S(1)}, u32[]{:S(2)}, u32[]{:S(2)}) collective-permute-start(bf16[16,512]{1,0:T(8,128)(2,1)S(1)} %pad_maximum_fusion.2), channel_id=1, source_target_pairs={{0,161},{1,160},{2,163},{3,162},{4,165},{5,164},{6,167},{7,166},{8... | collective-permute-start | bytes 49160 | tf_op jit(solution)/shard_map/ppermute | solution.py:334
  12.5 0.3 collective-permute-start.2
  12.7 3.2 %collective-permute-start.1 = (bf16[16,512]{1,0:T(8,128)(2,1)S(1)}, bf16[16,512]{1,0:T(8,128)(2,1)S(1)}, u32[]{:S(2)}, u32[]{:S(2)}) collective-permute-start(bf16[16,512]{1,0:T(8,128)(2,1)S(1)} %pad_maximum_fusion.2), channel_id=1, source_target_pairs={{0,225},{1,224},{2,227},{3,226},{4,229},{5,228},{6,231},{7,230},{8... | collective-permute-start | bytes 49160 | tf_op jit(solution)/shard_map/ppermute | solution.py:334
  15.9 0.1 collective-permute-start.7
  16.0 1.6 %collective-permute-start.8 = (bf16[128,512]{1,0:T(8,128)(2,1)S(1)}, bf16[128,512]{1,0:T(8,128)(2,1)S(1)}, u32[]{:S(2)}, u32[]{:S(2)}) collective-permute-start(bf16[128,512]{1,0:T(8,128)(2,1)S(1)} %get-tuple-element.82), channel_id=1, source_target_pairs={{0,31},{1,2},{2,1},{3,4},{4,3},{5,6},{6,5},{7,8},{8,7},{9,10},{10,... | collective-permute-start | bytes 393224 | tf_op jit(solution)/shard_map/ppermute | solution.py:315
  17.6 0.7 %project.1.table_ref = bf16[1024,512]{1,0:T(8,128)(2,1)S(1)} custom-call(bf16[512,512]{1,0:T(8,128)(2,1)S(1)} %get-tuple-element.72.node_ref, bf16[1536,512]{1,0:T(8,128)(2,1)S(1)} %get-tuple-element.74.w_ref.w_in_ref), custom_call_target="tpu_custom_call" | custom-call | flops 536870912 | bytes 4194304 | tf_op jit(solution)/shard_map/project/pallas_call | solution.py:257
  18.3 0.0 collective-permute-done.3
  18.3 0.0 collective-permute-done.2
  18.3 0.0 collective-permute-done.1
  18.3 2.7 %collective-permute-start.6 = (bf16[64,512]{1,0:T(8,128)(2,1)S(1)}, bf16[64,512]{1,0:T(8,128)(2,1)S(1)}, u32[]{:S(2)}, u32[]{:S(2)}) collective-permute-start(bf16[64,512]{1,0:T(8,128)(2,1)S(1)} %pad_maximum_fusion.1), channel_id=1, source_target_pairs={{0,16},{1,5},{2,18},{3,7},{4,20},{5,1},{6,22},{7,3},{8,24},{9,13},... | collective-permute-start | bytes 196616 | tf_op jit(solution)/shard_map/ppermute | solution.py:315
  21.1 1.1 %collective-permute-start.5 = (bf16[64,512]{1,0:T(8,128)(2,1)S(1)}, bf16[64,512]{1,0:T(8,128)(2,1)S(1)}, u32[]{:S(2)}, u32[]{:S(2)}) collective-permute-start(bf16[64,512]{1,0:T(8,128)(2,1)S(1)} %pad_maximum_fusion.1), channel_id=1, source_target_pairs={{0,24},{1,7},{2,26},{3,5},{4,28},{5,3},{6,30},{7,1},{8,16},{9,15},... | collective-permute-start | bytes 196616 | tf_op jit(solution)/shard_map/ppermute | solution.py:315
  22.1 0.0 collective-permute-start.4
  22.1 0.0 collective-permute-done.7.inner_ref
  22.1 0.0 collective-permute-done.8.outer_ref
  22.1 0.0 copy-done.3
  22.1 0.0 copy-done.5
  22.2 0.0 copy-done.6
  22.2 0.0 copy-done.7
  22.2 0.0 copy-done.10
  22.2 2.2 %fine_first.1 = (bf16[512,512]{1,0:T(8,128)(2,1)S(1)}, f32[512,512]{1,0:T(8,128)S(1)}, bf16[256,512]{1,0:T(8,128)(2,1)S(1)}) custom-call(bf16[1024,512]{1,0:T(8,128)(2,1)S(1)} %copy-done.3, s32[8,128]{1,0:T(8,128)S(1)} %bitcast.13, s32[8,128]{1,0:T(8,128)S(1)} %bitcast.15, bf16[1024,512]{1,0:T(8,128)(2,1)S(1)} %project.1.table_ref, ...), custom_call_target="tpu_custom_call" | custom-call | flops 2147483648 | bytes 4194304 | tf_op jit(solution)/shard_map/fine_first/pallas_call | solution.py:257
  24.4 0.0 collective-permute-done.6
  24.4 1.0 %collective-permute-done.5 = bf16[64,512]{1,0:T(8,128)(2,1)S(1)} collective-permute-done((bf16[64,512]{1,0:T(8,128)(2,1)S(1)}, bf16[64,512]{1,0:T(8,128)(2,1)S(1)}, u32[]{:S(2)}, u32[]{:S(2)}) %collective-permute-start.5) | collective-permute-done | bytes 65568 | tf_op jit(solution)/shard_map/ppermute | solution.py:315
  25.4 0.0 collective-permute-done.4
  25.4 2.8 %collective-permute-start.12 = (bf16[256,512]{1,0:T(8,128)(2,1)S(1)}, bf16[256,512]{1,0:T(8,128)(2,1)S(1)}, u32[]{:S(2)}, u32[]{:S(2)}) collective-permute-start(bf16[256,512]{1,0:T(8,128)(2,1)S(1)} %pad_maximum_fusion.mine_ref), channel_id=1, source_target_pairs={{0,4},{1,17},{2,6},{3,19},{4,0},{5,21},{6,2},{7,23},{8,12},{9,25},... | collective-permute-start | bytes 786440 | tf_op jit(solution)/shard_map/ppermute | solution.py:315
  28.2 1.0 %collective-permute-start.11 = (bf16[256,512]{1,0:T(8,128)(2,1)S(1)}, bf16[256,512]{1,0:T(8,128)(2,1)S(1)}, u32[]{:S(2)}, u32[]{:S(2)}) collective-permute-start(bf16[256,512]{1,0:T(8,128)(2,1)S(1)} %pad_maximum_fusion.mine_ref), channel_id=1, source_target_pairs={{0,6},{1,25},{2,4},{3,27},{4,2},{5,29},{6,0},{7,31},{8,14},{9,17},... | collective-permute-start | bytes 786440 | tf_op jit(solution)/shard_map/ppermute | solution.py:315
  29.2 0.0 collective-permute-start.10
  29.3 3.0 %collective-permute-start.9 = (bf16[256,512]{1,0:T(8,128)(2,1)S(1)}, bf16[256,512]{1,0:T(8,128)(2,1)S(1)}, u32[]{:S(2)}, u32[]{:S(2)}) collective-permute-start(bf16[256,512]{1,0:T(8,128)(2,1)S(1)} %pad_maximum_fusion.mine_ref), channel_id=1, source_target_pairs={{0,1},{1,0},{2,3},{3,2},{4,5},{5,4},{6,7},{7,6},{8,9},{9,8},{10,11... | collective-permute-start | bytes 786440 | tf_op jit(solution)/shard_map/ppermute | solution.py:315
  32.2 0.0 copy-start
  32.2 0.0 copy-start.1
  32.2 0.0 copy-start.2
  32.2 2.6 %fine_second.1 = (bf16[512,512]{1,0:T(8,128)(2,1)S(1)}, f32[512,512]{1,0:T(8,128)S(1)}, bf16[1024,512]{1,0:T(8,128)(2,1)}) custom-call(bf16[1024,512]{1,0:T(8,128)(2,1)S(1)} %copy-done.3, s32[8,128]{1,0:T(8,128)S(1)} %bitcast.14, s32[8,128]{1,0:T(8,128)S(1)} %bitcast.16, bf16[1024,512]{1,0:T(8,128)(2,1)S(1)} %project.1.table_ref, ...), custom_call_target="tpu_custom_call" | custom-call | flops 2147483648 | bytes 4194304 | tf_op jit(solution)/shard_map/fine_second/pallas_call | solution.py:257
  34.8 0.0 copy-done
  34.8 0.0 copy-done.1
  34.8 0.0 copy-done.2
  34.9 0.0 copy-start.4
  34.9 0.0 copy-start.8
  34.9 0.0 copy-start.9
  34.9 1.3 %node.1 = (bf16[512,512]{1,0:T(8,128)(2,1)S(1)}, f32[16,512]{1,0:T(8,128)S(1)}, f32[16,512]{1,0:T(8,128)S(1)}, bf16[1024,512]{1,0:T(8,128)(2,1)}) custom-call(bf16[512,512]{1,0:T(8,128)(2,1)S(1)} %get-tuple-element.72.node_ref, f32[512,512]{1,0:T(8,128)S(1)} %get-tuple-element.92.sum_ref, ...), custom_call_target="tpu_custom_call", output_to_operand_aliasing={{3}: (6, {})} | custom-call | flops 805306368 | bytes 4194304 | tf_op jit(solution)/shard_map/node/pallas_call | solution.py:257
  36.2 0.0 collective-permute-done.9.theirs_ref
  36.2 0.0 copy-done.4
  36.3 0.0 copy-done.8
  36.3 0.0 copy-done.9
  36.3 1.8 %early.1 = (s32[8,128]{1,0:T(8,128)S(1)}, s32[8,128]{1,0:T(8,128)S(1)}, bf16[1024,512]{1,0:T(8,128)(2,1)S(1)}, bf16[1024,512]{1,0:T(8,128)(2,1)S(1)}, f32[1024,512]{1,0:T(8,128)S(1)}) custom-call(bf16[1024,512]{1,0:T(8,128)(2,1)S(1)} %copy-done.4, s32[8,128]{1,0:T(8,128)S(1)} %bitcast.17, s32[8,128]{1,0:T(8,128)S(1)} %bitcast.18, ...), custom_call_target="tpu_custom_call" | custom-call | flops 2147483648 | bytes 4194304 | tf_op jit(solution)/shard_map/early/pallas_call | solution.py:257
  38.1 0.0 collective-permute-done.12
  38.1 0.0 collective-permute-done.11
  38.1 0.0 collective-permute-done.10
  38.2 1.4 %collective-permute-start.13 = (bf16[768,512]{1,0:T(8,128)(2,1)S(1)}, bf16[768,512]{1,0:T(8,128)(2,1)S(1)}, u32[]{:S(2)}, u32[]{:S(2)}) collective-permute-start(bf16[768,512]{1,0:T(8,128)(2,1)S(1)} %constant_dynamic-update-slice_fusion.table_ref), channel_id=1, source_target_pairs={{0,1},{1,0},{2,3},{3,2},{4,5},{5,4},{6,7},{7,6},{8,9},{9,8},{10,11... | collective-permute-start | bytes 2359304 | tf_op jit(solution)/shard_map/ppermute | solution.py:315
  39.6 1.9 %gather.1 = (bf16[1024,512]{1,0:T(8,128)(2,1)S(1)}, bf16[1024,512]{1,0:T(8,128)(2,1)S(1)}, bf16[512,512]{1,0:T(8,128)(2,1)}) custom-call(s32[8,128]{1,0:T(8,128)S(1)} %get-tuple-element.101.send_ref, s32[8,128]{1,0:T(8,128)S(1)} %get-tuple-element.102.recv_ref, bf16[1024,512]{1,0:T(8,128)(2,1)S(1)} %get-tuple-element.106.send_part, ...), custom_call_target="tpu_custom_call" | custom-call | flops 2147483648 | bytes 4194304 | tf_op jit(solution)/shard_map/gather/pallas_call | solution.py:257
  41.5 0.0 collective-permute-done.13.table_ref
  41.5 4.4 %coarse.1 = (bf16[1024,512]{1,0:T(8,128)(2,1)S(1)}, bf16[256,512]{1,0:T(8,128)(2,1)S(1)}) custom-call(bf16[1024,512]{1,0:T(8,128)(2,1)S(1)} %copy-done.4, f32[1024,512]{1,0:T(8,128)S(1)} %get-tuple-element.100.pre_ref, s32[8,128]{1,0:T(8,128)S(1)} %get-tuple-element.101.send_ref, s32[8,128]{1,0:T(8,128)S(1)} %get-tuple-element.102.recv_ref, ...), custom_call_target="tpu_custom_call" | custom-call | flops 4294967296 | bytes 4194304 | tf_op jit(solution)/shard_map/coarse/pallas_call | solution.py:257
  46.0 12.7 %all_to_all.5 = bf16[32,8,512]{2,1,0:T(8,128)(2,1)S(1)} all-to-all(bf16[32,8,512]{2,1,0:T(8,128)(2,1)S(1)} %bitcast.10), channel_id=1, replica_groups=mesh['group'=8,'patch'=32] {'patch'}, dimensions={0} | all-to-all | bytes 524288 | tf_op jit(solution)/shard_map/all_to_all | solution.py:389
  58.7 1.2 %tail.1 = (bf16[512,512]{1,0:T(8,128)(2,1)}, bf16[1024,512]{1,0:T(8,128)(2,1)}) custom-call(bf16[512,512]{1,0:T(8,128)(2,1)S(1)} %get-tuple-element.72.node_ref, f32[16,512]{1,0:T(8,128)S(1)} %get-tuple-element.96.sum_ref, f32[16,512]{1,0:T(8,128)S(1)} %get-tuple-element.97.pre_ref, bf16[256,512]{1,0:T(8,128)(2,1)S(1)} %bitcast.9, ...), custom_call_target="tpu_custom_call", output_to_operand_aliasing={{0}: (8, {})} | custom-call | flops 25165824 | bytes 4194304 | tf_op jit(solution)/shard_map/tail/pallas_call | solution.py:257
  (6 shorter events, 0.1 us)
Async XLA Ops:
  1.3 4.7 %collective-permute-start = (bf16[8,512]{1,0:T(8,128)(2,1)S(1)}, bf16[8,512]{1,0:T(8,128)(2,1)S(1)}, u32[]{:S(2)}, u32[]{:S(2)}) collective-permute-start(bf16[8,512]{1,0:T(8,128)(2,1)S(1)} %slice.3), channel_id=1, source_target_pairs={{0,33},{1,32},{2,35},{3,34},{4,37},{5,36},{6,39},{7,38},{8,41},{9,... | collective-permute-start | bytes 24584 | tf_op jit(solution)/shard_map/ppermute | solution.py:324
  6.0 16.1 %copy-start.3 = (bf16[1024,512]{1,0:T(8,128)(2,1)S(1)}, bf16[1024,512]{1,0:T(8,128)(2,1)}, u32[]{:S(2)}) copy-start(bf16[1024,512]{1,0:T(8,128)(2,1)} %edge_ref.5) | copy-start | bytes 3145732
  6.0 16.1 %copy-start.5 = (bf16[512,512]{1,0:T(8,128)(2,1)S(1)}, bf16[512,512]{1,0:T(8,128)(2,1)}, u32[]{:S(2)}) copy-start(bf16[512,512]{1,0:T(8,128)(2,1)} %w_out_ref.8) | copy-start | bytes 1572868
  6.0 16.1 %copy-start.6 = (s32[1024]{0:T(1024)S(1)}, s32[1024]{0:T(1024)}, u32[]{:S(2)}) copy-start(s32[1024]{0:T(1024)} %param.16) | copy-start | bytes 12292
  6.0 16.1 %copy-start.7 = (s32[1024]{0:T(1024)S(1)}, s32[1024]{0:T(1024)}, u32[]{:S(2)}) copy-start(s32[1024]{0:T(1024)} %param.17) | copy-start | bytes 12292
  6.1 16.1 %copy-start.10 = (f32[512]{0:T(512)S(1)}, f32[512]{0:T(512)}, u32[]{:S(2)}) copy-start(f32[512]{0:T(512)} %param.24) | copy-start | bytes 6148
  6.1 12.2 %collective-permute-start.3 = (bf16[16,512]{1,0:T(8,128)(2,1)S(1)}, bf16[16,512]{1,0:T(8,128)(2,1)S(1)}, u32[]{:S(2)}, u32[]{:S(2)}) collective-permute-start(bf16[16,512]{1,0:T(8,128)(2,1)S(1)} %pad_maximum_fusion.2), channel_id=1, source_target_pairs={{0,161},{1,160},{2,163},{3,162},{4,165},{5,164},{6,167},{7,166},{8... | collective-permute-start | bytes 49160 | tf_op jit(solution)/shard_map/ppermute | solution.py:334
  12.5 5.9 %collective-permute-start.2 = (bf16[16,512]{1,0:T(8,128)(2,1)S(1)}, bf16[16,512]{1,0:T(8,128)(2,1)S(1)}, u32[]{:S(2)}, u32[]{:S(2)}) collective-permute-start(bf16[16,512]{1,0:T(8,128)(2,1)S(1)} %pad_maximum_fusion.2), channel_id=1, source_target_pairs={{0,193},{1,192},{2,195},{3,194},{4,197},{5,196},{6,199},{7,198},{8... | collective-permute-start | bytes 49160 | tf_op jit(solution)/shard_map/ppermute | solution.py:334
  12.7 5.6 %collective-permute-start.1 = (bf16[16,512]{1,0:T(8,128)(2,1)S(1)}, bf16[16,512]{1,0:T(8,128)(2,1)S(1)}, u32[]{:S(2)}, u32[]{:S(2)}) collective-permute-start(bf16[16,512]{1,0:T(8,128)(2,1)S(1)} %pad_maximum_fusion.2), channel_id=1, source_target_pairs={{0,225},{1,224},{2,227},{3,226},{4,229},{5,228},{6,231},{7,230},{8... | collective-permute-start | bytes 49160 | tf_op jit(solution)/shard_map/ppermute | solution.py:334
  15.9 6.2 %collective-permute-start.7 = (bf16[128,512]{1,0:T(8,128)(2,1)S(1)}, bf16[128,512]{1,0:T(8,128)(2,1)S(1)}, u32[]{:S(2)}, u32[]{:S(2)}) collective-permute-start(bf16[128,512]{1,0:T(8,128)(2,1)S(1)} %get-tuple-element.81), channel_id=1, source_target_pairs={{0,1},{1,0},{2,3},{3,2},{4,5},{5,4},{6,7},{7,6},{8,9},{9,8},{10,11... | collective-permute-start | bytes 393224 | tf_op jit(solution)/shard_map/ppermute | solution.py:315
  16.0 6.2 %collective-permute-start.8 = (bf16[128,512]{1,0:T(8,128)(2,1)S(1)}, bf16[128,512]{1,0:T(8,128)(2,1)S(1)}, u32[]{:S(2)}, u32[]{:S(2)}) collective-permute-start(bf16[128,512]{1,0:T(8,128)(2,1)S(1)} %get-tuple-element.82), channel_id=1, source_target_pairs={{0,31},{1,2},{2,1},{3,4},{4,3},{5,6},{6,5},{7,8},{8,7},{9,10},{10,... | collective-permute-start | bytes 393224 | tf_op jit(solution)/shard_map/ppermute | solution.py:315
  18.3 6.1 %collective-permute-start.6 = (bf16[64,512]{1,0:T(8,128)(2,1)S(1)}, bf16[64,512]{1,0:T(8,128)(2,1)S(1)}, u32[]{:S(2)}, u32[]{:S(2)}) collective-permute-start(bf16[64,512]{1,0:T(8,128)(2,1)S(1)} %pad_maximum_fusion.1), channel_id=1, source_target_pairs={{0,16},{1,5},{2,18},{3,7},{4,20},{5,1},{6,22},{7,3},{8,24},{9,13},... | collective-permute-start | bytes 196616 | tf_op jit(solution)/shard_map/ppermute | solution.py:315
  21.1 4.3 %collective-permute-start.5 = (bf16[64,512]{1,0:T(8,128)(2,1)S(1)}, bf16[64,512]{1,0:T(8,128)(2,1)S(1)}, u32[]{:S(2)}, u32[]{:S(2)}) collective-permute-start(bf16[64,512]{1,0:T(8,128)(2,1)S(1)} %pad_maximum_fusion.1), channel_id=1, source_target_pairs={{0,24},{1,7},{2,26},{3,5},{4,28},{5,3},{6,30},{7,1},{8,16},{9,15},... | collective-permute-start | bytes 196616 | tf_op jit(solution)/shard_map/ppermute | solution.py:315
  22.1 3.3 %collective-permute-start.4 = (bf16[64,512]{1,0:T(8,128)(2,1)S(1)}, bf16[64,512]{1,0:T(8,128)(2,1)S(1)}, u32[]{:S(2)}, u32[]{:S(2)}) collective-permute-start(bf16[64,512]{1,0:T(8,128)(2,1)S(1)} %pad_maximum_fusion.1), channel_id=1, source_target_pairs={{0,8},{1,3},{2,10},{3,1},{4,12},{5,7},{6,14},{7,5},{8,0},{9,11},{1... | collective-permute-start | bytes 196616 | tf_op jit(solution)/shard_map/ppermute | solution.py:315
  25.4 12.7 %collective-permute-start.12 = (bf16[256,512]{1,0:T(8,128)(2,1)S(1)}, bf16[256,512]{1,0:T(8,128)(2,1)S(1)}, u32[]{:S(2)}, u32[]{:S(2)}) collective-permute-start(bf16[256,512]{1,0:T(8,128)(2,1)S(1)} %pad_maximum_fusion.mine_ref), channel_id=1, source_target_pairs={{0,4},{1,17},{2,6},{3,19},{4,0},{5,21},{6,2},{7,23},{8,12},{9,25},... | collective-permute-start | bytes 786440 | tf_op jit(solution)/shard_map/ppermute | solution.py:315
  28.2 9.9 %collective-permute-start.11 = (bf16[256,512]{1,0:T(8,128)(2,1)S(1)}, bf16[256,512]{1,0:T(8,128)(2,1)S(1)}, u32[]{:S(2)}, u32[]{:S(2)}) collective-permute-start(bf16[256,512]{1,0:T(8,128)(2,1)S(1)} %pad_maximum_fusion.mine_ref), channel_id=1, source_target_pairs={{0,6},{1,25},{2,4},{3,27},{4,2},{5,29},{6,0},{7,31},{8,14},{9,17},... | collective-permute-start | bytes 786440 | tf_op jit(solution)/shard_map/ppermute | solution.py:315
  29.2 8.9 %collective-permute-start.10 = (bf16[256,512]{1,0:T(8,128)(2,1)S(1)}, bf16[256,512]{1,0:T(8,128)(2,1)S(1)}, u32[]{:S(2)}, u32[]{:S(2)}) collective-permute-start(bf16[256,512]{1,0:T(8,128)(2,1)S(1)} %pad_maximum_fusion.mine_ref), channel_id=1, source_target_pairs={{0,2},{1,9},{2,0},{3,11},{4,6},{5,13},{6,4},{7,15},{8,10},{9,1},{1... | collective-permute-start | bytes 786440 | tf_op jit(solution)/shard_map/ppermute | solution.py:315
  29.3 7.0 %collective-permute-start.9 = (bf16[256,512]{1,0:T(8,128)(2,1)S(1)}, bf16[256,512]{1,0:T(8,128)(2,1)S(1)}, u32[]{:S(2)}, u32[]{:S(2)}) collective-permute-start(bf16[256,512]{1,0:T(8,128)(2,1)S(1)} %pad_maximum_fusion.mine_ref), channel_id=1, source_target_pairs={{0,1},{1,0},{2,3},{3,2},{4,5},{5,4},{6,7},{7,6},{8,9},{9,8},{10,11... | collective-permute-start | bytes 786440 | tf_op jit(solution)/shard_map/ppermute | solution.py:315
  32.2 2.6 %copy-start = (bf16[1024,512]{1,0:T(8,128)(2,1)S(1)}, bf16[1024,512]{1,0:T(8,128)(2,1)}, u32[]{:S(2)}) copy-start(bf16[1024,512]{1,0:T(8,128)(2,1)} %w_in_ref.3) | copy-start | bytes 3145732
  32.2 2.6 %copy-start.1 = (bf16[512,512]{1,0:T(8,128)(2,1)S(1)}, bf16[512,512]{1,0:T(8,128)(2,1)}, u32[]{:S(2)}) copy-start(bf16[512,512]{1,0:T(8,128)(2,1)} %w_out_ref.9) | copy-start | bytes 1572868
  32.2 2.6 %copy-start.2 = (f32[512]{0:T(512)S(1)}, f32[512]{0:T(512)}, u32[]{:S(2)}) copy-start(f32[512]{0:T(512)} %param.27) | copy-start | bytes 6148
  34.9 1.4 %copy-start.4 = (bf16[1024,512]{1,0:T(8,128)(2,1)S(1)}, bf16[1024,512]{1,0:T(8,128)(2,1)}, u32[]{:S(2)}) copy-start(bf16[1024,512]{1,0:T(8,128)(2,1)} %edge_ref.7) | copy-start | bytes 3145732
  34.9 1.4 %copy-start.8 = (s32[1024]{0:T(1024)S(1)}, s32[1024]{0:T(1024)}, u32[]{:S(2)}) copy-start(s32[1024]{0:T(1024)} %param.20) | copy-start | bytes 12292
  34.9 1.4 %copy-start.9 = (s32[1024]{0:T(1024)S(1)}, s32[1024]{0:T(1024)}, u32[]{:S(2)}) copy-start(s32[1024]{0:T(1024)} %param.21) | copy-start | bytes 12292
  38.2 3.3 %collective-permute-start.13 = (bf16[768,512]{1,0:T(8,128)(2,1)S(1)}, bf16[768,512]{1,0:T(8,128)(2,1)S(1)}, u32[]{:S(2)}, u32[]{:S(2)}) collective-permute-start(bf16[768,512]{1,0:T(8,128)(2,1)S(1)} %constant_dynamic-update-slice_fusion.table_ref), channel_id=1, source_target_pairs={{0,1},{1,0},{2,3},{3,2},{4,5},{5,4},{6,7},{7,6},{8,9},{9,8},{10,11... | collective-permute-start | bytes 2359304 | tf_op jit(solution)/shard_map/ppermute | solution.py:315

commit v8 on v7

--- a/solution.py
+++ b/solution.py
@@ -213,8 +213,9 @@
 
 
 def node_kernel(
-    node_ref, sum_ref, w_in_ref, w_out_ref, gain_ref, edge_rows, _, out_ref, first_ref, pre_ref,
-    new_ref, sem,
+    node_ref, sum_ref, w_in_ref, w_out_ref, gain_ref, edge_rows, coarse_ref, send_ref, recv_ref,
+    mine_ref, theirs_ref, w_edge_ref, _, out_ref, first_ref, pre_ref, send_place, recv_place,
+    send_out, recv_out, edge_pre_ref, new_ref, table_ref, sem,
 ):
     copy = put_rows(edge_rows, new_ref, HALF, sem)
     nodes = node_ref[...]
@@ -222,6 +223,10 @@
     pre_ref[...] = pre[:TAIL]
     first_ref[...] = sum_ref[:TAIL]
     pre = pre + dot(sum_ref[...].astype(BF), w_in_ref[D:])
+    early_kernel(
+        coarse_ref, send_ref, recv_ref, mine_ref, theirs_ref, w_edge_ref, send_place, recv_place,
+        send_out, recv_out, edge_pre_ref, table_ref,
+    )
     out_ref[...] = finish_nodes(pre, nodes, w_out_ref, gain_ref[...])
     copy.wait()
 
@@ -331,16 +336,16 @@
     pair, inner, outer, nodes, w_in = tie(pair, inner, outer, nodes, w_in)
     near = join(own, pair)
     near, inner, outer, nodes = tie(near, inner, outer, nodes)
-    others = [lax.ppermute(near, ("group", "patch"), to) for to in (Z_NEAR, Z_MID, Z_FAR)]
+    others = [lax.ppermute(near, ("group", "patch"), to) for to in (Z_FAR, Z_MID, Z_NEAR)]
     inner, outer = swap(inner, SWAP_CORE), swap(outer, OUTER)
     (table,) = call(
         project_kernel, (shape(2 * NODES),), 4 * 512 * 512 * 512, nodes, w_in, name="project"
     )
     *others, table = tie(*others, table)
-    block = join(near, others[0], others[1], others[2])
+    block = join(near, *others[::-1])
 
     block, table = tie(block, table)
-    others = [swap(block, crossed(k, 0)) for k in (1, 3, 2)]
+    others = [swap(block, crossed(k, 0)) for k in (2, 3, 1)]
     fine_args = (
         fine_edge_lat, grid(fine_send), grid(fine_recv), table, inner, outer, w_in, w_edge_out, edge_gain
     )
@@ -349,30 +354,33 @@
         2 << 30, *fine_args, name="fine_first",
     )
     *others, fine_sum = tie(*others, fine_sum)
-    block = join(block, others[0], others[1], others[2])
+    block = join(block, *others[::-1])
 
     block, fine_sum = tie(block, fine_sum)
-    others = [swap(block, crossed(k, 1)) for k in (1, 3, 2)]
+    others = [swap(block, crossed(k, 1)) for k in (2, 3, 1)]
     other_block = swap(block, SWAP_CORE)
     rows, fine_sum, fine_new = call(
         functools.partial(fine_kernel, HALF), (shape(HALF), shape(NODES, F32), shape(EDGES)),
         2 << 30, *fine_args, halo, fine_sum, rows, name="fine_second",
         scratch=[pltpu.SemaphoreType.DMA], out_any=(2,),
     )
-    node_rows, first_sum, first_pre, fine_new = call(
-        node_kernel, (shape(NODES), shape(TAIL, F32), shape(TAIL, F32), shape(EDGES)), 768 << 20,
-        nodes, fine_sum, w_node_in, w_node_out, node_gain, rows, fine_new, name="node",
-        scratch=[pltpu.SemaphoreType.DMA], out_any=(3,), in_any=(6,), aliases={6: 3},
-    )
-    other_block, first_sum = tie(other_block, first_sum)
     ids = jax.ShapeDtypeStruct((EDGES // 128, 128), jnp.int32)
-    send_place, recv_place, send_part, recv_part, pre = call(
-        early_kernel, (ids, ids, shape(EDGES), shape(EDGES), shape(EDGES, F32)), 2 << 30,
-        coarse_edge_lat, grid(coarse_send), grid(coarse_recv), block, other_block, w_in,
-        name="early", scratch=[pltpu.VMEM((2 * EARLY, D), BF)],
+    (
+        node_rows, first_sum, first_pre, send_place, recv_place, send_part, recv_part, pre,
+        fine_new,
+    ) = call(
+        node_kernel,
+        (
+            shape(NODES), shape(TAIL, F32), shape(TAIL, F32), ids, ids, shape(EDGES),
+            shape(EDGES), shape(EDGES, F32), shape(EDGES),
+        ),
+        3 << 30, nodes, fine_sum, w_node_in, w_node_out, node_gain, rows, coarse_edge_lat,
+        grid(coarse_send), grid(coarse_recv), block, other_block, w_in, fine_new, name="node",
+        scratch=[pltpu.VMEM((2 * EARLY, D), BF), pltpu.SemaphoreType.DMA], out_any=(8,),
+        in_any=(12,), aliases={12: 8},
     )
     *others, pre = tie(*others, pre)
-    part = join(others[0], others[1], others[2])
+    part = join(*others[::-1])
     other_part = swap(part, SWAP_CORE)
     send_part, recv_part, node_new = call(
         gather_kernel, (shape(EDGES), shape(EDGES), shape(NODES)), 2 << 30, send_place,

time: 60.2 us -> 61 us (1.013)
  blocking collectives: 12.7 us -> 13.5 us
  waiting for transfers between devices: 1.04 us -> 1.75 us
    ppermute x10, waiting for transfers between devices: 1.02 us -> 1.74 us  [shards(): swap = lambda rows, pairs: lax.ppermute(rows, 'patch', pairs)]
    all_to_all x1, blocking collectives: 12.7 us -> 13.5 us  [shards(): parts = lax.all_to_all(sums.reshape(PATCHES, COARSE_ROWS, D), 'patch', 0, 0)]
    pallas_call x9 -> x8, Pallas kernels: 17.7 us -> 17.5 us  [call(): pl.pallas_call(kernel, out_shape=outs, in_specs=[spec if at in in_any els...]
  transfers between devices with their start and end apart: 14 -> 14, of which waited for: 1 -> 2; matrix products, arithmetic and copies ran while one was open for 0% -> 0% of each run, Pallas kernels for 20% -> 20%
where the time goes in v8:
time: 61 us; the launch traced here: 60.8 us
  starting transfers between devices  26.1 us (43%)
  Pallas kernels  17.5 us (29%)
  blocking collectives  13.5 us (22%)
  waiting for transfers between devices  1.75 us (3%)
  between operations  1.11 us (2%)
  local copies, waits for them, and re-layouts  0.82 us (1%)
    pallas_call x8, Pallas kernels, call(): pl.pallas_call(kernel, out_shape=outs, in_specs=[spec if at in in_any els...  17.5 us
    all_to_all x1, blocking collectives, shards(): parts = lax.all_to_all(sums.reshape(PATCHES, COARSE_ROWS, D), 'patch', 0, 0)  13.5 us
    ppermute x10, starting transfers between devices, shards(): swap = lambda rows, pairs: lax.ppermute(rows, 'patch', pairs)  13.2 us
    ppermute x3, starting transfers between devices, shards(): lax.ppermute(near, ('group', 'patch'), to)  9.83 us
    ppermute x1, starting transfers between devices, shards(): pair = lax.ppermute(own, ('group', 'patch'), Z_PAIR)  3.03 us
    ppermute x10, waiting for transfers between devices, shards(): swap = lambda rows, pairs: lax.ppermute(rows, 'patch', pairs)  1.74 us
  transfers between devices with their start and end apart: 14, of which 2 were waited for; matrix products, arithmetic and copies ran while one was open for 0% of the time, Pallas kernels for 20%

profile of v8, /device:TPU:1, one launch (start us, length us, event | category | flops | bytes accessed | tf_op | source)
XLA Modules:
  0.0 60.8 jit_solution(11429263292215729597)
XLA Ops:
  0.6 0.7 %slice.3 = bf16[8,512]{1,0:T(8,128)(2,1)S(1)} slice(bf16[512,512]{1,0:T(8,128)(2,1)} %node_in), slice={[0:8], [0:512]} | slice | bytes 16384 | tf_op jit(solution)/shard_map/slice | solution.py:326
  1.3 3.0 %collective-permute-start = (bf16[8,512]{1,0:T(8,128)(2,1)S(1)}, bf16[8,512]{1,0:T(8,128)(2,1)S(1)}, u32[]{:S(2)}, u32[]{:S(2)}) collective-permute-start(bf16[8,512]{1,0:T(8,128)(2,1)S(1)} %slice.3), channel_id=1, source_target_pairs={{0,33},{1,32},{2,35},{3,34},{4,37},{5,36},{6,39},{7,38},{8,41},{9,... | collective-permute-start | bytes 24584 | tf_op jit(solution)/shard_map/ppermute | solution.py:329
  4.4 1.6 %pick.1 = (bf16[128,512]{1,0:T(8,128)(2,1)S(1)}, bf16[128,512]{1,0:T(8,128)(2,1)S(1)}, bf16[512,512]{1,0:T(8,128)(2,1)S(1)}, bf16[1536,512]{1,0:T(8,128)(2,1)S(1)}) custom-call(s32[2,128]{1,0:T(2,128)} %bitcast.23, bf16[512,512]{1,0:T(8,128)(2,1)} %node_in, bf16[1536,512]{1,0:T(8,128)(2,1)} %w_in), custom_call_target="tpu_custom_call" | custom-call | flops 134217728 | bytes 4194304 | tf_op jit(solution)/shard_map/pick/pallas_call | solution.py:262
  6.0 0.0 collective-permute-done
  6.0 0.0 copy-start.3
  6.0 0.0 copy-start.5
  6.0 0.0 copy-start.6
  6.0 0.0 copy-start.7
  6.1 0.0 copy-start.10
  6.1 6.4 %collective-permute-start.1 = (bf16[16,512]{1,0:T(8,128)(2,1)S(1)}, bf16[16,512]{1,0:T(8,128)(2,1)S(1)}, u32[]{:S(2)}, u32[]{:S(2)}) collective-permute-start(bf16[16,512]{1,0:T(8,128)(2,1)S(1)} %pad_maximum_fusion.2), channel_id=1, source_target_pairs={{0,161},{1,160},{2,163},{3,162},{4,165},{5,164},{6,167},{7,166},{8... | collective-permute-start | bytes 49160 | tf_op jit(solution)/shard_map/ppermute | solution.py:339
  12.5 0.3 collective-permute-start.2
  12.7 3.2 %collective-permute-start.3 = (bf16[16,512]{1,0:T(8,128)(2,1)S(1)}, bf16[16,512]{1,0:T(8,128)(2,1)S(1)}, u32[]{:S(2)}, u32[]{:S(2)}) collective-permute-start(bf16[16,512]{1,0:T(8,128)(2,1)S(1)} %pad_maximum_fusion.2), channel_id=1, source_target_pairs={{0,225},{1,224},{2,227},{3,226},{4,229},{5,228},{6,231},{7,230},{8... | collective-permute-start | bytes 49160 | tf_op jit(solution)/shard_map/ppermute | solution.py:339
  15.9 0.1 collective-permute-start.4
  16.0 1.6 %collective-permute-start.5 = (bf16[128,512]{1,0:T(8,128)(2,1)S(1)}, bf16[128,512]{1,0:T(8,128)(2,1)S(1)}, u32[]{:S(2)}, u32[]{:S(2)}) collective-permute-start(bf16[128,512]{1,0:T(8,128)(2,1)S(1)} %get-tuple-element.79), channel_id=1, source_target_pairs={{0,31},{1,2},{2,1},{3,4},{4,3},{5,6},{6,5},{7,8},{8,7},{9,10},{10,... | collective-permute-start | bytes 393224 | tf_op jit(solution)/shard_map/ppermute | solution.py:320
  17.6 0.7 %project.1.table_ref = bf16[1024,512]{1,0:T(8,128)(2,1)S(1)} custom-call(bf16[512,512]{1,0:T(8,128)(2,1)S(1)} %get-tuple-element.70.node_ref, bf16[1536,512]{1,0:T(8,128)(2,1)S(1)} %get-tuple-element.72.w_ref.w_in_ref.w_edge_ref), custom_call_target="tpu_custom_call" | custom-call | flops 536870912 | bytes 4194304 | tf_op jit(solution)/shard_map/project/pallas_call | solution.py:262
  18.3 0.0 collective-permute-done.1
  18.3 0.0 collective-permute-done.2
  18.3 0.0 collective-permute-done.3
  18.3 2.7 %collective-permute-start.6 = (bf16[64,512]{1,0:T(8,128)(2,1)S(1)}, bf16[64,512]{1,0:T(8,128)(2,1)S(1)}, u32[]{:S(2)}, u32[]{:S(2)}) collective-permute-start(bf16[64,512]{1,0:T(8,128)(2,1)S(1)} %pad_maximum_fusion.1), channel_id=1, source_target_pairs={{0,16},{1,5},{2,18},{3,7},{4,20},{5,1},{6,22},{7,3},{8,24},{9,13},... | collective-permute-start | bytes 196616 | tf_op jit(solution)/shard_map/ppermute | solution.py:320
  21.1 1.1 %collective-permute-start.7 = (bf16[64,512]{1,0:T(8,128)(2,1)S(1)}, bf16[64,512]{1,0:T(8,128)(2,1)S(1)}, u32[]{:S(2)}, u32[]{:S(2)}) collective-permute-start(bf16[64,512]{1,0:T(8,128)(2,1)S(1)} %pad_maximum_fusion.1), channel_id=1, source_target_pairs={{0,24},{1,7},{2,26},{3,5},{4,28},{5,3},{6,30},{7,1},{8,16},{9,15},... | collective-permute-start | bytes 196616 | tf_op jit(solution)/shard_map/ppermute | solution.py:320
  22.1 0.0 collective-permute-start.8
  22.1 0.0 collective-permute-done.4.inner_ref
  22.1 0.0 collective-permute-done.5.outer_ref
  22.1 0.0 copy-done.3
  22.1 0.0 copy-done.5
  22.2 0.0 copy-done.6
  22.2 0.0 copy-done.7
  22.2 0.0 copy-done.10
  22.2 2.2 %fine_first.1 = (bf16[512,512]{1,0:T(8,128)(2,1)S(1)}, f32[512,512]{1,0:T(8,128)S(1)}, bf16[256,512]{1,0:T(8,128)(2,1)S(1)}) custom-call(bf16[1024,512]{1,0:T(8,128)(2,1)S(1)} %copy-done.3, s32[8,128]{1,0:T(8,128)S(1)} %bitcast.13, s32[8,128]{1,0:T(8,128)S(1)} %bitcast.15, bf16[1024,512]{1,0:T(8,128)(2,1)S(1)} %project.1.table_ref, ...), custom_call_target="tpu_custom_call" | custom-call | flops 2147483648 | bytes 4194304 | tf_op jit(solution)/shard_map/fine_first/pallas_call | solution.py:262
  24.4 0.0 collective-permute-done.6
  24.4 1.0 %collective-permute-done.7 = bf16[64,512]{1,0:T(8,128)(2,1)S(1)} collective-permute-done((bf16[64,512]{1,0:T(8,128)(2,1)S(1)}, bf16[64,512]{1,0:T(8,128)(2,1)S(1)}, u32[]{:S(2)}, u32[]{:S(2)}) %collective-permute-start.7) | collective-permute-done | bytes 65568 | tf_op jit(solution)/shard_map/ppermute | solution.py:320
  25.4 0.0 collective-permute-done.8
  25.4 3.3 %collective-permute-start.9 = (bf16[256,512]{1,0:T(8,128)(2,1)S(1)}, bf16[256,512]{1,0:T(8,128)(2,1)S(1)}, u32[]{:S(2)}, u32[]{:S(2)}) collective-permute-start(bf16[256,512]{1,0:T(8,128)(2,1)S(1)} %pad_maximum_fusion.mine_ref), channel_id=1, source_target_pairs={{0,1},{1,0},{2,3},{3,2},{4,5},{5,4},{6,7},{7,6},{8,9},{9,8},{10,11... | collective-permute-start | bytes 786440 | tf_op jit(solution)/shard_map/ppermute | solution.py:320
  28.7 1.3 %collective-permute-start.10 = (bf16[256,512]{1,0:T(8,128)(2,1)S(1)}, bf16[256,512]{1,0:T(8,128)(2,1)S(1)}, u32[]{:S(2)}, u32[]{:S(2)}) collective-permute-start(bf16[256,512]{1,0:T(8,128)(2,1)S(1)} %pad_maximum_fusion.mine_ref), channel_id=1, source_target_pairs={{0,4},{1,17},{2,6},{3,19},{4,0},{5,21},{6,2},{7,23},{8,12},{9,25},... | collective-permute-start | bytes 786440 | tf_op jit(solution)/shard_map/ppermute | solution.py:320
  30.0 2.1 %collective-permute-start.11 = (bf16[256,512]{1,0:T(8,128)(2,1)S(1)}, bf16[256,512]{1,0:T(8,128)(2,1)S(1)}, u32[]{:S(2)}, u32[]{:S(2)}) collective-permute-start(bf16[256,512]{1,0:T(8,128)(2,1)S(1)} %pad_maximum_fusion.mine_ref), channel_id=1, source_target_pairs={{0,6},{1,25},{2,4},{3,27},{4,2},{5,29},{6,0},{7,31},{8,14},{9,17},... | collective-permute-start | bytes 786440 | tf_op jit(solution)/shard_map/ppermute | solution.py:320
  32.1 0.0 collective-permute-start.12
  32.1 0.0 copy-start
  32.1 0.0 copy-start.1
  32.1 0.0 copy-start.2
  32.1 0.0 copy-start.4
  32.2 0.0 copy-start.8
  32.2 0.0 copy-start.9
  32.2 2.6 %fine_second.1 = (bf16[512,512]{1,0:T(8,128)(2,1)S(1)}, f32[512,512]{1,0:T(8,128)S(1)}, bf16[1024,512]{1,0:T(8,128)(2,1)}) custom-call(bf16[1024,512]{1,0:T(8,128)(2,1)S(1)} %copy-done.3, s32[8,128]{1,0:T(8,128)S(1)} %bitcast.14, s32[8,128]{1,0:T(8,128)S(1)} %bitcast.16, bf16[1024,512]{1,0:T(8,128)(2,1)S(1)} %project.1.table_ref, ...), custom_call_target="tpu_custom_call" | custom-call | flops 2147483648 | bytes 4194304 | tf_op jit(solution)/shard_map/fine_second/pallas_call | solution.py:262
  34.8 0.0 collective-permute-done.9.theirs_ref
  34.8 0.0 copy-done
  34.8 0.0 copy-done.1
  34.8 0.0 copy-done.2
  34.8 0.0 copy-done.4
  34.8 0.0 copy-done.8
  34.8 0.0 copy-done.9
  34.8 3.0 %node.1 = (bf16[512,512]{1,0:T(8,128)(2,1)S(1)}, f32[16,512]{1,0:T(8,128)S(1)}, f32[16,512]{1,0:T(8,128)S(1)}, s32[8,128]{1,0:T(8,128)S(1)}, s32[8,128]{1,0:T(8,...) custom-call(bf16[512,512]{1,0:T(8,128)(2,1)S(1)} %get-tuple-element., ...), custom_call_target="tpu_custom_call", output_to_operand_aliasing={{8}: (12, {})} | custom-call | flops 3221225472 | bytes 4194304 | tf_op jit(solution)/shard_map/node/pallas_call | solution.py:262
  37.8 0.0 collective-permute-done.10
  37.8 0.7 %collective-permute-done.11 = bf16[256,512]{1,0:T(8,128)(2,1)S(1)} collective-permute-done((bf16[256,512]{1,0:T(8,128)(2,1)S(1)}, bf16[256,512]{1,0:T(8,128)(2,1)S(1)}, u32[]{:S(2)}, u32[]{:S(2)}) %collective-permute-start.11) | collective-permute-done | bytes 262176 | tf_op jit(solution)/shard_map/ppermute | solution.py:320
  38.6 0.0 collective-permute-done.12
  38.6 1.0 %collective-permute-start.13 = (bf16[768,512]{1,0:T(8,128)(2,1)S(1)}, bf16[768,512]{1,0:T(8,128)(2,1)S(1)}, u32[]{:S(2)}, u32[]{:S(2)}) collective-permute-start(bf16[768,512]{1,0:T(8,128)(2,1)S(1)} %constant_dynamic-update-slice_fusion.table_ref), channel_id=1, source_target_pairs={{0,1},{1,0},{2,3},{3,2},{4,5},{5,4},{6,7},{7,6},{8,9},{9,8},{10,11... | collective-permute-start | bytes 2359304 | tf_op jit(solution)/shard_map/ppermute | solution.py:320
  39.7 1.9 %gather.1 = (bf16[1024,512]{1,0:T(8,128)(2,1)S(1)}, bf16[1024,512]{1,0:T(8,128)(2,1)S(1)}, bf16[512,512]{1,0:T(8,128)(2,1)}) custom-call(s32[8,128]{1,0:T(8,128)S(1)} %get-tuple-element.97.send_ref, s32[8,128]{1,0:T(8,128)S(1)} %get-tuple-element.98.recv_ref, bf16[1024,512]{1,0:T(8,128)(2,1)S(1)} %get-tuple-element.102.send_part, ...), custom_call_target="tpu_custom_call" | custom-call | flops 2147483648 | bytes 4194304 | tf_op jit(solution)/shard_map/gather/pallas_call | solution.py:262
  41.6 0.0 collective-permute-done.13.table_ref
  41.6 4.4 %coarse.1 = (bf16[1024,512]{1,0:T(8,128)(2,1)S(1)}, bf16[256,512]{1,0:T(8,128)(2,1)S(1)}) custom-call(bf16[1024,512]{1,0:T(8,128)(2,1)S(1)} %copy-done.4, f32[1024,512]{1,0:T(8,128)S(1)} %get-tuple-element.96.pre_ref, s32[8,128]{1,0:T(8,128)S(1)} %get-tuple-element.97.send_ref, s32[8,128]{1,0:T(8,128)S(1)} %get-tuple-element.98.recv_ref, ...), custom_call_target="tpu_custom_call" | custom-call | flops 4294967296 | bytes 4194304 | tf_op jit(solution)/shard_map/coarse/pallas_call | solution.py:262
  46.0 13.5 %all_to_all.5 = bf16[32,8,512]{2,1,0:T(8,128)(2,1)S(1)} all-to-all(bf16[32,8,512]{2,1,0:T(8,128)(2,1)S(1)} %bitcast.10), channel_id=1, replica_groups=mesh['group'=8,'patch'=32] {'patch'}, dimensions={0} | all-to-all | bytes 524288 | tf_op jit(solution)/shard_map/all_to_all | solution.py:397
  59.5 1.2 %tail.1 = (bf16[512,512]{1,0:T(8,128)(2,1)}, bf16[1024,512]{1,0:T(8,128)(2,1)}) custom-call(bf16[512,512]{1,0:T(8,128)(2,1)S(1)} %get-tuple-element.70.node_ref, f32[16,512]{1,0:T(8,128)S(1)} %get-tuple-element.93.sum_ref, f32[16,512]{1,0:T(8,128)S(1)} %get-tuple-element.94.pre_ref, bf16[256,512]{1,0:T(8,128)(2,1)S(1)} %bitcast.9, ...), custom_call_target="tpu_custom_call", output_to_operand_aliasing={{0}: (8, {})} | custom-call | flops 25165824 | bytes 4194304 | tf_op jit(solution)/shard_map/tail/pallas_call | solution.py:262
  (6 shorter events, 0.1 us)
Async XLA Ops:
  1.3 4.7 %collective-permute-start = (bf16[8,512]{1,0:T(8,128)(2,1)S(1)}, bf16[8,512]{1,0:T(8,128)(2,1)S(1)}, u32[]{:S(2)}, u32[]{:S(2)}) collective-permute-start(bf16[8,512]{1,0:T(8,128)(2,1)S(1)} %slice.3), channel_id=1, source_target_pairs={{0,33},{1,32},{2,35},{3,34},{4,37},{5,36},{6,39},{7,38},{8,41},{9,... | collective-permute-start | bytes 24584 | tf_op jit(solution)/shard_map/ppermute | solution.py:329
  6.0 16.1 %copy-start.3 = (bf16[1024,512]{1,0:T(8,128)(2,1)S(1)}, bf16[1024,512]{1,0:T(8,128)(2,1)}, u32[]{:S(2)}) copy-start(bf16[1024,512]{1,0:T(8,128)(2,1)} %edge_ref.4) | copy-start | bytes 3145732
  6.0 16.1 %copy-start.5 = (bf16[512,512]{1,0:T(8,128)(2,1)S(1)}, bf16[512,512]{1,0:T(8,128)(2,1)}, u32[]{:S(2)}) copy-start(bf16[512,512]{1,0:T(8,128)(2,1)} %w_out_ref.8) | copy-start | bytes 1572868
  6.0 16.1 %copy-start.6 = (s32[1024]{0:T(1024)S(1)}, s32[1024]{0:T(1024)}, u32[]{:S(2)}) copy-start(s32[1024]{0:T(1024)} %param.16) | copy-start | bytes 12292
  6.0 16.1 %copy-start.7 = (s32[1024]{0:T(1024)S(1)}, s32[1024]{0:T(1024)}, u32[]{:S(2)}) copy-start(s32[1024]{0:T(1024)} %param.17) | copy-start | bytes 12292
  6.1 16.1 %copy-start.10 = (f32[512]{0:T(512)S(1)}, f32[512]{0:T(512)}, u32[]{:S(2)}) copy-start(f32[512]{0:T(512)} %param.24) | copy-start | bytes 6148
  6.1 12.2 %collective-permute-start.1 = (bf16[16,512]{1,0:T(8,128)(2,1)S(1)}, bf16[16,512]{1,0:T(8,128)(2,1)S(1)}, u32[]{:S(2)}, u32[]{:S(2)}) collective-permute-start(bf16[16,512]{1,0:T(8,128)(2,1)S(1)} %pad_maximum_fusion.2), channel_id=1, source_target_pairs={{0,161},{1,160},{2,163},{3,162},{4,165},{5,164},{6,167},{7,166},{8... | collective-permute-start | bytes 49160 | tf_op jit(solution)/shard_map/ppermute | solution.py:339
  12.5 5.9 %collective-permute-start.2 = (bf16[16,512]{1,0:T(8,128)(2,1)S(1)}, bf16[16,512]{1,0:T(8,128)(2,1)S(1)}, u32[]{:S(2)}, u32[]{:S(2)}) collective-permute-start(bf16[16,512]{1,0:T(8,128)(2,1)S(1)} %pad_maximum_fusion.2), channel_id=1, source_target_pairs={{0,193},{1,192},{2,195},{3,194},{4,197},{5,196},{6,199},{7,198},{8... | collective-permute-start | bytes 49160 | tf_op jit(solution)/shard_map/ppermute | solution.py:339
  12.7 5.6 %collective-permute-start.3 = (bf16[16,512]{1,0:T(8,128)(2,1)S(1)}, bf16[16,512]{1,0:T(8,128)(2,1)S(1)}, u32[]{:S(2)}, u32[]{:S(2)}) collective-permute-start(bf16[16,512]{1,0:T(8,128)(2,1)S(1)} %pad_maximum_fusion.2), channel_id=1, source_target_pairs={{0,225},{1,224},{2,227},{3,226},{4,229},{5,228},{6,231},{7,230},{8... | collective-permute-start | bytes 49160 | tf_op jit(solution)/shard_map/ppermute | solution.py:339
  15.9 6.2 %collective-permute-start.4 = (bf16[128,512]{1,0:T(8,128)(2,1)S(1)}, bf16[128,512]{1,0:T(8,128)(2,1)S(1)}, u32[]{:S(2)}, u32[]{:S(2)}) collective-permute-start(bf16[128,512]{1,0:T(8,128)(2,1)S(1)} %get-tuple-element.78), channel_id=1, source_target_pairs={{0,1},{1,0},{2,3},{3,2},{4,5},{5,4},{6,7},{7,6},{8,9},{9,8},{10,11... | collective-permute-start | bytes 393224 | tf_op jit(solution)/shard_map/ppermute | solution.py:320
  16.0 6.2 %collective-permute-start.5 = (bf16[128,512]{1,0:T(8,128)(2,1)S(1)}, bf16[128,512]{1,0:T(8,128)(2,1)S(1)}, u32[]{:S(2)}, u32[]{:S(2)}) collective-permute-start(bf16[128,512]{1,0:T(8,128)(2,1)S(1)} %get-tuple-element.79), channel_id=1, source_target_pairs={{0,31},{1,2},{2,1},{3,4},{4,3},{5,6},{6,5},{7,8},{8,7},{9,10},{10,... | collective-permute-start | bytes 393224 | tf_op jit(solution)/shard_map/ppermute | solution.py:320
  18.3 6.1 %collective-permute-start.6 = (bf16[64,512]{1,0:T(8,128)(2,1)S(1)}, bf16[64,512]{1,0:T(8,128)(2,1)S(1)}, u32[]{:S(2)}, u32[]{:S(2)}) collective-permute-start(bf16[64,512]{1,0:T(8,128)(2,1)S(1)} %pad_maximum_fusion.1), channel_id=1, source_target_pairs={{0,16},{1,5},{2,18},{3,7},{4,20},{5,1},{6,22},{7,3},{8,24},{9,13},... | collective-permute-start | bytes 196616 | tf_op jit(solution)/shard_map/ppermute | solution.py:320
  21.1 4.3 %collective-permute-start.7 = (bf16[64,512]{1,0:T(8,128)(2,1)S(1)}, bf16[64,512]{1,0:T(8,128)(2,1)S(1)}, u32[]{:S(2)}, u32[]{:S(2)}) collective-permute-start(bf16[64,512]{1,0:T(8,128)(2,1)S(1)} %pad_maximum_fusion.1), channel_id=1, source_target_pairs={{0,24},{1,7},{2,26},{3,5},{4,28},{5,3},{6,30},{7,1},{8,16},{9,15},... | collective-permute-start | bytes 196616 | tf_op jit(solution)/shard_map/ppermute | solution.py:320
  22.1 3.3 %collective-permute-start.8 = (bf16[64,512]{1,0:T(8,128)(2,1)S(1)}, bf16[64,512]{1,0:T(8,128)(2,1)S(1)}, u32[]{:S(2)}, u32[]{:S(2)}) collective-permute-start(bf16[64,512]{1,0:T(8,128)(2,1)S(1)} %pad_maximum_fusion.1), channel_id=1, source_target_pairs={{0,8},{1,3},{2,10},{3,1},{4,12},{5,7},{6,14},{7,5},{8,0},{9,11},{1... | collective-permute-start | bytes 196616 | tf_op jit(solution)/shard_map/ppermute | solution.py:320
  25.4 9.4 %collective-permute-start.9 = (bf16[256,512]{1,0:T(8,128)(2,1)S(1)}, bf16[256,512]{1,0:T(8,128)(2,1)S(1)}, u32[]{:S(2)}, u32[]{:S(2)}) collective-permute-start(bf16[256,512]{1,0:T(8,128)(2,1)S(1)} %pad_maximum_fusion.mine_ref), channel_id=1, source_target_pairs={{0,1},{1,0},{2,3},{3,2},{4,5},{5,4},{6,7},{7,6},{8,9},{9,8},{10,11... | collective-permute-start | bytes 786440 | tf_op jit(solution)/shard_map/ppermute | solution.py:320
  28.7 9.1 %collective-permute-start.10 = (bf16[256,512]{1,0:T(8,128)(2,1)S(1)}, bf16[256,512]{1,0:T(8,128)(2,1)S(1)}, u32[]{:S(2)}, u32[]{:S(2)}) collective-permute-start(bf16[256,512]{1,0:T(8,128)(2,1)S(1)} %pad_maximum_fusion.mine_ref), channel_id=1, source_target_pairs={{0,4},{1,17},{2,6},{3,19},{4,0},{5,21},{6,2},{7,23},{8,12},{9,25},... | collective-permute-start | bytes 786440 | tf_op jit(solution)/shard_map/ppermute | solution.py:320
  30.0 8.6 %collective-permute-start.11 = (bf16[256,512]{1,0:T(8,128)(2,1)S(1)}, bf16[256,512]{1,0:T(8,128)(2,1)S(1)}, u32[]{:S(2)}, u32[]{:S(2)}) collective-permute-start(bf16[256,512]{1,0:T(8,128)(2,1)S(1)} %pad_maximum_fusion.mine_ref), channel_id=1, source_target_pairs={{0,6},{1,25},{2,4},{3,27},{4,2},{5,29},{6,0},{7,31},{8,14},{9,17},... | collective-permute-start | bytes 786440 | tf_op jit(solution)/shard_map/ppermute | solution.py:320
  32.1 6.4 %collective-permute-start.12 = (bf16[256,512]{1,0:T(8,128)(2,1)S(1)}, bf16[256,512]{1,0:T(8,128)(2,1)S(1)}, u32[]{:S(2)}, u32[]{:S(2)}) collective-permute-start(bf16[256,512]{1,0:T(8,128)(2,1)S(1)} %pad_maximum_fusion.mine_ref), channel_id=1, source_target_pairs={{0,2},{1,9},{2,0},{3,11},{4,6},{5,13},{6,4},{7,15},{8,10},{9,1},{1... | collective-permute-start | bytes 786440 | tf_op jit(solution)/shard_map/ppermute | solution.py:320
  32.1 2.7 %copy-start = (bf16[1024,512]{1,0:T(8,128)(2,1)S(1)}, bf16[1024,512]{1,0:T(8,128)(2,1)}, u32[]{:S(2)}) copy-start(bf16[1024,512]{1,0:T(8,128)(2,1)} %w_in_ref.3) | copy-start | bytes 3145732
  32.1 2.7 %copy-start.1 = (bf16[512,512]{1,0:T(8,128)(2,1)S(1)}, bf16[512,512]{1,0:T(8,128)(2,1)}, u32[]{:S(2)}) copy-start(bf16[512,512]{1,0:T(8,128)(2,1)} %w_out_ref.9) | copy-start | bytes 1572868
  32.1 2.7 %copy-start.2 = (f32[512]{0:T(512)S(1)}, f32[512]{0:T(512)}, u32[]{:S(2)}) copy-start(f32[512]{0:T(512)} %param.27) | copy-start | bytes 6148
  32.1 2.7 %copy-start.4 = (bf16[1024,512]{1,0:T(8,128)(2,1)S(1)}, bf16[1024,512]{1,0:T(8,128)(2,1)}, u32[]{:S(2)}) copy-start(bf16[1024,512]{1,0:T(8,128)(2,1)} %edge_ref.5) | copy-start | bytes 3145732
  32.2 2.7 %copy-start.8 = (s32[1024]{0:T(1024)S(1)}, s32[1024]{0:T(1024)}, u32[]{:S(2)}) copy-start(s32[1024]{0:T(1024)} %param.20) | copy-start | bytes 12292
  32.2 2.7 %copy-start.9 = (s32[1024]{0:T(1024)S(1)}, s32[1024]{0:T(1024)}, u32[]{:S(2)}) copy-start(s32[1024]{0:T(1024)} %param.21) | copy-start | bytes 12292
  38.6 3.0 %collective-permute-start.13 = (bf16[768,512]{1,0:T(8,128)(2,1)S(1)}, bf16[768,512]{1,0:T(8,128)(2,1)S(1)}, u32[]{:S(2)}, u32[]{:S(2)}) collective-permute-start(bf16[768,512]{1,0:T(8,128)(2,1)S(1)} %constant_dynamic-update-slice_fusion.table_ref), channel_id=1, source_target_pairs={{0,1},{1,0},{2,3},{3,2},{4,5},{5,4},{6,7},{7,6},{8,9},{9,8},{10,11... | collective-permute-start | bytes 2359304 | tf_op jit(solution)/shard_map/ppermute | solution.py:320

commit v9 on v7

--- a/solution.py
+++ b/solution.py
@@ -108,7 +108,8 @@
         copy.wait()
 
 
-def project_kernel(node_ref, w_ref, out_ref):
+def project_kernel(node_ref, w_ref, edge_ref, out_ref, edge_pre_ref):
+    edge_pre_ref[...] = dot(edge_ref[...], w_ref[:D])
     nodes = node_ref[...]
     out_ref[:NODES] = dot(nodes, w_ref[2 * D :]).astype(BF)
     out_ref[NODES:] = dot(nodes, w_ref[D : 2 * D]).astype(BF)
@@ -164,12 +165,11 @@
 
 
 def early_kernel(
-    edge_ref, send_ref, recv_ref, mine_ref, theirs_ref, w_in_ref, send_place, recv_place,
-    send_out, recv_out, pre_ref, table_ref,
+    send_ref, recv_ref, mine_ref, theirs_ref, send_place, recv_place, send_out, recv_out,
+    table_ref,
 ):
     table_ref[:EARLY] = mine_ref[...]
     table_ref[EARLY:] = theirs_ref[...]
-    pre_ref[...] = dot(edge_ref[...], w_in_ref[:D])
     for ids_ref, place_ref, out_ref in (
         (send_ref, send_place, send_out), (recv_ref, recv_place, recv_out)
     ):
@@ -333,8 +333,9 @@
     near, inner, outer, nodes = tie(near, inner, outer, nodes)
     others = [lax.ppermute(near, ("group", "patch"), to) for to in (Z_NEAR, Z_MID, Z_FAR)]
     inner, outer = swap(inner, SWAP_CORE), swap(outer, OUTER)
-    (table,) = call(
-        project_kernel, (shape(2 * NODES),), 4 * 512 * 512 * 512, nodes, w_in, name="project"
+    table, pre = call(
+        project_kernel, (shape(2 * NODES), shape(EDGES, F32)), 1 << 30, nodes, w_in,
+        coarse_edge_lat, name="project",
     )
     *others, table = tie(*others, table)
     block = join(near, others[0], others[1], others[2])
@@ -366,12 +367,12 @@
     )
     other_block, first_sum = tie(other_block, first_sum)
     ids = jax.ShapeDtypeStruct((EDGES // 128, 128), jnp.int32)
-    send_place, recv_place, send_part, recv_part, pre = call(
-        early_kernel, (ids, ids, shape(EDGES), shape(EDGES), shape(EDGES, F32)), 2 << 30,
-        coarse_edge_lat, grid(coarse_send), grid(coarse_recv), block, other_block, w_in,
+    send_place, recv_place, send_part, recv_part = call(
+        early_kernel, (ids, ids, shape(EDGES), shape(EDGES)), 2 << 30, grid(coarse_send),
+        grid(coarse_recv), block, other_block,
         name="early", scratch=[pltpu.VMEM((2 * EARLY, D), BF)],
     )
-    *others, pre = tie(*others, pre)
+    *others, send_part = tie(*others, send_part)
     part = join(others[0], others[1], others[2])
     other_part = swap(part, SWAP_CORE)
     send_part, recv_part, node_new = call(

time: 60.2 us -> 60.7 us (level)
  transfers between devices with their start and end apart: 14 -> 14, of which waited for: 1 -> 2; matrix products, arithmetic and copies ran while one was open for 0% -> 0% of each run, Pallas kernels for 20% -> 20%
where the time goes in v9:
time: 60.7 us; the launch traced here: 60.5 us
  starting transfers between devices  27 us (44%)
  Pallas kernels  17.8 us (29%)
  blocking collectives  12.6 us (21%)
  between operations  1.12 us (2%)
  waiting for transfers between devices  1.05 us (2%)
  local copies, waits for them, and re-layouts  0.9 us (1%)
    pallas_call x9, Pallas kernels, call(): pl.pallas_call(kernel, out_shape=outs, in_specs=[spec if at in in_any els...  17.8 us
    ppermute x10, starting transfers between devices, shards(): swap = lambda rows, pairs: lax.ppermute(rows, 'patch', pairs)  14.2 us
    all_to_all x1, blocking collectives, shards(): parts = lax.all_to_all(sums.reshape(PATCHES, COARSE_ROWS, D), 'patch', 0, 0)  12.6 us
    ppermute x3, starting transfers between devices, shards(): lax.ppermute(near, ('group', 'patch'), to)  9.83 us
    ppermute x1, starting transfers between devices, shards(): pair = lax.ppermute(own, ('group', 'patch'), Z_PAIR)  3.03 us
  transfers between devices with their start and end apart: 14, of which 2 were waited for; matrix products, arithmetic and copies ran while one was open for 0% of the time, Pallas kernels for 20%

profile of v9, /device:TPU:1, one launch (start us, length us, event | category | flops | bytes accessed | tf_op | source)
XLA Modules:
  0.0 60.5 jit_solution(11025246858995142511)
XLA Ops:
  0.6 0.0 copy-start.4
  0.6 0.8 %slice.3 = bf16[8,512]{1,0:T(8,128)(2,1)S(1)} slice(bf16[512,512]{1,0:T(8,128)(2,1)} %node_in), slice={[0:8], [0:512]} | slice | bytes 16384 | tf_op jit(solution)/shard_map/slice | solution.py:321
  1.4 3.0 %collective-permute-start = (bf16[8,512]{1,0:T(8,128)(2,1)S(1)}, bf16[8,512]{1,0:T(8,128)(2,1)S(1)}, u32[]{:S(2)}, u32[]{:S(2)}) collective-permute-start(bf16[8,512]{1,0:T(8,128)(2,1)S(1)} %slice.3), channel_id=1, source_target_pairs={{0,33},{1,32},{2,35},{3,34},{4,37},{5,36},{6,39},{7,38},{8,41},{9,... | collective-permute-start | bytes 24584 | tf_op jit(solution)/shard_map/ppermute | solution.py:324
  4.5 1.6 %pick.1 = (bf16[128,512]{1,0:T(8,128)(2,1)S(1)}, bf16[128,512]{1,0:T(8,128)(2,1)S(1)}, bf16[512,512]{1,0:T(8,128)(2,1)S(1)}, bf16[1536,512]{1,0:T(8,128)(2,1)S(1)}) custom-call(s32[2,128]{1,0:T(2,128)} %bitcast.23, bf16[512,512]{1,0:T(8,128)(2,1)} %node_in, bf16[1536,512]{1,0:T(8,128)(2,1)} %w_in), custom_call_target="tpu_custom_call" | custom-call | flops 134217728 | bytes 4194304 | tf_op jit(solution)/shard_map/pick/pallas_call | solution.py:257
  6.1 0.0 collective-permute-done
  6.1 0.0 copy-start.3
  6.1 0.0 copy-start.5
  6.1 0.0 copy-start.6
  6.1 0.0 copy-start.7
  6.1 0.0 copy-start.10
  6.2 6.4 %collective-permute-start.3 = (bf16[16,512]{1,0:T(8,128)(2,1)S(1)}, bf16[16,512]{1,0:T(8,128)(2,1)S(1)}, u32[]{:S(2)}, u32[]{:S(2)}) collective-permute-start(bf16[16,512]{1,0:T(8,128)(2,1)S(1)} %pad_maximum_fusion.2), channel_id=1, source_target_pairs={{0,161},{1,160},{2,163},{3,162},{4,165},{5,164},{6,167},{7,166},{8... | collective-permute-start | bytes 49160 | tf_op jit(solution)/shard_map/ppermute | solution.py:334
  12.6 0.3 collective-permute-start.2
  12.8 3.2 %collective-permute-start.1 = (bf16[16,512]{1,0:T(8,128)(2,1)S(1)}, bf16[16,512]{1,0:T(8,128)(2,1)S(1)}, u32[]{:S(2)}, u32[]{:S(2)}) collective-permute-start(bf16[16,512]{1,0:T(8,128)(2,1)S(1)} %pad_maximum_fusion.2), channel_id=1, source_target_pairs={{0,225},{1,224},{2,227},{3,226},{4,229},{5,228},{6,231},{7,230},{8... | collective-permute-start | bytes 49160 | tf_op jit(solution)/shard_map/ppermute | solution.py:334
  16.0 0.1 collective-permute-start.7
  16.1 1.6 %collective-permute-start.8 = (bf16[128,512]{1,0:T(8,128)(2,1)S(1)}, bf16[128,512]{1,0:T(8,128)(2,1)S(1)}, u32[]{:S(2)}, u32[]{:S(2)}) collective-permute-start(bf16[128,512]{1,0:T(8,128)(2,1)S(1)} %get-tuple-element.84), channel_id=1, source_target_pairs={{0,31},{1,2},{2,1},{3,4},{4,3},{5,6},{6,5},{7,8},{8,7},{9,10},{10,... | collective-permute-start | bytes 393224 | tf_op jit(solution)/shard_map/ppermute | solution.py:315
  17.7 0.0 copy-done.4
  17.7 1.2 %project.1 = (bf16[1024,512]{1,0:T(8,128)(2,1)S(1)}, f32[1024,512]{1,0:T(8,128)S(1)}) custom-call(bf16[512,512]{1,0:T(8,128)(2,1)S(1)} %get-tuple-element.73.node_ref, bf16[1536,512]{1,0:T(8,128)(2,1)S(1)} %get-tuple-element.75.w_ref.w_in_ref, bf16[1024,512]{1,0:T(8,128)(2,1)S(1)} %copy-done.4), custom_call_target="tpu_custom_call" | custom-call | flops 1073741824 | bytes 4194304 | tf_op jit(solution)/shard_map/project/pallas_call | solution.py:257
  18.9 0.0 collective-permute-done.3
  19.0 0.0 collective-permute-done.2
  19.0 0.0 collective-permute-done.1
  19.0 2.7 %collective-permute-start.6 = (bf16[64,512]{1,0:T(8,128)(2,1)S(1)}, bf16[64,512]{1,0:T(8,128)(2,1)S(1)}, u32[]{:S(2)}, u32[]{:S(2)}) collective-permute-start(bf16[64,512]{1,0:T(8,128)(2,1)S(1)} %pad_maximum_fusion.1), channel_id=1, source_target_pairs={{0,16},{1,5},{2,18},{3,7},{4,20},{5,1},{6,22},{7,3},{8,24},{9,13},... | collective-permute-start | bytes 196616 | tf_op jit(solution)/shard_map/ppermute | solution.py:315
  21.7 1.1 %collective-permute-start.5 = (bf16[64,512]{1,0:T(8,128)(2,1)S(1)}, bf16[64,512]{1,0:T(8,128)(2,1)S(1)}, u32[]{:S(2)}, u32[]{:S(2)}) collective-permute-start(bf16[64,512]{1,0:T(8,128)(2,1)S(1)} %pad_maximum_fusion.1), channel_id=1, source_target_pairs={{0,24},{1,7},{2,26},{3,5},{4,28},{5,3},{6,30},{7,1},{8,16},{9,15},... | collective-permute-start | bytes 196616 | tf_op jit(solution)/shard_map/ppermute | solution.py:315
  22.8 0.0 collective-permute-start.4
  22.8 0.0 collective-permute-done.7.inner_ref
  22.8 0.0 collective-permute-done.8.outer_ref
  22.8 0.0 copy-done.3
  22.8 0.0 copy-done.5
  22.8 0.0 copy-done.6
  22.8 0.0 copy-done.7
  22.8 0.0 copy-done.10
  22.8 2.2 %fine_first.1 = (bf16[512,512]{1,0:T(8,128)(2,1)S(1)}, f32[512,512]{1,0:T(8,128)S(1)}, bf16[256,512]{1,0:T(8,128)(2,1)S(1)}) custom-call(bf16[1024,512]{1,0:T(8,128)(2,1)S(1)} %copy-done.3, s32[8,128]{1,0:T(8,128)S(1)} %bitcast.13, s32[8,128]{1,0:T(8,128)S(1)} %bitcast.15, bf16[1024,512]{1,0:T(8,128)(2,1)S(1)} %get-tuple-element.82.table_ref, ...), custom_call_target="tpu_custom_call" | custom-call | flops 2147483648 | bytes 4194304 | tf_op jit(solution)/shard_map/fine_first/pallas_call | solution.py:257
  25.0 0.0 collective-permute-done.6
  25.1 1.0 %collective-permute-done.5 = bf16[64,512]{1,0:T(8,128)(2,1)S(1)} collective-permute-done((bf16[64,512]{1,0:T(8,128)(2,1)S(1)}, bf16[64,512]{1,0:T(8,128)(2,1)S(1)}, u32[]{:S(2)}, u32[]{:S(2)}) %collective-permute-start.5) | collective-permute-done | bytes 65568 | tf_op jit(solution)/shard_map/ppermute | solution.py:315
  26.0 0.0 collective-permute-done.4
  26.1 2.8 %collective-permute-start.12 = (bf16[256,512]{1,0:T(8,128)(2,1)S(1)}, bf16[256,512]{1,0:T(8,128)(2,1)S(1)}, u32[]{:S(2)}, u32[]{:S(2)}) collective-permute-start(bf16[256,512]{1,0:T(8,128)(2,1)S(1)} %pad_maximum_fusion.mine_ref), channel_id=1, source_target_pairs={{0,4},{1,17},{2,6},{3,19},{4,0},{5,21},{6,2},{7,23},{8,12},{9,25},... | collective-permute-start | bytes 786440 | tf_op jit(solution)/shard_map/ppermute | solution.py:315
  28.9 1.0 %collective-permute-start.11 = (bf16[256,512]{1,0:T(8,128)(2,1)S(1)}, bf16[256,512]{1,0:T(8,128)(2,1)S(1)}, u32[]{:S(2)}, u32[]{:S(2)}) collective-permute-start(bf16[256,512]{1,0:T(8,128)(2,1)S(1)} %pad_maximum_fusion.mine_ref), channel_id=1, source_target_pairs={{0,6},{1,25},{2,4},{3,27},{4,2},{5,29},{6,0},{7,31},{8,14},{9,17},... | collective-permute-start | bytes 786440 | tf_op jit(solution)/shard_map/ppermute | solution.py:315
  29.9 0.0 collective-permute-start.10
  29.9 3.0 %collective-permute-start.9 = (bf16[256,512]{1,0:T(8,128)(2,1)S(1)}, bf16[256,512]{1,0:T(8,128)(2,1)S(1)}, u32[]{:S(2)}, u32[]{:S(2)}) collective-permute-start(bf16[256,512]{1,0:T(8,128)(2,1)S(1)} %pad_maximum_fusion.mine_ref), channel_id=1, source_target_pairs={{0,1},{1,0},{2,3},{3,2},{4,5},{5,4},{6,7},{7,6},{8,9},{9,8},{10,11... | collective-permute-start | bytes 786440 | tf_op jit(solution)/shard_map/ppermute | solution.py:315
  32.9 0.0 copy-start
  32.9 0.0 copy-start.1
  32.9 0.0 copy-start.2
  32.9 2.6 %fine_second.1 = (bf16[512,512]{1,0:T(8,128)(2,1)S(1)}, f32[512,512]{1,0:T(8,128)S(1)}, bf16[1024,512]{1,0:T(8,128)(2,1)}) custom-call(bf16[1024,512]{1,0:T(8,128)(2,1)S(1)} %copy-done.3, s32[8,128]{1,0:T(8,128)S(1)} %bitcast.14, s32[8,128]{1,0:T(8,128)S(1)} %bitcast.16, bf16[1024,512]{1,0:T(8,128)(2,1)S(1)} %get-tuple-element.82.table_ref, ...), custom_call_target="tpu_custom_call" | custom-call | flops 2147483648 | bytes 4194304 | tf_op jit(solution)/shard_map/fine_second/pallas_call | solution.py:257
  35.5 0.0 copy-done
  35.5 0.0 copy-done.1
  35.5 0.0 copy-done.2
  35.5 0.0 copy-start.8
  35.5 0.0 copy-start.9
  35.5 1.3 %node.1 = (bf16[512,512]{1,0:T(8,128)(2,1)S(1)}, f32[16,512]{1,0:T(8,128)S(1)}, f32[16,512]{1,0:T(8,128)S(1)}, bf16[1024,512]{1,0:T(8,128)(2,1)}) custom-call(bf16[512,512]{1,0:T(8,128)(2,1)S(1)} %get-tuple-element.73.node_ref, f32[512,512]{1,0:T(8,128)S(1)} %get-tuple-element.94.sum_ref, ...), custom_call_target="tpu_custom_call", output_to_operand_aliasing={{3}: (6, {})} | custom-call | flops 805306368 | bytes 4194304 | tf_op jit(solution)/shard_map/node/pallas_call | solution.py:257
  36.9 0.0 collective-permute-done.9.theirs_ref
  36.9 0.0 copy-done.8
  36.9 0.0 copy-done.9
  36.9 1.3 %early.1 = (s32[8,128]{1,0:T(8,128)S(1)}, s32[8,128]{1,0:T(8,128)S(1)}, bf16[1024,512]{1,0:T(8,128)(2,1)S(1)}, bf16[1024,512]{1,0:T(8,128)(2,1)S(1)}) custom-call(s32[8,128]{1,0:T(8,128)S(1)} %bitcast.17, s32[8,128]{1,0:T(8,128)S(1)} %bitcast.18, bf16[256,512]{1,0:T(8,128)(2,1)S(1)} %pad_maximum_fusion.mine_ref, ...), custom_call_target="tpu_custom_call" | custom-call | flops 2147483648 | bytes 4194304 | tf_op jit(solution)/shard_map/early/pallas_call | solution.py:257
  38.2 0.0 collective-permute-done.12
  38.3 0.0 collective-permute-done.11
  38.3 0.0 collective-permute-done.10
  38.4 1.9 %collective-permute-start.13 = (bf16[768,512]{1,0:T(8,128)(2,1)S(1)}, bf16[768,512]{1,0:T(8,128)(2,1)S(1)}, u32[]{:S(2)}, u32[]{:S(2)}) collective-permute-start(bf16[768,512]{1,0:T(8,128)(2,1)S(1)} %constant_dynamic-update-slice_fusion.table_ref), channel_id=1, source_target_pairs={{0,1},{1,0},{2,3},{3,2},{4,5},{5,4},{6,7},{7,6},{8,9},{9,8},{10,11... | collective-permute-start | bytes 2359304 | tf_op jit(solution)/shard_map/ppermute | solution.py:315
  40.2 1.9 %gather.1 = (bf16[1024,512]{1,0:T(8,128)(2,1)S(1)}, bf16[1024,512]{1,0:T(8,128)(2,1)S(1)}, bf16[512,512]{1,0:T(8,128)(2,1)}) custom-call(s32[8,128]{1,0:T(8,128)S(1)} %get-tuple-element.102.send_ref, s32[8,128]{1,0:T(8,128)S(1)} %get-tuple-element.103.recv_ref, bf16[1024,512]{1,0:T(8,128)(2,1)S(1)} %get-tuple-element.108.send_part, ...), custom_call_target="tpu_custom_call" | custom-call | flops 2147483648 | bytes 4194304 | tf_op jit(solution)/shard_map/gather/pallas_call | solution.py:257
  42.1 0.1 collective-permute-done.13.table_ref
  42.1 4.4 %coarse.1 = (bf16[1024,512]{1,0:T(8,128)(2,1)S(1)}, bf16[256,512]{1,0:T(8,128)(2,1)S(1)}) custom-call(bf16[1024,512]{1,0:T(8,128)(2,1)S(1)} %copy-done.4, f32[1024,512]{1,0:T(8,128)S(1)} %get-tuple-element.100.pre_ref, s32[8,128]{1,0:T(8,128)S(1)} %get-tuple-element.102.send_ref, s32[8,128]{1,0:T(8,128)S(1)} %get-tuple-element.103.recv_ref, ...), custom_call_target="tpu_custom_call" | custom-call | flops 4294967296 | bytes 4194304 | tf_op jit(solution)/shard_map/coarse/pallas_call | solution.py:257
  46.6 12.6 %all_to_all.5 = bf16[32,8,512]{2,1,0:T(8,128)(2,1)S(1)} all-to-all(bf16[32,8,512]{2,1,0:T(8,128)(2,1)S(1)} %bitcast.10), channel_id=1, replica_groups=mesh['group'=8,'patch'=32] {'patch'}, dimensions={0} | all-to-all | bytes 524288 | tf_op jit(solution)/shard_map/all_to_all | solution.py:390
  59.2 1.2 %tail.1 = (bf16[512,512]{1,0:T(8,128)(2,1)}, bf16[1024,512]{1,0:T(8,128)(2,1)}) custom-call(bf16[512,512]{1,0:T(8,128)(2,1)S(1)} %get-tuple-element.73.node_ref, f32[16,512]{1,0:T(8,128)S(1)} %get-tuple-element.98.sum_ref, f32[16,512]{1,0:T(8,128)S(1)} %get-tuple-element.99.pre_ref, bf16[256,512]{1,0:T(8,128)(2,1)S(1)} %bitcast.9, ...), custom_call_target="tpu_custom_call", output_to_operand_aliasing={{0}: (8, {})} | custom-call | flops 25165824 | bytes 4194304 | tf_op jit(solution)/shard_map/tail/pallas_call | solution.py:257
  (6 shorter events, 0.1 us)
Async XLA Ops:
  0.6 17.1 %copy-start.4 = (bf16[1024,512]{1,0:T(8,128)(2,1)S(1)}, bf16[1024,512]{1,0:T(8,128)(2,1)}, u32[]{:S(2)}) copy-start(bf16[1024,512]{1,0:T(8,128)(2,1)} %edge_ref.7) | copy-start | bytes 3145732
  1.4 4.7 %collective-permute-start = (bf16[8,512]{1,0:T(8,128)(2,1)S(1)}, bf16[8,512]{1,0:T(8,128)(2,1)S(1)}, u32[]{:S(2)}, u32[]{:S(2)}) collective-permute-start(bf16[8,512]{1,0:T(8,128)(2,1)S(1)} %slice.3), channel_id=1, source_target_pairs={{0,33},{1,32},{2,35},{3,34},{4,37},{5,36},{6,39},{7,38},{8,41},{9,... | collective-permute-start | bytes 24584 | tf_op jit(solution)/shard_map/ppermute | solution.py:324
  6.1 16.7 %copy-start.3 = (bf16[1024,512]{1,0:T(8,128)(2,1)S(1)}, bf16[1024,512]{1,0:T(8,128)(2,1)}, u32[]{:S(2)}) copy-start(bf16[1024,512]{1,0:T(8,128)(2,1)} %edge_ref.6) | copy-start | bytes 3145732
  6.1 16.7 %copy-start.5 = (bf16[512,512]{1,0:T(8,128)(2,1)S(1)}, bf16[512,512]{1,0:T(8,128)(2,1)}, u32[]{:S(2)}) copy-start(bf16[512,512]{1,0:T(8,128)(2,1)} %w_out_ref.8) | copy-start | bytes 1572868
  6.1 16.7 %copy-start.6 = (s32[1024]{0:T(1024)S(1)}, s32[1024]{0:T(1024)}, u32[]{:S(2)}) copy-start(s32[1024]{0:T(1024)} %param.16) | copy-start | bytes 12292
  6.1 16.7 %copy-start.7 = (s32[1024]{0:T(1024)S(1)}, s32[1024]{0:T(1024)}, u32[]{:S(2)}) copy-start(s32[1024]{0:T(1024)} %param.17) | copy-start | bytes 12292
  6.1 16.7 %copy-start.10 = (f32[512]{0:T(512)S(1)}, f32[512]{0:T(512)}, u32[]{:S(2)}) copy-start(f32[512]{0:T(512)} %param.24) | copy-start | bytes 6148
  6.2 12.8 %collective-permute-start.3 = (bf16[16,512]{1,0:T(8,128)(2,1)S(1)}, bf16[16,512]{1,0:T(8,128)(2,1)S(1)}, u32[]{:S(2)}, u32[]{:S(2)}) collective-permute-start(bf16[16,512]{1,0:T(8,128)(2,1)S(1)} %pad_maximum_fusion.2), channel_id=1, source_target_pairs={{0,161},{1,160},{2,163},{3,162},{4,165},{5,164},{6,167},{7,166},{8... | collective-permute-start | bytes 49160 | tf_op jit(solution)/shard_map/ppermute | solution.py:334
  12.6 6.4 %collective-permute-start.2 = (bf16[16,512]{1,0:T(8,128)(2,1)S(1)}, bf16[16,512]{1,0:T(8,128)(2,1)S(1)}, u32[]{:S(2)}, u32[]{:S(2)}) collective-permute-start(bf16[16,512]{1,0:T(8,128)(2,1)S(1)} %pad_maximum_fusion.2), channel_id=1, source_target_pairs={{0,193},{1,192},{2,195},{3,194},{4,197},{5,196},{6,199},{7,198},{8... | collective-permute-start | bytes 49160 | tf_op jit(solution)/shard_map/ppermute | solution.py:334
  12.8 6.1 %collective-permute-start.1 = (bf16[16,512]{1,0:T(8,128)(2,1)S(1)}, bf16[16,512]{1,0:T(8,128)(2,1)S(1)}, u32[]{:S(2)}, u32[]{:S(2)}) collective-permute-start(bf16[16,512]{1,0:T(8,128)(2,1)S(1)} %pad_maximum_fusion.2), channel_id=1, source_target_pairs={{0,225},{1,224},{2,227},{3,226},{4,229},{5,228},{6,231},{7,230},{8... | collective-permute-start | bytes 49160 | tf_op jit(solution)/shard_map/ppermute | solution.py:334
  16.0 6.8 %collective-permute-start.7 = (bf16[128,512]{1,0:T(8,128)(2,1)S(1)}, bf16[128,512]{1,0:T(8,128)(2,1)S(1)}, u32[]{:S(2)}, u32[]{:S(2)}) collective-permute-start(bf16[128,512]{1,0:T(8,128)(2,1)S(1)} %get-tuple-element.83), channel_id=1, source_target_pairs={{0,1},{1,0},{2,3},{3,2},{4,5},{5,4},{6,7},{7,6},{8,9},{9,8},{10,11... | collective-permute-start | bytes 393224 | tf_op jit(solution)/shard_map/ppermute | solution.py:315
  16.1 6.7 %collective-permute-start.8 = (bf16[128,512]{1,0:T(8,128)(2,1)S(1)}, bf16[128,512]{1,0:T(8,128)(2,1)S(1)}, u32[]{:S(2)}, u32[]{:S(2)}) collective-permute-start(bf16[128,512]{1,0:T(8,128)(2,1)S(1)} %get-tuple-element.84), channel_id=1, source_target_pairs={{0,31},{1,2},{2,1},{3,4},{4,3},{5,6},{6,5},{7,8},{8,7},{9,10},{10,... | collective-permute-start | bytes 393224 | tf_op jit(solution)/shard_map/ppermute | solution.py:315
  19.0 6.1 %collective-permute-start.6 = (bf16[64,512]{1,0:T(8,128)(2,1)S(1)}, bf16[64,512]{1,0:T(8,128)(2,1)S(1)}, u32[]{:S(2)}, u32[]{:S(2)}) collective-permute-start(bf16[64,512]{1,0:T(8,128)(2,1)S(1)} %pad_maximum_fusion.1), channel_id=1, source_target_pairs={{0,16},{1,5},{2,18},{3,7},{4,20},{5,1},{6,22},{7,3},{8,24},{9,13},... | collective-permute-start | bytes 196616 | tf_op jit(solution)/shard_map/ppermute | solution.py:315
  21.7 4.3 %collective-permute-start.5 = (bf16[64,512]{1,0:T(8,128)(2,1)S(1)}, bf16[64,512]{1,0:T(8,128)(2,1)S(1)}, u32[]{:S(2)}, u32[]{:S(2)}) collective-permute-start(bf16[64,512]{1,0:T(8,128)(2,1)S(1)} %pad_maximum_fusion.1), channel_id=1, source_target_pairs={{0,24},{1,7},{2,26},{3,5},{4,28},{5,3},{6,30},{7,1},{8,16},{9,15},... | collective-permute-start | bytes 196616 | tf_op jit(solution)/shard_map/ppermute | solution.py:315
  22.8 3.3 %collective-permute-start.4 = (bf16[64,512]{1,0:T(8,128)(2,1)S(1)}, bf16[64,512]{1,0:T(8,128)(2,1)S(1)}, u32[]{:S(2)}, u32[]{:S(2)}) collective-permute-start(bf16[64,512]{1,0:T(8,128)(2,1)S(1)} %pad_maximum_fusion.1), channel_id=1, source_target_pairs={{0,8},{1,3},{2,10},{3,1},{4,12},{5,7},{6,14},{7,5},{8,0},{9,11},{1... | collective-permute-start | bytes 196616 | tf_op jit(solution)/shard_map/ppermute | solution.py:315
  26.1 12.2 %collective-permute-start.12 = (bf16[256,512]{1,0:T(8,128)(2,1)S(1)}, bf16[256,512]{1,0:T(8,128)(2,1)S(1)}, u32[]{:S(2)}, u32[]{:S(2)}) collective-permute-start(bf16[256,512]{1,0:T(8,128)(2,1)S(1)} %pad_maximum_fusion.mine_ref), channel_id=1, source_target_pairs={{0,4},{1,17},{2,6},{3,19},{4,0},{5,21},{6,2},{7,23},{8,12},{9,25},... | collective-permute-start | bytes 786440 | tf_op jit(solution)/shard_map/ppermute | solution.py:315
  28.9 9.4 %collective-permute-start.11 = (bf16[256,512]{1,0:T(8,128)(2,1)S(1)}, bf16[256,512]{1,0:T(8,128)(2,1)S(1)}, u32[]{:S(2)}, u32[]{:S(2)}) collective-permute-start(bf16[256,512]{1,0:T(8,128)(2,1)S(1)} %pad_maximum_fusion.mine_ref), channel_id=1, source_target_pairs={{0,6},{1,25},{2,4},{3,27},{4,2},{5,29},{6,0},{7,31},{8,14},{9,17},... | collective-permute-start | bytes 786440 | tf_op jit(solution)/shard_map/ppermute | solution.py:315
  29.9 8.4 %collective-permute-start.10 = (bf16[256,512]{1,0:T(8,128)(2,1)S(1)}, bf16[256,512]{1,0:T(8,128)(2,1)S(1)}, u32[]{:S(2)}, u32[]{:S(2)}) collective-permute-start(bf16[256,512]{1,0:T(8,128)(2,1)S(1)} %pad_maximum_fusion.mine_ref), channel_id=1, source_target_pairs={{0,2},{1,9},{2,0},{3,11},{4,6},{5,13},{6,4},{7,15},{8,10},{9,1},{1... | collective-permute-start | bytes 786440 | tf_op jit(solution)/shard_map/ppermute | solution.py:315
  29.9 7.0 %collective-permute-start.9 = (bf16[256,512]{1,0:T(8,128)(2,1)S(1)}, bf16[256,512]{1,0:T(8,128)(2,1)S(1)}, u32[]{:S(2)}, u32[]{:S(2)}) collective-permute-start(bf16[256,512]{1,0:T(8,128)(2,1)S(1)} %pad_maximum_fusion.mine_ref), channel_id=1, source_target_pairs={{0,1},{1,0},{2,3},{3,2},{4,5},{5,4},{6,7},{7,6},{8,9},{9,8},{10,11... | collective-permute-start | bytes 786440 | tf_op jit(solution)/shard_map/ppermute | solution.py:315
  32.9 2.6 %copy-start = (bf16[1024,512]{1,0:T(8,128)(2,1)S(1)}, bf16[1024,512]{1,0:T(8,128)(2,1)}, u32[]{:S(2)}) copy-start(bf16[1024,512]{1,0:T(8,128)(2,1)} %w_in_ref.3) | copy-start | bytes 3145732
  32.9 2.6 %copy-start.1 = (bf16[512,512]{1,0:T(8,128)(2,1)S(1)}, bf16[512,512]{1,0:T(8,128)(2,1)}, u32[]{:S(2)}) copy-start(bf16[512,512]{1,0:T(8,128)(2,1)} %w_out_ref.9) | copy-start | bytes 1572868
  32.9 2.6 %copy-start.2 = (f32[512]{0:T(512)S(1)}, f32[512]{0:T(512)}, u32[]{:S(2)}) copy-start(f32[512]{0:T(512)} %param.27) | copy-start | bytes 6148
  35.5 1.4 %copy-start.8 = (s32[1024]{0:T(1024)S(1)}, s32[1024]{0:T(1024)}, u32[]{:S(2)}) copy-start(s32[1024]{0:T(1024)} %param.20) | copy-start | bytes 12292
  35.5 1.4 %copy-start.9 = (s32[1024]{0:T(1024)S(1)}, s32[1024]{0:T(1024)}, u32[]{:S(2)}) copy-start(s32[1024]{0:T(1024)} %param.21) | copy-start | bytes 12292
  38.4 3.8 %collective-permute-start.13 = (bf16[768,512]{1,0:T(8,128)(2,1)S(1)}, bf16[768,512]{1,0:T(8,128)(2,1)S(1)}, u32[]{:S(2)}, u32[]{:S(2)}) collective-permute-start(bf16[768,512]{1,0:T(8,128)(2,1)S(1)} %constant_dynamic-update-slice_fusion.table_ref), channel_id=1, source_target_pairs={{0,1},{1,0},{2,3},{3,2},{4,5},{5,4},{6,7},{7,6},{8,9},{9,8},{10,11... | collective-permute-start | bytes 2359304 | tf_op jit(solution)/shard_map/ppermute | solution.py:315
